TPU v7x, 32 devices: a whole 2x2x4 slice. The times are simulated.
32 devices in a mesh: wide: 4 (over y, x), narrow: 8 (over z, core).
Axes of the slice: x: 2, y: 2, z: 4, core: 2. Of those that a mesh axis runs over, the one named last changes fastest.
Arguments:
- messages: bfloat16 [49152, 512], P(('wide', 'narrow')), may hold values from -6 to 6
- reverse_position: int32 [49152], P(('wide', 'narrow')), may hold values from 0 to 383, as said below
- route_slot: int32 [49152], P(('wide', 'narrow')), may hold values from 0 to 3071, as said below
- atom_slots: int32 [49152], P(('wide', 'narrow')), may hold values from 0 to 3071, as said below
- angles: bfloat16 [1536, 1024], P(('wide', 'narrow')), may hold values from -1 to 1
- weight_message: bfloat16 [2, 512, 512], replicated, may hold values from -0.25 to 0.25
- weight_reverse: bfloat16 [2, 512, 512], replicated, may hold values from -0.25 to 0.25
- weight_combine: bfloat16 [2, 512, 512], replicated, may hold values from -0.25 to 0.25
- weight_inner: bfloat16 [2, 512, 512], replicated, may hold values from -0.25 to 0.25
- weight_outer: bfloat16 [2, 512, 512], replicated, may hold values from -0.25 to 0.25
- weight_lift: bfloat16 [2, 512, 512], replicated, may hold values from -0.25 to 0.25
- weight_expand: bfloat16 [2, 512, 512], replicated, may hold values from -0.25 to 0.25
- weight_reduce: bfloat16 [2, 512, 512], replicated, may hold values from -0.25 to 0.25
Outputs:
- updated: bfloat16 [49152, 512], P(('wide', 'narrow'))
Inputs may be any that keep to these rules, and one draw needn't show every extreme that they name: With e written as ((w * 8 + n) * 4 + s) * 384 + i, the reverse edge of e is ((s * 8 + n) * 4 + w) * 384 + reverse_position[e]; the reverse of the reverse is e, no edge is its own reverse, and the source atom of e is the target atom of its reverse. The target atom of an edge of device block w * 8 + n lies in atom block w * 8 + o (atom j in block j // 48), and route_slot = o * 384 + c with c distinct among the edges of one device block that have the same o. In every device block 384 edges have one o, none another o, and 192 each of the others; within each sub-block of the device block, 96 edges have that first o, none the second, and 48 each of the others. `atom_slots`: entry j * 32 + q, for atom j in block w * 8 + o, names the q-th incoming edge of j as n * 384 + c: the edge of device block w * 8 + n whose route_slot is o * 384 + c. Every atom has exactly 32 incoming edges, every edge is named once, and entries q from s * 8 to (s + 1) * 8 - 1 name edges of sub-block s.
All inputs are finite; a program needn't handle non-finite values.
Results may differ from a plain program's by a relative error of at most 0.015.
Values may be sent and summed in bfloat16 or wider, within the bound.
No kernel may reach another device: no remote copies, remote signals or barrier semaphores. Data moves between devices by JAX's collectives and lax.ppermute only.
A program may use at most 128 MiB of HBM per device.

v0:
```python
import functools

import jax
import jax.numpy as jnp
from jax import lax
from jax.experimental import pallas as pl
from jax.experimental.pallas import tpu as pltpu
from jax.sharding import PartitionSpec as P

SLOTS = 32
BLOCKS = 2
LANES = 128
HALF = LANES // 2
GROUP = 8


ROOT_HALF = 0.7071067811865476


def project(operand, weight):
    return jnp.dot(operand, weight, preferred_element_type=jnp.float32)


def residual(previous, branch):
    return ((previous.astype(jnp.float32) + branch) * ROOT_HALF).astype(jnp.bfloat16)


def reverse_edges(values, partner_rows):
    exchanged = lax.all_to_all(values, "wide", split_axis=0, concat_axis=0, tiled=True)
    return jnp.take(exchanged, partner_rows, axis=0)


def edge_front(current, reverse, weights, section_index):
    hidden = jax.nn.silu(
        project(current, weights[0][section_index]) + project(reverse, weights[1][section_index])
    ).astype(jnp.bfloat16)
    first_res = residual(current, project(hidden, weights[2][section_index]))
    inner_value = jax.nn.silu(project(first_res, weights[3][section_index])).astype(jnp.bfloat16)
    return residual(first_res, jax.nn.silu(project(inner_value, weights[4][section_index])))


def edge_back(second, turned, weights, section_index):
    third_res = residual(second, jax.nn.silu(project(turned, weights[5][section_index])))
    expand = jax.nn.silu(project(third_res, weights[6][section_index])).astype(jnp.bfloat16)
    return residual(third_res, jax.nn.silu(project(expand, weights[7][section_index])))


def owners_mix(second, route_slot, atom_slots, mixing):
    features = second.shape[1]
    buffer_rows = 2 * second.shape[0]
    outgoing = jnp.zeros((buffer_rows, features), jnp.bfloat16).at[route_slot].set(second)
    received = lax.all_to_all(outgoing, "narrow", split_axis=0, concat_axis=0, tiled=True)
    gathered = jnp.take(received, atom_slots, axis=0).reshape(mixing.shape[0], SLOTS, features)
    mixed_rows = jnp.einsum(
        "apq,aqd->apd", mixing, gathered, preferred_element_type=jnp.float32
    ).astype(jnp.bfloat16)
    return mixed_rows.reshape(-1, features)


def back_to_edges(mixed_flat, route_slot, atom_slots):
    features = mixed_flat.shape[1]
    buffer_rows = 2 * route_slot.shape[0]
    answer = jnp.zeros((buffer_rows, features), jnp.bfloat16).at[atom_slots].set(mixed_flat)
    incoming = lax.all_to_all(answer, "narrow", split_axis=0, concat_axis=0, tiled=True)
    return jnp.take(incoming, route_slot, axis=0)


def general_local(messages, reverse_position, route_slot, atom_slots, angles, weights):
    edge_rows = messages.shape[0]
    sub_rows = edge_rows // lax.axis_size("wide")
    partner_rows = jnp.arange(edge_rows, dtype=jnp.int32) // sub_rows * sub_rows + reverse_position
    mixing = angles.reshape(angles.shape[0], SLOTS, SLOTS)
    current = messages
    for section_index in range(BLOCKS):
        reverse = reverse_edges(current, partner_rows)
        second = edge_front(current, reverse, weights, section_index)
        mixed_flat = owners_mix(second, route_slot, atom_slots, mixing)
        returned = back_to_edges(mixed_flat, route_slot, atom_slots)
        turned = reverse_edges(returned, partner_rows)
        current = edge_back(second, turned, weights, section_index)
    return current


def silu(value):
    return 0.5 * value * (1.0 + jnp.tanh(0.5 * value))


def dot(left, right):
    return jnp.dot(left, right, preferred_element_type=jnp.float32)


def halve(previous, branch):
    return ((previous.astype(jnp.float32) + branch) * ROOT_HALF).astype(jnp.bfloat16)


def iotas(size):
    shape = (size, size)
    return lax.broadcasted_iota(jnp.int32, shape, 0), lax.broadcasted_iota(jnp.int32, shape, 1)


def as_column(row, rows_iota, lanes_iota):
    return jnp.sum(jnp.where(rows_iota == lanes_iota, row, 0), axis=1, keepdims=True)


def one_hot(mask):
    return jnp.where(mask, 1.0, 0.0).astype(jnp.bfloat16)


def front_kernel(own, count, where_ref, cur_ref, back_ref, rank_ref, wm, wr, wc, wi, wo, *refs):
    recv_refs, (second_ref, packed_ref, reverse_ref) = refs[:-3], refs[-3:]
    rows_iota, lanes_iota = iotas(cur_ref.shape[1])
    partner = as_column(back_ref[0], rows_iota, lanes_iota)
    hot = one_hot(partner == lanes_iota)
    sources = ([cur_ref.at[0]] if own else []) + list(recv_refs)
    for index in range(count):

        @pl.when(pl.program_id(0) == index)
        def _():
            reverse_ref[...] = dot(hot, sources[index][...]).astype(jnp.bfloat16)

    current = cur_ref[0]
    hidden = silu(dot(current, wm[0]) + dot(reverse_ref[...], wr[0])).astype(jnp.bfloat16)
    first_res = halve(current, dot(hidden, wc[0]))
    inner = silu(dot(first_res, wi[0])).astype(jnp.bfloat16)
    second = halve(first_res, silu(dot(inner, wo[0])))
    second_ref[0] = second
    ordered = dot(one_hot(rows_iota == rank_ref[0]), second)
    half = ordered.shape[0] // 2
    low = lax.broadcasted_iota(jnp.int32, (half, LANES), 1) < HALF
    for tile in range(ordered.shape[1] // LANES):
        top = ordered[:half, tile * LANES : (tile + 1) * LANES]
        bottom = ordered[half:, tile * LANES : (tile + 1) * LANES]
        packed_ref[2 * tile, 0] = jnp.where(low, top, pltpu.roll(bottom, HALF, 1)).astype(jnp.bfloat16)
        packed_ref[2 * tile + 1, 0] = jnp.where(low, pltpu.roll(top, HALF, 1), bottom).astype(jnp.bfloat16)


def back_kernel(layout, where_ref, second_ref, rank_ref, wl, we, wd, *refs):
    out_ref, ordered_ref = refs[-2:]
    rows_iota, lanes_iota = iotas(second_ref.shape[1])
    half = rows_iota.shape[0] // 2
    low = lax.broadcasted_iota(jnp.int32, (half, LANES), 1) < HALF
    for index, (array, side) in enumerate(layout):

        @pl.when(pl.program_id(0) == index)
        def _():
            for tile in range(second_ref.shape[2] // LANES):
                lanes = slice(tile * LANES, (tile + 1) * LANES)
                even = refs[array][2 * tile, side].astype(jnp.float32)
                odd = refs[array][2 * tile + 1, side].astype(jnp.float32)
                top = jnp.where(low, even, pltpu.roll(odd, HALF, 1))
                bottom = jnp.where(low, pltpu.roll(even, HALF, 1), odd)
                ordered_ref[:half, lanes] = top.astype(jnp.bfloat16)
                ordered_ref[half:, lanes] = bottom.astype(jnp.bfloat16)

    source = as_column(rank_ref[0], rows_iota, lanes_iota)
    turned = dot(one_hot(source == lanes_iota), ordered_ref[...]).astype(jnp.bfloat16)
    third_res = halve(second_ref[0], silu(dot(turned, wl[0])))
    expand = silu(dot(third_res, we[0])).astype(jnp.bfloat16)
    out_ref[0] = halve(third_res, silu(dot(expand, wd[0])))


def table_kernel(chunks, places_ref, wide_ref, entry_ref, angles_ref, take_ref, give_ref, blocks_ref):
    sides, _, size = entry_ref.shape[1:]
    count = sides // chunks
    group_id = wide_ref[0]
    rows_iota, lanes_iota = iotas(size)
    for side in range(sides):
        row = entry_ref[0, side]
        column = as_column(row, rows_iota, lanes_iota)
        rank_column = jnp.sum(jnp.where(row < column, 1, 0), axis=1, keepdims=True)
        rank_row = jnp.sum(jnp.where(column < row, 1, 0), axis=0, keepdims=True)
        take_ref[0, side] = one_hot(rank_column == lanes_iota)
        give_ref[0, side] = one_hot(rows_iota == rank_row)
    span = GROUP * SLOTS
    strip = span // sides
    rows_iota, lanes_iota = iotas(span)
    own = rows_iota % GROUP == lanes_iota % GROUP
    spread_rows = lax.broadcasted_iota(jnp.int32, (SLOTS, span), 0)
    spread_lanes = lax.broadcasted_iota(jnp.int32, (SLOTS, span), 1)
    place = spread_lanes // strip
    side_at = (place // count + place % count * chunks) ^ group_id
    spread = one_hot(side_at * (SLOTS // sides) + spread_lanes % strip // GROUP == spread_rows)
    for group in range(angles_ref.shape[1] // GROUP):
        local = angles_ref[0, group * GROUP : (group + 1) * GROUP, :].astype(jnp.float32)
        stacked = jnp.concatenate(
            [local[:, p * SLOTS : (p + 1) * SLOTS] for p in range(SLOTS)], axis=0
        ).astype(jnp.bfloat16)
        block = jnp.where(own, dot(stacked, spread), 0.0).astype(jnp.bfloat16)
        for side in range(sides):
            offset = group_id ^ side
            to = pl.multiple_of((offset % chunks * count + offset // chunks) * strip, strip)
            blocks_ref[0, group, pl.ds(to, strip), :] = block[side * strip : (side + 1) * strip]


def gather_kernel(owner_ref, place_ref, recv_ref, take_ref, out_ref, ins):
    step = pl.program_id(0)
    sides = take_ref.shape[1]
    devices = recv_ref.shape[0]
    unit = ins.shape[3]
    pairs = devices // 2

    @pl.when(step == 0)
    def _():
        @pl.loop(0, devices)
        def _(source):
            for index in range(devices):
                owner = owner_ref[source, index]
                place = place_ref[source, index]
                at = (index % pairs) * unit
                for side in range(sides):
                    block = recv_ref[source, side, at : at + unit, :]
                    if index >= pairs:
                        block = pltpu.roll(block.astype(jnp.float32), HALF, 1).astype(jnp.bfloat16)
                    ins[side, owner, place] = block

    for side in range(sides):
        operand = ins[side, step].reshape(devices * unit, LANES)
        out_ref[0, side] = dot(take_ref[0, side], operand).astype(jnp.bfloat16)


def mix_kernel(chunk, chunks, owner_ref, place_ref, give_ref, blocks_ref, *refs):
    gathered_refs, out_refs, outs = refs[:chunks], refs[chunks:-1], refs[-1]
    step = pl.program_id(0)
    count = give_ref.shape[1]
    devices = outs.shape[1]
    unit = outs.shape[3]
    groups = blocks_ref.shape[1]
    strip = blocks_ref.shape[2] // (chunks * count)
    pairs = devices // 2
    first = chunk * count * strip
    mixed = []
    for group in range(groups):
        operand = jnp.concatenate(
            [
                ref[0, index, group * strip : (group + 1) * strip, :]
                for ref in gathered_refs
                for index in range(count)
            ],
            axis=0,
        )
        mixing = blocks_ref[0, group, first : first + count * strip, :]
        mixed.append(dot(mixing, operand).astype(jnp.bfloat16))
    for side in range(count):
        operand = jnp.concatenate(
            [part[side * strip : (side + 1) * strip] for part in mixed], axis=0
        )
        outs[side, step] = (
            dot(give_ref[0, side], operand).astype(jnp.bfloat16).reshape(devices, unit, LANES)
        )

    @pl.when(step == pl.num_programs(0) - 1)
    def _():
        low = lax.broadcasted_iota(jnp.int32, (unit, LANES), 1) < HALF

        @pl.loop(0, devices)
        def _(source):
            for index in range(pairs):
                owner = owner_ref[source, index]
                place = place_ref[source, index]
                owner_far = owner_ref[source, index + pairs]
                place_far = place_ref[source, index + pairs]
                rows = slice(index * unit, (index + 1) * unit)
                for side in range(count):
                    near = outs[side, owner, place].astype(jnp.float32)
                    far = outs[side, owner_far, place_far].astype(jnp.float32)
                    joined = jnp.where(low, near, pltpu.roll(far, HALF, 1)).astype(jnp.bfloat16)
                    if len(out_refs) == 1:
                        out_refs[0][source, side, rows, :] = joined
                    else:
                        out_refs[side][source, 0, rows, :] = joined


VMEM_BYTES = 60 * 1024 * 1024


def params():
    return pltpu.CompilerParams(vmem_limit_bytes=VMEM_BYTES)


def cost(flops, moved, waves=0):
    return pl.CostEstimate(flops=flops, bytes_accessed=moved, transcendentals=waves)


def whole_spec(array):
    zeros = (0,) * array.ndim
    return pl.BlockSpec(array.shape, lambda i, *_: zeros)


def weight_spec(section, features):
    return pl.BlockSpec((1, features, features), lambda i, *_: (section, 0, 0))


def run_front(current, where, received, own, chunk, back_rows, rank_rows, weights, section, narrow):
    _, rows, features = current.shape
    count = where.shape[0]
    edge_spec = pl.BlockSpec((1, rows, features), lambda i, where: (i, 0, 0))
    row_spec = pl.BlockSpec((1, 1, rows), lambda i, where: (chunk * count + i, 0, 0))
    return pl.pallas_call(
        functools.partial(front_kernel, own, count),
        grid_spec=pltpu.PrefetchScalarGridSpec(
            num_scalar_prefetch=1,
            grid=(count,),
            in_specs=[
                pl.BlockSpec((1, rows, features), lambda i, where: (where[i], 0, 0)),
                row_spec,
                row_spec,
            ]
            + [weight_spec(section, features)] * 5
            + [whole_spec(array) for array in received],
            out_specs=[
                edge_spec,
                pl.BlockSpec((narrow, 1, rows // 2, LANES), lambda i, where: (0, i, 0, 0)),
            ],
            scratch_shapes=[pltpu.VMEM((rows, features), jnp.bfloat16)],
        ),
        out_shape=[
            jax.ShapeDtypeStruct((count, rows, features), jnp.bfloat16),
            jax.ShapeDtypeStruct((narrow, count, rows // 2, LANES), jnp.bfloat16),
        ],
        compiler_params=params(),
        cost_estimate=cost(12 * count * rows * features**2, 8 * count * rows * features),
        name="front",
    )(where, current, back_rows, rank_rows, *weights[:5], *received)


def run_back(second, packed, layout, chunk, rank_rows, weights, section, where, total, target):
    count, rows, features = second.shape
    edge_spec = pl.BlockSpec((1, rows, features), lambda i, where: (i, 0, 0))
    extra = [] if target is None else [target]
    return pl.pallas_call(
        functools.partial(back_kernel, layout),
        grid_spec=pltpu.PrefetchScalarGridSpec(
            num_scalar_prefetch=1,
            grid=(count,),
            in_specs=[
                edge_spec,
                pl.BlockSpec((1, 1, rows), lambda i, where: (chunk * count + i, 0, 0)),
            ]
            + [weight_spec(section, features)] * 3
            + [whole_spec(array) for array in packed]
            + [pl.BlockSpec(memory_space=pl.ANY)] * len(extra),
            out_specs=pl.BlockSpec((1, rows, features), lambda i, where: (where[i], 0, 0)),
            scratch_shapes=[pltpu.VMEM((rows, features), jnp.bfloat16)],
        ),
        out_shape=jax.ShapeDtypeStruct((total, rows, features), jnp.bfloat16),
        input_output_aliases={6 + len(packed): 0} if extra else {},
        compiler_params=params(),
        cost_estimate=cost(8 * count * rows * features**2, 6 * count * rows * features),
        name="back",
    )(where, second, rank_rows, *weights[5:], *packed, *extra)


def run_tables(places, group_id, entries, angles, chunks):
    owners, sides, _, rows = entries.shape
    atoms = angles.shape[1]
    groups = atoms // GROUP
    span = GROUP * SLOTS
    hot = jax.ShapeDtypeStruct((owners, sides, rows, rows), jnp.bfloat16)
    hot_spec = pl.BlockSpec((1, sides, rows, rows), lambda i, *_: (i, 0, 0, 0))
    return pl.pallas_call(
        functools.partial(table_kernel, chunks),
        grid_spec=pltpu.PrefetchScalarGridSpec(
            num_scalar_prefetch=2,
            grid=(owners,),
            in_specs=[
                pl.BlockSpec((1, sides, 1, rows), lambda i, *_: (i, 0, 0, 0)),
                pl.BlockSpec((1, atoms, angles.shape[2]), lambda i, places, _: (places[i], 0, 0)),
            ],
            out_specs=[
                hot_spec,
                hot_spec,
                pl.BlockSpec((1, groups, span, span), lambda i, *_: (i, 0, 0, 0)),
            ],
        ),
        out_shape=[hot, hot, jax.ShapeDtypeStruct((owners, groups, span, span), jnp.bfloat16)],
        compiler_params=params(),
        cost_estimate=cost(0, 4 * owners * (sides * rows**2 + groups * span**2)),
        name="tables",
    )(places, group_id, entries, angles)


def run_gather(owner_of, place_of, received, take, chunk):
    devices, count, half, _ = received.shape
    rows = 2 * half
    smem = pl.BlockSpec(memory_space=pltpu.SMEM)
    return pl.pallas_call(
        gather_kernel,
        grid=(devices,),
        in_specs=[
            smem,
            smem,
            whole_spec(received),
            pl.BlockSpec((1, count, rows, rows), lambda i: (i, chunk, 0, 0)),
        ],
        out_specs=pl.BlockSpec((1, count, rows, LANES), lambda i: (i, 0, 0, 0)),
        out_shape=jax.ShapeDtypeStruct((devices, count, rows, LANES), jnp.bfloat16),
        scratch_shapes=[
            pltpu.VMEM((count, devices, devices, rows // devices, LANES), jnp.bfloat16)
        ],
        compiler_params=params(),
        cost_estimate=cost(4 * devices * count * rows**2 * LANES, 4 * devices * count * rows**2),
        name="gather",
    )(owner_of, place_of, received, take)


def run_mix(owner_of, place_of, gathered, give, blocks, chunk, apart):
    chunks = len(gathered)
    devices, count, rows, _ = gathered[0].shape
    half = rows // 2
    smem = pl.BlockSpec(memory_space=pltpu.SMEM)
    shapes = [(devices, 1, half, LANES)] * count if apart else [(devices, count, half, LANES)]
    shapes = [jax.ShapeDtypeStruct(shape, jnp.bfloat16) for shape in shapes]
    part_spec = pl.BlockSpec((1, count, rows, LANES), lambda i: (i, 0, 0, 0))
    return pl.pallas_call(
        functools.partial(mix_kernel, chunk, chunks),
        grid=(devices,),
        in_specs=[
            smem,
            smem,
            pl.BlockSpec((1, count, rows, rows), lambda i: (i, chunk, 0, 0)),
            pl.BlockSpec((1,) + blocks.shape[1:], lambda i: (i, 0, 0, 0)),
        ]
        + [part_spec] * chunks,
        out_specs=[whole_spec(shape) for shape in shapes],
        out_shape=shapes,
        scratch_shapes=[
            pltpu.VMEM((count, devices, devices, rows // devices, LANES), jnp.bfloat16)
        ],
        compiler_params=params(),
        cost_estimate=cost(6 * devices * count * rows**2 * LANES, 6 * devices * count * rows**2),
        name="mix",
    )(owner_of, place_of, give, blocks, *gathered)


def unit_tables(entries, capacity, unit):
    owners, sides, rows = entries.shape
    ids = jnp.arange(owners, dtype=jnp.int32)
    source = entries.reshape(owners, sides * rows) // capacity
    counts = jnp.sum((source[None] == ids[:, None, None]).astype(jnp.int32), axis=2) // (unit * sides)
    before = ids[:, None] < ids[None, :]
    starts = jnp.sum(jnp.where(before[None], counts[:, :, None], 0), axis=1)
    places = jnp.sum(jnp.where(before[:, :, None], counts[:, None, :], 0), axis=0)
    inside = (starts[:, :, None] <= ids) & (ids < (starts + counts)[:, :, None])
    owner_of = jnp.sum(jnp.where(inside, ids[None, :, None], 0), axis=1)
    place_of = jnp.sum(jnp.where(inside, (places - starts)[:, :, None] + ids, 0), axis=1)
    return owner_of, place_of


def ranks(values):
    return jnp.sum((values[:, :, None] < values[:, None, :]).astype(jnp.int32), axis=1)


CHUNKS = 2


def reorder(values, order):
    hits = order[:, None] == jnp.arange(values.shape[0], dtype=jnp.int32)
    return jnp.sum(jnp.where(hits[:, :, None], values[None], 0), axis=1)


def shift(values, offset, wide):
    if offset == 0:
        return values
    return lax.ppermute(values, "wide", [(i, i ^ offset) for i in range(wide)])


def swap(values):
    return lax.all_to_all(values, "narrow", 0, 0, tiled=True)


BASE = 64


def share_lists(listed, angles):
    narrow = lax.axis_size("narrow")
    atoms, width = angles.shape
    digits = jnp.stack([listed // BASE, listed % BASE]).reshape(atoms, -1).astype(jnp.bfloat16)
    shared = jnp.concatenate([angles, digits], axis=1)[None]
    held = [0]
    hop = narrow // 2
    while hop:
        other = lax.ppermute(shared, "narrow", [(i, i ^ hop) for i in range(narrow)])
        shared = jnp.concatenate([shared, other], axis=0)
        held += [offset ^ hop for offset in held]
        hop //= 2
    inverse = jnp.array([held.index(offset) for offset in range(narrow)], jnp.int32)
    mine = lax.axis_index("narrow").astype(jnp.int32)
    owners = jnp.arange(narrow, dtype=jnp.int32) ^ mine
    places = jnp.sum(jnp.where(owners[:, None] == jnp.arange(narrow), inverse, 0), axis=1)
    digits = shared[:, :, width:].reshape((narrow, 2) + listed.shape).astype(jnp.int32)
    entries = digits[:, 0] * BASE + digits[:, 1]
    entries = reorder(entries.reshape(narrow, -1), places).reshape(entries.shape)
    return entries, shared, places


def tiled_local(messages, reverse_position, route_slot, atom_slots, angles, weights):
    wide = lax.axis_size("wide")
    narrow = lax.axis_size("narrow")
    edge_rows, features = messages.shape
    rows = edge_rows // wide
    unit = rows // narrow
    capacity = 2 * edge_rows // narrow
    atoms = angles.shape[0]
    count = wide // CHUNKS
    offsets = [[chunk + index * CHUNKS for index in range(count)] for chunk in range(CHUNKS)]
    group_id = lax.axis_index("wide").astype(jnp.int32)
    order = group_id ^ jnp.array(sum(offsets, []), jnp.int32)
    places = [order[chunk * count : (chunk + 1) * count] for chunk in range(CHUNKS)]
    plain = jnp.arange(count, dtype=jnp.int32)

    blocks_of = messages.reshape(wide, rows, features)
    received = [
        [
            shift(lax.dynamic_index_in_dim(blocks_of, group_id ^ offset, 0, False), offset, wide)
            for offset in offsets[chunk]
            if offset
        ]
        for chunk in range(CHUNKS)
    ]
    listed = atom_slots.reshape(atoms // GROUP, GROUP, wide, SLOTS // wide)
    listed = reorder(jnp.transpose(listed, (2, 0, 3, 1)).reshape(wide, rows), order)
    entries, all_angles, owner_places = share_lists(listed, angles)
    rank = ranks(route_slot.reshape(wide, rows))
    back_rows = reverse_position.reshape(wide, rows)
    back_rows = reorder(back_rows, order)
    rank = reorder(rank, order)
    partner_rank = jnp.stack(
        [shift(rank[place], offset, wide) for place, offset in enumerate(sum(offsets, []))]
    )
    hits = back_rows[:, :, None] == jnp.arange(rows, dtype=jnp.int32)
    turned_rank = jnp.sum(jnp.where(hits, partner_rank[:, None, :], 0), axis=2)[:, None, :]
    back_rows = back_rows[:, None, :]
    rank = rank[:, None, :]

    current = [blocks_of] * CHUNKS
    where = places
    chunk_order = list(range(CHUNKS))
    target = None
    tables = None
    for section in range(BLOCKS):
        last = section == BLOCKS - 1
        seconds, spreads = {}, {}
        for chunk in chunk_order:
            seconds[chunk], packed = run_front(
                current[chunk], where[chunk], received[chunk], offsets[chunk][0] == 0, chunk,
                back_rows, rank, weights, section, narrow,
            )
            spreads[chunk] = packed
        if tables is None:
            held = [spreads[chunk] for chunk in chunk_order]
            entries, all_angles, held[-1] = lax.optimization_barrier((entries, all_angles, held[-1]))
            spreads = dict(zip(chunk_order, held))
            owner_of, place_of = unit_tables(entries, capacity, unit)
            tables = run_tables(owner_places, group_id[None], entries[:, :, None, :], all_angles, CHUNKS)
        take, give, blocks = tables
        gathered = [None] * CHUNKS
        for chunk in chunk_order:
            gathered[chunk] = run_gather(owner_of, place_of, swap(spreads[chunk]), take, chunk)
        chunk_order = list(range(CHUNKS))[::-1]
        returned = {}
        for chunk in chunk_order:
            early = chunk == 0
            mixed = list(run_mix(owner_of, place_of, gathered, give, blocks, chunk, early))
            if chunk != chunk_order[-1]:
                mixed[0], gathered[0] = lax.optimization_barrier((mixed[0], gathered[0]))
            if early:
                mixed = [shift(part, offset, wide) for part, offset in zip(mixed, offsets[chunk])]
                parts = [swap(jnp.concatenate(mixed, axis=1))]
                layout = [(0, index) for index in range(count)]
            else:
                whole = swap(mixed[0])
                parts = [
                    shift(whole[:, index : index + 1], offset, wide)
                    for index, offset in enumerate(offsets[chunk])
                ]
                layout = [(index, 0) for index in range(count)]
            returned[chunk] = (parts, layout)
        current = [None] * CHUNKS
        received = [None] * CHUNKS
        for chunk in chunk_order:
            parts, layout = returned[chunk]
            result = run_back(
                seconds[chunk], parts, layout, chunk, turned_rank, weights, section,
                places[chunk] if last else plain, wide if last else count, target,
            )
            if last:
                target = result
            else:
                current[chunk] = result
                received[chunk] = [
                    shift(result[index], offset, wide)
                    for index, offset in enumerate(offsets[chunk])
                    if offset
                ]
        where = [plain] * CHUNKS
    return target.reshape(edge_rows, features)


def local(
    messages,
    reverse_position,
    route_slot,
    atom_slots,
    angles,
    weight_message,
    weight_reverse,
    weight_combine,
    weight_inner,
    weight_outer,
    weight_lift,
    weight_expand,
    weight_reduce,
):
    weights = (
        weight_message,
        weight_reverse,
        weight_combine,
        weight_inner,
        weight_outer,
        weight_lift,
        weight_expand,
        weight_reduce,
    )
    wide = lax.axis_size("wide")
    narrow = lax.axis_size("narrow")
    edge_rows, features = messages.shape
    unit = edge_rows // wide // narrow
    fits = (
        features == narrow * HALF
        and unit % 16 == 0
        and narrow % 2 == 0
        and wide % CHUNKS == 0
        and wide & (wide - 1) == 0
        and narrow & (narrow - 1) == 0
        and angles.shape[0] % GROUP == 0
        and (SLOTS // wide * GROUP) % 16 == 0
    )
    run = tiled_local if fits else general_local
    return run(messages, reverse_position, route_slot, atom_slots, angles, weights)


def solution(mesh):
    in_specs = (
        P(("wide", "narrow"), None),
        P(("wide", "narrow")),
        P(("wide", "narrow")),
        P(("wide", "narrow")),
        P(("wide", "narrow"), None),
        P(),
        P(),
        P(),
        P(),
        P(),
        P(),
        P(),
        P(),
    )
    out_specs = P(("wide", "narrow"), None)
    return jax.shard_map(local, mesh=mesh, in_specs=in_specs, out_specs=out_specs, check_vma=False)
```

profile of v0, /device:TPU:0, one launch (start us, length us, event | category | flops | bytes accessed | tf_op | source)
XLA Modules:
  0.0 350.5 jit_solution(7965072042535613880)
XLA Ops:
  14.3 5.4 %collective-permute-done.5 = bf16[2,48,1088]{2,1,0:T(8,128)(2,1)S(1)} collective-permute-done((bf16[2,48,1088]{2,1,0:T(8,128)(2,1)S(1)}, bf16[2,48,1088]{2,1,0:T(8,128)(2,1)S(1)}, u32[]{:S(2)}, u32[]{:S(2)}) %collective-permute-start.5) | collective-permute-done | bytes 208928 | tf_op jit(solution)/shard_map/ppermute | solution.py:482
  20.6 8.4 %front.4 = (bf16[2,384,512]{2,1,0:T(8,128)(2,1)}, bf16[8,2,192,128]{3,2,1,0:T(8,128)(2,1)}) custom-call(s32[2]{0:T(128)} %get-tuple-element.74.where_ref, bf16[4,384,512]{2,1,0:T(8,128)(2,1)} %bitcast.53, s32[4,1,384]{2,1,0:T(1,128)} %broadcast_in_dim.187.back_ref, s32[4,1,384]{2,1,0:T(1,128)} %broadcast_in_dim.189.rank_ref, bf16[2,512,512]{2,1,0:T(8,128)(2,1)} %wm.7, ...), custom_call_target="tpu_custom_call" | custom-call | flops 2415919104 | bytes 3145728 | tf_op jit(solution)/shard_map/front/pallas_call | solution.py:298
  28.9 5.9 %all-to-all-start = ((bf16[8,2,192,128]{3,2,1,0:T(8,128)(2,1)}), bf16[8,2,192,128]{3,2,1,0:T(8,128)(2,1)S(1)}, u32[]{:S(2)}, u32[]{:S(2)}) async-start(bf16[8,2,192,128]{3,2,1,0:T(8,128)(2,1)} %get-tuple-element.33), calls=%async_computation | async-start | bytes 1572864 | tf_op jit(solution)/shard_map/all_to_all | solution.py:468
  34.9 8.6 %front.5 = (bf16[2,384,512]{2,1,0:T(8,128)(2,1)}, bf16[8,2,192,128]{3,2,1,0:T(8,128)(2,1)}) custom-call(s32[2]{0:T(128)} %get-tuple-element.73.where_ref, bf16[4,384,512]{2,1,0:T(8,128)(2,1)} %bitcast.54, s32[4,1,384]{2,1,0:T(1,128)} %broadcast_in_dim.187.back_ref, s32[4,1,384]{2,1,0:T(1,128)} %broadcast_in_dim.189.rank_ref, bf16[2,512,512]{2,1,0:T(8,128)(2,1)} %wm.7, ...), custom_call_target="tpu_custom_call" | custom-call | flops 2415919104 | bytes 3145728 | tf_op jit(solution)/shard_map/front/pallas_call | solution.py:298
  44.1 11.8 %all-to-all-done.recv_ref = bf16[8,2,192,128]{3,2,1,0:T(8,128)(2,1)S(1)} async-done(((bf16[8,2,192,128]{3,2,1,0:T(8,128)(2,1)}), bf16[8,2,192,128]{3,2,1,0:T(8,128)(2,1)S(1)}, u32[]{:S(2)}, u32[]{:S(2)}) %all-to-all-start) | async-done | bytes 786464 | tf_op jit(solution)/shard_map/all_to_all | solution.py:468
  60.2 19.2 %tables.1 = (bf16[8,4,384,384]{3,2,1,0:T(8,128)(2,1)}, bf16[8,4,384,384]{3,2,1,0:T(8,128)(2,1)}, bf16[8,6,256,256]{3,2,1,0:T(8,128)(2,1)}) custom-call(s32[8]{0:T(128)} %copy-done.12, s32[1]{0:T(128)} %bitcast.7.wide_ref, s32[8,4,1,384]{3,2,1,0:T(1,128)} %broadcast_in_dim.208.entry_ref, bf16[8,48,1088]{2,1,0:T(8,128)(2,1)} %copy-done), custom_call_target="tpu_custom_call" | custom-call | bytes 31457280 | tf_op jit(solution)/shard_map/tables/pallas_call | solution.py:360
  80.5 8.2 %gather.4.refs_0_ = bf16[8,2,384,128]{3,2,1,0:T(8,128)(2,1)} custom-call(s32[8,8]{1,0:T(8,128)} %get-tuple-element.50.owner_ref, s32[8,8]{1,0:T(8,128)} %get-tuple-element.49.place_ref, bf16[8,2,192,128]{3,2,1,0:T(8,128)(2,1)} %copy-done.1, bf16[8,4,384,384]{3,2,1,0:T(8,128)(2,1)} %get-tuple-element.34.take_ref), custom_call_target="tpu_custom_call" | custom-call | flops 1207959552 | bytes 9437184 | tf_op jit(solution)/shard_map/gather/pallas_call | solution.py:386
  89.6 8.2 %gather.5.refs_1_ = bf16[8,2,384,128]{3,2,1,0:T(8,128)(2,1)} custom-call(s32[8,8]{1,0:T(8,128)} %get-tuple-element.50.owner_ref, s32[8,8]{1,0:T(8,128)} %get-tuple-element.49.place_ref, bf16[8,2,192,128]{3,2,1,0:T(8,128)(2,1)} %copy-done.3, bf16[8,4,384,384]{3,2,1,0:T(8,128)(2,1)} %get-tuple-element.34.take_ref), custom_call_target="tpu_custom_call" | custom-call | flops 1207959552 | bytes 9437184 | tf_op jit(solution)/shard_map/gather/pallas_call | solution.py:386
  97.9 10.4 %mix.4 = bf16[8,2,192,128]{3,2,1,0:T(8,128)(2,1)} custom-call(s32[8,8]{1,0:T(8,128)} %get-tuple-element.50.owner_ref, s32[8,8]{1,0:T(8,128)} %get-tuple-element.49.place_ref, bf16[8,4,384,384]{3,2,1,0:T(8,128)(2,1)} %get-tuple-element.31.give_ref, bf16[8,6,256,256]{3,2,1,0:T(8,128)(2,1)} %get-tuple-element.32.blocks_ref, ...), custom_call_target="tpu_custom_call" | custom-call | flops 1811939328 | bytes 14155776 | tf_op jit(solution)/shard_map/mix/pallas_call | solution.py:414
  108.2 10.5 %mix.5 = (bf16[8,1,192,128]{3,2,1,0:T(8,128)(2,1)}, bf16[8,1,192,128]{3,2,1,0:T(8,128)(2,1)}) custom-call(s32[8,8]{1,0:T(8,128)} %get-tuple-element.50.owner_ref, s32[8,8]{1,0:T(8,128)} %get-tuple-element.49.place_ref, bf16[8,4,384,384]{3,2,1,0:T(8,128)(2,1)} %get-tuple-element.31.give_ref, bf16[8,6,256,256]{3,2,1,0:T(8,128)(2,1)} %get-tuple-element.32.blocks_ref, ...), custom_call_target="tpu_custom_call" | custom-call | flops 1811939328 | bytes 14155776 | tf_op jit(solution)/shard_map/mix/pallas_call | solution.py:414
  119.2 11.2 %collective-permute-done.9 = bf16[8,1,192,128]{3,2,1,0:T(8,128)(2,1)S(1)} collective-permute-done((bf16[8,1,192,128]{3,2,1,0:T(8,128)(2,1)}, bf16[8,1,192,128]{3,2,1,0:T(8,128)(2,1)S(1)}, u32[]{:S(2)}, u32[]{:S(2)}) %collective-permute-start.9) | collective-permute-done | bytes 393248 | tf_op jit(solution)/shard_map/ppermute | solution.py:464
  131.4 25.6 %all_to_all.40.refs_0_ = bf16[8,2,192,128]{3,2,1,0:T(8,128)(2,1)} all-to-all(bf16[8,2,192,128]{3,2,1,0:T(8,128)(2,1)S(1)} %pad_maximum_fusion.1), channel_id=1, replica_groups=mesh['wide'=4,'narrow'=8] {'narrow'}, dimensions={0} | all-to-all | bytes 1572864 | tf_op jit(solution)/shard_map/all_to_all | solution.py:468
  168.2 6.5 %back.4.cur_ref = bf16[2,384,512]{2,1,0:T(8,128)(2,1)} custom-call(s32[2]{0:T(128)} %iota.67.where_ref, bf16[2,384,512]{2,1,0:T(8,128)(2,1)} %get-tuple-element.27.second_ref, s32[4,1,384]{2,1,0:T(1,128)} %broadcast_in_dim.192.rank_ref, bf16[2,512,512]{2,1,0:T(8,128)(2,1)} %wl.7, bf16[2,512,512]{2,1,0:T(8,128)(2,1)} %we.7, bf16[2,512,512]{2,1,0:T(8,128)(2,1)} %wd.7, ...), custom_call_target="tpu_custom_call" | custom-call | flops 1610612736 | bytes 2359296 | tf_op jit(solution)/shard_map/back/pallas_call | solution.py:330
  177.2 4.3 %all-to-all-done.4 = bf16[8,2,192,128]{3,2,1,0:T(8,128)(2,1)S(1)} async-done(((bf16[8,2,192,128]{3,2,1,0:T(8,128)(2,1)}), bf16[8,2,192,128]{3,2,1,0:T(8,128)(2,1)S(1)}, u32[]{:S(2)}, u32[]{:S(2)}) %all-to-all-start.4) | async-done | bytes 786464 | tf_op jit(solution)/shard_map/all_to_all | solution.py:468
  186.3 8.4 %front.6 = (bf16[2,384,512]{2,1,0:T(8,128)(2,1)}, bf16[8,2,192,128]{3,2,1,0:T(8,128)(2,1)}) custom-call(s32[2]{0:T(128)} %iota.66.where_ref, bf16[2,384,512]{2,1,0:T(8,128)(2,1)} %back.4.cur_ref, s32[4,1,384]{2,1,0:T(1,128)} %broadcast_in_dim.187.back_ref, s32[4,1,384]{2,1,0:T(1,128)} %broadcast_in_dim.189.rank_ref, bf16[2,512,512]{2,1,0:T(8,128)(2,1)} %wm.7, ...), custom_call_target="tpu_custom_call" | custom-call | flops 2415919104 | bytes 3145728 | tf_op jit(solution)/shard_map/front/pallas_call | solution.py:298
  194.7 4.8 %all-to-all-start.3 = ((bf16[8,2,192,128]{3,2,1,0:T(8,128)(2,1)}), bf16[8,2,192,128]{3,2,1,0:T(8,128)(2,1)S(1)}, u32[]{:S(2)}, u32[]{:S(2)}) async-start(bf16[8,2,192,128]{3,2,1,0:T(8,128)(2,1)} %get-tuple-element.40), calls=%async_computation.3 | async-start | bytes 1572864 | tf_op jit(solution)/shard_map/all_to_all | solution.py:468
  201.4 6.5 %back.5.cur_ref = bf16[2,384,512]{2,1,0:T(8,128)(2,1)} custom-call(s32[2]{0:T(128)} %iota.70.where_ref, bf16[2,384,512]{2,1,0:T(8,128)(2,1)} %get-tuple-element.41.second_ref, s32[4,1,384]{2,1,0:T(1,128)} %broadcast_in_dim.192.rank_ref, bf16[2,512,512]{2,1,0:T(8,128)(2,1)} %wl.7, bf16[2,512,512]{2,1,0:T(8,128)(2,1)} %we.7, bf16[2,512,512]{2,1,0:T(8,128)(2,1)} %wd.7, ...), custom_call_target="tpu_custom_call" | custom-call | flops 1610612736 | bytes 2359296 | tf_op jit(solution)/shard_map/back/pallas_call | solution.py:330
  212.1 9.1 %collective-permute-done.13.refs_0_ = bf16[384,512]{1,0:T(8,128)(2,1)S(1)} collective-permute-done((bf16[384,512]{1,0:T(8,128)(2,1)S(1)}, bf16[384,512]{1,0:T(8,128)(2,1)S(1)}, u32[]{:S(2)}, u32[]{:S(2)}) %collective-permute-start.13) | collective-permute-done | bytes 393248 | tf_op jit(solution)/shard_map/ppermute | solution.py:464
  221.2 7.8 %collective-permute-done.14.refs_1_ = bf16[384,512]{1,0:T(8,128)(2,1)S(1)} collective-permute-done((bf16[384,512]{1,0:T(8,128)(2,1)S(1)}, bf16[384,512]{1,0:T(8,128)(2,1)S(1)}, u32[]{:S(2)}, u32[]{:S(2)}) %collective-permute-start.14) | collective-permute-done | bytes 393248 | tf_op jit(solution)/shard_map/ppermute | solution.py:464
  229.8 8.5 %front.7 = (bf16[2,384,512]{2,1,0:T(8,128)(2,1)}, bf16[8,2,192,128]{3,2,1,0:T(8,128)(2,1)}) custom-call(s32[2]{0:T(128)} %iota.69.where_ref, bf16[2,384,512]{2,1,0:T(8,128)(2,1)} %back.5.cur_ref, s32[4,1,384]{2,1,0:T(1,128)} %broadcast_in_dim.187.back_ref, s32[4,1,384]{2,1,0:T(1,128)} %broadcast_in_dim.189.rank_ref, bf16[2,512,512]{2,1,0:T(8,128)(2,1)} %wm.7, ...), custom_call_target="tpu_custom_call" | custom-call | flops 2415919104 | bytes 3145728 | tf_op jit(solution)/shard_map/front/pallas_call | solution.py:298
  238.3 4.7 %all-to-all-start.5 = ((bf16[8,2,192,128]{3,2,1,0:T(8,128)(2,1)}), bf16[8,2,192,128]{3,2,1,0:T(8,128)(2,1)S(1)}, u32[]{:S(2)}, u32[]{:S(2)}) async-start(bf16[8,2,192,128]{3,2,1,0:T(8,128)(2,1)} %get-tuple-element.43), calls=%async_computation.5 | async-start | bytes 1572864 | tf_op jit(solution)/shard_map/all_to_all | solution.py:468
  243.0 8.2 %gather.6.refs_0_ = bf16[8,2,384,128]{3,2,1,0:T(8,128)(2,1)} custom-call(s32[8,8]{1,0:T(8,128)} %get-tuple-element.50.owner_ref, s32[8,8]{1,0:T(8,128)} %get-tuple-element.49.place_ref, bf16[8,2,192,128]{3,2,1,0:T(8,128)(2,1)} %copy-done.2, bf16[8,4,384,384]{3,2,1,0:T(8,128)(2,1)} %get-tuple-element.34.take_ref), custom_call_target="tpu_custom_call" | custom-call | flops 1207959552 | bytes 9437184 | tf_op jit(solution)/shard_map/gather/pallas_call | solution.py:386
  251.3 12.7 %all-to-all-done.5.recv_ref = bf16[8,2,192,128]{3,2,1,0:T(8,128)(2,1)S(1)} async-done(((bf16[8,2,192,128]{3,2,1,0:T(8,128)(2,1)}), bf16[8,2,192,128]{3,2,1,0:T(8,128)(2,1)S(1)}, u32[]{:S(2)}, u32[]{:S(2)}) %all-to-all-start.5) | async-done | bytes 786464 | tf_op jit(solution)/shard_map/all_to_all | solution.py:468
  264.9 8.2 %gather.7.refs_1_ = bf16[8,2,384,128]{3,2,1,0:T(8,128)(2,1)} custom-call(s32[8,8]{1,0:T(8,128)} %get-tuple-element.50.owner_ref, s32[8,8]{1,0:T(8,128)} %get-tuple-element.49.place_ref, bf16[8,2,192,128]{3,2,1,0:T(8,128)(2,1)} %copy-done.5, bf16[8,4,384,384]{3,2,1,0:T(8,128)(2,1)} %get-tuple-element.34.take_ref), custom_call_target="tpu_custom_call" | custom-call | flops 1207959552 | bytes 9437184 | tf_op jit(solution)/shard_map/gather/pallas_call | solution.py:386
  273.2 10.4 %mix.6 = bf16[8,2,192,128]{3,2,1,0:T(8,128)(2,1)} custom-call(s32[8,8]{1,0:T(8,128)} %get-tuple-element.50.owner_ref, s32[8,8]{1,0:T(8,128)} %get-tuple-element.49.place_ref, bf16[8,4,384,384]{3,2,1,0:T(8,128)(2,1)} %get-tuple-element.31.give_ref, bf16[8,6,256,256]{3,2,1,0:T(8,128)(2,1)} %get-tuple-element.32.blocks_ref, ...), custom_call_target="tpu_custom_call" | custom-call | flops 1811939328 | bytes 14155776 | tf_op jit(solution)/shard_map/mix/pallas_call | solution.py:414
  287.1 10.4 %mix.7 = (bf16[8,1,192,128]{3,2,1,0:T(8,128)(2,1)}, bf16[8,1,192,128]{3,2,1,0:T(8,128)(2,1)}) custom-call(s32[8,8]{1,0:T(8,128)} %get-tuple-element.50.owner_ref, s32[8,8]{1,0:T(8,128)} %get-tuple-element.49.place_ref, bf16[8,4,384,384]{3,2,1,0:T(8,128)(2,1)} %get-tuple-element.31.give_ref, bf16[8,6,256,256]{3,2,1,0:T(8,128)(2,1)} %get-tuple-element.32.blocks_ref, ...), custom_call_target="tpu_custom_call" | custom-call | flops 1811939328 | bytes 14155776 | tf_op jit(solution)/shard_map/mix/pallas_call | solution.py:414
  298.0 11.1 %collective-permute-done.15 = bf16[8,1,192,128]{3,2,1,0:T(8,128)(2,1)S(1)} collective-permute-done((bf16[8,1,192,128]{3,2,1,0:T(8,128)(2,1)}, bf16[8,1,192,128]{3,2,1,0:T(8,128)(2,1)S(1)}, u32[]{:S(2)}, u32[]{:S(2)}) %collective-permute-start.15) | collective-permute-done | bytes 393248 | tf_op jit(solution)/shard_map/ppermute | solution.py:464
  311.1 4.8 %all-to-all-start.6 = ((bf16[8,2,192,128]{3,2,1,0:T(8,128)(2,1)}), bf16[8,2,192,128]{3,2,1,0:T(8,128)(2,1)S(1)}, u32[]{:S(2)}, u32[]{:S(2)}) async-start(bf16[8,2,192,128]{3,2,1,0:T(8,128)(2,1)} %pad_maximum_fusion.2), calls=%async_computation.6 | async-start | bytes 1572864 | tf_op jit(solution)/shard_map/all_to_all | solution.py:468
  318.0 9.9 %collective-permute-done.16.refs_0_ = bf16[8,1,192,128]{3,2,1,0:T(8,128)(2,1)S(1)} collective-permute-done((bf16[8,1,192,128]{3,2,1,0:T(8,128)(2,1)S(1)}, bf16[8,1,192,128]{3,2,1,0:T(8,128)(2,1)S(1)}, u32[]{:S(2)}, u32[]{:S(2)}) %collective-permute-start.16) | collective-permute-done | bytes 393248 | tf_op jit(solution)/shard_map/ppermute | solution.py:464
  327.9 8.0 %collective-permute-done.17.refs_1_ = bf16[8,1,192,128]{3,2,1,0:T(8,128)(2,1)S(1)} collective-permute-done((bf16[8,1,192,128]{3,2,1,0:T(8,128)(2,1)S(1)}, bf16[8,1,192,128]{3,2,1,0:T(8,128)(2,1)S(1)}, u32[]{:S(2)}, u32[]{:S(2)}) %collective-permute-start.17) | collective-permute-done | bytes 393248 | tf_op jit(solution)/shard_map/ppermute | solution.py:464
  336.6 6.5 %back.6.refs_1_ = bf16[4,384,512]{2,1,0:T(8,128)(2,1)} custom-call(s32[2]{0:T(128)} %get-tuple-element.73.where_ref, bf16[2,384,512]{2,1,0:T(8,128)(2,1)} %get-tuple-element.47.second_ref, s32[4,1,384]{2,1,0:T(1,128)} %broadcast_in_dim.192.rank_ref, bf16[2,512,512]{2,1,0:T(8,128)(2,1)} %wl.7, bf16[2,512,512]{2,1,0:T(8,128)(2,1)} %we.7, ...), custom_call_target="tpu_custom_call" | custom-call | flops 1610612736 | bytes 2359296 | tf_op jit(solution)/shard_map/back/pallas_call | solution.py:330
  344.0 6.5 %back.7 = bf16[4,384,512]{2,1,0:T(8,128)(2,1)} custom-call(s32[2]{0:T(128)} %get-tuple-element.74.where_ref, bf16[2,384,512]{2,1,0:T(8,128)(2,1)} %get-tuple-element.39.second_ref, s32[4,1,384]{2,1,0:T(1,128)} %broadcast_in_dim.192.rank_ref, bf16[2,512,512]{2,1,0:T(8,128)(2,1)} %wl.7, bf16[2,512,512]{2,1,0:T(8,128)(2,1)} %we.7, ...), custom_call_target="tpu_custom_call", output_to_operand_aliasing={{}: (7, {})} | custom-call | flops 1610612736 | bytes 2359296 | tf_op jit(solution)/shard_map/back/pallas_call | solution.py:330
  (136 shorter events, 59.4 us)
Async XLA Ops:
  0.0 12.0 %copy-start.19 = (s32[8]{0:T(128)S(1)}, s32[8]{0:T(128)}, u32[]{:S(2)}) copy-start(s32[8]{0:T(128)} %constant.73.clone) | copy-start | bytes 100
  0.0 5.5 %copy-start.8 = (bf16[48,1024]{1,0:T(8,128)(2,1)S(1)}, bf16[48,1024]{1,0:T(8,128)(2,1)}, u32[]{:S(2)}) copy-start(bf16[48,1024]{1,0:T(8,128)(2,1)} %param.19) | copy-start | bytes 294916
  1.4 18.4 %collective-permute-start = (bf16[384,512]{1,0:T(8,128)(2,1)S(1)}, bf16[384,512]{1,0:T(8,128)(2,1)S(1)}, u32[]{:S(2)}, u32[]{:S(2)}) collective-permute-start(bf16[384,512]{1,0:T(8,128)(2,1)S(1)} %get-tuple-element.61), channel_id=1, source_target_pairs={{0,16},{8,24},{16,0},{24,8},{1,17},{9,25},{17,1},{25,9},{2,18},{10... | collective-permute-start | bytes 1179656 | tf_op jit(solution)/shard_map/ppermute | solution.py:464
  5.6 7.9 %collective-permute-start.4 = (bf16[1,48,1088]{2,1,0:T(8,128)(2,1)S(1)}, bf16[1,48,1088]{2,1,0:T(8,128)(2,1)S(1)}, u32[]{:S(2)}, u32[]{:S(2)}) collective-permute-start(bf16[1,48,1088]{2,1,0:T(8,128)(2,1)S(1)} %maximum_bitcast_fusion), channel_id=1, source_target_pairs={{0,4},{1,5},{2,6},{3,7},{4,0},{5,1},{6,2},{7,3},{8,12},{9,13},{10,... | collective-permute-start | bytes 313352 | tf_op jit(solution)/shard_map/ppermute | solution.py:482
  8.2 26.7 %collective-permute-start.7 = (bf16[384,512]{1,0:T(8,128)(2,1)S(1)}, bf16[384,512]{1,0:T(8,128)(2,1)}, u32[]{:S(2)}, u32[]{:S(2)}) collective-permute-start(bf16[384,512]{1,0:T(8,128)(2,1)S(1)} %get-tuple-element.60), channel_id=1, source_target_pairs={{0,8},{8,0},{16,24},{24,16},{1,9},{9,1},{17,25},{25,17},{2,10},{10... | collective-permute-start | bytes 1179656 | tf_op jit(solution)/shard_map/ppermute | solution.py:464
  9.7 25.2 %collective-permute-start.8 = (bf16[384,512]{1,0:T(8,128)(2,1)S(1)}, bf16[384,512]{1,0:T(8,128)(2,1)}, u32[]{:S(2)}, u32[]{:S(2)}) collective-permute-start(bf16[384,512]{1,0:T(8,128)(2,1)S(1)} %get-tuple-element.59), channel_id=1, source_target_pairs={{0,24},{8,16},{16,8},{24,0},{1,25},{9,17},{17,9},{25,1},{2,26},{10... | collective-permute-start | bytes 1179656 | tf_op jit(solution)/shard_map/ppermute | solution.py:464
  12.2 16.7 %copy-start.12 = (s32[8]{0:T(128)}, s32[8]{0:T(128)S(1)}, u32[]{:S(2)}) copy-start(s32[8]{0:T(128)S(1)} %select_reduce_fusion.9.places_ref) | copy-start | bytes 100
  13.4 6.2 %collective-permute-start.5 = (bf16[2,48,1088]{2,1,0:T(8,128)(2,1)S(1)}, bf16[2,48,1088]{2,1,0:T(8,128)(2,1)S(1)}, u32[]{:S(2)}, u32[]{:S(2)}) collective-permute-start(bf16[2,48,1088]{2,1,0:T(8,128)(2,1)S(1)} %pad_maximum_fusion.4), channel_id=1, source_target_pairs={{0,2},{1,3},{2,0},{3,1},{4,6},{5,7},{6,4},{7,5},{8,10},{9,11},{10,... | collective-permute-start | bytes 626696 | tf_op jit(solution)/shard_map/ppermute | solution.py:482
  19.7 23.8 %collective-permute-start.6 = (bf16[4,48,1088]{2,1,0:T(8,128)(2,1)S(1)}, bf16[4,48,1088]{2,1,0:T(8,128)(2,1)S(1)}, u32[]{:S(2)}, u32[]{:S(2)}) collective-permute-start(bf16[4,48,1088]{2,1,0:T(8,128)(2,1)S(1)} %pad_maximum_fusion.3), channel_id=1, source_target_pairs={{0,1},{1,0},{2,3},{3,2},{4,5},{5,4},{6,7},{7,6},{8,9},{9,8},{10,11... | collective-permute-start | bytes 1253384 | tf_op jit(solution)/shard_map/ppermute | solution.py:482
  28.9 26.9 %all-to-all-start = ((bf16[8,2,192,128]{3,2,1,0:T(8,128)(2,1)}), bf16[8,2,192,128]{3,2,1,0:T(8,128)(2,1)S(1)}, u32[]{:S(2)}, u32[]{:S(2)}) async-start(bf16[8,2,192,128]{3,2,1,0:T(8,128)(2,1)} %get-tuple-element.33), calls=%async_computation | async-start | bytes 1572864 | tf_op jit(solution)/shard_map/all_to_all | solution.py:468
  43.6 16.5 %copy-start = (bf16[8,48,1088]{2,1,0:T(8,128)(2,1)}, bf16[8,48,1088]{2,1,0:T(8,128)(2,1)S(1)}, u32[]{:S(2)}) copy-start(bf16[8,48,1088]{2,1,0:T(8,128)(2,1)S(1)} %pad_maximum_fusion.angles_ref) | copy-start | bytes 2506756
  55.9 24.6 %copy-start.1 = (bf16[8,2,192,128]{3,2,1,0:T(8,128)(2,1)}, bf16[8,2,192,128]{3,2,1,0:T(8,128)(2,1)S(1)}, u32[]{:S(2)}) copy-start(bf16[8,2,192,128]{3,2,1,0:T(8,128)(2,1)S(1)} %all-to-all-done.recv_ref) | copy-start | bytes 2359300
  55.9 32.8 %all-to-all-start.1 = ((bf16[8,2,192,128]{3,2,1,0:T(8,128)(2,1)}), bf16[8,2,192,128]{3,2,1,0:T(8,128)(2,1)S(1)}, u32[]{:S(2)}, u32[]{:S(2)}) async-start(bf16[8,2,192,128]{3,2,1,0:T(8,128)(2,1)} %get-tuple-element.35), calls=%async_computation.1 | async-start | bytes 1572864 | tf_op jit(solution)/shard_map/all_to_all | solution.py:468
  118.7 11.7 %collective-permute-start.9 = (bf16[8,1,192,128]{3,2,1,0:T(8,128)(2,1)}, bf16[8,1,192,128]{3,2,1,0:T(8,128)(2,1)S(1)}, u32[]{:S(2)}, u32[]{:S(2)}) collective-permute-start(bf16[8,1,192,128]{3,2,1,0:T(8,128)(2,1)} %get-tuple-element.38), channel_id=1, source_target_pairs={{0,16},{8,24},{16,0},{24,8},{1,17},{9,25},{17,1},{25,9},{2,18},{10... | collective-permute-start | bytes 1179656 | tf_op jit(solution)/shard_map/ppermute | solution.py:464
  157.1 24.5 %all-to-all-start.4 = ((bf16[8,2,192,128]{3,2,1,0:T(8,128)(2,1)}), bf16[8,2,192,128]{3,2,1,0:T(8,128)(2,1)S(1)}, u32[]{:S(2)}, u32[]{:S(2)}) async-start(bf16[8,2,192,128]{3,2,1,0:T(8,128)(2,1)} %mix.4), calls=%async_computation.4 | async-start | bytes 1572864 | tf_op jit(solution)/shard_map/all_to_all | solution.py:468
  160.8 4.5 %collective-permute-start.3 = (s32[384]{0:T(512)S(1)}, s32[384]{0:T(512)S(1)}, u32[]{:S(2)}, u32[]{:S(2)}) collective-permute-start(s32[384]{0:T(512)S(1)} %get-tuple-element.52), channel_id=1, source_target_pairs={{0,24},{8,16},{16,8},{24,0},{1,25},{9,17},{17,9},{25,1},{2,26},{10... | collective-permute-start | bytes 4616 | tf_op jit(solution)/shard_map/ppermute | solution.py:464
  162.3 3.6 %collective-permute-start.2 = (s32[384]{0:T(512)S(1)}, s32[384]{0:T(512)S(1)}, u32[]{:S(2)}, u32[]{:S(2)}) collective-permute-start(s32[384]{0:T(512)S(1)} %get-tuple-element.53), channel_id=1, source_target_pairs={{0,8},{8,0},{16,24},{24,16},{1,9},{9,1},{17,25},{25,17},{2,10},{10... | collective-permute-start | bytes 4616 | tf_op jit(solution)/shard_map/ppermute | solution.py:464
  162.9 3.6 %collective-permute-start.1 = (s32[384]{0:T(512)S(1)}, s32[384]{0:T(512)S(1)}, u32[]{:S(2)}, u32[]{:S(2)}) collective-permute-start(s32[384]{0:T(512)S(1)} %get-tuple-element.51), channel_id=1, source_target_pairs={{0,16},{8,24},{16,0},{24,8},{1,17},{9,25},{17,1},{25,9},{2,18},{10... | collective-permute-start | bytes 4616 | tf_op jit(solution)/shard_map/ppermute | solution.py:464
  175.7 9.9 %collective-permute-start.10 = (bf16[384,512]{1,0:T(8,128)(2,1)S(1)}, bf16[384,512]{1,0:T(8,128)(2,1)S(1)}, u32[]{:S(2)}, u32[]{:S(2)}) collective-permute-start(bf16[384,512]{1,0:T(8,128)(2,1)S(1)} %slice_bitcast_fusion.2), channel_id=1, source_target_pairs={{0,16},{8,24},{16,0},{24,8},{1,17},{9,25},{17,1},{25,9},{2,18},{10... | collective-permute-start | bytes 1179656 | tf_op jit(solution)/shard_map/ppermute | solution.py:464
  181.6 17.9 %collective-permute-start.11 = (bf16[8,1,192,128]{3,2,1,0:T(8,128)(2,1)S(1)}, bf16[8,1,192,128]{3,2,1,0:T(8,128)(2,1)S(1)}, u32[]{:S(2)}, u32[]{:S(2)}) collective-permute-start(bf16[8,1,192,128]{3,2,1,0:T(8,128)(2,1)S(1)} %get-tuple-element.67), channel_id=1, source_target_pairs={{0,8},{8,0},{16,24},{24,16},{1,9},{9,1},{17,25},{25,17},{2,10},{10... | collective-permute-start | bytes 1179656 | tf_op jit(solution)/shard_map/ppermute | solution.py:464
  183.1 17.5 %collective-permute-start.12 = (bf16[8,1,192,128]{3,2,1,0:T(8,128)(2,1)S(1)}, bf16[8,1,192,128]{3,2,1,0:T(8,128)(2,1)S(1)}, u32[]{:S(2)}, u32[]{:S(2)}) collective-permute-start(bf16[8,1,192,128]{3,2,1,0:T(8,128)(2,1)S(1)} %get-tuple-element.66), channel_id=1, source_target_pairs={{0,24},{8,16},{16,8},{24,0},{1,25},{9,17},{17,9},{25,1},{2,26},{10... | collective-permute-start | bytes 1179656 | tf_op jit(solution)/shard_map/ppermute | solution.py:464
  194.7 43.6 %all-to-all-start.3 = ((bf16[8,2,192,128]{3,2,1,0:T(8,128)(2,1)}), bf16[8,2,192,128]{3,2,1,0:T(8,128)(2,1)S(1)}, u32[]{:S(2)}, u32[]{:S(2)}) async-start(bf16[8,2,192,128]{3,2,1,0:T(8,128)(2,1)} %get-tuple-element.40), calls=%async_computation.3 | async-start | bytes 1572864 | tf_op jit(solution)/shard_map/all_to_all | solution.py:468
  209.0 12.1 %collective-permute-start.13 = (bf16[384,512]{1,0:T(8,128)(2,1)S(1)}, bf16[384,512]{1,0:T(8,128)(2,1)S(1)}, u32[]{:S(2)}, u32[]{:S(2)}) collective-permute-start(bf16[384,512]{1,0:T(8,128)(2,1)S(1)} %get-tuple-element.65), channel_id=1, source_target_pairs={{0,8},{8,0},{16,24},{24,16},{1,9},{9,1},{17,25},{25,17},{2,10},{10... | collective-permute-start | bytes 1179656 | tf_op jit(solution)/shard_map/ppermute | solution.py:464
  210.6 18.4 %collective-permute-start.14 = (bf16[384,512]{1,0:T(8,128)(2,1)S(1)}, bf16[384,512]{1,0:T(8,128)(2,1)S(1)}, u32[]{:S(2)}, u32[]{:S(2)}) collective-permute-start(bf16[384,512]{1,0:T(8,128)(2,1)S(1)} %get-tuple-element.64), channel_id=1, source_target_pairs={{0,24},{8,16},{16,8},{24,0},{1,25},{9,17},{17,9},{25,1},{2,26},{10... | collective-permute-start | bytes 1179656 | tf_op jit(solution)/shard_map/ppermute | solution.py:464
  221.2 8.4 %copy-start.17 = (bf16[384,512]{1,0:T(8,128)(2,1)}, bf16[384,512]{1,0:T(8,128)(2,1)S(1)}, u32[]{:S(2)}) copy-start(bf16[384,512]{1,0:T(8,128)(2,1)S(1)} %collective-permute-done.13.refs_0_) | copy-start | bytes 1179652
  238.3 25.7 %all-to-all-start.5 = ((bf16[8,2,192,128]{3,2,1,0:T(8,128)(2,1)}), bf16[8,2,192,128]{3,2,1,0:T(8,128)(2,1)S(1)}, u32[]{:S(2)}, u32[]{:S(2)}) async-start(bf16[8,2,192,128]{3,2,1,0:T(8,128)(2,1)} %get-tuple-element.43), calls=%async_computation.5 | async-start | bytes 1572864 | tf_op jit(solution)/shard_map/all_to_all | solution.py:468
  283.5 27.6 %all-to-all-start.7 = ((bf16[8,2,192,128]{3,2,1,0:T(8,128)(2,1)}), bf16[8,2,192,128]{3,2,1,0:T(8,128)(2,1)S(1)}, u32[]{:S(2)}, u32[]{:S(2)}) async-start(bf16[8,2,192,128]{3,2,1,0:T(8,128)(2,1)} %mix.6), calls=%async_computation.7 | async-start | bytes 1572864 | tf_op jit(solution)/shard_map/all_to_all | solution.py:468
  297.5 11.6 %collective-permute-start.15 = (bf16[8,1,192,128]{3,2,1,0:T(8,128)(2,1)}, bf16[8,1,192,128]{3,2,1,0:T(8,128)(2,1)S(1)}, u32[]{:S(2)}, u32[]{:S(2)}) collective-permute-start(bf16[8,1,192,128]{3,2,1,0:T(8,128)(2,1)} %get-tuple-element.46), channel_id=1, source_target_pairs={{0,16},{8,24},{16,0},{24,8},{1,17},{9,25},{17,1},{25,9},{2,18},{10... | collective-permute-start | bytes 1179656 | tf_op jit(solution)/shard_map/ppermute | solution.py:464
  311.1 32.0 %all-to-all-start.6 = ((bf16[8,2,192,128]{3,2,1,0:T(8,128)(2,1)}), bf16[8,2,192,128]{3,2,1,0:T(8,128)(2,1)S(1)}, u32[]{:S(2)}, u32[]{:S(2)}) async-start(bf16[8,2,192,128]{3,2,1,0:T(8,128)(2,1)} %pad_maximum_fusion.2), calls=%async_computation.6 | async-start | bytes 1572864 | tf_op jit(solution)/shard_map/all_to_all | solution.py:468
  315.9 12.0 %collective-permute-start.16 = (bf16[8,1,192,128]{3,2,1,0:T(8,128)(2,1)S(1)}, bf16[8,1,192,128]{3,2,1,0:T(8,128)(2,1)S(1)}, u32[]{:S(2)}, u32[]{:S(2)}) collective-permute-start(bf16[8,1,192,128]{3,2,1,0:T(8,128)(2,1)S(1)} %get-tuple-element.63), channel_id=1, source_target_pairs={{0,8},{8,0},{16,24},{24,16},{1,9},{9,1},{17,25},{25,17},{2,10},{10... | collective-permute-start | bytes 1179656 | tf_op jit(solution)/shard_map/ppermute | solution.py:464
  317.5 18.4 %collective-permute-start.17 = (bf16[8,1,192,128]{3,2,1,0:T(8,128)(2,1)S(1)}, bf16[8,1,192,128]{3,2,1,0:T(8,128)(2,1)S(1)}, u32[]{:S(2)}, u32[]{:S(2)}) collective-permute-start(bf16[8,1,192,128]{3,2,1,0:T(8,128)(2,1)S(1)} %get-tuple-element.62), channel_id=1, source_target_pairs={{0,24},{8,16},{16,8},{24,0},{1,25},{9,17},{17,9},{25,1},{2,26},{10... | collective-permute-start | bytes 1179656 | tf_op jit(solution)/shard_map/ppermute | solution.py:464
  327.9 8.0 %copy-start.6 = (bf16[8,1,192,128]{3,2,1,0:T(8,128)(2,1)}, bf16[8,1,192,128]{3,2,1,0:T(8,128)(2,1)S(1)}, u32[]{:S(2)}) copy-start(bf16[8,1,192,128]{3,2,1,0:T(8,128)(2,1)S(1)} %collective-permute-done.16.refs_0_) | copy-start | bytes 1179652
  (14 other events, 32.0 us)
where the time goes:
time: 353 us; the launch traced here: 351 us
  Pallas kernels  154 us (44%)
  waiting for transfers between devices  97.7 us (28%)
  starting transfers between devices  52.8 us (15%)
  blocking collectives  25.6 us (7%)
  local copies, waits for them, and re-layouts  14.4 us (4%)
  other arithmetic  6.02 us (2%)
    ppermute x15, waiting for transfers between devices, shift(): return lax.ppermute(values, 'wide', [(i, i ^ offset) for i in range(wide)])  62.2 us
    pallas_call x4, Pallas kernels, run_mix(): pl.pallas_call(functools.partial(mix_kernel, chunk, chunks), grid=(device...  41.7 us
    pallas_call x4, Pallas kernels, run_front(): pl.pallas_call(functools.partial(front_kernel, own, count), grid_spec=plt...  33.9 us
    pallas_call x4, Pallas kernels, run_gather(): pl.pallas_call(gather_kernel, grid=(devices,), in_specs=[smem, smem, whol...  32.9 us
    all_to_all x7, starting transfers between devices, swap(): return lax.all_to_all(values, 'narrow', 0, 0, tiled=True)  31.1 us
    all_to_all x7, waiting for transfers between devices, swap(): return lax.all_to_all(values, 'narrow', 0, 0, tiled=True)  28.8 us
    pallas_call x4, Pallas kernels, run_back(): pl.pallas_call(functools.partial(back_kernel, layout), grid_spec=pltpu.Pr...  25.9 us
    all_to_all x1, blocking collectives, swap(): return lax.all_to_all(values, 'narrow', 0, 0, tiled=True)  25.6 us
  transfers between devices with their start and end apart: 25, of which 16 were waited for; matrix products, arithmetic and copies ran while one was open for 4% of the time, Pallas kernels for 28%

commit v1 on v0

--- a/solution.py
+++ b/solution.py
@@ -159,26 +159,22 @@
     out_ref[0] = halve(third_res, silu(dot(expand, wd[0])))
 
 
-def table_kernel(chunks, places_ref, wide_ref, entry_ref, angles_ref, take_ref, give_ref, blocks_ref):
+def table_kernel(places_ref, order_ref, position_ref, entry_ref, angles_ref, rank_ref, blocks_ref):
     sides, _, size = entry_ref.shape[1:]
-    count = sides // chunks
-    group_id = wide_ref[0]
     rows_iota, lanes_iota = iotas(size)
     for side in range(sides):
         row = entry_ref[0, side]
         column = as_column(row, rows_iota, lanes_iota)
-        rank_column = jnp.sum(jnp.where(row < column, 1, 0), axis=1, keepdims=True)
-        rank_row = jnp.sum(jnp.where(column < row, 1, 0), axis=0, keepdims=True)
-        take_ref[0, side] = one_hot(rank_column == lanes_iota)
-        give_ref[0, side] = one_hot(rows_iota == rank_row)
+        rank_ref[0, side] = jnp.sum(jnp.where(column < row, 1, 0), axis=0, keepdims=True)
     span = GROUP * SLOTS
     strip = span // sides
     rows_iota, lanes_iota = iotas(span)
     own = rows_iota % GROUP == lanes_iota % GROUP
     spread_rows = lax.broadcasted_iota(jnp.int32, (SLOTS, span), 0)
     spread_lanes = lax.broadcasted_iota(jnp.int32, (SLOTS, span), 1)
-    place = spread_lanes // strip
-    side_at = (place // count + place % count * chunks) ^ group_id
+    side_at = jnp.zeros((SLOTS, span), jnp.int32)
+    for place in range(sides):
+        side_at = jnp.where(spread_lanes // strip == place, order_ref[place], side_at)
     spread = one_hot(side_at * (SLOTS // sides) + spread_lanes % strip // GROUP == spread_rows)
     for group in range(angles_ref.shape[1] // GROUP):
         local = angles_ref[0, group * GROUP : (group + 1) * GROUP, :].astype(jnp.float32)
@@ -187,14 +183,13 @@
         ).astype(jnp.bfloat16)
         block = jnp.where(own, dot(stacked, spread), 0.0).astype(jnp.bfloat16)
         for side in range(sides):
-            offset = group_id ^ side
-            to = pl.multiple_of((offset % chunks * count + offset // chunks) * strip, strip)
+            to = pl.multiple_of(position_ref[side] * strip, strip)
             blocks_ref[0, group, pl.ds(to, strip), :] = block[side * strip : (side + 1) * strip]
 
 
-def gather_kernel(owner_ref, place_ref, recv_ref, take_ref, out_ref, ins):
+def gather_kernel(chunk, owner_ref, place_ref, recv_ref, rank_ref, out_ref, ins):
     step = pl.program_id(0)
-    sides = take_ref.shape[1]
+    sides = recv_ref.shape[1]
     devices = recv_ref.shape[0]
     unit = ins.shape[3]
     pairs = devices // 2
@@ -213,21 +208,23 @@
                         block = pltpu.roll(block.astype(jnp.float32), HALF, 1).astype(jnp.bfloat16)
                     ins[side, owner, place] = block
 
+    rows_iota, lanes_iota = iotas(devices * unit)
     for side in range(sides):
         operand = ins[side, step].reshape(devices * unit, LANES)
-        out_ref[0, side] = dot(take_ref[0, side], operand).astype(jnp.bfloat16)
-
-
-def mix_kernel(chunk, chunks, owner_ref, place_ref, give_ref, blocks_ref, *refs):
+        source = as_column(rank_ref[0, chunk * sides + side], rows_iota, lanes_iota)
+        out_ref[0, side] = dot(one_hot(source == lanes_iota), operand).astype(jnp.bfloat16)
+
+
+def mix_kernel(chunk, chunks, owner_ref, place_ref, rank_ref, blocks_ref, *refs):
     gathered_refs, out_refs, outs = refs[:chunks], refs[chunks:-1], refs[-1]
     step = pl.program_id(0)
-    count = give_ref.shape[1]
+    count = outs.shape[0]
     devices = outs.shape[1]
     unit = outs.shape[3]
     groups = blocks_ref.shape[1]
-    strip = blocks_ref.shape[2] // (chunks * count)
+    strip = blocks_ref.shape[2] // count
     pairs = devices // 2
-    first = chunk * count * strip
+    rows_iota = iotas(devices * unit)[0]
     mixed = []
     for group in range(groups):
         operand = jnp.concatenate(
@@ -238,14 +235,15 @@
             ],
             axis=0,
         )
-        mixing = blocks_ref[0, group, first : first + count * strip, :]
-        mixed.append(dot(mixing, operand).astype(jnp.bfloat16))
+        mixed.append(dot(blocks_ref[0, group], operand).astype(jnp.bfloat16))
     for side in range(count):
         operand = jnp.concatenate(
             [part[side * strip : (side + 1) * strip] for part in mixed], axis=0
         )
         outs[side, step] = (
-            dot(give_ref[0, side], operand).astype(jnp.bfloat16).reshape(devices, unit, LANES)
+            dot(one_hot(rows_iota == rank_ref[0, chunk * count + side]), operand)
+            .astype(jnp.bfloat16)
+            .reshape(devices, unit, LANES)
         )
 
     @pl.when(step == pl.num_programs(0) - 1)
@@ -270,7 +268,7 @@
                         out_refs[side][source, 0, rows, :] = joined
 
 
-VMEM_BYTES = 60 * 1024 * 1024
+VMEM_BYTES = 24 * 1024 * 1024
 
 
 def params():
@@ -350,47 +348,51 @@
     )(where, second, rank_rows, *weights[5:], *packed, *extra)
 
 
-def run_tables(places, group_id, entries, angles, chunks):
-    owners, sides, _, rows = entries.shape
+def rank_spec(entries):
+    return pl.BlockSpec((1,) + entries.shape[1:], lambda i, *_: (i, 0, 0, 0))
+
+
+def run_tables(places, order, position, entries, angles):
+    owners = entries.shape[0]
     atoms = angles.shape[1]
     groups = atoms // GROUP
     span = GROUP * SLOTS
-    hot = jax.ShapeDtypeStruct((owners, sides, rows, rows), jnp.bfloat16)
-    hot_spec = pl.BlockSpec((1, sides, rows, rows), lambda i, *_: (i, 0, 0, 0))
     return pl.pallas_call(
-        functools.partial(table_kernel, chunks),
+        table_kernel,
         grid_spec=pltpu.PrefetchScalarGridSpec(
-            num_scalar_prefetch=2,
+            num_scalar_prefetch=3,
             grid=(owners,),
             in_specs=[
-                pl.BlockSpec((1, sides, 1, rows), lambda i, *_: (i, 0, 0, 0)),
-                pl.BlockSpec((1, atoms, angles.shape[2]), lambda i, places, _: (places[i], 0, 0)),
+                rank_spec(entries),
+                pl.BlockSpec((1, atoms, angles.shape[2]), lambda i, places, *_: (places[i], 0, 0)),
             ],
             out_specs=[
-                hot_spec,
-                hot_spec,
+                rank_spec(entries),
                 pl.BlockSpec((1, groups, span, span), lambda i, *_: (i, 0, 0, 0)),
             ],
         ),
-        out_shape=[hot, hot, jax.ShapeDtypeStruct((owners, groups, span, span), jnp.bfloat16)],
+        out_shape=[
+            jax.ShapeDtypeStruct(entries.shape, jnp.int32),
+            jax.ShapeDtypeStruct((owners, groups, span, span), jnp.bfloat16),
+        ],
         compiler_params=params(),
-        cost_estimate=cost(0, 4 * owners * (sides * rows**2 + groups * span**2)),
+        cost_estimate=cost(0, 8 * owners * groups * span**2),
         name="tables",
-    )(places, group_id, entries, angles)
-
-
-def run_gather(owner_of, place_of, received, take, chunk):
+    )(places, order, position, entries, angles)
+
+
+def run_gather(owner_of, place_of, received, rank, chunk):
     devices, count, half, _ = received.shape
     rows = 2 * half
     smem = pl.BlockSpec(memory_space=pltpu.SMEM)
     return pl.pallas_call(
-        gather_kernel,
+        functools.partial(gather_kernel, chunk),
         grid=(devices,),
         in_specs=[
             smem,
             smem,
             whole_spec(received),
-            pl.BlockSpec((1, count, rows, rows), lambda i: (i, chunk, 0, 0)),
+            rank_spec(rank),
         ],
         out_specs=pl.BlockSpec((1, count, rows, LANES), lambda i: (i, 0, 0, 0)),
         out_shape=jax.ShapeDtypeStruct((devices, count, rows, LANES), jnp.bfloat16),
@@ -400,13 +402,14 @@
         compiler_params=params(),
         cost_estimate=cost(4 * devices * count * rows**2 * LANES, 4 * devices * count * rows**2),
         name="gather",
-    )(owner_of, place_of, received, take)
-
-
-def run_mix(owner_of, place_of, gathered, give, blocks, chunk, apart):
+    )(owner_of, place_of, received, rank)
+
+
+def run_mix(owner_of, place_of, gathered, rank, blocks, chunk, apart):
     chunks = len(gathered)
     devices, count, rows, _ = gathered[0].shape
     half = rows // 2
+    groups, span = blocks.shape[1:3]
     smem = pl.BlockSpec(memory_space=pltpu.SMEM)
     shapes = [(devices, 1, half, LANES)] * count if apart else [(devices, count, half, LANES)]
     shapes = [jax.ShapeDtypeStruct(shape, jnp.bfloat16) for shape in shapes]
@@ -417,8 +420,8 @@
         in_specs=[
             smem,
             smem,
-            pl.BlockSpec((1, count, rows, rows), lambda i: (i, chunk, 0, 0)),
-            pl.BlockSpec((1,) + blocks.shape[1:], lambda i: (i, 0, 0, 0)),
+            rank_spec(rank),
+            pl.BlockSpec((1, groups, span // chunks, span), lambda i: (i, 0, chunk, 0)),
         ]
         + [part_spec] * chunks,
         out_specs=[whole_spec(shape) for shape in shapes],
@@ -429,7 +432,7 @@
         compiler_params=params(),
         cost_estimate=cost(6 * devices * count * rows**2 * LANES, 6 * devices * count * rows**2),
         name="mix",
-    )(owner_of, place_of, give, blocks, *gathered)
+    )(owner_of, place_of, rank, blocks, *gathered)
 
 
 def unit_tables(entries, capacity, unit):
@@ -502,9 +505,13 @@
     capacity = 2 * edge_rows // narrow
     atoms = angles.shape[0]
     count = wide // CHUNKS
-    offsets = [[chunk + index * CHUNKS for index in range(count)] for chunk in range(CHUNKS)]
+    spread_out = [offset for index in range(wide // 2) for offset in (index, wide - 1 - index)]
+    offsets = [spread_out[chunk * count : (chunk + 1) * count] for chunk in range(CHUNKS)]
     group_id = lax.axis_index("wide").astype(jnp.int32)
     order = group_id ^ jnp.array(sum(offsets, []), jnp.int32)
+    inverse = jnp.array([spread_out.index(offset) for offset in range(wide)], jnp.int32)
+    owners_wide = (jnp.arange(wide, dtype=jnp.int32) ^ group_id)[:, None]
+    position = jnp.sum(jnp.where(owners_wide == jnp.arange(wide), inverse, 0), axis=1)
     places = [order[chunk * count : (chunk + 1) * count] for chunk in range(CHUNKS)]
     plain = jnp.arange(count, dtype=jnp.int32)
 
@@ -551,34 +558,40 @@
             entries, all_angles, held[-1] = lax.optimization_barrier((entries, all_angles, held[-1]))
             spreads = dict(zip(chunk_order, held))
             owner_of, place_of = unit_tables(entries, capacity, unit)
-            tables = run_tables(owner_places, group_id[None], entries[:, :, None, :], all_angles, CHUNKS)
-        take, give, blocks = tables
+            tables = run_tables(owner_places, order, position, entries[:, :, None, :], all_angles)
+        listed_rank, blocks = tables
         gathered = [None] * CHUNKS
         for chunk in chunk_order:
-            gathered[chunk] = run_gather(owner_of, place_of, swap(spreads[chunk]), take, chunk)
+            gathered[chunk] = run_gather(owner_of, place_of, swap(spreads[chunk]), listed_rank, chunk)
         chunk_order = list(range(CHUNKS))[::-1]
         returned = {}
+        sent = None
         for chunk in chunk_order:
             early = chunk == 0
-            mixed = list(run_mix(owner_of, place_of, gathered, give, blocks, chunk, early))
+            mixed = list(run_mix(owner_of, place_of, gathered, listed_rank, blocks, chunk, early))
             if chunk != chunk_order[-1]:
                 mixed[0], gathered[0] = lax.optimization_barrier((mixed[0], gathered[0]))
             if early:
                 mixed = [shift(part, offset, wide) for part, offset in zip(mixed, offsets[chunk])]
+                if sent is not None:
+                    sent, mixed[0] = lax.optimization_barrier((sent, mixed[0]))
+                    returned[chunk_order[0]] = (sent, returned[chunk_order[0]][1])
                 parts = [swap(jnp.concatenate(mixed, axis=1))]
                 layout = [(0, index) for index in range(count)]
             else:
-                whole = swap(mixed[0])
-                parts = [
-                    shift(whole[:, index : index + 1], offset, wide)
-                    for index, offset in enumerate(offsets[chunk])
-                ]
+                sent = swap(mixed[0])
+                parts = sent
                 layout = [(index, 0) for index in range(count)]
             returned[chunk] = (parts, layout)
         current = [None] * CHUNKS
         received = [None] * CHUNKS
         for chunk in chunk_order:
             parts, layout = returned[chunk]
+            if chunk:
+                parts = [
+                    shift(parts[:, index : index + 1], offset, wide)
+                    for index, offset in enumerate(offsets[chunk])
+                ]
             result = run_back(
                 seconds[chunk], parts, layout, chunk, turned_rank, weights, section,
                 places[chunk] if last else plain, wide if last else count, target,

time: 353 us -> 311 us (0.88)
  Pallas kernels: 154 us -> 97.8 us
  local copies, waits for them, and re-layouts: 14.4 us -> 46 us
  blocking collectives: 25.6 us -> 0 us
  starting transfers between devices: 52.8 us -> 56.9 us
    unnamed x45 -> x119, local copies, waits for them, and re-layouts: 4.77 us -> 40.4 us
    all_to_all x1 -> x0, blocking collectives: 25.6 us -> none  [swap(): return lax.all_to_all(values, 'narrow', 0, 0, tiled=True)]
    pallas_call x5, Pallas kernels: 52.2 us -> 27.3 us  [the longest x4 20.3 us: run_gather(): pl.pallas_call(functools.partial(gather_kernel, chunk), grid=(devices,),...]
    ppermute x15, waiting for transfers between devices: 62.2 us -> 41.7 us  [shift(): return lax.ppermute(values, 'wide', [(i, i ^ offset) for i in range(wide)])]
    all_to_all x7 -> x8, waiting for transfers between devices: 28.8 us -> 48.4 us  [swap(): return lax.all_to_all(values, 'narrow', 0, 0, tiled=True)]
    pallas_call x4, Pallas kernels: 41.7 us -> 25.5 us  [run_mix(): pl.pallas_call(functools.partial(mix_kernel, chunk, chunks), grid=(device...]
    pallas_call x4, Pallas kernels: 33.9 us -> 25.5 us  [run_front(): pl.pallas_call(functools.partial(front_kernel, own, count), grid_spec=plt...]
    pallas_call x4, Pallas kernels: 25.9 us -> 19.5 us  [run_back(): pl.pallas_call(functools.partial(back_kernel, layout), grid_spec=pltpu.Pr...]
  transfers between devices with their start and end apart: 25 -> 26, of which waited for: 16 -> 16; matrix products, arithmetic and copies ran while one was open for 4% -> 3% of each run, Pallas kernels for 28% -> 23%
where the time goes in v1:
time: 311 us; the launch traced here: 309 us
  waiting for transfers between devices  99.2 us (32%)
  Pallas kernels  97.8 us (31%)
  starting transfers between devices  56.9 us (18%)
  local copies, waits for them, and re-layouts  46 us (15%)
  other arithmetic  8.83 us (3%)
    all_to_all x8, waiting for transfers between devices, swap(): return lax.all_to_all(values, 'narrow', 0, 0, tiled=True)  48.4 us
    ppermute x15, waiting for transfers between devices, shift(): return lax.ppermute(values, 'wide', [(i, i ^ offset) for i in range(wide)])  41.7 us
    unnamed x119, local copies, waits for them, and re-layouts  40.4 us
    all_to_all x8, starting transfers between devices, swap(): return lax.all_to_all(values, 'narrow', 0, 0, tiled=True)  36.4 us
    pallas_call x4, Pallas kernels, run_mix(): pl.pallas_call(functools.partial(mix_kernel, chunk, chunks), grid=(device...  25.5 us
    pallas_call x4, Pallas kernels, run_front(): pl.pallas_call(functools.partial(front_kernel, own, count), grid_spec=plt...  25.5 us
    pallas_call x4, Pallas kernels, run_gather(): pl.pallas_call(functools.partial(gather_kernel, chunk), grid=(devices,),...  20.3 us
    pallas_call x4, Pallas kernels, run_back(): pl.pallas_call(functools.partial(back_kernel, layout), grid_spec=pltpu.Pr...  19.5 us
  transfers between devices with their start and end apart: 26, of which 16 were waited for; matrix products, arithmetic and copies ran while one was open for 3% of the time, Pallas kernels for 23%

profile of v1, /device:TPU:0, one launch (start us, length us, event | category | flops | bytes accessed | tf_op | source)
XLA Modules:
  0.0 309.4 jit_solution(12097775411557021867)
XLA Ops:
  16.4 5.2 %collective-permute-done.5 = bf16[2,48,1088]{2,1,0:T(8,128)(2,1)S(1)} collective-permute-done((bf16[2,48,1088]{2,1,0:T(8,128)(2,1)S(1)}, bf16[2,48,1088]{2,1,0:T(8,128)(2,1)S(1)}, u32[]{:S(2)}, u32[]{:S(2)}) %collective-permute-start.5) | collective-permute-done | bytes 208928 | tf_op jit(solution)/shard_map/ppermute | solution.py:485
  27.4 6.3 %front.4 = (bf16[2,384,512]{2,1,0:T(8,128)(2,1)S(1)}, bf16[8,2,192,128]{3,2,1,0:T(8,128)(2,1)}) custom-call(s32[2]{0:T(128)S(1)} %get-tuple-element.80.where_ref, bf16[4,384,512]{2,1,0:T(8,128)(2,1)S(1)} %bitcast.52, s32[4,1,384]{2,1,0:T(1,128)S(1)} %broadcast_in_dim.194.back_ref, s32[4,1,384]{2,1,0:T(1,128)S(1)} %broadcast_in_dim.196.rank_ref, ...), custom_call_target="tpu_custom_call" | custom-call | flops 2415919104 | bytes 3145728 | tf_op jit(solution)/shard_map/front/pallas_call | solution.py:296
  34.5 5.9 %all-to-all-start = ((bf16[8,2,192,128]{3,2,1,0:T(8,128)(2,1)}), bf16[8,2,192,128]{3,2,1,0:T(8,128)(2,1)S(1)}, u32[]{:S(2)}, u32[]{:S(2)}) async-start(bf16[8,2,192,128]{3,2,1,0:T(8,128)(2,1)} %get-tuple-element.36), calls=%async_computation | async-start | bytes 1572864 | tf_op jit(solution)/shard_map/all_to_all | solution.py:471
  46.6 7.4 %front.5 = (bf16[2,384,512]{2,1,0:T(8,128)(2,1)S(1)}, bf16[8,2,192,128]{3,2,1,0:T(8,128)(2,1)}) custom-call(s32[2]{0:T(128)S(1)} %get-tuple-element.79.where_ref, bf16[4,384,512]{2,1,0:T(8,128)(2,1)S(1)} %bitcast.53, s32[4,1,384]{2,1,0:T(1,128)S(1)} %broadcast_in_dim.194.back_ref, s32[4,1,384]{2,1,0:T(1,128)S(1)} %broadcast_in_dim.196.rank_ref, ...), custom_call_target="tpu_custom_call" | custom-call | flops 2415919104 | bytes 3145728 | tf_op jit(solution)/shard_map/front/pallas_call | solution.py:296
  55.9 5.5 %all-to-all-done.recv_ref = bf16[8,2,192,128]{3,2,1,0:T(8,128)(2,1)S(1)} async-done(((bf16[8,2,192,128]{3,2,1,0:T(8,128)(2,1)}), bf16[8,2,192,128]{3,2,1,0:T(8,128)(2,1)S(1)}, u32[]{:S(2)}, u32[]{:S(2)}) %all-to-all-start) | async-done | bytes 786464 | tf_op jit(solution)/shard_map/all_to_all | solution.py:471
  65.1 7.0 %tables.1 = (s32[8,4,1,384]{3,2,1,0:T(1,128)S(1)}, bf16[8,6,256,256]{3,2,1,0:T(8,128)(2,1)S(1)}) custom-call(s32[8]{0:T(128)S(1)} %select_reduce_fusion.9.places_ref, s32[4]{0:T(128)S(1)} %get-tuple-element.82.order_ref, s32[4]{0:T(128)S(1)} %select_reduce_fusion.10.position_ref, s32[8,4,1,384]{3,2,1,0:T(1,128)S(1)} %broadcast_in_dim.216.entry_ref, ...), custom_call_target="tpu_custom_call" | custom-call | bytes 25165824 | tf_op jit(solution)/shard_map/tables/pallas_call | solution.py:360
  75.3 5.0 %gather.4.refs_0_ = bf16[8,2,384,128]{3,2,1,0:T(8,128)(2,1)S(1)} custom-call(s32[8,8]{1,0:T(8,128)S(1)} %get-tuple-element.56.owner_ref, s32[8,8]{1,0:T(8,128)S(1)} %get-tuple-element.55.place_ref, bf16[8,2,192,128]{3,2,1,0:T(8,128)(2,1)S(1)} %all-to-all-done.recv_ref, s32[8,4,1,384]{3,2,1,0:T(1,128)S(1)} %get-tuple-element.34.rank_ref), custom_call_target="tpu_custom_call" | custom-call | flops 1207959552 | bytes 9437184 | tf_op jit(solution)/shard_map/gather/pallas_call | solution.py:388
  80.3 5.6 %all-to-all-done.1.recv_ref = bf16[8,2,192,128]{3,2,1,0:T(8,128)(2,1)S(1)} async-done(((bf16[8,2,192,128]{3,2,1,0:T(8,128)(2,1)}), bf16[8,2,192,128]{3,2,1,0:T(8,128)(2,1)S(1)}, u32[]{:S(2)}, u32[]{:S(2)}) %all-to-all-start.1) | async-done | bytes 786464 | tf_op jit(solution)/shard_map/all_to_all | solution.py:471
  87.9 4.9 %gather.5.refs_1_ = bf16[8,2,384,128]{3,2,1,0:T(8,128)(2,1)S(1)} custom-call(s32[8,8]{1,0:T(8,128)S(1)} %get-tuple-element.56.owner_ref, s32[8,8]{1,0:T(8,128)S(1)} %get-tuple-element.55.place_ref, bf16[8,2,192,128]{3,2,1,0:T(8,128)(2,1)S(1)} %copy-done.17, s32[8,4,1,384]{3,2,1,0:T(1,128)S(1)} %get-tuple-element.34.rank_ref), custom_call_target="tpu_custom_call" | custom-call | flops 1207959552 | bytes 9437184 | tf_op jit(solution)/shard_map/gather/pallas_call | solution.py:388
  95.6 6.0 %mix.4 = bf16[8,2,192,128]{3,2,1,0:T(8,128)(2,1)S(1)} custom-call(s32[8,8]{1,0:T(8,128)S(1)} %get-tuple-element.56.owner_ref, s32[8,8]{1,0:T(8,128)S(1)} %get-tuple-element.55.place_ref, s32[8,4,1,384]{3,2,1,0:T(1,128)S(1)} %get-tuple-element.34.rank_ref, bf16[8,6,256,256]{3,2,1,0:T(8,128)(2,1)S(1)} %copy-done.1, ...), custom_call_target="tpu_custom_call" | custom-call | flops 1811939328 | bytes 14155776 | tf_op jit(solution)/shard_map/mix/pallas_call | solution.py:417
  102.5 4.2 %all-to-all-start.2 = ((bf16[8,2,192,128]{3,2,1,0:T(8,128)(2,1)}), bf16[8,2,192,128]{3,2,1,0:T(8,128)(2,1)}, u32[]{:S(2)}, u32[]{:S(2)}) async-start(bf16[8,2,192,128]{3,2,1,0:T(8,128)(2,1)} %copy-done.12), calls=%async_computation.2 | async-start | bytes 1572864 | tf_op jit(solution)/shard_map/all_to_all | solution.py:471
  109.5 6.8 %mix.5 = (bf16[8,1,192,128]{3,2,1,0:T(8,128)(2,1)S(1)}, bf16[8,1,192,128]{3,2,1,0:T(8,128)(2,1)}) custom-call(s32[8,8]{1,0:T(8,128)S(1)} %get-tuple-element.56.owner_ref, s32[8,8]{1,0:T(8,128)S(1)} %get-tuple-element.55.place_ref, s32[8,4,1,384]{3,2,1,0:T(1,128)S(1)} %get-tuple-element.34.rank_ref, bf16[8,6,256,256]{3,2,1,0:T(8,128)(2,1)S(1)} %copy-done.2, ...), custom_call_target="tpu_custom_call" | custom-call | flops 1811939328 | bytes 14155776 | tf_op jit(solution)/shard_map/mix/pallas_call | solution.py:417
  117.6 10.2 %all-to-all-done.2 = bf16[8,2,192,128]{3,2,1,0:T(8,128)(2,1)} async-done(((bf16[8,2,192,128]{3,2,1,0:T(8,128)(2,1)}), bf16[8,2,192,128]{3,2,1,0:T(8,128)(2,1)}, u32[]{:S(2)}, u32[]{:S(2)}) %all-to-all-start.2) | async-done | bytes 786464 | tf_op jit(solution)/shard_map/all_to_all | solution.py:471
  131.8 4.8 %all-to-all-start.3 = ((bf16[8,2,192,128]{3,2,1,0:T(8,128)(2,1)}), bf16[8,2,192,128]{3,2,1,0:T(8,128)(2,1)}, u32[]{:S(2)}, u32[]{:S(2)}) async-start(bf16[8,2,192,128]{3,2,1,0:T(8,128)(2,1)} %pad_maximum_fusion.1), calls=%async_computation.3 | async-start | bytes 1572864 | tf_op jit(solution)/shard_map/all_to_all | solution.py:471
  142.4 7.2 %collective-permute-done.3 = s32[384]{0:T(512)S(1)} collective-permute-done((s32[384]{0:T(512)S(1)}, s32[384]{0:T(512)S(1)}, u32[]{:S(2)}, u32[]{:S(2)}) %collective-permute-start.3) | collective-permute-done | bytes 1568 | tf_op jit(solution)/shard_map/ppermute | solution.py:467
  157.5 8.5 %collective-permute-done.13.refs_0_ = bf16[384,512]{1,0:T(8,128)(2,1)S(1)} collective-permute-done((bf16[384,512]{1,0:T(8,128)(2,1)S(1)}, bf16[384,512]{1,0:T(8,128)(2,1)S(1)}, u32[]{:S(2)}, u32[]{:S(2)}) %collective-permute-start.13) | collective-permute-done | bytes 393248 | tf_op jit(solution)/shard_map/ppermute | solution.py:467
  167.3 5.6 %front.7 = (bf16[2,384,512]{2,1,0:T(8,128)(2,1)S(1)}, bf16[8,2,192,128]{3,2,1,0:T(8,128)(2,1)S(1)}) custom-call(s32[2]{0:T(128)S(1)} %iota.77.where_ref, bf16[2,384,512]{2,1,0:T(8,128)(2,1)S(1)} %back.5.cur_ref, s32[4,1,384]{2,1,0:T(1,128)S(1)} %broadcast_in_dim.194.back_ref, s32[4,1,384]{2,1,0:T(1,128)S(1)} %broadcast_in_dim.196.rank_ref, ...), custom_call_target="tpu_custom_call" | custom-call | flops 2415919104 | bytes 3145728 | tf_op jit(solution)/shard_map/front/pallas_call | solution.py:296
  174.7 4.2 %all-to-all-start.5 = ((bf16[8,2,192,128]{3,2,1,0:T(8,128)(2,1)}), bf16[8,2,192,128]{3,2,1,0:T(8,128)(2,1)}, u32[]{:S(2)}, u32[]{:S(2)}) async-start(bf16[8,2,192,128]{3,2,1,0:T(8,128)(2,1)} %copy-done.18), calls=%async_computation.5 | async-start | bytes 1572864 | tf_op jit(solution)/shard_map/all_to_all | solution.py:471
  180.1 5.3 %back.4.cur_ref = bf16[2,384,512]{2,1,0:T(8,128)(2,1)S(1)} custom-call(s32[2]{0:T(128)S(1)} %iota.74.where_ref, bf16[2,384,512]{2,1,0:T(8,128)(2,1)S(1)} %copy-done.46, s32[4,1,384]{2,1,0:T(1,128)S(1)} %broadcast_in_dim.199.rank_ref, bf16[2,512,512]{2,1,0:T(8,128)(2,1)S(1)} %copy-done.5, bf16[2,512,512]{2,1,0:T(8,128)(2,1)S(1)} %copy-done.7, ...), custom_call_target="tpu_custom_call" | custom-call | flops 1610612736 | bytes 2359296 | tf_op jit(solution)/shard_map/back/pallas_call | solution.py:328
  187.0 11.0 %collective-permute-done.10.refs_0_ = bf16[384,512]{1,0:T(8,128)(2,1)S(1)} collective-permute-done((bf16[384,512]{1,0:T(8,128)(2,1)S(1)}, bf16[384,512]{1,0:T(8,128)(2,1)S(1)}, u32[]{:S(2)}, u32[]{:S(2)}) %collective-permute-start.10) | collective-permute-done | bytes 393248 | tf_op jit(solution)/shard_map/ppermute | solution.py:467
  198.0 6.2 %front.6 = (bf16[2,384,512]{2,1,0:T(8,128)(2,1)S(1)}, bf16[8,2,192,128]{3,2,1,0:T(8,128)(2,1)}) custom-call(s32[2]{0:T(128)S(1)} %iota.73.where_ref, bf16[2,384,512]{2,1,0:T(8,128)(2,1)S(1)} %back.4.cur_ref, s32[4,1,384]{2,1,0:T(1,128)S(1)} %broadcast_in_dim.194.back_ref, s32[4,1,384]{2,1,0:T(1,128)S(1)} %broadcast_in_dim.196.rank_ref, ...), custom_call_target="tpu_custom_call" | custom-call | flops 2415919104 | bytes 3145728 | tf_op jit(solution)/shard_map/front/pallas_call | solution.py:296
  205.1 4.8 %all-to-all-start.4 = ((bf16[8,2,192,128]{3,2,1,0:T(8,128)(2,1)}), bf16[8,2,192,128]{3,2,1,0:T(8,128)(2,1)S(1)}, u32[]{:S(2)}, u32[]{:S(2)}) async-start(bf16[8,2,192,128]{3,2,1,0:T(8,128)(2,1)} %get-tuple-element.44), calls=%async_computation.4 | async-start | bytes 1572864 | tf_op jit(solution)/shard_map/all_to_all | solution.py:471
  209.8 5.5 %gather.7.refs_1_ = bf16[8,2,384,128]{3,2,1,0:T(8,128)(2,1)S(1)} custom-call(s32[8,8]{1,0:T(8,128)S(1)} %get-tuple-element.56.owner_ref, s32[8,8]{1,0:T(8,128)S(1)} %get-tuple-element.55.place_ref, bf16[8,2,192,128]{3,2,1,0:T(8,128)(2,1)} %all-to-all-done.5.recv_ref, s32[8,4,1,384]{3,2,1,0:T(1,128)S(1)} %get-tuple-element.34.rank_ref), custom_call_target="tpu_custom_call" | custom-call | flops 1207959552 | bytes 9437184 | tf_op jit(solution)/shard_map/gather/pallas_call | solution.py:388
  215.3 15.5 %all-to-all-done.4.recv_ref = bf16[8,2,192,128]{3,2,1,0:T(8,128)(2,1)S(1)} async-done(((bf16[8,2,192,128]{3,2,1,0:T(8,128)(2,1)}), bf16[8,2,192,128]{3,2,1,0:T(8,128)(2,1)S(1)}, u32[]{:S(2)}, u32[]{:S(2)}) %all-to-all-start.4) | async-done | bytes 786464 | tf_op jit(solution)/shard_map/all_to_all | solution.py:471
  232.8 4.9 %gather.6.refs_0_ = bf16[8,2,384,128]{3,2,1,0:T(8,128)(2,1)S(1)} custom-call(s32[8,8]{1,0:T(8,128)S(1)} %get-tuple-element.56.owner_ref, s32[8,8]{1,0:T(8,128)S(1)} %get-tuple-element.55.place_ref, bf16[8,2,192,128]{3,2,1,0:T(8,128)(2,1)S(1)} %copy-done.20, s32[8,4,1,384]{3,2,1,0:T(1,128)S(1)} %get-tuple-element.34.rank_ref), custom_call_target="tpu_custom_call" | custom-call | flops 1207959552 | bytes 9437184 | tf_op jit(solution)/shard_map/gather/pallas_call | solution.py:388
  240.6 6.0 %mix.6 = bf16[8,2,192,128]{3,2,1,0:T(8,128)(2,1)S(1)} custom-call(s32[8,8]{1,0:T(8,128)S(1)} %get-tuple-element.56.owner_ref, s32[8,8]{1,0:T(8,128)S(1)} %get-tuple-element.55.place_ref, s32[8,4,1,384]{3,2,1,0:T(1,128)S(1)} %get-tuple-element.34.rank_ref, bf16[8,6,256,256]{3,2,1,0:T(8,128)(2,1)S(1)} %copy-done.3, ...), custom_call_target="tpu_custom_call" | custom-call | flops 1811939328 | bytes 14155776 | tf_op jit(solution)/shard_map/mix/pallas_call | solution.py:417
  254.5 6.7 %mix.7 = (bf16[8,1,192,128]{3,2,1,0:T(8,128)(2,1)S(1)}, bf16[8,1,192,128]{3,2,1,0:T(8,128)(2,1)}) custom-call(s32[8,8]{1,0:T(8,128)S(1)} %get-tuple-element.56.owner_ref, s32[8,8]{1,0:T(8,128)S(1)} %get-tuple-element.55.place_ref, s32[8,4,1,384]{3,2,1,0:T(1,128)S(1)} %get-tuple-element.34.rank_ref, bf16[8,6,256,256]{3,2,1,0:T(8,128)(2,1)S(1)} %copy-done.4, ...), custom_call_target="tpu_custom_call" | custom-call | flops 1811939328 | bytes 14155776 | tf_op jit(solution)/shard_map/mix/pallas_call | solution.py:417
  263.3 9.3 %all-to-all-done.6 = bf16[8,2,192,128]{3,2,1,0:T(8,128)(2,1)} async-done(((bf16[8,2,192,128]{3,2,1,0:T(8,128)(2,1)}), bf16[8,2,192,128]{3,2,1,0:T(8,128)(2,1)}, u32[]{:S(2)}, u32[]{:S(2)}) %all-to-all-start.6) | async-done | bytes 786464 | tf_op jit(solution)/shard_map/all_to_all | solution.py:471
  276.7 4.8 %all-to-all-start.7 = ((bf16[8,2,192,128]{3,2,1,0:T(8,128)(2,1)}), bf16[8,2,192,128]{3,2,1,0:T(8,128)(2,1)}, u32[]{:S(2)}, u32[]{:S(2)}) async-start(bf16[8,2,192,128]{3,2,1,0:T(8,128)(2,1)} %pad_maximum_fusion.2), calls=%async_computation.7 | async-start | bytes 1572864 | tf_op jit(solution)/shard_map/all_to_all | solution.py:471
  284.6 9.6 %collective-permute-done.16.refs_0_ = bf16[8,1,192,128]{3,2,1,0:T(8,128)(2,1)S(1)} collective-permute-done((bf16[8,1,192,128]{3,2,1,0:T(8,128)(2,1)S(1)}, bf16[8,1,192,128]{3,2,1,0:T(8,128)(2,1)S(1)}, u32[]{:S(2)}, u32[]{:S(2)}) %collective-permute-start.16) | collective-permute-done | bytes 393248 | tf_op jit(solution)/shard_map/ppermute | solution.py:467
  295.6 4.6 %back.6.refs_1_ = bf16[4,384,512]{2,1,0:T(8,128)(2,1)} custom-call(s32[2]{0:T(128)S(1)} %get-tuple-element.79.where_ref, bf16[2,384,512]{2,1,0:T(8,128)(2,1)S(1)} %copy-done.22, s32[4,1,384]{2,1,0:T(1,128)S(1)} %broadcast_in_dim.199.rank_ref, bf16[2,512,512]{2,1,0:T(8,128)(2,1)S(1)} %copy-done.6, bf16[2,512,512]{2,1,0:T(8,128)(2,1)S(1)} %copy-done.8, ...), custom_call_target="tpu_custom_call" | custom-call | flops 1610612736 | bytes 2359296 | tf_op jit(solution)/shard_map/back/pallas_call | solution.py:328
  303.7 5.7 %back.7 = bf16[4,384,512]{2,1,0:T(8,128)(2,1)} custom-call(s32[2]{0:T(128)S(1)} %get-tuple-element.80.where_ref, bf16[2,384,512]{2,1,0:T(8,128)(2,1)S(1)} %copy-done.15, s32[4,1,384]{2,1,0:T(1,128)S(1)} %broadcast_in_dim.199.rank_ref, bf16[2,512,512]{2,1,0:T(8,128)(2,1)S(1)} %copy-done.6, ...), custom_call_target="tpu_custom_call", output_to_operand_aliasing={{}: (7, {})} | custom-call | flops 1610612736 | bytes 2359296 | tf_op jit(solution)/shard_map/back/pallas_call | solution.py:328
  (212 shorter events, 98.4 us)
Async XLA Ops:
  0.0 22.5 %copy-start.13 = (bf16[1536,512]{1,0:T(8,128)(2,1)S(1)}, bf16[1536,512]{1,0:T(8,128)(2,1)}, u32[]{:S(2)}) copy-start(bf16[1536,512]{1,0:T(8,128)(2,1)} %param.16) | copy-start | bytes 4718596
  0.0 22.4 %copy-start.25 = (bf16[2,512,512]{2,1,0:T(8,128)(2,1)S(1)}, bf16[2,512,512]{2,1,0:T(8,128)(2,1)}, u32[]{:S(2)}) copy-start(bf16[2,512,512]{2,1,0:T(8,128)(2,1)} %wm.7) | copy-start | bytes 3145732
  2.5 20.0 %collective-permute-start = (bf16[384,512]{1,0:T(8,128)(2,1)}, bf16[384,512]{1,0:T(8,128)(2,1)S(1)}, u32[]{:S(2)}, u32[]{:S(2)}) collective-permute-start(bf16[384,512]{1,0:T(8,128)(2,1)} %get-tuple-element.67), channel_id=1, source_target_pairs={{0,24},{8,16},{16,8},{24,0},{1,25},{9,17},{17,9},{25,1},{2,26},{10... | collective-permute-start | bytes 1179656 | tf_op jit(solution)/shard_map/ppermute | solution.py:467
  7.5 7.9 %collective-permute-start.4 = (bf16[1,48,1088]{2,1,0:T(8,128)(2,1)S(1)}, bf16[1,48,1088]{2,1,0:T(8,128)(2,1)S(1)}, u32[]{:S(2)}, u32[]{:S(2)}) collective-permute-start(bf16[1,48,1088]{2,1,0:T(8,128)(2,1)S(1)} %maximum_bitcast_fusion), channel_id=1, source_target_pairs={{0,4},{1,5},{2,6},{3,7},{4,0},{5,1},{6,2},{7,3},{8,12},{9,13},{10,... | collective-permute-start | bytes 313352 | tf_op jit(solution)/shard_map/ppermute | solution.py:485
  10.2 30.3 %collective-permute-start.7 = (bf16[384,512]{1,0:T(8,128)(2,1)}, bf16[384,512]{1,0:T(8,128)(2,1)}, u32[]{:S(2)}, u32[]{:S(2)}) collective-permute-start(bf16[384,512]{1,0:T(8,128)(2,1)} %get-tuple-element.66), channel_id=1, source_target_pairs={{0,8},{8,0},{16,24},{24,16},{1,9},{9,1},{17,25},{25,17},{2,10},{10... | collective-permute-start | bytes 1179656 | tf_op jit(solution)/shard_map/ppermute | solution.py:467
  10.7 29.8 %collective-permute-start.8 = (bf16[384,512]{1,0:T(8,128)(2,1)}, bf16[384,512]{1,0:T(8,128)(2,1)}, u32[]{:S(2)}, u32[]{:S(2)}) collective-permute-start(bf16[384,512]{1,0:T(8,128)(2,1)} %get-tuple-element.65), channel_id=1, source_target_pairs={{0,16},{8,24},{16,0},{24,8},{1,17},{9,25},{17,1},{25,9},{2,18},{10... | collective-permute-start | bytes 1179656 | tf_op jit(solution)/shard_map/ppermute | solution.py:467
  15.4 6.2 %collective-permute-start.5 = (bf16[2,48,1088]{2,1,0:T(8,128)(2,1)S(1)}, bf16[2,48,1088]{2,1,0:T(8,128)(2,1)S(1)}, u32[]{:S(2)}, u32[]{:S(2)}) collective-permute-start(bf16[2,48,1088]{2,1,0:T(8,128)(2,1)S(1)} %pad_maximum_fusion.4), channel_id=1, source_target_pairs={{0,2},{1,3},{2,0},{3,1},{4,6},{5,7},{6,4},{7,5},{8,10},{9,11},{10,... | collective-permute-start | bytes 626696 | tf_op jit(solution)/shard_map/ppermute | solution.py:485
  22.4 31.6 %collective-permute-start.6 = (bf16[4,48,1088]{2,1,0:T(8,128)(2,1)}, bf16[4,48,1088]{2,1,0:T(8,128)(2,1)}, u32[]{:S(2)}, u32[]{:S(2)}) collective-permute-start(bf16[4,48,1088]{2,1,0:T(8,128)(2,1)} %pad_maximum_fusion.3), channel_id=1, source_target_pairs={{0,1},{1,0},{2,3},{3,2},{4,5},{5,4},{6,7},{7,6},{8,9},{9,8},{10,11... | collective-permute-start | bytes 1253384 | tf_op jit(solution)/shard_map/ppermute | solution.py:485
  34.5 26.9 %all-to-all-start = ((bf16[8,2,192,128]{3,2,1,0:T(8,128)(2,1)}), bf16[8,2,192,128]{3,2,1,0:T(8,128)(2,1)S(1)}, u32[]{:S(2)}, u32[]{:S(2)}) async-start(bf16[8,2,192,128]{3,2,1,0:T(8,128)(2,1)} %get-tuple-element.36), calls=%async_computation | async-start | bytes 1572864 | tf_op jit(solution)/shard_map/all_to_all | solution.py:471
  61.4 24.5 %all-to-all-start.1 = ((bf16[8,2,192,128]{3,2,1,0:T(8,128)(2,1)}), bf16[8,2,192,128]{3,2,1,0:T(8,128)(2,1)S(1)}, u32[]{:S(2)}, u32[]{:S(2)}) async-start(bf16[8,2,192,128]{3,2,1,0:T(8,128)(2,1)} %get-tuple-element.37), calls=%async_computation.1 | async-start | bytes 1572864 | tf_op jit(solution)/shard_map/all_to_all | solution.py:471
  102.5 25.2 %all-to-all-start.2 = ((bf16[8,2,192,128]{3,2,1,0:T(8,128)(2,1)}), bf16[8,2,192,128]{3,2,1,0:T(8,128)(2,1)}, u32[]{:S(2)}, u32[]{:S(2)}) async-start(bf16[8,2,192,128]{3,2,1,0:T(8,128)(2,1)} %copy-done.12), calls=%async_computation.2 | async-start | bytes 1572864 | tf_op jit(solution)/shard_map/all_to_all | solution.py:471
  117.1 12.6 %collective-permute-start.9 = (bf16[8,1,192,128]{3,2,1,0:T(8,128)(2,1)}, bf16[8,1,192,128]{3,2,1,0:T(8,128)(2,1)}, u32[]{:S(2)}, u32[]{:S(2)}) collective-permute-start(bf16[8,1,192,128]{3,2,1,0:T(8,128)(2,1)} %get-tuple-element.42), channel_id=1, source_target_pairs={{0,24},{8,16},{16,8},{24,0},{1,25},{9,17},{17,9},{25,1},{2,26},{10... | collective-permute-start | bytes 1179656 | tf_op jit(solution)/shard_map/ppermute | solution.py:467
  127.7 22.5 %copy-start.5 = (bf16[2,512,512]{2,1,0:T(8,128)(2,1)S(1)}, bf16[2,512,512]{2,1,0:T(8,128)(2,1)}, u32[]{:S(2)}) copy-start(bf16[2,512,512]{2,1,0:T(8,128)(2,1)} %wl.7) | copy-start | bytes 3145732
  127.7 22.6 %copy-start.7 = (bf16[2,512,512]{2,1,0:T(8,128)(2,1)S(1)}, bf16[2,512,512]{2,1,0:T(8,128)(2,1)}, u32[]{:S(2)}) copy-start(bf16[2,512,512]{2,1,0:T(8,128)(2,1)} %we.7) | copy-start | bytes 3145732
  127.7 22.6 %copy-start.9 = (bf16[2,512,512]{2,1,0:T(8,128)(2,1)S(1)}, bf16[2,512,512]{2,1,0:T(8,128)(2,1)}, u32[]{:S(2)}) copy-start(bf16[2,512,512]{2,1,0:T(8,128)(2,1)} %wd.7) | copy-start | bytes 3145732
  131.8 43.0 %all-to-all-start.3 = ((bf16[8,2,192,128]{3,2,1,0:T(8,128)(2,1)}), bf16[8,2,192,128]{3,2,1,0:T(8,128)(2,1)}, u32[]{:S(2)}, u32[]{:S(2)}) async-start(bf16[8,2,192,128]{3,2,1,0:T(8,128)(2,1)} %pad_maximum_fusion.1), calls=%async_computation.3 | async-start | bytes 1572864 | tf_op jit(solution)/shard_map/all_to_all | solution.py:471
  137.7 12.5 %collective-permute-start.11 = (bf16[8,1,192,128]{3,2,1,0:T(8,128)(2,1)S(1)}, bf16[8,1,192,128]{3,2,1,0:T(8,128)(2,1)S(1)}, u32[]{:S(2)}, u32[]{:S(2)}) collective-permute-start(bf16[8,1,192,128]{3,2,1,0:T(8,128)(2,1)S(1)} %get-tuple-element.73), channel_id=1, source_target_pairs={{0,8},{8,0},{16,24},{24,16},{1,9},{9,1},{17,25},{25,17},{2,10},{10... | collective-permute-start | bytes 1179656 | tf_op jit(solution)/shard_map/ppermute | solution.py:467
  138.3 12.0 %collective-permute-start.12 = (bf16[8,1,192,128]{3,2,1,0:T(8,128)(2,1)S(1)}, bf16[8,1,192,128]{3,2,1,0:T(8,128)(2,1)S(1)}, u32[]{:S(2)}, u32[]{:S(2)}) collective-permute-start(bf16[8,1,192,128]{3,2,1,0:T(8,128)(2,1)S(1)} %get-tuple-element.72), channel_id=1, source_target_pairs={{0,16},{8,24},{16,0},{24,8},{1,17},{9,25},{17,1},{25,9},{2,18},{10... | collective-permute-start | bytes 1179656 | tf_op jit(solution)/shard_map/ppermute | solution.py:467
  138.8 10.8 %collective-permute-start.3 = (s32[384]{0:T(512)S(1)}, s32[384]{0:T(512)S(1)}, u32[]{:S(2)}, u32[]{:S(2)}) collective-permute-start(s32[384]{0:T(512)S(1)} %get-tuple-element.58), channel_id=1, source_target_pairs={{0,16},{8,24},{16,0},{24,8},{1,17},{9,25},{17,1},{25,9},{2,18},{10... | collective-permute-start | bytes 4616 | tf_op jit(solution)/shard_map/ppermute | solution.py:467
  140.4 9.2 %collective-permute-start.2 = (s32[384]{0:T(512)S(1)}, s32[384]{0:T(512)S(1)}, u32[]{:S(2)}, u32[]{:S(2)}) collective-permute-start(s32[384]{0:T(512)S(1)} %get-tuple-element.59), channel_id=1, source_target_pairs={{0,8},{8,0},{16,24},{24,16},{1,9},{9,1},{17,25},{25,17},{2,10},{10... | collective-permute-start | bytes 4616 | tf_op jit(solution)/shard_map/ppermute | solution.py:467
  141.9 7.7 %collective-permute-start.1 = (s32[384]{0:T(512)S(1)}, s32[384]{0:T(512)S(1)}, u32[]{:S(2)}, u32[]{:S(2)}) collective-permute-start(s32[384]{0:T(512)S(1)} %get-tuple-element.57), channel_id=1, source_target_pairs={{0,24},{8,16},{16,8},{24,0},{1,25},{9,17},{17,9},{25,1},{2,26},{10... | collective-permute-start | bytes 4616 | tf_op jit(solution)/shard_map/ppermute | solution.py:467
  155.4 10.6 %collective-permute-start.13 = (bf16[384,512]{1,0:T(8,128)(2,1)S(1)}, bf16[384,512]{1,0:T(8,128)(2,1)S(1)}, u32[]{:S(2)}, u32[]{:S(2)}) collective-permute-start(bf16[384,512]{1,0:T(8,128)(2,1)S(1)} %get-tuple-element.71), channel_id=1, source_target_pairs={{0,8},{8,0},{16,24},{24,16},{1,9},{9,1},{17,25},{25,17},{2,10},{10... | collective-permute-start | bytes 1179656 | tf_op jit(solution)/shard_map/ppermute | solution.py:467
  157.0 10.3 %collective-permute-start.14 = (bf16[384,512]{1,0:T(8,128)(2,1)S(1)}, bf16[384,512]{1,0:T(8,128)(2,1)S(1)}, u32[]{:S(2)}, u32[]{:S(2)}) collective-permute-start(bf16[384,512]{1,0:T(8,128)(2,1)S(1)} %get-tuple-element.70), channel_id=1, source_target_pairs={{0,16},{8,24},{16,0},{24,8},{1,17},{9,25},{17,1},{25,9},{2,18},{10... | collective-permute-start | bytes 1179656 | tf_op jit(solution)/shard_map/ppermute | solution.py:467
  174.7 30.3 %all-to-all-start.5 = ((bf16[8,2,192,128]{3,2,1,0:T(8,128)(2,1)}), bf16[8,2,192,128]{3,2,1,0:T(8,128)(2,1)}, u32[]{:S(2)}, u32[]{:S(2)}) async-start(bf16[8,2,192,128]{3,2,1,0:T(8,128)(2,1)} %copy-done.18), calls=%async_computation.5 | async-start | bytes 1572864 | tf_op jit(solution)/shard_map/all_to_all | solution.py:471
  185.4 12.5 %collective-permute-start.10 = (bf16[384,512]{1,0:T(8,128)(2,1)S(1)}, bf16[384,512]{1,0:T(8,128)(2,1)S(1)}, u32[]{:S(2)}, u32[]{:S(2)}) collective-permute-start(bf16[384,512]{1,0:T(8,128)(2,1)S(1)} %slice_bitcast_fusion.2), channel_id=1, source_target_pairs={{0,24},{8,16},{16,8},{24,0},{1,25},{9,17},{17,9},{25,1},{2,26},{10... | collective-permute-start | bytes 1179656 | tf_op jit(solution)/shard_map/ppermute | solution.py:467
  205.1 25.7 %all-to-all-start.4 = ((bf16[8,2,192,128]{3,2,1,0:T(8,128)(2,1)}), bf16[8,2,192,128]{3,2,1,0:T(8,128)(2,1)S(1)}, u32[]{:S(2)}, u32[]{:S(2)}) async-start(bf16[8,2,192,128]{3,2,1,0:T(8,128)(2,1)} %get-tuple-element.44), calls=%async_computation.4 | async-start | bytes 1572864 | tf_op jit(solution)/shard_map/all_to_all | solution.py:471
  247.5 25.2 %all-to-all-start.6 = ((bf16[8,2,192,128]{3,2,1,0:T(8,128)(2,1)}), bf16[8,2,192,128]{3,2,1,0:T(8,128)(2,1)}, u32[]{:S(2)}, u32[]{:S(2)}) async-start(bf16[8,2,192,128]{3,2,1,0:T(8,128)(2,1)} %copy-done.11), calls=%async_computation.6 | async-start | bytes 1572864 | tf_op jit(solution)/shard_map/all_to_all | solution.py:471
  262.0 12.6 %collective-permute-start.15 = (bf16[8,1,192,128]{3,2,1,0:T(8,128)(2,1)}, bf16[8,1,192,128]{3,2,1,0:T(8,128)(2,1)}, u32[]{:S(2)}, u32[]{:S(2)}) collective-permute-start(bf16[8,1,192,128]{3,2,1,0:T(8,128)(2,1)} %get-tuple-element.52), channel_id=1, source_target_pairs={{0,24},{8,16},{16,8},{24,0},{1,25},{9,17},{17,9},{25,1},{2,26},{10... | collective-permute-start | bytes 1179656 | tf_op jit(solution)/shard_map/ppermute | solution.py:467
  272.7 21.8 %copy-start.10 = (bf16[2,512,512]{2,1,0:T(8,128)(2,1)S(1)}, bf16[2,512,512]{2,1,0:T(8,128)(2,1)}, u32[]{:S(2)}) copy-start(bf16[2,512,512]{2,1,0:T(8,128)(2,1)} %wd.7) | copy-start | bytes 3145732
  276.7 25.8 %all-to-all-start.7 = ((bf16[8,2,192,128]{3,2,1,0:T(8,128)(2,1)}), bf16[8,2,192,128]{3,2,1,0:T(8,128)(2,1)}, u32[]{:S(2)}, u32[]{:S(2)}) async-start(bf16[8,2,192,128]{3,2,1,0:T(8,128)(2,1)} %pad_maximum_fusion.2), calls=%async_computation.7 | async-start | bytes 1572864 | tf_op jit(solution)/shard_map/all_to_all | solution.py:471
  282.6 11.6 %collective-permute-start.16 = (bf16[8,1,192,128]{3,2,1,0:T(8,128)(2,1)S(1)}, bf16[8,1,192,128]{3,2,1,0:T(8,128)(2,1)S(1)}, u32[]{:S(2)}, u32[]{:S(2)}) collective-permute-start(bf16[8,1,192,128]{3,2,1,0:T(8,128)(2,1)S(1)} %get-tuple-element.69), channel_id=1, source_target_pairs={{0,8},{8,0},{16,24},{24,16},{1,9},{9,1},{17,25},{25,17},{2,10},{10... | collective-permute-start | bytes 1179656 | tf_op jit(solution)/shard_map/ppermute | solution.py:467
  283.3 11.2 %collective-permute-start.17 = (bf16[8,1,192,128]{3,2,1,0:T(8,128)(2,1)S(1)}, bf16[8,1,192,128]{3,2,1,0:T(8,128)(2,1)S(1)}, u32[]{:S(2)}, u32[]{:S(2)}) collective-permute-start(bf16[8,1,192,128]{3,2,1,0:T(8,128)(2,1)S(1)} %get-tuple-element.68), channel_id=1, source_target_pairs={{0,16},{8,24},{16,0},{24,8},{1,17},{9,25},{17,1},{25,9},{2,18},{10... | collective-permute-start | bytes 1179656 | tf_op jit(solution)/shard_map/ppermute | solution.py:467
  (52 other events, 329.5 us)

commit v2 on v1

--- a/solution.py
+++ b/solution.py
@@ -106,8 +106,32 @@
     return jnp.where(mask, 1.0, 0.0).astype(jnp.bfloat16)
 
 
-def front_kernel(own, count, where_ref, cur_ref, back_ref, rank_ref, wm, wr, wc, wi, wo, *refs):
-    recv_refs, (second_ref, packed_ref, reverse_ref) = refs[:-3], refs[-3:]
+def fetcher(weight_refs, section, held, sems):
+    first = pl.program_id(0) == 0
+    copies = [
+        pltpu.make_async_copy(ref.at[section], held.at[index], sems.at[index])
+        for index, ref in enumerate(weight_refs)
+    ]
+
+    @pl.when(first)
+    def _():
+        for copy in copies:
+            copy.start()
+
+    def weight(index):
+        @pl.when(first)
+        def _():
+            copies[index].wait()
+
+        return held[index]
+
+    return weight
+
+
+def front_kernel(own, count, section, where_ref, cur_ref, back_ref, rank_ref, *refs):
+    weight_refs, refs = refs[:5], refs[5:]
+    recv_refs, (second_ref, packed_ref, reverse_ref, held, sems) = refs[:-5], refs[-5:]
+    weight = fetcher(weight_refs, section, held, sems)
     rows_iota, lanes_iota = iotas(cur_ref.shape[1])
     partner = as_column(back_ref[0], rows_iota, lanes_iota)
     hot = one_hot(partner == lanes_iota)
@@ -119,10 +143,11 @@
             reverse_ref[...] = dot(hot, sources[index][...]).astype(jnp.bfloat16)
 
     current = cur_ref[0]
-    hidden = silu(dot(current, wm[0]) + dot(reverse_ref[...], wr[0])).astype(jnp.bfloat16)
-    first_res = halve(current, dot(hidden, wc[0]))
-    inner = silu(dot(first_res, wi[0])).astype(jnp.bfloat16)
-    second = halve(first_res, silu(dot(inner, wo[0])))
+    own_part = dot(current, weight(0))
+    hidden = silu(own_part + dot(reverse_ref[...], weight(1))).astype(jnp.bfloat16)
+    first_res = halve(current, dot(hidden, weight(2)))
+    inner = silu(dot(first_res, weight(3))).astype(jnp.bfloat16)
+    second = halve(first_res, silu(dot(inner, weight(4))))
     second_ref[0] = second
     ordered = dot(one_hot(rows_iota == rank_ref[0]), second)
     half = ordered.shape[0] // 2
@@ -134,8 +159,10 @@
         packed_ref[2 * tile + 1, 0] = jnp.where(low, pltpu.roll(top, HALF, 1), bottom).astype(jnp.bfloat16)
 
 
-def back_kernel(layout, where_ref, second_ref, rank_ref, wl, we, wd, *refs):
-    out_ref, ordered_ref = refs[-2:]
+def back_kernel(layout, section, where_ref, second_ref, rank_ref, *refs):
+    weight_refs, refs = refs[:3], refs[3:]
+    out_ref, ordered_ref, held, sems = refs[-4:]
+    weight = fetcher(weight_refs, section, held, sems)
     rows_iota, lanes_iota = iotas(second_ref.shape[1])
     half = rows_iota.shape[0] // 2
     low = lax.broadcasted_iota(jnp.int32, (half, LANES), 1) < HALF
@@ -154,9 +181,9 @@
 
     source = as_column(rank_ref[0], rows_iota, lanes_iota)
     turned = dot(one_hot(source == lanes_iota), ordered_ref[...]).astype(jnp.bfloat16)
-    third_res = halve(second_ref[0], silu(dot(turned, wl[0])))
-    expand = silu(dot(third_res, we[0])).astype(jnp.bfloat16)
-    out_ref[0] = halve(third_res, silu(dot(expand, wd[0])))
+    third_res = halve(second_ref[0], silu(dot(turned, weight(0))))
+    expand = silu(dot(third_res, weight(1))).astype(jnp.bfloat16)
+    out_ref[0] = halve(third_res, silu(dot(expand, weight(2))))
 
 
 def table_kernel(places_ref, order_ref, position_ref, entry_ref, angles_ref, rank_ref, blocks_ref):
@@ -216,13 +243,25 @@
 
 
 def mix_kernel(chunk, chunks, owner_ref, place_ref, rank_ref, blocks_ref, *refs):
-    gathered_refs, out_refs, outs = refs[:chunks], refs[chunks:-1], refs[-1]
+    gathered_refs, out_refs, (outs, held, sems) = refs[:chunks], refs[chunks:-3], refs[-3:]
     step = pl.program_id(0)
+    part = held.shape[2]
+
+    def fetch(owner):
+        rows = pl.ds(chunk * part, part)
+        return pltpu.make_async_copy(blocks_ref.at[owner, :, rows, :], held.at[owner], sems.at[owner])
+
+    @pl.when(step == 0)
+    def _():
+        for owner in range(held.shape[0]):
+            fetch(owner).start()
+
+    fetch(step).wait()
     count = outs.shape[0]
     devices = outs.shape[1]
     unit = outs.shape[3]
     groups = blocks_ref.shape[1]
-    strip = blocks_ref.shape[2] // count
+    strip = part // count
     pairs = devices // 2
     rows_iota = iotas(devices * unit)[0]
     mixed = []
@@ -235,10 +274,10 @@
             ],
             axis=0,
         )
-        mixed.append(dot(blocks_ref[0, group], operand).astype(jnp.bfloat16))
+        mixed.append(dot(held[step, group], operand).astype(jnp.bfloat16))
     for side in range(count):
         operand = jnp.concatenate(
-            [part[side * strip : (side + 1) * strip] for part in mixed], axis=0
+            [rows[side * strip : (side + 1) * strip] for rows in mixed], axis=0
         )
         outs[side, step] = (
             dot(one_hot(rows_iota == rank_ref[0, chunk * count + side]), operand)
@@ -268,7 +307,7 @@
                         out_refs[side][source, 0, rows, :] = joined
 
 
-VMEM_BYTES = 24 * 1024 * 1024
+VMEM_BYTES = 60 * 1024 * 1024
 
 
 def params():
@@ -284,8 +323,14 @@
     return pl.BlockSpec(array.shape, lambda i, *_: zeros)
 
 
-def weight_spec(section, features):
-    return pl.BlockSpec((1, features, features), lambda i, *_: (section, 0, 0))
+HBM_SPEC = pl.BlockSpec(memory_space=pltpu.HBM)
+
+
+def weight_scratch(number, features):
+    return [
+        pltpu.VMEM((number, features, features), jnp.bfloat16),
+        pltpu.SemaphoreType.DMA((number,)),
+    ]
 
 
 def run_front(current, where, received, own, chunk, back_rows, rank_rows, weights, section, narrow):
@@ -294,7 +339,7 @@
     edge_spec = pl.BlockSpec((1, rows, features), lambda i, where: (i, 0, 0))
     row_spec = pl.BlockSpec((1, 1, rows), lambda i, where: (chunk * count + i, 0, 0))
     return pl.pallas_call(
-        functools.partial(front_kernel, own, count),
+        functools.partial(front_kernel, own, count, section),
         grid_spec=pltpu.PrefetchScalarGridSpec(
             num_scalar_prefetch=1,
             grid=(count,),
@@ -303,13 +348,13 @@
                 row_spec,
                 row_spec,
             ]
-            + [weight_spec(section, features)] * 5
+            + [HBM_SPEC] * 5
             + [whole_spec(array) for array in received],
             out_specs=[
                 edge_spec,
                 pl.BlockSpec((narrow, 1, rows // 2, LANES), lambda i, where: (0, i, 0, 0)),
             ],
-            scratch_shapes=[pltpu.VMEM((rows, features), jnp.bfloat16)],
+            scratch_shapes=[pltpu.VMEM((rows, features), jnp.bfloat16)] + weight_scratch(5, features),
         ),
         out_shape=[
             jax.ShapeDtypeStruct((count, rows, features), jnp.bfloat16),
@@ -326,7 +371,7 @@
     edge_spec = pl.BlockSpec((1, rows, features), lambda i, where: (i, 0, 0))
     extra = [] if target is None else [target]
     return pl.pallas_call(
-        functools.partial(back_kernel, layout),
+        functools.partial(back_kernel, layout, section),
         grid_spec=pltpu.PrefetchScalarGridSpec(
             num_scalar_prefetch=1,
             grid=(count,),
@@ -334,11 +379,11 @@
                 edge_spec,
                 pl.BlockSpec((1, 1, rows), lambda i, where: (chunk * count + i, 0, 0)),
             ]
-            + [weight_spec(section, features)] * 3
+            + [HBM_SPEC] * 3
             + [whole_spec(array) for array in packed]
-            + [pl.BlockSpec(memory_space=pl.ANY)] * len(extra),
+            + [HBM_SPEC] * len(extra),
             out_specs=pl.BlockSpec((1, rows, features), lambda i, where: (where[i], 0, 0)),
-            scratch_shapes=[pltpu.VMEM((rows, features), jnp.bfloat16)],
+            scratch_shapes=[pltpu.VMEM((rows, features), jnp.bfloat16)] + weight_scratch(3, features),
         ),
         out_shape=jax.ShapeDtypeStruct((total, rows, features), jnp.bfloat16),
         input_output_aliases={6 + len(packed): 0} if extra else {},
@@ -421,13 +466,15 @@
             smem,
             smem,
             rank_spec(rank),
-            pl.BlockSpec((1, groups, span // chunks, span), lambda i: (i, 0, chunk, 0)),
+            HBM_SPEC,
         ]
         + [part_spec] * chunks,
         out_specs=[whole_spec(shape) for shape in shapes],
         out_shape=shapes,
         scratch_shapes=[
-            pltpu.VMEM((count, devices, devices, rows // devices, LANES), jnp.bfloat16)
+            pltpu.VMEM((count, devices, devices, rows // devices, LANES), jnp.bfloat16),
+            pltpu.VMEM((devices, groups, span // chunks, span), jnp.bfloat16),
+            pltpu.SemaphoreType.DMA((devices,)),
         ],
         compiler_params=params(),
         cost_estimate=cost(6 * devices * count * rows**2 * LANES, 6 * devices * count * rows**2),
@@ -526,7 +573,6 @@
     ]
     listed = atom_slots.reshape(atoms // GROUP, GROUP, wide, SLOTS // wide)
     listed = reorder(jnp.transpose(listed, (2, 0, 3, 1)).reshape(wide, rows), order)
-    entries, all_angles, owner_places = share_lists(listed, angles)
     rank = ranks(route_slot.reshape(wide, rows))
     back_rows = reverse_position.reshape(wide, rows)
     back_rows = reorder(back_rows, order)
@@ -552,6 +598,9 @@
                 current[chunk], where[chunk], received[chunk], offsets[chunk][0] == 0, chunk,
                 back_rows, rank, weights, section, narrow,
             )
+            if tables is None and chunk == chunk_order[0]:
+                listed, packed = lax.optimization_barrier((listed, packed))
+                entries, all_angles, owner_places = share_lists(listed, angles)
             spreads[chunk] = packed
         if tables is None:
             held = [spreads[chunk] for chunk in chunk_order]
@@ -574,12 +623,13 @@
             if early:
                 mixed = [shift(part, offset, wide) for part, offset in zip(mixed, offsets[chunk])]
                 if sent is not None:
-                    sent, mixed[0] = lax.optimization_barrier((sent, mixed[0]))
+                    *sent, mixed[0] = lax.optimization_barrier((*sent, mixed[0]))
                     returned[chunk_order[0]] = (sent, returned[chunk_order[0]][1])
                 parts = [swap(jnp.concatenate(mixed, axis=1))]
                 layout = [(0, index) for index in range(count)]
             else:
-                sent = swap(mixed[0])
+                whole = swap(mixed[0])
+                sent = [whole[:, index : index + 1] for index in range(count)]
                 parts = sent
                 layout = [(index, 0) for index in range(count)]
             returned[chunk] = (parts, layout)
@@ -588,10 +638,7 @@
         for chunk in chunk_order:
             parts, layout = returned[chunk]
             if chunk:
-                parts = [
-                    shift(parts[:, index : index + 1], offset, wide)
-                    for index, offset in enumerate(offsets[chunk])
-                ]
+                parts = [shift(part, offset, wide) for part, offset in zip(parts, offsets[chunk])]
             result = run_back(
                 seconds[chunk], parts, layout, chunk, turned_rank, weights, section,
                 places[chunk] if last else plain, wide if last else count, target,

time: 311 us -> 330 us (1.061)
  Pallas kernels: 97.8 us -> 144 us
  local copies, waits for them, and re-layouts: 46 us -> 15.3 us
  starting transfers between devices: 56.9 us -> 62.6 us
    unnamed x119 -> x53, local copies, waits for them, and re-layouts: 40.4 us -> 5.68 us
    pallas_call x8, Pallas kernels: 44.9 us -> 66.1 us  [the longest x4 37 us: run_front(): pl.pallas_call(functools.partial(front_kernel, own, count, section), grid...]
    pallas_call x4, Pallas kernels: 25.5 us -> 39.4 us  [run_mix(): pl.pallas_call(functools.partial(mix_kernel, chunk, chunks), grid=(device...]
    pallas_call x4, Pallas kernels: 20.3 us -> 29.1 us  [run_gather(): pl.pallas_call(functools.partial(gather_kernel, chunk), grid=(devices,),...]
    ppermute x15, starting transfers between devices: 17.1 us -> 21.8 us  [shift(): return lax.ppermute(values, 'wide', [(i, i ^ offset) for i in range(wide)])]
    ppermute x15, waiting for transfers between devices: 41.7 us -> 45.8 us  [shift(): return lax.ppermute(values, 'wide', [(i, i ^ offset) for i in range(wide)])]
    all_to_all x8, waiting for transfers between devices: 48.4 us -> 44.6 us  [swap(): return lax.all_to_all(values, 'narrow', 0, 0, tiled=True)]
  transfers between devices with their start and end apart: 26 -> 26, of which waited for: 16 -> 17; matrix products, arithmetic and copies ran while one was open for 3% -> 4% of each run, Pallas kernels for 23% -> 31%
where the time goes in v2:
time: 330 us; the launch traced here: 327 us
  Pallas kernels  144 us (44%)
  waiting for transfers between devices  96.7 us (29%)
  starting transfers between devices  62.6 us (19%)
  local copies, waits for them, and re-layouts  15.3 us (5%)
  other arithmetic  7.57 us (2%)
    ppermute x15, waiting for transfers between devices, shift(): return lax.ppermute(values, 'wide', [(i, i ^ offset) for i in range(wide)])  45.8 us
    all_to_all x8, waiting for transfers between devices, swap(): return lax.all_to_all(values, 'narrow', 0, 0, tiled=True)  44.6 us
    pallas_call x4, Pallas kernels, run_mix(): pl.pallas_call(functools.partial(mix_kernel, chunk, chunks), grid=(device...  39.4 us
    pallas_call x4, Pallas kernels, run_front(): pl.pallas_call(functools.partial(front_kernel, own, count, section), grid...  37 us
    all_to_all x8, starting transfers between devices, swap(): return lax.all_to_all(values, 'narrow', 0, 0, tiled=True)  35.3 us
    pallas_call x4, Pallas kernels, run_back(): pl.pallas_call(functools.partial(back_kernel, layout, section), grid_spec...  29.1 us
    pallas_call x4, Pallas kernels, run_gather(): pl.pallas_call(functools.partial(gather_kernel, chunk), grid=(devices,),...  29.1 us
    ppermute x15, starting transfers between devices, shift(): return lax.ppermute(values, 'wide', [(i, i ^ offset) for i in range(wide)])  21.8 us
  transfers between devices with their start and end apart: 26, of which 17 were waited for; matrix products, arithmetic and copies ran while one was open for 4% of the time, Pallas kernels for 31%

profile of v2, /device:TPU:0, one launch (start us, length us, event | category | flops | bytes accessed | tf_op | source)
XLA Modules:
  0.0 327.2 jit_solution(1317035310607530235)
XLA Ops:
  1.4 4.0 %collective-permute-start = (bf16[384,512]{1,0:T(8,128)(2,1)S(1)}, bf16[384,512]{1,0:T(8,128)(2,1)S(1)}, u32[]{:S(2)}, u32[]{:S(2)}) collective-permute-start(bf16[384,512]{1,0:T(8,128)(2,1)S(1)} %get-tuple-element.75), channel_id=1, source_target_pairs={{0,24},{8,16},{16,8},{24,0},{1,25},{9,17},{17,9},{25,1},{2,26},{10... | collective-permute-start | bytes 1179656 | tf_op jit(solution)/shard_map/ppermute | solution.py:514
  8.8 6.6 %collective-permute-done.refs_5_ = bf16[384,512]{1,0:T(8,128)(2,1)S(1)} collective-permute-done((bf16[384,512]{1,0:T(8,128)(2,1)S(1)}, bf16[384,512]{1,0:T(8,128)(2,1)S(1)}, u32[]{:S(2)}, u32[]{:S(2)}) %collective-permute-start) | collective-permute-done | bytes 393248 | tf_op jit(solution)/shard_map/ppermute | solution.py:514
  16.1 9.3 %front.4 = (bf16[2,384,512]{2,1,0:T(8,128)(2,1)}, bf16[8,2,192,128]{3,2,1,0:T(8,128)(2,1)}) custom-call(s32[2]{0:T(128)} %get-tuple-element.88.where_ref, bf16[4,384,512]{2,1,0:T(8,128)(2,1)} %bitcast.34, s32[4,1,384]{2,1,0:T(1,128)} %broadcast_in_dim.194.back_ref, s32[4,1,384]{2,1,0:T(1,128)} %broadcast_in_dim.196.rank_ref, bf16[2,512,512]{2,1,0:T(8,128)(2,1)} %refs_0_.13, ...), custom_call_target="tpu_custom_call" | custom-call | flops 2415919104 | bytes 3145728 | tf_op jit(solution)/shard_map/front/pallas_call | solution.py:341
  38.5 6.3 %all-to-all-start = ((bf16[8,2,192,128]{3,2,1,0:T(8,128)(2,1)}), bf16[8,2,192,128]{3,2,1,0:T(8,128)(2,1)S(1)}, u32[]{:S(2)}, u32[]{:S(2)}) async-start(bf16[8,2,192,128]{3,2,1,0:T(8,128)(2,1)} %get-tuple-element.42), calls=%async_computation | async-start | bytes 1572864 | tf_op jit(solution)/shard_map/all_to_all | solution.py:518
  45.5 9.3 %front.5 = (bf16[2,384,512]{2,1,0:T(8,128)(2,1)}, bf16[8,2,192,128]{3,2,1,0:T(8,128)(2,1)}) custom-call(s32[2]{0:T(128)} %get-tuple-element.87.where_ref, bf16[4,384,512]{2,1,0:T(8,128)(2,1)} %bitcast.35, s32[4,1,384]{2,1,0:T(1,128)} %broadcast_in_dim.194.back_ref, s32[4,1,384]{2,1,0:T(1,128)} %broadcast_in_dim.196.rank_ref, bf16[2,512,512]{2,1,0:T(8,128)(2,1)} %refs_0_.13, ...), custom_call_target="tpu_custom_call" | custom-call | flops 2415919104 | bytes 3145728 | tf_op jit(solution)/shard_map/front/pallas_call | solution.py:341
  55.4 10.3 %all-to-all-done.recv_ref = bf16[8,2,192,128]{3,2,1,0:T(8,128)(2,1)S(1)} async-done(((bf16[8,2,192,128]{3,2,1,0:T(8,128)(2,1)}), bf16[8,2,192,128]{3,2,1,0:T(8,128)(2,1)S(1)}, u32[]{:S(2)}, u32[]{:S(2)}) %all-to-all-start) | async-done | bytes 786464 | tf_op jit(solution)/shard_map/all_to_all | solution.py:518
  70.0 9.9 %tables.1 = (s32[8,4,1,384]{3,2,1,0:T(1,128)}, bf16[8,6,256,256]{3,2,1,0:T(8,128)(2,1)}) custom-call(s32[8]{0:T(128)} %copy-done.14, s32[4]{0:T(128)} %copy-done.10, s32[4]{0:T(128)} %select_reduce_fusion.10.position_ref, s32[8,4,1,384]{3,2,1,0:T(1,128)} %broadcast_in_dim.216.entry_ref, bf16[8,48,1088]{2,1,0:T(8,128)(2,1)} %copy-done), custom_call_target="tpu_custom_call" | custom-call | bytes 25165824 | tf_op jit(solution)/shard_map/tables/pallas_call | solution.py:405
  81.0 7.3 %gather.4.refs_0_ = bf16[8,2,384,128]{3,2,1,0:T(8,128)(2,1)} custom-call(s32[8,8]{1,0:T(8,128)} %get-tuple-element.64.owner_ref, s32[8,8]{1,0:T(8,128)} %get-tuple-element.63.place_ref, bf16[8,2,192,128]{3,2,1,0:T(8,128)(2,1)} %copy-done.3, s32[8,4,1,384]{3,2,1,0:T(1,128)} %get-tuple-element.40.rank_ref), custom_call_target="tpu_custom_call" | custom-call | flops 1207959552 | bytes 9437184 | tf_op jit(solution)/shard_map/gather/pallas_call | solution.py:433
  91.0 7.3 %gather.5.refs_1_ = bf16[8,2,384,128]{3,2,1,0:T(8,128)(2,1)} custom-call(s32[8,8]{1,0:T(8,128)} %get-tuple-element.64.owner_ref, s32[8,8]{1,0:T(8,128)} %get-tuple-element.63.place_ref, bf16[8,2,192,128]{3,2,1,0:T(8,128)(2,1)} %copy-done.4, s32[8,4,1,384]{3,2,1,0:T(1,128)} %get-tuple-element.40.rank_ref), custom_call_target="tpu_custom_call" | custom-call | flops 1207959552 | bytes 9437184 | tf_op jit(solution)/shard_map/gather/pallas_call | solution.py:433
  98.3 9.8 %mix.4 = bf16[8,2,192,128]{3,2,1,0:T(8,128)(2,1)} custom-call(s32[8,8]{1,0:T(8,128)} %get-tuple-element.64.owner_ref, s32[8,8]{1,0:T(8,128)} %get-tuple-element.63.place_ref, s32[8,4,1,384]{3,2,1,0:T(1,128)} %get-tuple-element.40.rank_ref, bf16[8,6,256,256]{3,2,1,0:T(8,128)(2,1)} %get-tuple-element.41.blocks_ref, bf16[8,2,384,128]{3,2,1,0:T(8,128)(2,1)} %gather.4.refs_0_, ...), custom_call_target="tpu_custom_call" | custom-call | flops 1811939328 | bytes 14155776 | tf_op jit(solution)/shard_map/mix/pallas_call | solution.py:462
  111.7 9.9 %mix.5 = (bf16[8,1,192,128]{3,2,1,0:T(8,128)(2,1)}, bf16[8,1,192,128]{3,2,1,0:T(8,128)(2,1)}) custom-call(s32[8,8]{1,0:T(8,128)} %get-tuple-element.64.owner_ref, s32[8,8]{1,0:T(8,128)} %get-tuple-element.63.place_ref, s32[8,4,1,384]{3,2,1,0:T(1,128)} %get-tuple-element.40.rank_ref, bf16[8,6,256,256]{3,2,1,0:T(8,128)(2,1)} %get-tuple-element.41.blocks_ref, ...), custom_call_target="tpu_custom_call" | custom-call | flops 1811939328 | bytes 14155776 | tf_op jit(solution)/shard_map/mix/pallas_call | solution.py:462
  124.1 8.5 %all-to-all-done.2 = bf16[8,2,192,128]{3,2,1,0:T(8,128)(2,1)S(1)} async-done(((bf16[8,2,192,128]{3,2,1,0:T(8,128)(2,1)}), bf16[8,2,192,128]{3,2,1,0:T(8,128)(2,1)S(1)}, u32[]{:S(2)}, u32[]{:S(2)}) %all-to-all-start.2) | async-done | bytes 786464 | tf_op jit(solution)/shard_map/all_to_all | solution.py:518
  136.1 4.8 %all-to-all-start.3 = ((bf16[8,2,192,128]{3,2,1,0:T(8,128)(2,1)}), bf16[8,2,192,128]{3,2,1,0:T(8,128)(2,1)S(1)}, u32[]{:S(2)}, u32[]{:S(2)}) async-start(bf16[8,2,192,128]{3,2,1,0:T(8,128)(2,1)} %pad_maximum_fusion.1), calls=%async_computation.3 | async-start | bytes 1572864 | tf_op jit(solution)/shard_map/all_to_all | solution.py:518
  147.4 6.2 %collective-permute-done.3 = s32[384]{0:T(512)S(1)} collective-permute-done((s32[384]{0:T(512)S(1)}, s32[384]{0:T(512)S(1)}, u32[]{:S(2)}, u32[]{:S(2)}) %collective-permute-start.3) | collective-permute-done | bytes 1568 | tf_op jit(solution)/shard_map/ppermute | solution.py:514
  155.8 7.3 %back.5.cur_ref = bf16[2,384,512]{2,1,0:T(8,128)(2,1)} custom-call(s32[2]{0:T(128)} %iota.78.where_ref, bf16[2,384,512]{2,1,0:T(8,128)(2,1)} %get-tuple-element.51.second_ref, s32[4,1,384]{2,1,0:T(1,128)} %broadcast_in_dim.199.rank_ref, bf16[2,512,512]{2,1,0:T(8,128)(2,1)} %refs_0_.15, bf16[2,512,512]{2,1,0:T(8,128)(2,1)} %refs_1_.15, ...), custom_call_target="tpu_custom_call" | custom-call | flops 1610612736 | bytes 2359296 | tf_op jit(solution)/shard_map/back/pallas_call | solution.py:373
  166.4 8.4 %collective-permute-done.13.refs_5_ = bf16[384,512]{1,0:T(8,128)(2,1)S(1)} collective-permute-done((bf16[384,512]{1,0:T(8,128)(2,1)S(1)}, bf16[384,512]{1,0:T(8,128)(2,1)S(1)}, u32[]{:S(2)}, u32[]{:S(2)}) %collective-permute-start.13) | collective-permute-done | bytes 393248 | tf_op jit(solution)/shard_map/ppermute | solution.py:514
  176.7 9.3 %front.7 = (bf16[2,384,512]{2,1,0:T(8,128)(2,1)}, bf16[8,2,192,128]{3,2,1,0:T(8,128)(2,1)}) custom-call(s32[2]{0:T(128)} %iota.77.where_ref, bf16[2,384,512]{2,1,0:T(8,128)(2,1)} %back.5.cur_ref, s32[4,1,384]{2,1,0:T(1,128)} %broadcast_in_dim.194.back_ref, s32[4,1,384]{2,1,0:T(1,128)} %broadcast_in_dim.196.rank_ref, bf16[2,512,512]{2,1,0:T(8,128)(2,1)} %refs_0_.13, ...), custom_call_target="tpu_custom_call" | custom-call | flops 2415919104 | bytes 3145728 | tf_op jit(solution)/shard_map/front/pallas_call | solution.py:341
  186.1 4.0 %all-to-all-start.5 = ((bf16[8,2,192,128]{3,2,1,0:T(8,128)(2,1)}), bf16[8,2,192,128]{3,2,1,0:T(8,128)(2,1)S(1)}, u32[]{:S(2)}, u32[]{:S(2)}) async-start(bf16[8,2,192,128]{3,2,1,0:T(8,128)(2,1)} %get-tuple-element.54), calls=%async_computation.5 | async-start | bytes 1572864 | tf_op jit(solution)/shard_map/all_to_all | solution.py:518
  190.7 7.3 %back.4.cur_ref = bf16[2,384,512]{2,1,0:T(8,128)(2,1)} custom-call(s32[2]{0:T(128)} %iota.74.where_ref, bf16[2,384,512]{2,1,0:T(8,128)(2,1)} %get-tuple-element.34.second_ref, s32[4,1,384]{2,1,0:T(1,128)} %broadcast_in_dim.199.rank_ref, bf16[2,512,512]{2,1,0:T(8,128)(2,1)} %refs_0_.15, bf16[2,512,512]{2,1,0:T(8,128)(2,1)} %refs_1_.15, ...), custom_call_target="tpu_custom_call" | custom-call | flops 1610612736 | bytes 2359296 | tf_op jit(solution)/shard_map/back/pallas_call | solution.py:373
  200.8 10.7 %collective-permute-done.10.refs_5_ = bf16[384,512]{1,0:T(8,128)(2,1)S(1)} collective-permute-done((bf16[384,512]{1,0:T(8,128)(2,1)S(1)}, bf16[384,512]{1,0:T(8,128)(2,1)S(1)}, u32[]{:S(2)}, u32[]{:S(2)}) %collective-permute-start.10) | collective-permute-done | bytes 393248 | tf_op jit(solution)/shard_map/ppermute | solution.py:514
  212.3 9.1 %front.6 = (bf16[2,384,512]{2,1,0:T(8,128)(2,1)}, bf16[8,2,192,128]{3,2,1,0:T(8,128)(2,1)}) custom-call(s32[2]{0:T(128)} %iota.73.where_ref, bf16[2,384,512]{2,1,0:T(8,128)(2,1)} %back.4.cur_ref, s32[4,1,384]{2,1,0:T(1,128)} %broadcast_in_dim.194.back_ref, s32[4,1,384]{2,1,0:T(1,128)} %broadcast_in_dim.196.rank_ref, bf16[2,512,512]{2,1,0:T(8,128)(2,1)} %refs_0_.13, ...), custom_call_target="tpu_custom_call" | custom-call | flops 2415919104 | bytes 3145728 | tf_op jit(solution)/shard_map/front/pallas_call | solution.py:341
  221.4 4.8 %all-to-all-start.4 = ((bf16[8,2,192,128]{3,2,1,0:T(8,128)(2,1)}), bf16[8,2,192,128]{3,2,1,0:T(8,128)(2,1)S(1)}, u32[]{:S(2)}, u32[]{:S(2)}) async-start(bf16[8,2,192,128]{3,2,1,0:T(8,128)(2,1)} %get-tuple-element.50), calls=%async_computation.4 | async-start | bytes 1572864 | tf_op jit(solution)/shard_map/all_to_all | solution.py:518
  226.2 7.3 %gather.7.refs_1_ = bf16[8,2,384,128]{3,2,1,0:T(8,128)(2,1)} custom-call(s32[8,8]{1,0:T(8,128)} %get-tuple-element.64.owner_ref, s32[8,8]{1,0:T(8,128)} %get-tuple-element.63.place_ref, bf16[8,2,192,128]{3,2,1,0:T(8,128)(2,1)} %copy-done.5, s32[8,4,1,384]{3,2,1,0:T(1,128)} %get-tuple-element.40.rank_ref), custom_call_target="tpu_custom_call" | custom-call | flops 1207959552 | bytes 9437184 | tf_op jit(solution)/shard_map/gather/pallas_call | solution.py:433
  233.5 13.7 %all-to-all-done.4.recv_ref = bf16[8,2,192,128]{3,2,1,0:T(8,128)(2,1)S(1)} async-done(((bf16[8,2,192,128]{3,2,1,0:T(8,128)(2,1)}), bf16[8,2,192,128]{3,2,1,0:T(8,128)(2,1)S(1)}, u32[]{:S(2)}, u32[]{:S(2)}) %all-to-all-start.4) | async-done | bytes 786464 | tf_op jit(solution)/shard_map/all_to_all | solution.py:518
  248.0 7.3 %gather.6.refs_0_ = bf16[8,2,384,128]{3,2,1,0:T(8,128)(2,1)} custom-call(s32[8,8]{1,0:T(8,128)} %get-tuple-element.64.owner_ref, s32[8,8]{1,0:T(8,128)} %get-tuple-element.63.place_ref, bf16[8,2,192,128]{3,2,1,0:T(8,128)(2,1)} %copy-done.6, s32[8,4,1,384]{3,2,1,0:T(1,128)} %get-tuple-element.40.rank_ref), custom_call_target="tpu_custom_call" | custom-call | flops 1207959552 | bytes 9437184 | tf_op jit(solution)/shard_map/gather/pallas_call | solution.py:433
  255.3 9.8 %mix.6 = bf16[8,2,192,128]{3,2,1,0:T(8,128)(2,1)} custom-call(s32[8,8]{1,0:T(8,128)} %get-tuple-element.64.owner_ref, s32[8,8]{1,0:T(8,128)} %get-tuple-element.63.place_ref, s32[8,4,1,384]{3,2,1,0:T(1,128)} %get-tuple-element.40.rank_ref, bf16[8,6,256,256]{3,2,1,0:T(8,128)(2,1)} %get-tuple-element.41.blocks_ref, bf16[8,2,384,128]{3,2,1,0:T(8,128)(2,1)} %gather.6.refs_0_, ...), custom_call_target="tpu_custom_call" | custom-call | flops 1811939328 | bytes 14155776 | tf_op jit(solution)/shard_map/mix/pallas_call | solution.py:462
  268.7 9.9 %mix.7 = (bf16[8,1,192,128]{3,2,1,0:T(8,128)(2,1)}, bf16[8,1,192,128]{3,2,1,0:T(8,128)(2,1)}) custom-call(s32[8,8]{1,0:T(8,128)} %get-tuple-element.64.owner_ref, s32[8,8]{1,0:T(8,128)} %get-tuple-element.63.place_ref, s32[8,4,1,384]{3,2,1,0:T(1,128)} %get-tuple-element.40.rank_ref, bf16[8,6,256,256]{3,2,1,0:T(8,128)(2,1)} %get-tuple-element.41.blocks_ref, ...), custom_call_target="tpu_custom_call" | custom-call | flops 1811939328 | bytes 14155776 | tf_op jit(solution)/shard_map/mix/pallas_call | solution.py:462
  280.4 9.2 %all-to-all-done.6 = bf16[8,2,192,128]{3,2,1,0:T(8,128)(2,1)S(1)} async-done(((bf16[8,2,192,128]{3,2,1,0:T(8,128)(2,1)}), bf16[8,2,192,128]{3,2,1,0:T(8,128)(2,1)S(1)}, u32[]{:S(2)}, u32[]{:S(2)}) %all-to-all-start.6) | async-done | bytes 786464 | tf_op jit(solution)/shard_map/all_to_all | solution.py:518
  293.1 4.8 %all-to-all-start.7 = ((bf16[8,2,192,128]{3,2,1,0:T(8,128)(2,1)}), bf16[8,2,192,128]{3,2,1,0:T(8,128)(2,1)S(1)}, u32[]{:S(2)}, u32[]{:S(2)}) async-start(bf16[8,2,192,128]{3,2,1,0:T(8,128)(2,1)} %pad_maximum_fusion.2), calls=%async_computation.7 | async-start | bytes 1572864 | tf_op jit(solution)/shard_map/all_to_all | solution.py:518
  300.2 9.2 %collective-permute-done.16.refs_3_ = bf16[8,1,192,128]{3,2,1,0:T(8,128)(2,1)S(1)} collective-permute-done((bf16[8,1,192,128]{3,2,1,0:T(8,128)(2,1)S(1)}, bf16[8,1,192,128]{3,2,1,0:T(8,128)(2,1)S(1)}, u32[]{:S(2)}, u32[]{:S(2)}) %collective-permute-start.16) | collective-permute-done | bytes 393248 | tf_op jit(solution)/shard_map/ppermute | solution.py:514
  310.6 7.3 %back.6.refs_4_ = bf16[4,384,512]{2,1,0:T(8,128)(2,1)} custom-call(s32[2]{0:T(128)} %get-tuple-element.87.where_ref, bf16[2,384,512]{2,1,0:T(8,128)(2,1)} %get-tuple-element.60.second_ref, s32[4,1,384]{2,1,0:T(1,128)} %broadcast_in_dim.199.rank_ref, bf16[2,512,512]{2,1,0:T(8,128)(2,1)} %refs_0_.15, bf16[2,512,512]{2,1,0:T(8,128)(2,1)} %refs_1_.15, ...), custom_call_target="tpu_custom_call" | custom-call | flops 1610612736 | bytes 2359296 | tf_op jit(solution)/shard_map/back/pallas_call | solution.py:373
  319.8 7.3 %back.7 = bf16[4,384,512]{2,1,0:T(8,128)(2,1)} custom-call(s32[2]{0:T(128)} %get-tuple-element.88.where_ref, bf16[2,384,512]{2,1,0:T(8,128)(2,1)} %get-tuple-element.49.second_ref, s32[4,1,384]{2,1,0:T(1,128)} %broadcast_in_dim.199.rank_ref, bf16[2,512,512]{2,1,0:T(8,128)(2,1)} %refs_0_.15, ...), custom_call_target="tpu_custom_call", output_to_operand_aliasing={{}: (7, {})} | custom-call | flops 1610612736 | bytes 2359296 | tf_op jit(solution)/shard_map/back/pallas_call | solution.py:373
  (146 shorter events, 70.8 us)
Async XLA Ops:
  1.4 13.9 %collective-permute-start = (bf16[384,512]{1,0:T(8,128)(2,1)S(1)}, bf16[384,512]{1,0:T(8,128)(2,1)S(1)}, u32[]{:S(2)}, u32[]{:S(2)}) collective-permute-start(bf16[384,512]{1,0:T(8,128)(2,1)S(1)} %get-tuple-element.75), channel_id=1, source_target_pairs={{0,24},{8,16},{16,8},{24,0},{1,25},{9,17},{17,9},{25,1},{2,26},{10... | collective-permute-start | bytes 1179656 | tf_op jit(solution)/shard_map/ppermute | solution.py:514
  5.3 39.4 %collective-permute-start.7 = (bf16[384,512]{1,0:T(8,128)(2,1)S(1)}, bf16[384,512]{1,0:T(8,128)(2,1)S(1)}, u32[]{:S(2)}, u32[]{:S(2)}) collective-permute-start(bf16[384,512]{1,0:T(8,128)(2,1)S(1)} %get-tuple-element.74), channel_id=1, source_target_pairs={{0,8},{8,0},{16,24},{24,16},{1,9},{9,1},{17,25},{25,17},{2,10},{10... | collective-permute-start | bytes 1179656 | tf_op jit(solution)/shard_map/ppermute | solution.py:514
  5.9 38.9 %collective-permute-start.8 = (bf16[384,512]{1,0:T(8,128)(2,1)S(1)}, bf16[384,512]{1,0:T(8,128)(2,1)}, u32[]{:S(2)}, u32[]{:S(2)}) collective-permute-start(bf16[384,512]{1,0:T(8,128)(2,1)S(1)} %get-tuple-element.73), channel_id=1, source_target_pairs={{0,16},{8,24},{16,0},{24,8},{1,17},{9,25},{17,1},{25,9},{2,18},{10... | collective-permute-start | bytes 1179656 | tf_op jit(solution)/shard_map/ppermute | solution.py:514
  6.0 19.4 %copy-start.10 = (s32[4]{0:T(128)}, s32[4]{0:T(128)S(1)}, u32[]{:S(2)}) copy-start(s32[4]{0:T(128)S(1)} %get-tuple-element.90.order_ref) | copy-start | bytes 52
  16.1 12.6 %copy-start.24 = (s32[8]{0:T(128)S(1)}, s32[8]{0:T(128)}, u32[]{:S(2)}) copy-start(s32[8]{0:T(128)} %constant.76.clone) | copy-start | bytes 100
  16.1 21.7 %copy-start.23 = (s32[4]{0:T(128)S(1)}, s32[4]{0:T(128)}, u32[]{:S(2)}) copy-start(s32[4]{0:T(128)} %constant.75.clone) | copy-start | bytes 52
  25.5 5.9 %collective-permute-start.4 = (bf16[1,48,1088]{2,1,0:T(8,128)(2,1)S(1)}, bf16[1,48,1088]{2,1,0:T(8,128)(2,1)S(1)}, u32[]{:S(2)}, u32[]{:S(2)}) collective-permute-start(bf16[1,48,1088]{2,1,0:T(8,128)(2,1)S(1)} %maximum_bitcast_fusion), channel_id=1, source_target_pairs={{0,4},{1,5},{2,6},{3,7},{4,0},{5,1},{6,2},{7,3},{8,12},{9,13},{10,... | collective-permute-start | bytes 313352 | tf_op jit(solution)/shard_map/ppermute | solution.py:532
  28.9 25.9 %copy-start.14 = (s32[8]{0:T(128)}, s32[8]{0:T(128)S(1)}, u32[]{:S(2)}) copy-start(s32[8]{0:T(128)S(1)} %select_reduce_fusion.9.places_ref) | copy-start | bytes 100
  31.5 6.2 %collective-permute-start.5 = (bf16[2,48,1088]{2,1,0:T(8,128)(2,1)S(1)}, bf16[2,48,1088]{2,1,0:T(8,128)(2,1)S(1)}, u32[]{:S(2)}, u32[]{:S(2)}) collective-permute-start(bf16[2,48,1088]{2,1,0:T(8,128)(2,1)S(1)} %pad_maximum_fusion.4), channel_id=1, source_target_pairs={{0,2},{1,3},{2,0},{3,1},{4,6},{5,7},{6,4},{7,5},{8,10},{9,11},{10,... | collective-permute-start | bytes 626696 | tf_op jit(solution)/shard_map/ppermute | solution.py:532
  37.7 17.1 %collective-permute-start.6 = (bf16[4,48,1088]{2,1,0:T(8,128)(2,1)S(1)}, bf16[4,48,1088]{2,1,0:T(8,128)(2,1)S(1)}, u32[]{:S(2)}, u32[]{:S(2)}) collective-permute-start(bf16[4,48,1088]{2,1,0:T(8,128)(2,1)S(1)} %pad_maximum_fusion.3), channel_id=1, source_target_pairs={{0,1},{1,0},{2,3},{3,2},{4,5},{5,4},{6,7},{7,6},{8,9},{9,8},{10,11... | collective-permute-start | bytes 1253384 | tf_op jit(solution)/shard_map/ppermute | solution.py:532
  38.5 27.3 %all-to-all-start = ((bf16[8,2,192,128]{3,2,1,0:T(8,128)(2,1)}), bf16[8,2,192,128]{3,2,1,0:T(8,128)(2,1)S(1)}, u32[]{:S(2)}, u32[]{:S(2)}) async-start(bf16[8,2,192,128]{3,2,1,0:T(8,128)(2,1)} %get-tuple-element.42), calls=%async_computation | async-start | bytes 1572864 | tf_op jit(solution)/shard_map/all_to_all | solution.py:518
  55.0 15.0 %copy-start = (bf16[8,48,1088]{2,1,0:T(8,128)(2,1)}, bf16[8,48,1088]{2,1,0:T(8,128)(2,1)S(1)}, u32[]{:S(2)}) copy-start(bf16[8,48,1088]{2,1,0:T(8,128)(2,1)S(1)} %pad_maximum_fusion.angles_ref) | copy-start | bytes 2506756
  65.7 15.2 %copy-start.3 = (bf16[8,2,192,128]{3,2,1,0:T(8,128)(2,1)}, bf16[8,2,192,128]{3,2,1,0:T(8,128)(2,1)S(1)}, u32[]{:S(2)}) copy-start(bf16[8,2,192,128]{3,2,1,0:T(8,128)(2,1)S(1)} %all-to-all-done.recv_ref) | copy-start | bytes 2359300
  65.7 24.5 %all-to-all-start.1 = ((bf16[8,2,192,128]{3,2,1,0:T(8,128)(2,1)}), bf16[8,2,192,128]{3,2,1,0:T(8,128)(2,1)S(1)}, u32[]{:S(2)}, u32[]{:S(2)}) async-start(bf16[8,2,192,128]{3,2,1,0:T(8,128)(2,1)} %get-tuple-element.43), calls=%async_computation.1 | async-start | bytes 1572864 | tf_op jit(solution)/shard_map/all_to_all | solution.py:518
  108.1 24.5 %all-to-all-start.2 = ((bf16[8,2,192,128]{3,2,1,0:T(8,128)(2,1)}), bf16[8,2,192,128]{3,2,1,0:T(8,128)(2,1)S(1)}, u32[]{:S(2)}, u32[]{:S(2)}) async-start(bf16[8,2,192,128]{3,2,1,0:T(8,128)(2,1)} %mix.4), calls=%async_computation.2 | async-start | bytes 1572864 | tf_op jit(solution)/shard_map/all_to_all | solution.py:518
  121.6 12.6 %collective-permute-start.9 = (bf16[8,1,192,128]{3,2,1,0:T(8,128)(2,1)}, bf16[8,1,192,128]{3,2,1,0:T(8,128)(2,1)S(1)}, u32[]{:S(2)}, u32[]{:S(2)}) collective-permute-start(bf16[8,1,192,128]{3,2,1,0:T(8,128)(2,1)} %get-tuple-element.48), channel_id=1, source_target_pairs={{0,24},{8,16},{16,8},{24,0},{1,25},{9,17},{17,9},{25,1},{2,26},{10... | collective-permute-start | bytes 1179656 | tf_op jit(solution)/shard_map/ppermute | solution.py:514
  136.1 50.0 %all-to-all-start.3 = ((bf16[8,2,192,128]{3,2,1,0:T(8,128)(2,1)}), bf16[8,2,192,128]{3,2,1,0:T(8,128)(2,1)S(1)}, u32[]{:S(2)}, u32[]{:S(2)}) async-start(bf16[8,2,192,128]{3,2,1,0:T(8,128)(2,1)} %pad_maximum_fusion.1), calls=%async_computation.3 | async-start | bytes 1572864 | tf_op jit(solution)/shard_map/all_to_all | solution.py:518
  140.9 14.0 %collective-permute-start.11 = (bf16[8,1,192,128]{3,2,1,0:T(8,128)(2,1)S(1)}, bf16[8,1,192,128]{3,2,1,0:T(8,128)(2,1)S(1)}, u32[]{:S(2)}, u32[]{:S(2)}) collective-permute-start(bf16[8,1,192,128]{3,2,1,0:T(8,128)(2,1)S(1)} %get-tuple-element.52), channel_id=1, source_target_pairs={{0,8},{8,0},{16,24},{24,16},{1,9},{9,1},{17,25},{25,17},{2,10},{10... | collective-permute-start | bytes 1179656 | tf_op jit(solution)/shard_map/ppermute | solution.py:514
  142.4 12.5 %collective-permute-start.12 = (bf16[8,1,192,128]{3,2,1,0:T(8,128)(2,1)S(1)}, bf16[8,1,192,128]{3,2,1,0:T(8,128)(2,1)S(1)}, u32[]{:S(2)}, u32[]{:S(2)}) collective-permute-start(bf16[8,1,192,128]{3,2,1,0:T(8,128)(2,1)S(1)} %get-tuple-element.53), channel_id=1, source_target_pairs={{0,16},{8,24},{16,0},{24,8},{1,17},{9,25},{17,1},{25,9},{2,18},{10... | collective-permute-start | bytes 1179656 | tf_op jit(solution)/shard_map/ppermute | solution.py:514
  143.9 9.8 %collective-permute-start.3 = (s32[384]{0:T(512)S(1)}, s32[384]{0:T(512)S(1)}, u32[]{:S(2)}, u32[]{:S(2)}) collective-permute-start(s32[384]{0:T(512)S(1)} %get-tuple-element.66), channel_id=1, source_target_pairs={{0,16},{8,24},{16,0},{24,8},{1,17},{9,25},{17,1},{25,9},{2,18},{10... | collective-permute-start | bytes 4616 | tf_op jit(solution)/shard_map/ppermute | solution.py:514
  144.5 9.2 %collective-permute-start.2 = (s32[384]{0:T(512)S(1)}, s32[384]{0:T(512)S(1)}, u32[]{:S(2)}, u32[]{:S(2)}) collective-permute-start(s32[384]{0:T(512)S(1)} %get-tuple-element.67), channel_id=1, source_target_pairs={{0,8},{8,0},{16,24},{24,16},{1,9},{9,1},{17,25},{25,17},{2,10},{10... | collective-permute-start | bytes 4616 | tf_op jit(solution)/shard_map/ppermute | solution.py:514
  145.0 8.7 %collective-permute-start.1 = (s32[384]{0:T(512)S(1)}, s32[384]{0:T(512)S(1)}, u32[]{:S(2)}, u32[]{:S(2)}) collective-permute-start(s32[384]{0:T(512)S(1)} %get-tuple-element.65), channel_id=1, source_target_pairs={{0,24},{8,16},{16,8},{24,0},{1,25},{9,17},{17,9},{25,1},{2,26},{10... | collective-permute-start | bytes 4616 | tf_op jit(solution)/shard_map/ppermute | solution.py:514
  164.2 10.5 %collective-permute-start.13 = (bf16[384,512]{1,0:T(8,128)(2,1)S(1)}, bf16[384,512]{1,0:T(8,128)(2,1)S(1)}, u32[]{:S(2)}, u32[]{:S(2)}) collective-permute-start(bf16[384,512]{1,0:T(8,128)(2,1)S(1)} %get-tuple-element.79), channel_id=1, source_target_pairs={{0,8},{8,0},{16,24},{24,16},{1,9},{9,1},{17,25},{25,17},{2,10},{10... | collective-permute-start | bytes 1179656 | tf_op jit(solution)/shard_map/ppermute | solution.py:514
  165.5 10.5 %collective-permute-start.14 = (bf16[384,512]{1,0:T(8,128)(2,1)S(1)}, bf16[384,512]{1,0:T(8,128)(2,1)S(1)}, u32[]{:S(2)}, u32[]{:S(2)}) collective-permute-start(bf16[384,512]{1,0:T(8,128)(2,1)S(1)} %get-tuple-element.78), channel_id=1, source_target_pairs={{0,16},{8,24},{16,0},{24,8},{1,17},{9,25},{17,1},{25,9},{2,18},{10... | collective-permute-start | bytes 1179656 | tf_op jit(solution)/shard_map/ppermute | solution.py:514
  186.1 35.3 %all-to-all-start.5 = ((bf16[8,2,192,128]{3,2,1,0:T(8,128)(2,1)}), bf16[8,2,192,128]{3,2,1,0:T(8,128)(2,1)S(1)}, u32[]{:S(2)}, u32[]{:S(2)}) async-start(bf16[8,2,192,128]{3,2,1,0:T(8,128)(2,1)} %get-tuple-element.54), calls=%async_computation.5 | async-start | bytes 1572864 | tf_op jit(solution)/shard_map/all_to_all | solution.py:518
  199.0 12.5 %collective-permute-start.10 = (bf16[384,512]{1,0:T(8,128)(2,1)S(1)}, bf16[384,512]{1,0:T(8,128)(2,1)S(1)}, u32[]{:S(2)}, u32[]{:S(2)}) collective-permute-start(bf16[384,512]{1,0:T(8,128)(2,1)S(1)} %slice_bitcast_fusion.2), channel_id=1, source_target_pairs={{0,24},{8,16},{16,8},{24,0},{1,25},{9,17},{17,9},{25,1},{2,26},{10... | collective-permute-start | bytes 1179656 | tf_op jit(solution)/shard_map/ppermute | solution.py:514
  221.4 25.7 %all-to-all-start.4 = ((bf16[8,2,192,128]{3,2,1,0:T(8,128)(2,1)}), bf16[8,2,192,128]{3,2,1,0:T(8,128)(2,1)S(1)}, u32[]{:S(2)}, u32[]{:S(2)}) async-start(bf16[8,2,192,128]{3,2,1,0:T(8,128)(2,1)} %get-tuple-element.50), calls=%async_computation.4 | async-start | bytes 1572864 | tf_op jit(solution)/shard_map/all_to_all | solution.py:518
  265.1 24.5 %all-to-all-start.6 = ((bf16[8,2,192,128]{3,2,1,0:T(8,128)(2,1)}), bf16[8,2,192,128]{3,2,1,0:T(8,128)(2,1)S(1)}, u32[]{:S(2)}, u32[]{:S(2)}) async-start(bf16[8,2,192,128]{3,2,1,0:T(8,128)(2,1)} %mix.6), calls=%async_computation.6 | async-start | bytes 1572864 | tf_op jit(solution)/shard_map/all_to_all | solution.py:518
  278.5 12.6 %collective-permute-start.15 = (bf16[8,1,192,128]{3,2,1,0:T(8,128)(2,1)}, bf16[8,1,192,128]{3,2,1,0:T(8,128)(2,1)S(1)}, u32[]{:S(2)}, u32[]{:S(2)}) collective-permute-start(bf16[8,1,192,128]{3,2,1,0:T(8,128)(2,1)} %get-tuple-element.59), channel_id=1, source_target_pairs={{0,24},{8,16},{16,8},{24,0},{1,25},{9,17},{17,9},{25,1},{2,26},{10... | collective-permute-start | bytes 1179656 | tf_op jit(solution)/shard_map/ppermute | solution.py:514
  293.1 25.8 %all-to-all-start.7 = ((bf16[8,2,192,128]{3,2,1,0:T(8,128)(2,1)}), bf16[8,2,192,128]{3,2,1,0:T(8,128)(2,1)S(1)}, u32[]{:S(2)}, u32[]{:S(2)}) async-start(bf16[8,2,192,128]{3,2,1,0:T(8,128)(2,1)} %pad_maximum_fusion.2), calls=%async_computation.7 | async-start | bytes 1572864 | tf_op jit(solution)/shard_map/all_to_all | solution.py:518
  297.9 11.5 %collective-permute-start.16 = (bf16[8,1,192,128]{3,2,1,0:T(8,128)(2,1)S(1)}, bf16[8,1,192,128]{3,2,1,0:T(8,128)(2,1)S(1)}, u32[]{:S(2)}, u32[]{:S(2)}) collective-permute-start(bf16[8,1,192,128]{3,2,1,0:T(8,128)(2,1)S(1)} %get-tuple-element.61), channel_id=1, source_target_pairs={{0,8},{8,0},{16,24},{24,16},{1,9},{9,1},{17,25},{25,17},{2,10},{10... | collective-permute-start | bytes 1179656 | tf_op jit(solution)/shard_map/ppermute | solution.py:514
  298.6 11.2 %collective-permute-start.17 = (bf16[8,1,192,128]{3,2,1,0:T(8,128)(2,1)S(1)}, bf16[8,1,192,128]{3,2,1,0:T(8,128)(2,1)S(1)}, u32[]{:S(2)}, u32[]{:S(2)}) collective-permute-start(bf16[8,1,192,128]{3,2,1,0:T(8,128)(2,1)S(1)} %get-tuple-element.62), channel_id=1, source_target_pairs={{0,16},{8,24},{16,0},{24,8},{1,17},{9,25},{17,1},{25,9},{2,18},{10... | collective-permute-start | bytes 1179656 | tf_op jit(solution)/shard_map/ppermute | solution.py:514
  (19 other events, 54.6 us)

commit v3 on v1

--- a/solution.py
+++ b/solution.py
@@ -107,7 +107,7 @@
 
 
 def front_kernel(own, count, where_ref, cur_ref, back_ref, rank_ref, wm, wr, wc, wi, wo, *refs):
-    recv_refs, (second_ref, packed_ref, reverse_ref) = refs[:-3], refs[-3:]
+    recv_refs, (second_ref, packed_ref, reverse_ref) = refs[: count - own], refs[-3:]
     rows_iota, lanes_iota = iotas(cur_ref.shape[1])
     partner = as_column(back_ref[0], rows_iota, lanes_iota)
     hot = one_hot(partner == lanes_iota)
@@ -134,26 +134,21 @@
         packed_ref[2 * tile + 1, 0] = jnp.where(low, pltpu.roll(top, HALF, 1), bottom).astype(jnp.bfloat16)
 
 
-def back_kernel(layout, where_ref, second_ref, rank_ref, wl, we, wd, *refs):
-    out_ref, ordered_ref = refs[-2:]
+def back_kernel(from_ref, to_ref, second_ref, packed_ref, rank_ref, wl, we, wd, out_ref):
     rows_iota, lanes_iota = iotas(second_ref.shape[1])
     half = rows_iota.shape[0] // 2
     low = lax.broadcasted_iota(jnp.int32, (half, LANES), 1) < HALF
-    for index, (array, side) in enumerate(layout):
-
-        @pl.when(pl.program_id(0) == index)
-        def _():
-            for tile in range(second_ref.shape[2] // LANES):
-                lanes = slice(tile * LANES, (tile + 1) * LANES)
-                even = refs[array][2 * tile, side].astype(jnp.float32)
-                odd = refs[array][2 * tile + 1, side].astype(jnp.float32)
-                top = jnp.where(low, even, pltpu.roll(odd, HALF, 1))
-                bottom = jnp.where(low, pltpu.roll(even, HALF, 1), odd)
-                ordered_ref[:half, lanes] = top.astype(jnp.bfloat16)
-                ordered_ref[half:, lanes] = bottom.astype(jnp.bfloat16)
-
+    tops, bottoms = [], []
+    for tile in range(second_ref.shape[2] // LANES):
+        even = packed_ref[0, 2 * tile].astype(jnp.float32)
+        odd = packed_ref[0, 2 * tile + 1].astype(jnp.float32)
+        tops.append(jnp.where(low, even, pltpu.roll(odd, HALF, 1)).astype(jnp.bfloat16))
+        bottoms.append(jnp.where(low, pltpu.roll(even, HALF, 1), odd).astype(jnp.bfloat16))
+    ordered = jnp.concatenate(
+        [jnp.concatenate(tops, axis=1), jnp.concatenate(bottoms, axis=1)], axis=0
+    )
     source = as_column(rank_ref[0], rows_iota, lanes_iota)
-    turned = dot(one_hot(source == lanes_iota), ordered_ref[...]).astype(jnp.bfloat16)
+    turned = dot(one_hot(source == lanes_iota), ordered).astype(jnp.bfloat16)
     third_res = halve(second_ref[0], silu(dot(turned, wl[0])))
     expand = silu(dot(third_res, we[0])).astype(jnp.bfloat16)
     out_ref[0] = halve(third_res, silu(dot(expand, wd[0])))
@@ -187,11 +182,13 @@
             blocks_ref[0, group, pl.ds(to, strip), :] = block[side * strip : (side + 1) * strip]
 
 
-def gather_kernel(chunk, owner_ref, place_ref, recv_ref, rank_ref, out_ref, ins):
+def mix_kernel(owner_ref, place_ref, order_ref, recv_ref, rank_ref, blocks_ref, out_ref, ins, outs):
     step = pl.program_id(0)
-    sides = recv_ref.shape[1]
-    devices = recv_ref.shape[0]
+    devices, sides = recv_ref.shape[:2]
     unit = ins.shape[3]
+    rows = devices * unit
+    groups = blocks_ref.shape[1]
+    strip = blocks_ref.shape[2] // sides
     pairs = devices // 2
 
     @pl.when(step == 0)
@@ -208,40 +205,24 @@
                         block = pltpu.roll(block.astype(jnp.float32), HALF, 1).astype(jnp.bfloat16)
                     ins[side, owner, place] = block
 
-    rows_iota, lanes_iota = iotas(devices * unit)
+    rows_iota, lanes_iota = iotas(rows)
+    gathered = []
     for side in range(sides):
-        operand = ins[side, step].reshape(devices * unit, LANES)
-        source = as_column(rank_ref[0, chunk * sides + side], rows_iota, lanes_iota)
-        out_ref[0, side] = dot(one_hot(source == lanes_iota), operand).astype(jnp.bfloat16)
-
-
-def mix_kernel(chunk, chunks, owner_ref, place_ref, rank_ref, blocks_ref, *refs):
-    gathered_refs, out_refs, outs = refs[:chunks], refs[chunks:-1], refs[-1]
-    step = pl.program_id(0)
-    count = outs.shape[0]
-    devices = outs.shape[1]
-    unit = outs.shape[3]
-    groups = blocks_ref.shape[1]
-    strip = blocks_ref.shape[2] // count
-    pairs = devices // 2
-    rows_iota = iotas(devices * unit)[0]
+        source = as_column(rank_ref[0, side], rows_iota, lanes_iota)
+        operand = ins[side, step].reshape(rows, LANES)
+        gathered.append(dot(one_hot(source == lanes_iota), operand).astype(jnp.bfloat16))
     mixed = []
     for group in range(groups):
         operand = jnp.concatenate(
-            [
-                ref[0, index, group * strip : (group + 1) * strip, :]
-                for ref in gathered_refs
-                for index in range(count)
-            ],
-            axis=0,
+            [part[group * strip : (group + 1) * strip] for part in gathered], axis=0
         )
         mixed.append(dot(blocks_ref[0, group], operand).astype(jnp.bfloat16))
-    for side in range(count):
+    for side in range(sides):
         operand = jnp.concatenate(
             [part[side * strip : (side + 1) * strip] for part in mixed], axis=0
         )
         outs[side, step] = (
-            dot(one_hot(rows_iota == rank_ref[0, chunk * count + side]), operand)
+            dot(one_hot(rows_iota == rank_ref[0, side]), operand)
             .astype(jnp.bfloat16)
             .reshape(devices, unit, LANES)
         )
@@ -257,15 +238,11 @@
                 place = place_ref[source, index]
                 owner_far = owner_ref[source, index + pairs]
                 place_far = place_ref[source, index + pairs]
-                rows = slice(index * unit, (index + 1) * unit)
-                for side in range(count):
+                for side in range(sides):
                     near = outs[side, owner, place].astype(jnp.float32)
                     far = outs[side, owner_far, place_far].astype(jnp.float32)
                     joined = jnp.where(low, near, pltpu.roll(far, HALF, 1)).astype(jnp.bfloat16)
-                    if len(out_refs) == 1:
-                        out_refs[0][source, side, rows, :] = joined
-                    else:
-                        out_refs[side][source, 0, rows, :] = joined
+                    out_ref[order_ref[side], source, index * unit : (index + 1) * unit, :] = joined
 
 
 VMEM_BYTES = 24 * 1024 * 1024
@@ -288,11 +265,12 @@
     return pl.BlockSpec((1, features, features), lambda i, *_: (section, 0, 0))
 
 
-def run_front(current, where, received, own, chunk, back_rows, rank_rows, weights, section, narrow):
+def run_front(current, where, received, own, start, sides, back_rows, rank_rows, weights, section, targets):
     _, rows, features = current.shape
     count = where.shape[0]
-    edge_spec = pl.BlockSpec((1, rows, features), lambda i, where: (i, 0, 0))
-    row_spec = pl.BlockSpec((1, 1, rows), lambda i, where: (chunk * count + i, 0, 0))
+    narrow = features // HALF
+    row_spec = pl.BlockSpec((1, 1, rows), lambda i, where: (start + i, 0, 0))
+    first_target = 9 + len(received)
     return pl.pallas_call(
         functools.partial(front_kernel, own, count),
         grid_spec=pltpu.PrefetchScalarGridSpec(
@@ -304,48 +282,47 @@
                 row_spec,
             ]
             + [weight_spec(section, features)] * 5
-            + [whole_spec(array) for array in received],
+            + [whole_spec(array) for array in received]
+            + [pl.BlockSpec(memory_space=pl.ANY)] * len(targets),
             out_specs=[
-                edge_spec,
-                pl.BlockSpec((narrow, 1, rows // 2, LANES), lambda i, where: (0, i, 0, 0)),
+                pl.BlockSpec((1, rows, features), lambda i, where: (start + i, 0, 0)),
+                pl.BlockSpec((narrow, 1, rows // 2, LANES), lambda i, where: (0, start + i, 0, 0)),
             ],
             scratch_shapes=[pltpu.VMEM((rows, features), jnp.bfloat16)],
         ),
         out_shape=[
-            jax.ShapeDtypeStruct((count, rows, features), jnp.bfloat16),
-            jax.ShapeDtypeStruct((narrow, count, rows // 2, LANES), jnp.bfloat16),
+            jax.ShapeDtypeStruct((sides, rows, features), jnp.bfloat16),
+            jax.ShapeDtypeStruct((narrow, sides, rows // 2, LANES), jnp.bfloat16),
         ],
+        input_output_aliases={first_target + index: index for index in range(len(targets))},
         compiler_params=params(),
         cost_estimate=cost(12 * count * rows * features**2, 8 * count * rows * features),
         name="front",
-    )(where, current, back_rows, rank_rows, *weights[:5], *received)
-
-
-def run_back(second, packed, layout, chunk, rank_rows, weights, section, where, total, target):
-    count, rows, features = second.shape
-    edge_spec = pl.BlockSpec((1, rows, features), lambda i, where: (i, 0, 0))
-    extra = [] if target is None else [target]
+    )(where, current, back_rows, rank_rows, *weights[:5], *received, *targets)
+
+
+def run_back(second, packed, where, to, start, rank_rows, weights, section, total):
+    _, rows, features = second.shape
+    count = where.shape[0]
+    narrow = packed.shape[1]
     return pl.pallas_call(
-        functools.partial(back_kernel, layout),
+        back_kernel,
         grid_spec=pltpu.PrefetchScalarGridSpec(
-            num_scalar_prefetch=1,
+            num_scalar_prefetch=2,
             grid=(count,),
             in_specs=[
-                edge_spec,
-                pl.BlockSpec((1, 1, rows), lambda i, where: (chunk * count + i, 0, 0)),
+                pl.BlockSpec((1, rows, features), lambda i, *_: (start + i, 0, 0)),
+                pl.BlockSpec((1, narrow, rows // 2, LANES), lambda i, where, to: (where[i], 0, 0, 0)),
+                pl.BlockSpec((1, 1, rows), lambda i, *_: (start + i, 0, 0)),
             ]
-            + [weight_spec(section, features)] * 3
-            + [whole_spec(array) for array in packed]
-            + [pl.BlockSpec(memory_space=pl.ANY)] * len(extra),
-            out_specs=pl.BlockSpec((1, rows, features), lambda i, where: (where[i], 0, 0)),
-            scratch_shapes=[pltpu.VMEM((rows, features), jnp.bfloat16)],
+            + [weight_spec(section, features)] * 3,
+            out_specs=pl.BlockSpec((1, rows, features), lambda i, where, to: (to[i], 0, 0)),
         ),
         out_shape=jax.ShapeDtypeStruct((total, rows, features), jnp.bfloat16),
-        input_output_aliases={6 + len(packed): 0} if extra else {},
         compiler_params=params(),
         cost_estimate=cost(8 * count * rows * features**2, 6 * count * rows * features),
         name="back",
-    )(where, second, rank_rows, *weights[5:], *packed, *extra)
+    )(where, to, second, packed, rank_rows, *weights[5:])
 
 
 def rank_spec(entries):
@@ -381,58 +358,30 @@
     )(places, order, position, entries, angles)
 
 
-def run_gather(owner_of, place_of, received, rank, chunk):
-    devices, count, half, _ = received.shape
-    rows = 2 * half
+def run_mix(owner_of, place_of, order, received, rank, blocks):
+    devices, sides, half, _ = received.shape
+    unit = 2 * half // devices
     smem = pl.BlockSpec(memory_space=pltpu.SMEM)
+    shape = (sides, devices, half, LANES)
+    scratch = pltpu.VMEM((sides, devices, devices, unit, LANES), jnp.bfloat16)
     return pl.pallas_call(
-        functools.partial(gather_kernel, chunk),
+        mix_kernel,
         grid=(devices,),
         in_specs=[
             smem,
             smem,
+            smem,
             whole_spec(received),
             rank_spec(rank),
+            pl.BlockSpec((1,) + blocks.shape[1:], lambda i: (i, 0, 0, 0)),
         ],
-        out_specs=pl.BlockSpec((1, count, rows, LANES), lambda i: (i, 0, 0, 0)),
-        out_shape=jax.ShapeDtypeStruct((devices, count, rows, LANES), jnp.bfloat16),
-        scratch_shapes=[
-            pltpu.VMEM((count, devices, devices, rows // devices, LANES), jnp.bfloat16)
-        ],
+        out_specs=pl.BlockSpec(shape, lambda i: (0, 0, 0, 0)),
+        out_shape=jax.ShapeDtypeStruct(shape, jnp.bfloat16),
+        scratch_shapes=[scratch, scratch],
         compiler_params=params(),
-        cost_estimate=cost(4 * devices * count * rows**2 * LANES, 4 * devices * count * rows**2),
-        name="gather",
-    )(owner_of, place_of, received, rank)
-
-
-def run_mix(owner_of, place_of, gathered, rank, blocks, chunk, apart):
-    chunks = len(gathered)
-    devices, count, rows, _ = gathered[0].shape
-    half = rows // 2
-    groups, span = blocks.shape[1:3]
-    smem = pl.BlockSpec(memory_space=pltpu.SMEM)
-    shapes = [(devices, 1, half, LANES)] * count if apart else [(devices, count, half, LANES)]
-    shapes = [jax.ShapeDtypeStruct(shape, jnp.bfloat16) for shape in shapes]
-    part_spec = pl.BlockSpec((1, count, rows, LANES), lambda i: (i, 0, 0, 0))
-    return pl.pallas_call(
-        functools.partial(mix_kernel, chunk, chunks),
-        grid=(devices,),
-        in_specs=[
-            smem,
-            smem,
-            rank_spec(rank),
-            pl.BlockSpec((1, groups, span // chunks, span), lambda i: (i, 0, chunk, 0)),
-        ]
-        + [part_spec] * chunks,
-        out_specs=[whole_spec(shape) for shape in shapes],
-        out_shape=shapes,
-        scratch_shapes=[
-            pltpu.VMEM((count, devices, devices, rows // devices, LANES), jnp.bfloat16)
-        ],
-        compiler_params=params(),
-        cost_estimate=cost(6 * devices * count * rows**2 * LANES, 6 * devices * count * rows**2),
+        cost_estimate=cost(10 * devices * sides * half**2 * LANES, 16 * devices * sides * half**2),
         name="mix",
-    )(owner_of, place_of, rank, blocks, *gathered)
+    )(owner_of, place_of, order, received, rank, blocks)
 
 
 def unit_tables(entries, capacity, unit):
@@ -504,109 +453,64 @@
     unit = rows // narrow
     capacity = 2 * edge_rows // narrow
     atoms = angles.shape[0]
-    count = wide // CHUNKS
-    spread_out = [offset for index in range(wide // 2) for offset in (index, wide - 1 - index)]
-    offsets = [spread_out[chunk * count : (chunk + 1) * count] for chunk in range(CHUNKS)]
     group_id = lax.axis_index("wide").astype(jnp.int32)
-    order = group_id ^ jnp.array(sum(offsets, []), jnp.int32)
-    inverse = jnp.array([spread_out.index(offset) for offset in range(wide)], jnp.int32)
+    offsets = [offset for index in range(wide // 2) for offset in (index, wide - 1 - index)]
+    order = group_id ^ jnp.array(offsets, jnp.int32)
+    inverse = jnp.array([offsets.index(offset) for offset in range(wide)], jnp.int32)
     owners_wide = (jnp.arange(wide, dtype=jnp.int32) ^ group_id)[:, None]
     position = jnp.sum(jnp.where(owners_wide == jnp.arange(wide), inverse, 0), axis=1)
-    places = [order[chunk * count : (chunk + 1) * count] for chunk in range(CHUNKS)]
-    plain = jnp.arange(count, dtype=jnp.int32)
+    half = wide // 2
+    pieces = [(0, 1), (1, half - 1), (half, wide - half)]
+    halves = [(0, half), (half, wide - half)]
 
     blocks_of = messages.reshape(wide, rows, features)
-    received = [
-        [
-            shift(lax.dynamic_index_in_dim(blocks_of, group_id ^ offset, 0, False), offset, wide)
-            for offset in offsets[chunk]
-            if offset
-        ]
-        for chunk in range(CHUNKS)
-    ]
+    received = {
+        offset: shift(lax.dynamic_index_in_dim(blocks_of, group_id ^ offset, 0, False), offset, wide)
+        for offset in offsets[1:]
+    }
     listed = atom_slots.reshape(atoms // GROUP, GROUP, wide, SLOTS // wide)
     listed = reorder(jnp.transpose(listed, (2, 0, 3, 1)).reshape(wide, rows), order)
-    entries, all_angles, owner_places = share_lists(listed, angles)
-    rank = ranks(route_slot.reshape(wide, rows))
-    back_rows = reverse_position.reshape(wide, rows)
-    back_rows = reorder(back_rows, order)
-    rank = reorder(rank, order)
-    partner_rank = jnp.stack(
-        [shift(rank[place], offset, wide) for place, offset in enumerate(sum(offsets, []))]
-    )
-    hits = back_rows[:, :, None] == jnp.arange(rows, dtype=jnp.int32)
-    turned_rank = jnp.sum(jnp.where(hits, partner_rank[:, None, :], 0), axis=2)[:, None, :]
-    back_rows = back_rows[:, None, :]
-    rank = rank[:, None, :]
-
-    current = [blocks_of] * CHUNKS
-    where = places
-    chunk_order = list(range(CHUNKS))
-    target = None
+    rank = reorder(ranks(route_slot.reshape(wide, rows)), order)
+    back_rows = reorder(reverse_position.reshape(wide, rows), order)
+
+    current = {start: (blocks_of, order[start : start + count]) for start, count in pieces}
     tables = None
     for section in range(BLOCKS):
         last = section == BLOCKS - 1
-        seconds, spreads = {}, {}
-        for chunk in chunk_order:
-            seconds[chunk], packed = run_front(
-                current[chunk], where[chunk], received[chunk], offsets[chunk][0] == 0, chunk,
-                back_rows, rank, weights, section, narrow,
+        targets = []
+        for start, count in halves if section else pieces:
+            array, where = current[start]
+            needed = [received[offset] for offset in offsets[start : start + count] if offset]
+            targets = run_front(
+                array, where, needed, start == 0, start, wide,
+                back_rows[:, None, :], rank[:, None, :], weights, section, targets,
             )
-            spreads[chunk] = packed
+        second, packed = targets
         if tables is None:
-            held = [spreads[chunk] for chunk in chunk_order]
-            entries, all_angles, held[-1] = lax.optimization_barrier((entries, all_angles, held[-1]))
-            spreads = dict(zip(chunk_order, held))
+            packed, listed, late_rank = lax.optimization_barrier((packed, listed, rank))
+            entries, all_angles, owner_places = share_lists(listed, angles)
             owner_of, place_of = unit_tables(entries, capacity, unit)
             tables = run_tables(owner_places, order, position, entries[:, :, None, :], all_angles)
-        listed_rank, blocks = tables
-        gathered = [None] * CHUNKS
-        for chunk in chunk_order:
-            gathered[chunk] = run_gather(owner_of, place_of, swap(spreads[chunk]), listed_rank, chunk)
-        chunk_order = list(range(CHUNKS))[::-1]
-        returned = {}
-        sent = None
-        for chunk in chunk_order:
-            early = chunk == 0
-            mixed = list(run_mix(owner_of, place_of, gathered, listed_rank, blocks, chunk, early))
-            if chunk != chunk_order[-1]:
-                mixed[0], gathered[0] = lax.optimization_barrier((mixed[0], gathered[0]))
-            if early:
-                mixed = [shift(part, offset, wide) for part, offset in zip(mixed, offsets[chunk])]
-                if sent is not None:
-                    sent, mixed[0] = lax.optimization_barrier((sent, mixed[0]))
-                    returned[chunk_order[0]] = (sent, returned[chunk_order[0]][1])
-                parts = [swap(jnp.concatenate(mixed, axis=1))]
-                layout = [(0, index) for index in range(count)]
-            else:
-                sent = swap(mixed[0])
-                parts = sent
-                layout = [(index, 0) for index in range(count)]
-            returned[chunk] = (parts, layout)
-        current = [None] * CHUNKS
-        received = [None] * CHUNKS
-        for chunk in chunk_order:
-            parts, layout = returned[chunk]
-            if chunk:
-                parts = [
-                    shift(parts[:, index : index + 1], offset, wide)
-                    for index, offset in enumerate(offsets[chunk])
-                ]
-            result = run_back(
-                seconds[chunk], parts, layout, chunk, turned_rank, weights, section,
-                places[chunk] if last else plain, wide if last else count, target,
+            partner_rank = jnp.stack(
+                [shift(late_rank[place], offset, wide) for place, offset in enumerate(offsets)]
             )
-            if last:
-                target = result
-            else:
-                current[chunk] = result
-                received[chunk] = [
-                    shift(result[index], offset, wide)
-                    for index, offset in enumerate(offsets[chunk])
-                    if offset
-                ]
-        where = [plain] * CHUNKS
-    return target.reshape(edge_rows, features)
+            hits = back_rows[:, :, None] == jnp.arange(rows, dtype=jnp.int32)
+            turned_rank = jnp.sum(jnp.where(hits, partner_rank[:, None, :], 0), axis=2)[:, None, :]
+        mixed = run_mix(owner_of, place_of, order, swap(packed), *tables)
+        mixed = mixed.reshape(wide * narrow, rows // 2, LANES)
+        returned = lax.all_to_all(mixed, ("wide", "narrow"), 0, 0, tiled=True)
+        returned = returned.reshape(wide, narrow, rows // 2, LANES)
+        if last:
+            current = run_back(second, returned, order, order, 0, turned_rank, weights, section, wide)
+            return current.reshape(edge_rows, features)
+        for start, count in halves:
+            plain = jnp.arange(count, dtype=jnp.int32)
+            where = order[start : start + count]
+            result = run_back(second, returned, where, plain, start, turned_rank, weights, section, count)
+            current[start] = (result, plain)
+            for index, offset in enumerate(offsets[start : start + count]):
+                if offset:
+                    received[offset] = shift(result[index], offset, wide)
 
 
 def local(
@@ -642,7 +546,7 @@
         features == narrow * HALF
         and unit % 16 == 0
         and narrow % 2 == 0
-        and wide % CHUNKS == 0
+        and wide >= 4
         and wide & (wide - 1) == 0
         and narrow & (narrow - 1) == 0
         and angles.shape[0] % GROUP == 0

time: 311 us -> 297 us (0.955)
  blocking collectives: 0 us -> 81.1 us
  starting transfers between devices: 56.9 us -> 24.5 us
  waiting for transfers between devices: 99.2 us -> 72.1 us
  Pallas kernels: 97.8 us -> 76.6 us
  local copies, waits for them, and re-layouts: 46 us -> 33.3 us
    all_to_all x0 -> x2, blocking collectives: none -> 81.1 us  [the longest x1 40.9 us: tiled_local(): returned = lax.all_to_all(mixed, ('wide', 'narrow'), 0, 0, tiled=True)]
    all_to_all x8 -> x1, starting transfers between devices: 36.4 us -> 4.8 us  [swap(): return lax.all_to_all(values, 'narrow', 0, 0, tiled=True)]
    all_to_all x0 -> x1, waiting for transfers between devices: none -> 27.7 us  [tiled_local(): returned = lax.all_to_all(mixed, ('wide', 'narrow'), 0, 0, tiled=True)]
    all_to_all x8 -> x1, waiting for transfers between devices: 48.4 us -> 21.1 us  [swap(): return lax.all_to_all(values, 'narrow', 0, 0, tiled=True)]
    ppermute x15 -> x9, waiting for transfers between devices: 41.7 us -> 17.6 us  [shift(): return lax.ppermute(values, 'wide', [(i, i ^ offset) for i in range(wide)])]
    pallas_call x12 -> x5, Pallas kernels: 65.3 us -> 45.1 us  [the longest x2 26 us: run_mix(): pl.pallas_call(mix_kernel, grid=(devices,), in_specs=[smem, smem, smem, w...]
    unnamed x119 -> x95, local copies, waits for them, and re-layouts: 40.4 us -> 28.3 us
    ppermute x15 -> x9, starting transfers between devices: 17.1 us -> 11.6 us  [shift(): return lax.ppermute(values, 'wide', [(i, i ^ offset) for i in range(wide)])]
  transfers between devices with their start and end apart: 26 -> 14, of which waited for: 16 -> 8; matrix products, arithmetic and copies ran while one was open for 3% -> 3% of each run, Pallas kernels for 23% -> 7%
where the time goes in v3:
time: 297 us; the launch traced here: 295 us
  blocking collectives  81.1 us (27%)
  Pallas kernels  76.6 us (26%)
  waiting for transfers between devices  72.1 us (24%)
  local copies, waits for them, and re-layouts  33.3 us (11%)
  starting transfers between devices  24.5 us (8%)
  other arithmetic  7.18 us (2%)
    all_to_all x1, blocking collectives, tiled_local(): returned = lax.all_to_all(mixed, ('wide', 'narrow'), 0, 0, tiled=True)  40.9 us
    all_to_all x1, blocking collectives, swap(): return lax.all_to_all(values, 'narrow', 0, 0, tiled=True)  40.3 us
    unnamed x95, local copies, waits for them, and re-layouts  28.3 us
    all_to_all x1, waiting for transfers between devices, tiled_local(): returned = lax.all_to_all(mixed, ('wide', 'narrow'), 0, 0, tiled=True)  27.7 us
    pallas_call x2, Pallas kernels, run_mix(): pl.pallas_call(mix_kernel, grid=(devices,), in_specs=[smem, smem, smem, w...  26 us
    pallas_call x5, Pallas kernels, run_front(): pl.pallas_call(functools.partial(front_kernel, own, count), grid_spec=plt...  24.5 us
    all_to_all x1, waiting for transfers between devices, swap(): return lax.all_to_all(values, 'narrow', 0, 0, tiled=True)  21.1 us
    pallas_call x3, Pallas kernels, run_back(): pl.pallas_call(back_kernel, grid_spec=pltpu.PrefetchScalarGridSpec(num_sc...  19.1 us
  transfers between devices with their start and end apart: 14, of which 8 were waited for; matrix products, arithmetic and copies ran while one was open for 3% of the time, Pallas kernels for 7%

profile of v3, /device:TPU:0, one launch (start us, length us, event | category | flops | bytes accessed | tf_op | source)
XLA Modules:
  0.0 295.4 jit_solution(13737931851188482400)
XLA Ops:
  0.0 2.4 dynamic-slice_bitcast_fusion
  2.4 3.9 %collective-permute-start.2 = (bf16[384,512]{1,0:T(8,128)(2,1)}, bf16[384,512]{1,0:T(8,128)(2,1)}, u32[]{:S(2)}, u32[]{:S(2)}) collective-permute-start(bf16[384,512]{1,0:T(8,128)(2,1)} %get-tuple-element.45), channel_id=1, source_target_pairs={{0,24},{8,16},{16,8},{24,0},{1,25},{9,17},{17,9},{25,1},{2,26},{10... | collective-permute-start | bytes 1179656 | tf_op jit(solution)/shard_map/ppermute | solution.py:416
  10.3 1.2 copy-done.6
  11.5 1.2 copy-done.9
  15.2 2.9 front.5
  26.6 1.4 copy-done.19
  28.0 3.9 %front.6 = (bf16[4,384,512]{2,1,0:T(8,128)(2,1)S(1)}, bf16[8,4,192,128]{3,2,1,0:T(8,128)(2,1)S(1)}) custom-call(s32[1]{0:T(128)} %get-tuple-element.58.where_ref, bf16[4,384,512]{2,1,0:T(8,128)(2,1)S(1)} %bitcast.35, s32[4,1,384]{2,1,0:T(1,128)S(1)} %broadcast_in_dim.199.back_ref, ...), custom_call_target="tpu_custom_call", output_to_operand_aliasing={{0}: (10, {}), {1}: (11, {})} | custom-call | flops 1207959552 | bytes 1572864 | tf_op jit(solution)/shard_map/front/pallas_call | solution.py:274
  31.9 6.6 %front.7 = (bf16[4,384,512]{2,1,0:T(8,128)(2,1)S(1)}, bf16[8,4,192,128]{3,2,1,0:T(8,128)(2,1)S(1)}) custom-call(s32[2]{0:T(128)S(1)} %get-tuple-element.56.where_ref.from_ref, bf16[4,384,512]{2,1,0:T(8,128)(2,1)S(1)} %bitcast.36, s32[4,1,384]{2,1,0:T(1,128)S(1)} %broadcast_in_dim.199.back_ref, ...), custom_call_target="tpu_custom_call", output_to_operand_aliasing={{0}: (11, {}), {1}: (12, {})} | custom-call | flops 2415919104 | bytes 3145728 | tf_op jit(solution)/shard_map/front/pallas_call | solution.py:274
  40.7 3.1 %collective-permute-start.3 = (bf16[1,48,1088]{2,1,0:T(8,128)(2,1)S(1)}, bf16[1,48,1088]{2,1,0:T(8,128)(2,1)S(1)}, u32[]{:S(2)}, u32[]{:S(2)}) collective-permute-start(bf16[1,48,1088]{2,1,0:T(8,128)(2,1)S(1)} %maximum_bitcast_fusion), channel_id=1, source_target_pairs={{0,4},{1,5},{2,6},{3,7},{4,0},{5,1},{6,2},{7,3},{8,12},{9,13},{10,... | collective-permute-start | bytes 313352 | tf_op jit(solution)/shard_map/ppermute | solution.py:434
  43.8 4.6 %collective-permute-done.3 = bf16[1,48,1088]{2,1,0:T(8,128)(2,1)S(1)} collective-permute-done((bf16[1,48,1088]{2,1,0:T(8,128)(2,1)S(1)}, bf16[1,48,1088]{2,1,0:T(8,128)(2,1)S(1)}, u32[]{:S(2)}, u32[]{:S(2)}) %collective-permute-start.3) | collective-permute-done | bytes 104480 | tf_op jit(solution)/shard_map/ppermute | solution.py:434
  50.7 4.8 %all-to-all-start = ((bf16[8,4,192,128]{3,2,1,0:T(8,128)(2,1)}), bf16[8,4,192,128]{3,2,1,0:T(8,128)(2,1)S(1)}, u32[]{:S(2)}, u32[]{:S(2)}) async-start(bf16[8,4,192,128]{3,2,1,0:T(8,128)(2,1)} %copy-done.20), calls=%async_computation | async-start | bytes 3145728 | tf_op jit(solution)/shard_map/all_to_all | solution.py:420
  62.1 7.0 %tables.1 = (s32[8,4,1,384]{3,2,1,0:T(1,128)S(1)}, bf16[8,6,256,256]{3,2,1,0:T(8,128)(2,1)S(1)}) custom-call(s32[8]{0:T(128)S(1)} %select_reduce_fusion.9.places_ref, s32[4]{0:T(128)S(1)} %copy-done.31, s32[4]{0:T(128)S(1)} %select_reduce_fusion.10.position_ref, s32[8,4,1,384]{3,2,1,0:T(1,128)S(1)} %broadcast_in_dim_reshape.2.entry_ref, ...), custom_call_target="tpu_custom_call" | custom-call | bytes 25165824 | tf_op jit(solution)/shard_map/tables/pallas_call | solution.py:337
  69.1 2.6 copy-done
  72.3 21.1 %all-to-all-done.recv_ref = bf16[8,4,192,128]{3,2,1,0:T(8,128)(2,1)S(1)} async-done(((bf16[8,4,192,128]{3,2,1,0:T(8,128)(2,1)}), bf16[8,4,192,128]{3,2,1,0:T(8,128)(2,1)S(1)}, u32[]{:S(2)}, u32[]{:S(2)}) %all-to-all-start) | async-done | bytes 1572896 | tf_op jit(solution)/shard_map/all_to_all | solution.py:420
  93.3 2.8 copy-done.1
  96.1 13.0 %mix.2 = bf16[4,8,192,128]{3,2,1,0:T(8,128)(2,1)S(1)} custom-call(s32[8,8]{1,0:T(8,128)S(1)} %get-tuple-element.36.owner_ref, s32[8,8]{1,0:T(8,128)S(1)} %get-tuple-element.35.place_ref, s32[4]{0:T(128)S(1)} %copy-done.31, bf16[8,4,192,128]{3,2,1,0:T(8,128)(2,1)S(1)} %all-to-all-done.recv_ref, s32[8,4,1,384]{3,2,1,0:T(1,128)S(1)} %get-tuple-element.28.rank_ref, ...), custom_call_target="tpu_custom_call" | custom-call | flops 1509949440 | bytes 18874368 | tf_op jit(solution)/shard_map/mix/pallas_call | solution.py:367
  110.3 3.7 %all-to-all-start.1 = ((bf16[32,192,128]{2,1,0:T(8,128)(2,1)}), bf16[32,192,128]{2,1,0:T(8,128)(2,1)S(1)}, u32[]{:S(2)}, u32[]{:S(2)}) async-start(bf16[32,192,128]{2,1,0:T(8,128)(2,1)} %bitcast.39), calls=%async_computation.1 | async-start | bytes 3145728 | tf_op jit(solution)/shard_map/all_to_all | solution.py:501
  114.0 2.6 collective-permute-start.6
  117.6 6.6 %collective-permute-done.6 = s32[384]{0:T(512)S(1)} collective-permute-done((s32[384]{0:T(512)S(1)}, s32[384]{0:T(512)S(1)}, u32[]{:S(2)}, u32[]{:S(2)}) %collective-permute-start.6) | collective-permute-done | bytes 1568 | tf_op jit(solution)/shard_map/ppermute | solution.py:416
  125.0 27.7 %all-to-all-done.1 = bf16[32,192,128]{2,1,0:T(8,128)(2,1)S(1)} async-done(((bf16[32,192,128]{2,1,0:T(8,128)(2,1)}), bf16[32,192,128]{2,1,0:T(8,128)(2,1)S(1)}, u32[]{:S(2)}, u32[]{:S(2)}) %all-to-all-start.1) | async-done | bytes 1572896 | tf_op jit(solution)/shard_map/all_to_all | solution.py:501
  152.7 1.2 copy-done.22
  156.3 4.7 %back.3.cur_ref = bf16[2,384,512]{2,1,0:T(8,128)(2,1)S(1)} custom-call(s32[2]{0:T(128)S(1)} %copy-done.33, s32[2]{0:T(128)S(1)} %iota.75.to_ref, bf16[4,384,512]{2,1,0:T(8,128)(2,1)S(1)} %get-tuple-element.24.second_ref, bf16[4,8,192,128]{3,2,1,0:T(8,128)(2,1)S(1)} %bitcast.37, s32[4,1,384]{2,1,0:T(1,128)S(1)} %broadcast_in_dim.220.rank_ref, ...), custom_call_target="tpu_custom_call" | custom-call | flops 1610612736 | bytes 2359296 | tf_op jit(solution)/shard_map/back/pallas_call | solution.py:308
  161.2 4.7 %back.4.cur_ref = bf16[2,384,512]{2,1,0:T(8,128)(2,1)S(1)} custom-call(s32[2]{0:T(128)S(1)} %copy-done.34, s32[2]{0:T(128)S(1)} %iota.79.to_ref, bf16[4,384,512]{2,1,0:T(8,128)(2,1)S(1)} %get-tuple-element.24.second_ref, bf16[4,8,192,128]{3,2,1,0:T(8,128)(2,1)S(1)} %bitcast.38, s32[4,1,384]{2,1,0:T(1,128)S(1)} %broadcast_in_dim.220.rank_ref, ...), custom_call_target="tpu_custom_call" | custom-call | flops 1610612736 | bytes 2359296 | tf_op jit(solution)/shard_map/back/pallas_call | solution.py:308
  167.2 2.4 collective-permute-start.9
  169.6 9.4 %collective-permute-done.11.refs_0_ = bf16[384,512]{1,0:T(8,128)(2,1)S(1)} collective-permute-done((bf16[384,512]{1,0:T(8,128)(2,1)S(1)}, bf16[384,512]{1,0:T(8,128)(2,1)S(1)}, u32[]{:S(2)}, u32[]{:S(2)}) %collective-permute-start.11) | collective-permute-done | bytes 393248 | tf_op jit(solution)/shard_map/ppermute | solution.py:416
  179.0 5.6 %front.8 = (bf16[4,384,512]{2,1,0:T(8,128)(2,1)S(1)}, bf16[8,4,192,128]{3,2,1,0:T(8,128)(2,1)S(1)}) custom-call(s32[2]{0:T(128)S(1)} %iota.78.where_ref, bf16[2,384,512]{2,1,0:T(8,128)(2,1)S(1)} %back.4.cur_ref, s32[4,1,384]{2,1,0:T(1,128)S(1)} %broadcast_in_dim.199.back_ref, s32[4,1,384]{2,1,0:T(1,128)S(1)} %broadcast_in_dim.201.rank_ref, ...), custom_call_target="tpu_custom_call" | custom-call | flops 2415919104 | bytes 3145728 | tf_op jit(solution)/shard_map/front/pallas_call | solution.py:274
  184.6 1.4 collective-permute-done.10.refs_1_
  186.0 5.6 %front.9 = (bf16[4,384,512]{2,1,0:T(8,128)(2,1)S(1)}, bf16[8,4,192,128]{3,2,1,0:T(8,128)(2,1)S(1)}) custom-call(s32[2]{0:T(128)S(1)} %iota.74.where_ref, bf16[2,384,512]{2,1,0:T(8,128)(2,1)S(1)} %back.3.cur_ref, s32[4,1,384]{2,1,0:T(1,128)S(1)} %broadcast_in_dim.199.back_ref, ...), custom_call_target="tpu_custom_call", output_to_operand_aliasing={{0}: (11, {}), {1}: (12, {})} | custom-call | flops 2415919104 | bytes 3145728 | tf_op jit(solution)/shard_map/front/pallas_call | solution.py:274
  191.6 40.3 %all_to_all.20.recv_ref = bf16[8,4,192,128]{3,2,1,0:T(8,128)(2,1)S(1)} all-to-all(bf16[8,4,192,128]{3,2,1,0:T(8,128)(2,1)S(1)} %get-tuple-element.34), channel_id=1, replica_groups=mesh['wide'=4,'narrow'=8] {'narrow'}, dimensions={0} | all-to-all | bytes 3145728 | tf_op jit(solution)/shard_map/all_to_all | solution.py:420
  231.9 13.0 %mix.3 = bf16[4,8,192,128]{3,2,1,0:T(8,128)(2,1)S(1)} custom-call(s32[8,8]{1,0:T(8,128)S(1)} %get-tuple-element.36.owner_ref, s32[8,8]{1,0:T(8,128)S(1)} %get-tuple-element.35.place_ref, s32[4]{0:T(128)S(1)} %copy-done.31, bf16[8,4,192,128]{3,2,1,0:T(8,128)(2,1)S(1)} %all_to_all.20.recv_ref, s32[8,4,1,384]{3,2,1,0:T(1,128)S(1)} %get-tuple-element.28.rank_ref, ...), custom_call_target="tpu_custom_call" | custom-call | flops 1509949440 | bytes 18874368 | tf_op jit(solution)/shard_map/mix/pallas_call | solution.py:367
  244.9 40.9 %all_to_all.21 = bf16[32,192,128]{2,1,0:T(8,128)(2,1)S(1)} all-to-all(bf16[32,192,128]{2,1,0:T(8,128)(2,1)S(1)} %bitcast.40), channel_id=1, replica_groups=mesh['wide'=4,'narrow'=8] {'wide','narrow'}, dimensions={0} | all-to-all | bytes 3145728 | tf_op jit(solution)/shard_map/all_to_all | solution.py:501
  285.8 9.6 %back.5 = bf16[4,384,512]{2,1,0:T(8,128)(2,1)} custom-call(s32[4]{0:T(128)S(1)} %copy-done.31, s32[4]{0:T(128)S(1)} %copy-done.31, bf16[4,384,512]{2,1,0:T(8,128)(2,1)S(1)} %get-tuple-element.33.second_ref, bf16[4,8,192,128]{3,2,1,0:T(8,128)(2,1)S(1)} %bitcast.41, s32[4,1,384]{2,1,0:T(1,128)S(1)} %broadcast_in_dim.220.rank_ref, ...), custom_call_target="tpu_custom_call" | custom-call | flops 3221225472 | bytes 4718592 | tf_op jit(solution)/shard_map/back/pallas_call | solution.py:308
  (156 shorter events, 33.1 us)
Async XLA Ops:
  0.0 6.9 %copy-start.44 = (s32[4]{0:T(128)S(1)}, s32[4]{0:T(128)}, u32[]{:S(2)}) copy-start(s32[4]{0:T(128)} %constant.74.clone) | copy-start | bytes 52
  0.0 9.1 %copy-start.2 = (bf16[1536,512]{1,0:T(8,128)(2,1)S(1)}, bf16[1536,512]{1,0:T(8,128)(2,1)}, u32[]{:S(2)}) copy-start(bf16[1536,512]{1,0:T(8,128)(2,1)} %param.16) | copy-start | bytes 4718596
  0.0 7.0 %copy-start.40 = (s32[1536]{0:T(1024)S(1)}, s32[1536]{0:T(1024)}, u32[]{:S(2)}) copy-start(s32[1536]{0:T(1024)} %param.17) | copy-start | bytes 18436
  0.0 7.0 %copy-start.41 = (s32[1536]{0:T(1024)S(1)}, s32[1536]{0:T(1024)}, u32[]{:S(2)}) copy-start(s32[1536]{0:T(1024)} %param.18) | copy-start | bytes 18436
  0.0 7.3 %copy-start.42 = (s32[1536]{0:T(1024)S(1)}, s32[1536]{0:T(1024)}, u32[]{:S(2)}) copy-start(s32[1536]{0:T(1024)} %param.19) | copy-start | bytes 18436
  2.4 18.1 %collective-permute-start.2 = (bf16[384,512]{1,0:T(8,128)(2,1)}, bf16[384,512]{1,0:T(8,128)(2,1)}, u32[]{:S(2)}, u32[]{:S(2)}) collective-permute-start(bf16[384,512]{1,0:T(8,128)(2,1)} %get-tuple-element.45), channel_id=1, source_target_pairs={{0,24},{8,16},{16,8},{24,0},{1,25},{9,17},{17,9},{25,1},{2,26},{10... | collective-permute-start | bytes 1179656 | tf_op jit(solution)/shard_map/ppermute | solution.py:416
  6.3 25.6 %collective-permute-start.1 = (bf16[384,512]{1,0:T(8,128)(2,1)}, bf16[384,512]{1,0:T(8,128)(2,1)S(1)}, u32[]{:S(2)}, u32[]{:S(2)}) collective-permute-start(bf16[384,512]{1,0:T(8,128)(2,1)} %get-tuple-element.46), channel_id=1, source_target_pairs={{0,16},{8,24},{16,0},{24,8},{1,17},{9,25},{17,1},{25,9},{2,18},{10... | collective-permute-start | bytes 1179656 | tf_op jit(solution)/shard_map/ppermute | solution.py:416
  6.8 25.1 %collective-permute-start = (bf16[384,512]{1,0:T(8,128)(2,1)}, bf16[384,512]{1,0:T(8,128)(2,1)}, u32[]{:S(2)}, u32[]{:S(2)}) collective-permute-start(bf16[384,512]{1,0:T(8,128)(2,1)} %get-tuple-element.47), channel_id=1, source_target_pairs={{0,8},{8,0},{16,24},{24,16},{1,9},{9,1},{17,25},{25,17},{2,10},{10... | collective-permute-start | bytes 1179656 | tf_op jit(solution)/shard_map/ppermute | solution.py:416
  20.5 11.4 %copy-start.32 = (s32[2]{0:T(128)}, s32[2]{0:T(128)S(1)}, u32[]{:S(2)}) copy-start(s32[2]{0:T(128)S(1)} %get-tuple-element.56.where_ref.from_ref) | copy-start | bytes 28
  31.9 7.7 %copy-start.39 = (s32[4,384]{1,0:T(4,128)S(1)}, s32[4,384]{1,0:T(4,128)}, u32[]{:S(2)}) copy-start(s32[4,384]{1,0:T(4,128)} %get-tuple-element.26) | copy-start | bytes 18436
  40.7 7.7 %collective-permute-start.3 = (bf16[1,48,1088]{2,1,0:T(8,128)(2,1)S(1)}, bf16[1,48,1088]{2,1,0:T(8,128)(2,1)S(1)}, u32[]{:S(2)}, u32[]{:S(2)}) collective-permute-start(bf16[1,48,1088]{2,1,0:T(8,128)(2,1)S(1)} %maximum_bitcast_fusion), channel_id=1, source_target_pairs={{0,4},{1,5},{2,6},{3,7},{4,0},{5,1},{6,2},{7,3},{8,12},{9,13},{10,... | collective-permute-start | bytes 313352 | tf_op jit(solution)/shard_map/ppermute | solution.py:434
  49.1 6.4 %collective-permute-start.4 = (bf16[2,48,1088]{2,1,0:T(8,128)(2,1)}, bf16[2,48,1088]{2,1,0:T(8,128)(2,1)}, u32[]{:S(2)}, u32[]{:S(2)}) collective-permute-start(bf16[2,48,1088]{2,1,0:T(8,128)(2,1)} %pad_maximum_fusion.2), channel_id=1, source_target_pairs={{0,2},{1,3},{2,0},{3,1},{4,6},{5,7},{6,4},{7,5},{8,10},{9,11},{10,... | collective-permute-start | bytes 626696 | tf_op jit(solution)/shard_map/ppermute | solution.py:434
  50.7 6.4 %copy-start.43 = (s32[4]{0:T(128)S(1)}, s32[4]{0:T(128)}, u32[]{:S(2)}) copy-start(s32[4]{0:T(128)} %constant.75.clone) | copy-start | bytes 52
  50.7 42.6 %all-to-all-start = ((bf16[8,4,192,128]{3,2,1,0:T(8,128)(2,1)}), bf16[8,4,192,128]{3,2,1,0:T(8,128)(2,1)S(1)}, u32[]{:S(2)}, u32[]{:S(2)}) async-start(bf16[8,4,192,128]{3,2,1,0:T(8,128)(2,1)} %copy-done.20), calls=%async_computation | async-start | bytes 3145728 | tf_op jit(solution)/shard_map/all_to_all | solution.py:420
  56.5 2.0 collective-permute-start.5
  110.3 14.1 %copy-start.38 = (s32[4,384]{1,0:T(4,128)S(1)}, s32[4,384]{1,0:T(4,128)}, u32[]{:S(2)}) copy-start(s32[4,384]{1,0:T(4,128)} %copy-done.37) | copy-start | bytes 18436
  110.3 42.4 %copy-start.33 = (s32[2]{0:T(128)S(1)}, s32[2]{0:T(128)}, u32[]{:S(2)}) copy-start(s32[2]{0:T(128)} %copy-done.32) | copy-start | bytes 28
  110.3 42.4 %all-to-all-start.1 = ((bf16[32,192,128]{2,1,0:T(8,128)(2,1)}), bf16[32,192,128]{2,1,0:T(8,128)(2,1)S(1)}, u32[]{:S(2)}, u32[]{:S(2)}) async-start(bf16[32,192,128]{2,1,0:T(8,128)(2,1)} %bitcast.39), calls=%async_computation.1 | async-start | bytes 3145728 | tf_op jit(solution)/shard_map/all_to_all | solution.py:501
  114.0 10.2 %collective-permute-start.6 = (s32[384]{0:T(512)S(1)}, s32[384]{0:T(512)S(1)}, u32[]{:S(2)}, u32[]{:S(2)}) collective-permute-start(s32[384]{0:T(512)S(1)} %get-tuple-element.37), channel_id=1, source_target_pairs={{0,24},{8,16},{16,8},{24,0},{1,25},{9,17},{17,9},{25,1},{2,26},{10... | collective-permute-start | bytes 4616 | tf_op jit(solution)/shard_map/ppermute | solution.py:416
  116.6 7.6 %collective-permute-start.8 = (s32[384]{0:T(512)S(1)}, s32[384]{0:T(512)S(1)}, u32[]{:S(2)}, u32[]{:S(2)}) collective-permute-start(s32[384]{0:T(512)S(1)} %get-tuple-element.38), channel_id=1, source_target_pairs={{0,16},{8,24},{16,0},{24,8},{1,17},{9,25},{17,1},{25,9},{2,18},{10... | collective-permute-start | bytes 4616 | tf_op jit(solution)/shard_map/ppermute | solution.py:416
  117.1 7.3 %collective-permute-start.7 = (s32[384]{0:T(512)S(1)}, s32[384]{0:T(512)S(1)}, u32[]{:S(2)}, u32[]{:S(2)}) collective-permute-start(s32[384]{0:T(512)S(1)} %get-tuple-element.39), channel_id=1, source_target_pairs={{0,8},{8,0},{16,24},{24,16},{1,9},{9,1},{17,25},{25,17},{2,10},{10... | collective-permute-start | bytes 4616 | tf_op jit(solution)/shard_map/ppermute | solution.py:416
  156.3 4.8 %copy-start.34 = (s32[2]{0:T(128)S(1)}, s32[2]{0:T(128)}, u32[]{:S(2)}) copy-start(s32[2]{0:T(128)} %get-tuple-element.55.from_ref) | copy-start | bytes 28
  161.1 17.9 %copy-start.11 = (bf16[2,512,512]{2,1,0:T(8,128)(2,1)S(1)}, bf16[2,512,512]{2,1,0:T(8,128)(2,1)}, u32[]{:S(2)}) copy-start(bf16[2,512,512]{2,1,0:T(8,128)(2,1)} %wc.9) | copy-start | bytes 3145732
  161.1 17.9 %copy-start.14 = (bf16[2,512,512]{2,1,0:T(8,128)(2,1)S(1)}, bf16[2,512,512]{2,1,0:T(8,128)(2,1)}, u32[]{:S(2)}) copy-start(bf16[2,512,512]{2,1,0:T(8,128)(2,1)} %wi.9) | copy-start | bytes 3145732
  161.2 17.8 %copy-start.17 = (bf16[2,512,512]{2,1,0:T(8,128)(2,1)S(1)}, bf16[2,512,512]{2,1,0:T(8,128)(2,1)}, u32[]{:S(2)}) copy-start(bf16[2,512,512]{2,1,0:T(8,128)(2,1)} %wo.9) | copy-start | bytes 3145732
  165.9 13.1 %copy-start.5 = (bf16[2,512,512]{2,1,0:T(8,128)(2,1)S(1)}, bf16[2,512,512]{2,1,0:T(8,128)(2,1)}, u32[]{:S(2)}) copy-start(bf16[2,512,512]{2,1,0:T(8,128)(2,1)} %wm.9) | copy-start | bytes 3145732
  165.9 13.1 %copy-start.8 = (bf16[2,512,512]{2,1,0:T(8,128)(2,1)S(1)}, bf16[2,512,512]{2,1,0:T(8,128)(2,1)}, u32[]{:S(2)}) copy-start(bf16[2,512,512]{2,1,0:T(8,128)(2,1)} %wr.9) | copy-start | bytes 3145732
  166.0 13.0 %collective-permute-start.11 = (bf16[384,512]{1,0:T(8,128)(2,1)S(1)}, bf16[384,512]{1,0:T(8,128)(2,1)S(1)}, u32[]{:S(2)}, u32[]{:S(2)}) collective-permute-start(bf16[384,512]{1,0:T(8,128)(2,1)S(1)} %slice_bitcast_fusion), channel_id=1, source_target_pairs={{0,24},{8,16},{16,8},{24,0},{1,25},{9,17},{17,9},{25,1},{2,26},{10... | collective-permute-start | bytes 1179656 | tf_op jit(solution)/shard_map/ppermute | solution.py:416
  166.6 19.4 %collective-permute-start.10 = (bf16[384,512]{1,0:T(8,128)(2,1)S(1)}, bf16[384,512]{1,0:T(8,128)(2,1)S(1)}, u32[]{:S(2)}, u32[]{:S(2)}) collective-permute-start(bf16[384,512]{1,0:T(8,128)(2,1)S(1)} %get-tuple-element.48), channel_id=1, source_target_pairs={{0,16},{8,24},{16,0},{24,8},{1,17},{9,25},{17,1},{25,9},{2,18},{10... | collective-permute-start | bytes 1179656 | tf_op jit(solution)/shard_map/ppermute | solution.py:416
  167.2 18.8 %collective-permute-start.9 = (bf16[384,512]{1,0:T(8,128)(2,1)S(1)}, bf16[384,512]{1,0:T(8,128)(2,1)S(1)}, u32[]{:S(2)}, u32[]{:S(2)}) collective-permute-start(bf16[384,512]{1,0:T(8,128)(2,1)S(1)} %get-tuple-element.49), channel_id=1, source_target_pairs={{0,8},{8,0},{16,24},{24,16},{1,9},{9,1},{17,25},{25,17},{2,10},{10... | collective-permute-start | bytes 1179656 | tf_op jit(solution)/shard_map/ppermute | solution.py:416
  179.0 52.8 %slice-start = ((s8[6291456]{0:T(1024)(128)(4,1)}), s8[4194304]{0:T(1024)(128)(4,1)S(1)}, s32[]{:S(2)}) async-start(s8[6291456]{0:T(1024)(128)(4,1)} %bitcast.31), calls=%async_computation.4 | async-start | bytes 8388608
  186.0 45.8 %slice-start.1 = ((s8[6291456]{0:T(1024)(128)(4,1)}), s8[2097152]{0:T(1024)(128)(4,1)S(1)}, s32[]{:S(2)}) async-start(s8[6291456]{0:T(1024)(128)(4,1)} %bitcast.31), calls=%async_computation.5 | async-start | bytes 4194304
  (29 other events, 54.1 us)

commit v4 on v3

--- a/solution.py
+++ b/solution.py
@@ -246,10 +246,11 @@
 
 
 VMEM_BYTES = 24 * 1024 * 1024
-
-
-def params():
-    return pltpu.CompilerParams(vmem_limit_bytes=VMEM_BYTES)
+VMEM_MOST = 60 * 1024 * 1024
+
+
+def params(limit=VMEM_BYTES):
+    return pltpu.CompilerParams(vmem_limit_bytes=limit)
 
 
 def cost(flops, moved, waves=0):
@@ -295,7 +296,7 @@
             jax.ShapeDtypeStruct((narrow, sides, rows // 2, LANES), jnp.bfloat16),
         ],
         input_output_aliases={first_target + index: index for index in range(len(targets))},
-        compiler_params=params(),
+        compiler_params=params(VMEM_BYTES if section else VMEM_MOST),
         cost_estimate=cost(12 * count * rows * features**2, 8 * count * rows * features),
         name="front",
     )(where, current, back_rows, rank_rows, *weights[:5], *received, *targets)
@@ -423,7 +424,7 @@
 BASE = 64
 
 
-def share_lists(listed, angles):
+def share_lists(listed, angles, after):
     narrow = lax.axis_size("narrow")
     atoms, width = angles.shape
     digits = jnp.stack([listed // BASE, listed % BASE]).reshape(atoms, -1).astype(jnp.bfloat16)
@@ -431,6 +432,8 @@
     held = [0]
     hop = narrow // 2
     while hop:
+        if hop == 1:
+            shared, after = lax.optimization_barrier((shared, after))
         other = lax.ppermute(shared, "narrow", [(i, i ^ hop) for i in range(narrow)])
         shared = jnp.concatenate([shared, other], axis=0)
         held += [offset ^ hop for offset in held]
@@ -442,7 +445,7 @@
     digits = shared[:, :, width:].reshape((narrow, 2) + listed.shape).astype(jnp.int32)
     entries = digits[:, 0] * BASE + digits[:, 1]
     entries = reorder(entries.reshape(narrow, -1), places).reshape(entries.shape)
-    return entries, shared, places
+    return entries, shared, places, after
 
 
 def tiled_local(messages, reverse_position, route_slot, atom_slots, angles, weights):
@@ -460,7 +463,7 @@
     owners_wide = (jnp.arange(wide, dtype=jnp.int32) ^ group_id)[:, None]
     position = jnp.sum(jnp.where(owners_wide == jnp.arange(wide), inverse, 0), axis=1)
     half = wide // 2
-    pieces = [(0, 1), (1, half - 1), (half, wide - half)]
+    pieces = [(0, 1), (1, wide - 1)]
     halves = [(0, half), (half, wide - half)]
 
     blocks_of = messages.reshape(wide, rows, features)
@@ -487,8 +490,8 @@
             )
         second, packed = targets
         if tables is None:
-            packed, listed, late_rank = lax.optimization_barrier((packed, listed, rank))
-            entries, all_angles, owner_places = share_lists(listed, angles)
+            entries, all_angles, owner_places, packed = share_lists(listed, angles, packed)
+            packed, late_rank = lax.optimization_barrier((packed, rank))
             owner_of, place_of = unit_tables(entries, capacity, unit)
             tables = run_tables(owner_places, order, position, entries[:, :, None, :], all_angles)
             partner_rank = jnp.stack(

time: 297 us -> 281 us (0.946)
  local copies, waits for them, and re-layouts: 33.3 us -> 15.3 us
  Pallas kernels: 76.6 us -> 80.8 us
  other arithmetic: 7.18 us -> 3.92 us
    unnamed x95 -> x50, local copies, waits for them, and re-layouts: 28.3 us -> 9.25 us
    all_to_all x1, waiting for transfers between devices: 21.1 us -> 25 us  [swap(): return lax.all_to_all(values, 'narrow', 0, 0, tiled=True)]
    pallas_call x5 -> x4, Pallas kernels: 24.5 us -> 27.7 us  [run_front(): pl.pallas_call(functools.partial(front_kernel, own, count), grid_spec=plt...]
  transfers between devices with their start and end apart: 14 -> 14, of which waited for: 8 -> 9; matrix products, arithmetic and copies ran while one was open for 3% -> 2% of each run, Pallas kernels for 7% -> 8%
where the time goes in v4:
time: 281 us; the launch traced here: 280 us
  blocking collectives  81.1 us (29%)
  Pallas kernels  80.8 us (29%)
  waiting for transfers between devices  74.3 us (26%)
  starting transfers between devices  24.2 us (9%)
  local copies, waits for them, and re-layouts  15.3 us (5%)
  other arithmetic  3.92 us (1%)
    all_to_all x1, blocking collectives, tiled_local(): returned = lax.all_to_all(mixed, ('wide', 'narrow'), 0, 0, tiled=True)  40.9 us
    all_to_all x1, blocking collectives, swap(): return lax.all_to_all(values, 'narrow', 0, 0, tiled=True)  40.3 us
    pallas_call x4, Pallas kernels, run_front(): pl.pallas_call(functools.partial(front_kernel, own, count), grid_spec=plt...  27.7 us
    all_to_all x1, waiting for transfers between devices, tiled_local(): returned = lax.all_to_all(mixed, ('wide', 'narrow'), 0, 0, tiled=True)  27.7 us
    pallas_call x2, Pallas kernels, run_mix(): pl.pallas_call(mix_kernel, grid=(devices,), in_specs=[smem, smem, smem, w...  27 us
    all_to_all x1, waiting for transfers between devices, swap(): return lax.all_to_all(values, 'narrow', 0, 0, tiled=True)  25 us
    pallas_call x3, Pallas kernels, run_back(): pl.pallas_call(back_kernel, grid_spec=pltpu.PrefetchScalarGridSpec(num_sc...  19.1 us
    ppermute x9, waiting for transfers between devices, shift(): return lax.ppermute(values, 'wide', [(i, i ^ offset) for i in range(wide)])  16.7 us
  transfers between devices with their start and end apart: 14, of which 9 were waited for; matrix products, arithmetic and copies ran while one was open for 2% of the time, Pallas kernels for 8%

profile of v4, /device:TPU:0, one launch (start us, length us, event | category | flops | bytes accessed | tf_op | source)
XLA Modules:
  0.0 280.1 jit_solution(11107102287202489035)
XLA Ops:
  4.7 4.1 %collective-permute-start.3 = (bf16[1,48,1088]{2,1,0:T(8,128)(2,1)S(1)}, bf16[1,48,1088]{2,1,0:T(8,128)(2,1)S(1)}, u32[]{:S(2)}, u32[]{:S(2)}) collective-permute-start(bf16[1,48,1088]{2,1,0:T(8,128)(2,1)S(1)} %maximum_bitcast_fusion), channel_id=1, source_target_pairs={{0,4},{1,5},{2,6},{3,7},{4,0},{5,1},{6,2},{7,3},{8,12},{9,13},{10,... | collective-permute-start | bytes 313352 | tf_op jit(solution)/shard_map/ppermute | solution.py:437
  8.8 1.3 dynamic-slice_bitcast_fusion
  10.1 1.6 collective-permute-start.2
  11.7 1.5 collective-permute-start.1
  14.9 5.4 %front.4 = (bf16[4,384,512]{2,1,0:T(8,128)(2,1)}, bf16[8,4,192,128]{3,2,1,0:T(8,128)(2,1)}) custom-call(s32[1]{0:T(128)} %bitcast.56, bf16[4,384,512]{2,1,0:T(8,128)(2,1)} %bitcast.58, s32[4,1,384]{2,1,0:T(1,128)} %broadcast_in_dim.197.back_ref, s32[4,1,384]{2,1,0:T(1,128)} %broadcast_in_dim.199.rank_ref, bf16[2,512,512]{2,1,0:T(8,128)(2,1)} %wm.7, ...), custom_call_target="tpu_custom_call" | custom-call | flops 1207959552 | bytes 1572864 | tf_op jit(solution)/shard_map/front/pallas_call | solution.py:275
  20.4 1.6 collective-permute-start.4
  22.8 3.7 %collective-permute-done.4 = bf16[2,48,1088]{2,1,0:T(8,128)(2,1)S(1)} collective-permute-done((bf16[2,48,1088]{2,1,0:T(8,128)(2,1)S(1)}, bf16[2,48,1088]{2,1,0:T(8,128)(2,1)S(1)}, u32[]{:S(2)}, u32[]{:S(2)}) %collective-permute-start.4) | collective-permute-done | bytes 208928 | tf_op jit(solution)/shard_map/ppermute | solution.py:437
  26.6 3.9 %collective-permute-done.refs_0_ = bf16[384,512]{1,0:T(8,128)(2,1)} collective-permute-done((bf16[384,512]{1,0:T(8,128)(2,1)S(1)}, bf16[384,512]{1,0:T(8,128)(2,1)}, u32[]{:S(2)}, u32[]{:S(2)}) %collective-permute-start) | collective-permute-done | bytes 393248 | tf_op jit(solution)/shard_map/ppermute | solution.py:417
  30.5 11.2 %front.5 = (bf16[4,384,512]{2,1,0:T(8,128)(2,1)}, bf16[8,4,192,128]{3,2,1,0:T(8,128)(2,1)}) custom-call(s32[3]{0:T(128)} %slice.43.where_ref, bf16[4,384,512]{2,1,0:T(8,128)(2,1)} %bitcast.59, s32[4,1,384]{2,1,0:T(1,128)} %broadcast_in_dim.197.back_ref, s32[4,1,384]{2,1,0:T(1,128)} %broadcast_in_dim.199.rank_ref, ...), custom_call_target="tpu_custom_call", output_to_operand_aliasing={{0}: (12, {}), {1}: (13, {})} | custom-call | flops 3623878656 | bytes 4718592 | tf_op jit(solution)/shard_map/front/pallas_call | solution.py:275
  41.7 3.6 %all-to-all-start = ((bf16[8,4,192,128]{3,2,1,0:T(8,128)(2,1)}), bf16[8,4,192,128]{3,2,1,0:T(8,128)(2,1)S(1)}, u32[]{:S(2)}, u32[]{:S(2)}) async-start(bf16[8,4,192,128]{3,2,1,0:T(8,128)(2,1)} %get-tuple-element.25), calls=%async_computation | async-start | bytes 3145728 | tf_op jit(solution)/shard_map/all_to_all | solution.py:421
  46.0 1.3 collective-permute-done.5
  47.8 7.0 %tables.1 = (s32[8,4,1,384]{3,2,1,0:T(1,128)S(1)}, bf16[8,6,256,256]{3,2,1,0:T(8,128)(2,1)S(1)}) custom-call(s32[8]{0:T(128)S(1)} %select_reduce_fusion.9.places_ref, s32[4]{0:T(128)S(1)} %copy-done.17, s32[4]{0:T(128)S(1)} %select_reduce_fusion.10.position_ref, s32[8,4,1,384]{3,2,1,0:T(1,128)S(1)} %broadcast_in_dim_reshape.2.entry_ref, ...), custom_call_target="tpu_custom_call" | custom-call | bytes 25165824 | tf_op jit(solution)/shard_map/tables/pallas_call | solution.py:338
  54.9 2.7 copy-done
  58.0 25.0 %all-to-all-done.recv_ref = bf16[8,4,192,128]{3,2,1,0:T(8,128)(2,1)S(1)} async-done(((bf16[8,4,192,128]{3,2,1,0:T(8,128)(2,1)}), bf16[8,4,192,128]{3,2,1,0:T(8,128)(2,1)S(1)}, u32[]{:S(2)}, u32[]{:S(2)}) %all-to-all-start) | async-done | bytes 1572896 | tf_op jit(solution)/shard_map/all_to_all | solution.py:421
  83.0 2.8 copy-done.1
  85.8 14.1 %mix.2 = bf16[4,8,192,128]{3,2,1,0:T(8,128)(2,1)} custom-call(s32[8,8]{1,0:T(8,128)S(1)} %get-tuple-element.34.owner_ref, s32[8,8]{1,0:T(8,128)S(1)} %get-tuple-element.33.place_ref, s32[4]{0:T(128)S(1)} %copy-done.17, bf16[8,4,192,128]{3,2,1,0:T(8,128)(2,1)S(1)} %all-to-all-done.recv_ref, s32[8,4,1,384]{3,2,1,0:T(1,128)S(1)} %get-tuple-element.26.rank_ref, ...), custom_call_target="tpu_custom_call" | custom-call | flops 1509949440 | bytes 18874368 | tf_op jit(solution)/shard_map/mix/pallas_call | solution.py:368
  99.9 3.7 %all-to-all-start.1 = ((bf16[32,192,128]{2,1,0:T(8,128)(2,1)}), bf16[32,192,128]{2,1,0:T(8,128)(2,1)S(1)}, u32[]{:S(2)}, u32[]{:S(2)}) async-start(bf16[32,192,128]{2,1,0:T(8,128)(2,1)} %bitcast.7), calls=%async_computation.1 | async-start | bytes 3145728 | tf_op jit(solution)/shard_map/all_to_all | solution.py:504
  103.6 2.6 collective-permute-start.6
  107.2 6.6 %collective-permute-done.6 = s32[384]{0:T(512)S(1)} collective-permute-done((s32[384]{0:T(512)S(1)}, s32[384]{0:T(512)S(1)}, u32[]{:S(2)}, u32[]{:S(2)}) %collective-permute-start.6) | collective-permute-done | bytes 1568 | tf_op jit(solution)/shard_map/ppermute | solution.py:417
  114.6 27.7 %all-to-all-done.1 = bf16[32,192,128]{2,1,0:T(8,128)(2,1)S(1)} async-done(((bf16[32,192,128]{2,1,0:T(8,128)(2,1)}), bf16[32,192,128]{2,1,0:T(8,128)(2,1)S(1)}, u32[]{:S(2)}, u32[]{:S(2)}) %all-to-all-start.1) | async-done | bytes 1572896 | tf_op jit(solution)/shard_map/all_to_all | solution.py:504
  142.3 1.2 copy-done.8
  145.9 4.7 %back.4.cur_ref = bf16[2,384,512]{2,1,0:T(8,128)(2,1)S(1)} custom-call(s32[2]{0:T(128)S(1)} %get-tuple-element.53.from_ref, s32[2]{0:T(128)S(1)} %iota.79.to_ref, bf16[4,384,512]{2,1,0:T(8,128)(2,1)S(1)} %copy-done.2, bf16[4,8,192,128]{3,2,1,0:T(8,128)(2,1)S(1)} %bitcast.52, s32[4,1,384]{2,1,0:T(1,128)S(1)} %broadcast_in_dim.218.rank_ref, ...), custom_call_target="tpu_custom_call" | custom-call | flops 1610612736 | bytes 2359296 | tf_op jit(solution)/shard_map/back/pallas_call | solution.py:309
  151.4 4.7 %back.3.cur_ref = bf16[2,384,512]{2,1,0:T(8,128)(2,1)S(1)} custom-call(s32[2]{0:T(128)S(1)} %get-tuple-element.54.from_ref, s32[2]{0:T(128)S(1)} %iota.75.to_ref, bf16[4,384,512]{2,1,0:T(8,128)(2,1)S(1)} %copy-done.2, bf16[4,8,192,128]{3,2,1,0:T(8,128)(2,1)S(1)} %bitcast.53, s32[4,1,384]{2,1,0:T(1,128)S(1)} %broadcast_in_dim.218.rank_ref, ...), custom_call_target="tpu_custom_call" | custom-call | flops 1610612736 | bytes 2359296 | tf_op jit(solution)/shard_map/back/pallas_call | solution.py:309
  156.8 2.4 collective-permute-start.9
  159.2 4.5 %collective-permute-done.11.refs_0_ = bf16[384,512]{1,0:T(8,128)(2,1)S(1)} collective-permute-done((bf16[384,512]{1,0:T(8,128)(2,1)S(1)}, bf16[384,512]{1,0:T(8,128)(2,1)S(1)}, u32[]{:S(2)}, u32[]{:S(2)}) %collective-permute-start.11) | collective-permute-done | bytes 393248 | tf_op jit(solution)/shard_map/ppermute | solution.py:417
  163.8 5.5 %front.6 = (bf16[4,384,512]{2,1,0:T(8,128)(2,1)S(1)}, bf16[8,4,192,128]{3,2,1,0:T(8,128)(2,1)S(1)}) custom-call(s32[2]{0:T(128)S(1)} %iota.78.where_ref, bf16[2,384,512]{2,1,0:T(8,128)(2,1)S(1)} %back.4.cur_ref, s32[4,1,384]{2,1,0:T(1,128)S(1)} %copy-done.15, s32[4,1,384]{2,1,0:T(1,128)S(1)} %copy-done.14, bf16[2,512,512]{2,1,0:T(8,128)(2,1)S(1)} %copy-done.3, ...), custom_call_target="tpu_custom_call" | custom-call | flops 2415919104 | bytes 3145728 | tf_op jit(solution)/shard_map/front/pallas_call | solution.py:275
  169.4 1.4 collective-permute-done.10.refs_1_
  170.8 5.6 %front.7 = (bf16[4,384,512]{2,1,0:T(8,128)(2,1)S(1)}, bf16[8,4,192,128]{3,2,1,0:T(8,128)(2,1)S(1)}) custom-call(s32[2]{0:T(128)S(1)} %iota.74.where_ref, bf16[2,384,512]{2,1,0:T(8,128)(2,1)S(1)} %back.3.cur_ref, s32[4,1,384]{2,1,0:T(1,128)S(1)} %copy-done.15, s32[4,1,384]{2,1,0:T(1,128)S(1)} %copy-done.14, ...), custom_call_target="tpu_custom_call", output_to_operand_aliasing={{0}: (11, {}), {1}: (12, {})} | custom-call | flops 2415919104 | bytes 3145728 | tf_op jit(solution)/shard_map/front/pallas_call | solution.py:275
  176.4 40.3 %all_to_all.20.recv_ref = bf16[8,4,192,128]{3,2,1,0:T(8,128)(2,1)S(1)} all-to-all(bf16[8,4,192,128]{3,2,1,0:T(8,128)(2,1)S(1)} %get-tuple-element.32), channel_id=1, replica_groups=mesh['wide'=4,'narrow'=8] {'narrow'}, dimensions={0} | all-to-all | bytes 3145728 | tf_op jit(solution)/shard_map/all_to_all | solution.py:421
  216.6 12.9 %mix.3 = bf16[4,8,192,128]{3,2,1,0:T(8,128)(2,1)S(1)} custom-call(s32[8,8]{1,0:T(8,128)S(1)} %get-tuple-element.34.owner_ref, s32[8,8]{1,0:T(8,128)S(1)} %get-tuple-element.33.place_ref, s32[4]{0:T(128)S(1)} %copy-done.17, bf16[8,4,192,128]{3,2,1,0:T(8,128)(2,1)S(1)} %all_to_all.20.recv_ref, s32[8,4,1,384]{3,2,1,0:T(1,128)S(1)} %get-tuple-element.26.rank_ref, ...), custom_call_target="tpu_custom_call" | custom-call | flops 1509949440 | bytes 18874368 | tf_op jit(solution)/shard_map/mix/pallas_call | solution.py:368
  229.6 40.9 %all_to_all.21 = bf16[32,192,128]{2,1,0:T(8,128)(2,1)S(1)} all-to-all(bf16[32,192,128]{2,1,0:T(8,128)(2,1)S(1)} %bitcast.54), channel_id=1, replica_groups=mesh['wide'=4,'narrow'=8] {'wide','narrow'}, dimensions={0} | all-to-all | bytes 3145728 | tf_op jit(solution)/shard_map/all_to_all | solution.py:504
  270.5 9.7 %back.5 = bf16[4,384,512]{2,1,0:T(8,128)(2,1)} custom-call(s32[4]{0:T(128)S(1)} %copy-done.17, s32[4]{0:T(128)S(1)} %copy-done.17, bf16[4,384,512]{2,1,0:T(8,128)(2,1)S(1)} %get-tuple-element.31.second_ref, bf16[4,8,192,128]{3,2,1,0:T(8,128)(2,1)S(1)} %bitcast.55, s32[4,1,384]{2,1,0:T(1,128)S(1)} %broadcast_in_dim.218.rank_ref, ...), custom_call_target="tpu_custom_call" | custom-call | flops 3221225472 | bytes 4718592 | tf_op jit(solution)/shard_map/back/pallas_call | solution.py:309
  (110 shorter events, 14.6 us)
Async XLA Ops:
  0.7 9.5 %copy-start.16 = (s32[4]{0:T(128)}, s32[4]{0:T(128)S(1)}, u32[]{:S(2)}) copy-start(s32[4]{0:T(128)S(1)} %broadcast_xor_fusion.order_ref.from_ref.to_ref) | copy-start | bytes 52
  4.7 15.6 %collective-permute-start.3 = (bf16[1,48,1088]{2,1,0:T(8,128)(2,1)S(1)}, bf16[1,48,1088]{2,1,0:T(8,128)(2,1)S(1)}, u32[]{:S(2)}, u32[]{:S(2)}) collective-permute-start(bf16[1,48,1088]{2,1,0:T(8,128)(2,1)S(1)} %maximum_bitcast_fusion), channel_id=1, source_target_pairs={{0,4},{1,5},{2,6},{3,7},{4,0},{5,1},{6,2},{7,3},{8,12},{9,13},{10,... | collective-permute-start | bytes 313352 | tf_op jit(solution)/shard_map/ppermute | solution.py:437
  10.1 16.4 %collective-permute-start.2 = (bf16[384,512]{1,0:T(8,128)(2,1)S(1)}, bf16[384,512]{1,0:T(8,128)(2,1)S(1)}, u32[]{:S(2)}, u32[]{:S(2)}) collective-permute-start(bf16[384,512]{1,0:T(8,128)(2,1)S(1)} %get-tuple-element.43), channel_id=1, source_target_pairs={{0,16},{8,24},{16,0},{24,8},{1,17},{9,25},{17,1},{25,9},{2,18},{10... | collective-permute-start | bytes 1179656 | tf_op jit(solution)/shard_map/ppermute | solution.py:417
  11.7 14.8 %collective-permute-start.1 = (bf16[384,512]{1,0:T(8,128)(2,1)S(1)}, bf16[384,512]{1,0:T(8,128)(2,1)S(1)}, u32[]{:S(2)}, u32[]{:S(2)}) collective-permute-start(bf16[384,512]{1,0:T(8,128)(2,1)S(1)} %get-tuple-element.44), channel_id=1, source_target_pairs={{0,8},{8,0},{16,24},{24,16},{1,9},{9,1},{17,25},{25,17},{2,10},{10... | collective-permute-start | bytes 1179656 | tf_op jit(solution)/shard_map/ppermute | solution.py:417
  13.2 17.3 %collective-permute-start = (bf16[384,512]{1,0:T(8,128)(2,1)S(1)}, bf16[384,512]{1,0:T(8,128)(2,1)}, u32[]{:S(2)}, u32[]{:S(2)}) collective-permute-start(bf16[384,512]{1,0:T(8,128)(2,1)S(1)} %get-tuple-element.45), channel_id=1, source_target_pairs={{0,24},{8,16},{16,8},{24,0},{1,25},{9,17},{17,9},{25,1},{2,26},{10... | collective-permute-start | bytes 1179656 | tf_op jit(solution)/shard_map/ppermute | solution.py:417
  14.9 7.1 %copy-start.17 = (s32[4]{0:T(128)S(1)}, s32[4]{0:T(128)}, u32[]{:S(2)}) copy-start(s32[4]{0:T(128)} %copy-done.16) | copy-start | bytes 52
  14.9 7.7 %copy-start.21 = (s32[8]{0:T(128)S(1)}, s32[8]{0:T(128)}, u32[]{:S(2)}) copy-start(s32[8]{0:T(128)} %constant.76.clone) | copy-start | bytes 100
  20.4 6.1 %collective-permute-start.4 = (bf16[2,48,1088]{2,1,0:T(8,128)(2,1)S(1)}, bf16[2,48,1088]{2,1,0:T(8,128)(2,1)S(1)}, u32[]{:S(2)}, u32[]{:S(2)}) collective-permute-start(bf16[2,48,1088]{2,1,0:T(8,128)(2,1)S(1)} %pad_maximum_fusion.1), channel_id=1, source_target_pairs={{0,2},{1,3},{2,0},{3,1},{4,6},{5,7},{6,4},{7,5},{8,10},{9,11},{10,... | collective-permute-start | bytes 626696 | tf_op jit(solution)/shard_map/ppermute | solution.py:437
  26.5 3.9 %copy-start.18 = (bf16[384,512]{1,0:T(8,128)(2,1)}, bf16[384,512]{1,0:T(8,128)(2,1)S(1)}, u32[]{:S(2)}) copy-start(bf16[384,512]{1,0:T(8,128)(2,1)S(1)} %collective-permute-done.2.refs_2_) | copy-start | bytes 1179652
  26.6 3.9 %copy-start.19 = (bf16[384,512]{1,0:T(8,128)(2,1)}, bf16[384,512]{1,0:T(8,128)(2,1)S(1)}, u32[]{:S(2)}) copy-start(bf16[384,512]{1,0:T(8,128)(2,1)S(1)} %collective-permute-done.1.refs_1_) | copy-start | bytes 1179652
  41.7 41.3 %all-to-all-start = ((bf16[8,4,192,128]{3,2,1,0:T(8,128)(2,1)}), bf16[8,4,192,128]{3,2,1,0:T(8,128)(2,1)S(1)}, u32[]{:S(2)}, u32[]{:S(2)}) async-start(bf16[8,4,192,128]{3,2,1,0:T(8,128)(2,1)} %get-tuple-element.25), calls=%async_computation | async-start | bytes 3145728 | tf_op jit(solution)/shard_map/all_to_all | solution.py:421
  45.5 1.9 collective-permute-start.5
  99.9 42.4 %copy-start.2 = (bf16[4,384,512]{2,1,0:T(8,128)(2,1)S(1)}, bf16[4,384,512]{2,1,0:T(8,128)(2,1)}, u32[]{:S(2)}) copy-start(bf16[4,384,512]{2,1,0:T(8,128)(2,1)} %get-tuple-element.21.second_ref) | copy-start | bytes 4718596
  99.9 42.4 %all-to-all-start.1 = ((bf16[32,192,128]{2,1,0:T(8,128)(2,1)}), bf16[32,192,128]{2,1,0:T(8,128)(2,1)S(1)}, u32[]{:S(2)}, u32[]{:S(2)}) async-start(bf16[32,192,128]{2,1,0:T(8,128)(2,1)} %bitcast.7), calls=%async_computation.1 | async-start | bytes 3145728 | tf_op jit(solution)/shard_map/all_to_all | solution.py:504
  103.6 10.2 %collective-permute-start.6 = (s32[384]{0:T(512)S(1)}, s32[384]{0:T(512)S(1)}, u32[]{:S(2)}, u32[]{:S(2)}) collective-permute-start(s32[384]{0:T(512)S(1)} %get-tuple-element.35), channel_id=1, source_target_pairs={{0,24},{8,16},{16,8},{24,0},{1,25},{9,17},{17,9},{25,1},{2,26},{10... | collective-permute-start | bytes 4616 | tf_op jit(solution)/shard_map/ppermute | solution.py:417
  106.2 7.6 %collective-permute-start.8 = (s32[384]{0:T(512)S(1)}, s32[384]{0:T(512)S(1)}, u32[]{:S(2)}, u32[]{:S(2)}) collective-permute-start(s32[384]{0:T(512)S(1)} %get-tuple-element.36), channel_id=1, source_target_pairs={{0,16},{8,24},{16,0},{24,8},{1,17},{9,25},{17,1},{25,9},{2,18},{10... | collective-permute-start | bytes 4616 | tf_op jit(solution)/shard_map/ppermute | solution.py:417
  106.7 7.3 %collective-permute-start.7 = (s32[384]{0:T(512)S(1)}, s32[384]{0:T(512)S(1)}, u32[]{:S(2)}, u32[]{:S(2)}) collective-permute-start(s32[384]{0:T(512)S(1)} %get-tuple-element.37), channel_id=1, source_target_pairs={{0,8},{8,0},{16,24},{24,16},{1,9},{9,1},{17,25},{25,17},{2,10},{10... | collective-permute-start | bytes 4616 | tf_op jit(solution)/shard_map/ppermute | solution.py:417
  145.9 5.4 %copy-start.9 = (bf16[2,512,512]{2,1,0:T(8,128)(2,1)S(1)}, bf16[2,512,512]{2,1,0:T(8,128)(2,1)}, u32[]{:S(2)}) copy-start(bf16[2,512,512]{2,1,0:T(8,128)(2,1)} %wl.5) | copy-start | bytes 3145732
  150.7 13.0 %collective-permute-start.11 = (bf16[384,512]{1,0:T(8,128)(2,1)S(1)}, bf16[384,512]{1,0:T(8,128)(2,1)S(1)}, u32[]{:S(2)}, u32[]{:S(2)}) collective-permute-start(bf16[384,512]{1,0:T(8,128)(2,1)S(1)} %slice_bitcast_fusion), channel_id=1, source_target_pairs={{0,24},{8,16},{16,8},{24,0},{1,25},{9,17},{17,9},{25,1},{2,26},{10... | collective-permute-start | bytes 1179656 | tf_op jit(solution)/shard_map/ppermute | solution.py:417
  151.3 12.4 %copy-start.4 = (bf16[2,512,512]{2,1,0:T(8,128)(2,1)S(1)}, bf16[2,512,512]{2,1,0:T(8,128)(2,1)}, u32[]{:S(2)}) copy-start(bf16[2,512,512]{2,1,0:T(8,128)(2,1)} %wr.7) | copy-start | bytes 3145732
  151.3 12.4 %copy-start.5 = (bf16[2,512,512]{2,1,0:T(8,128)(2,1)S(1)}, bf16[2,512,512]{2,1,0:T(8,128)(2,1)}, u32[]{:S(2)}) copy-start(bf16[2,512,512]{2,1,0:T(8,128)(2,1)} %wc.7) | copy-start | bytes 3145732
  151.3 12.4 %copy-start.6 = (bf16[2,512,512]{2,1,0:T(8,128)(2,1)S(1)}, bf16[2,512,512]{2,1,0:T(8,128)(2,1)}, u32[]{:S(2)}) copy-start(bf16[2,512,512]{2,1,0:T(8,128)(2,1)} %wi.7) | copy-start | bytes 3145732
  151.3 12.4 %copy-start.7 = (bf16[2,512,512]{2,1,0:T(8,128)(2,1)S(1)}, bf16[2,512,512]{2,1,0:T(8,128)(2,1)}, u32[]{:S(2)}) copy-start(bf16[2,512,512]{2,1,0:T(8,128)(2,1)} %wo.7) | copy-start | bytes 3145732
  156.1 7.7 %copy-start.3 = (bf16[2,512,512]{2,1,0:T(8,128)(2,1)S(1)}, bf16[2,512,512]{2,1,0:T(8,128)(2,1)}, u32[]{:S(2)}) copy-start(bf16[2,512,512]{2,1,0:T(8,128)(2,1)} %wm.7) | copy-start | bytes 3145732
  156.1 7.7 %copy-start.14 = (s32[4,1,384]{2,1,0:T(1,128)S(1)}, s32[4,1,384]{2,1,0:T(1,128)}, u32[]{:S(2)}) copy-start(s32[4,1,384]{2,1,0:T(1,128)} %broadcast_in_dim.199.rank_ref) | copy-start | bytes 18436
  156.1 7.7 %copy-start.15 = (s32[4,1,384]{2,1,0:T(1,128)S(1)}, s32[4,1,384]{2,1,0:T(1,128)}, u32[]{:S(2)}) copy-start(s32[4,1,384]{2,1,0:T(1,128)} %broadcast_in_dim.197.back_ref) | copy-start | bytes 18436
  156.2 14.6 %collective-permute-start.10 = (bf16[384,512]{1,0:T(8,128)(2,1)S(1)}, bf16[384,512]{1,0:T(8,128)(2,1)S(1)}, u32[]{:S(2)}, u32[]{:S(2)}) collective-permute-start(bf16[384,512]{1,0:T(8,128)(2,1)S(1)} %get-tuple-element.46), channel_id=1, source_target_pairs={{0,16},{8,24},{16,0},{24,8},{1,17},{9,25},{17,1},{25,9},{2,18},{10... | collective-permute-start | bytes 1179656 | tf_op jit(solution)/shard_map/ppermute | solution.py:417
  156.8 14.0 %collective-permute-start.9 = (bf16[384,512]{1,0:T(8,128)(2,1)S(1)}, bf16[384,512]{1,0:T(8,128)(2,1)S(1)}, u32[]{:S(2)}, u32[]{:S(2)}) collective-permute-start(bf16[384,512]{1,0:T(8,128)(2,1)S(1)} %get-tuple-element.47), channel_id=1, source_target_pairs={{0,8},{8,0},{16,24},{24,16},{1,9},{9,1},{17,25},{25,17},{2,10},{10... | collective-permute-start | bytes 1179656 | tf_op jit(solution)/shard_map/ppermute | solution.py:417
  163.8 52.8 %slice-start = ((s8[6291456]{0:T(1024)(128)(4,1)}), s8[4194304]{0:T(1024)(128)(4,1)S(1)}, s32[]{:S(2)}) async-start(s8[6291456]{0:T(1024)(128)(4,1)} %bitcast.50), calls=%async_computation.4 | async-start | bytes 8388608
  170.8 45.8 %slice-start.1 = ((s8[6291456]{0:T(1024)(128)(4,1)}), s8[2097152]{0:T(1024)(128)(4,1)S(1)}, s32[]{:S(2)}) async-start(s8[6291456]{0:T(1024)(128)(4,1)} %bitcast.50), calls=%async_computation.5 | async-start | bytes 4194304
  229.6 40.9 %copy-start.11 = (bf16[2,512,512]{2,1,0:T(8,128)(2,1)S(1)}, bf16[2,512,512]{2,1,0:T(8,128)(2,1)}, u32[]{:S(2)}) copy-start(bf16[2,512,512]{2,1,0:T(8,128)(2,1)} %we.5) | copy-start | bytes 3145732
  229.6 40.9 %copy-start.13 = (bf16[2,512,512]{2,1,0:T(8,128)(2,1)S(1)}, bf16[2,512,512]{2,1,0:T(8,128)(2,1)}, u32[]{:S(2)}) copy-start(bf16[2,512,512]{2,1,0:T(8,128)(2,1)} %wd.5) | copy-start | bytes 3145732
  (6 other events, 12.7 us)

commit v5 on v4

--- a/solution.py
+++ b/solution.py
@@ -302,7 +302,7 @@
     )(where, current, back_rows, rank_rows, *weights[:5], *received, *targets)
 
 
-def run_back(second, packed, where, to, start, rank_rows, weights, section, total):
+def run_back(second, packed, where, to, start, rank_rows, weights, at, total):
     _, rows, features = second.shape
     count = where.shape[0]
     narrow = packed.shape[1]
@@ -316,14 +316,14 @@
                 pl.BlockSpec((1, narrow, rows // 2, LANES), lambda i, where, to: (where[i], 0, 0, 0)),
                 pl.BlockSpec((1, 1, rows), lambda i, *_: (start + i, 0, 0)),
             ]
-            + [weight_spec(section, features)] * 3,
+            + [weight_spec(index, features) for index in at],
             out_specs=pl.BlockSpec((1, rows, features), lambda i, where, to: (to[i], 0, 0)),
         ),
         out_shape=jax.ShapeDtypeStruct((total, rows, features), jnp.bfloat16),
         compiler_params=params(),
         cost_estimate=cost(8 * count * rows * features**2, 6 * count * rows * features),
         name="back",
-    )(where, to, second, packed, rank_rows, *weights[5:])
+    )(where, to, second, packed, rank_rows, *weights)
 
 
 def rank_spec(entries):
@@ -467,10 +467,11 @@
     halves = [(0, half), (half, wide - half)]
 
     blocks_of = messages.reshape(wide, rows, features)
-    received = {
-        offset: shift(lax.dynamic_index_in_dim(blocks_of, group_id ^ offset, 0, False), offset, wide)
-        for offset in offsets[1:]
-    }
+    sent = [
+        lax.dynamic_index_in_dim(blocks_of, group_id ^ offset, 0, False) for offset in offsets[1:]
+    ]
+    *sent, atom_slots = lax.optimization_barrier((*sent, atom_slots))
+    received = {offset: shift(part, offset, wide) for offset, part in zip(offsets[1:], sent)}
     listed = atom_slots.reshape(atoms // GROUP, GROUP, wide, SLOTS // wide)
     listed = reorder(jnp.transpose(listed, (2, 0, 3, 1)).reshape(wide, rows), order)
     rank = reorder(ranks(route_slot.reshape(wide, rows)), order)
@@ -484,10 +485,10 @@
         for start, count in halves if section else pieces:
             array, where = current[start]
             needed = [received[offset] for offset in offsets[start : start + count] if offset]
-            targets = run_front(
+            targets = list(run_front(
                 array, where, needed, start == 0, start, wide,
                 back_rows[:, None, :], rank[:, None, :], weights, section, targets,
-            )
+            ))
         second, packed = targets
         if tables is None:
             entries, all_angles, owner_places, packed = share_lists(listed, angles, packed)
@@ -500,16 +501,20 @@
             hits = back_rows[:, :, None] == jnp.arange(rows, dtype=jnp.int32)
             turned_rank = jnp.sum(jnp.where(hits, partner_rank[:, None, :], 0), axis=2)[:, None, :]
         mixed = run_mix(owner_of, place_of, order, swap(packed), *tables)
+        late, at = weights[5:], [section] * 3
+        if not last:
+            mixed, *late = lax.optimization_barrier((mixed, *late))
+            late, at = [jnp.stack([weight[section] for weight in late])] * 3, range(3)
         mixed = mixed.reshape(wide * narrow, rows // 2, LANES)
         returned = lax.all_to_all(mixed, ("wide", "narrow"), 0, 0, tiled=True)
         returned = returned.reshape(wide, narrow, rows // 2, LANES)
         if last:
-            current = run_back(second, returned, order, order, 0, turned_rank, weights, section, wide)
+            current = run_back(second, returned, order, order, 0, turned_rank, late, at, wide)
             return current.reshape(edge_rows, features)
         for start, count in halves:
             plain = jnp.arange(count, dtype=jnp.int32)
             where = order[start : start + count]
-            result = run_back(second, returned, where, plain, start, turned_rank, weights, section, count)
+            result = run_back(second, returned, where, plain, start, turned_rank, late, at, count)
             current[start] = (result, plain)
             for index, offset in enumerate(offsets[start : start + count]):
                 if offset:

time: 281 us -> 277 us (0.986)
  no operation moved by 1% of the time
where the time goes in v5:
time: 277 us; the launch traced here: 276 us
  blocking collectives  81.1 us (29%)
  Pallas kernels  81 us (29%)
  waiting for transfers between devices  72.5 us (26%)
  starting transfers between devices  23.4 us (8%)
  local copies, waits for them, and re-layouts  14.5 us (5%)
  other arithmetic  3.23 us (1%)
    all_to_all x1, blocking collectives, tiled_local(): returned = lax.all_to_all(mixed, ('wide', 'narrow'), 0, 0, tiled=True)  40.9 us
    all_to_all x1, blocking collectives, swap(): return lax.all_to_all(values, 'narrow', 0, 0, tiled=True)  40.3 us
    pallas_call x4, Pallas kernels, run_front(): pl.pallas_call(functools.partial(front_kernel, own, count), grid_spec=plt...  27.7 us
    pallas_call x2, Pallas kernels, run_mix(): pl.pallas_call(mix_kernel, grid=(devices,), in_specs=[smem, smem, smem, w...  27.2 us
    all_to_all x1, waiting for transfers between devices, tiled_local(): returned = lax.all_to_all(mixed, ('wide', 'narrow'), 0, 0, tiled=True)  26.1 us
    all_to_all x1, waiting for transfers between devices, swap(): return lax.all_to_all(values, 'narrow', 0, 0, tiled=True)  25 us
    pallas_call x3, Pallas kernels, run_back(): pl.pallas_call(back_kernel, grid_spec=pltpu.PrefetchScalarGridSpec(num_sc...  19.1 us
    ppermute x9, waiting for transfers between devices, shift(): return lax.ppermute(values, 'wide', [(i, i ^ offset) for i in range(wide)])  16.4 us
  transfers between devices with their start and end apart: 14, of which 9 were waited for; matrix products, arithmetic and copies ran while one was open for 2% of the time, Pallas kernels for 8%

profile of v5, /device:TPU:0, one launch (start us, length us, event | category | flops | bytes accessed | tf_op | source)
XLA Modules:
  0.0 276.1 jit_solution(3302717073578847728)
XLA Ops:
  2.5 1.3 dynamic-slice_bitcast_fusion
  4.5 4.1 %collective-permute-start.3 = (bf16[1,48,1088]{2,1,0:T(8,128)(2,1)S(1)}, bf16[1,48,1088]{2,1,0:T(8,128)(2,1)S(1)}, u32[]{:S(2)}, u32[]{:S(2)}) collective-permute-start(bf16[1,48,1088]{2,1,0:T(8,128)(2,1)S(1)} %maximum_bitcast_fusion), channel_id=1, source_target_pairs={{0,4},{1,5},{2,6},{3,7},{4,0},{5,1},{6,2},{7,3},{8,12},{9,13},{10,... | collective-permute-start | bytes 313352 | tf_op jit(solution)/shard_map/ppermute | solution.py:437
  8.6 2.4 collective-permute-start
  13.3 5.4 %front.4 = (bf16[4,384,512]{2,1,0:T(8,128)(2,1)}, bf16[8,4,192,128]{3,2,1,0:T(8,128)(2,1)}) custom-call(s32[1]{0:T(128)} %bitcast.56, bf16[4,384,512]{2,1,0:T(8,128)(2,1)} %bitcast.58, s32[4,1,384]{2,1,0:T(1,128)} %broadcast_in_dim.197.back_ref, s32[4,1,384]{2,1,0:T(1,128)} %broadcast_in_dim.199.rank_ref, bf16[2,512,512]{2,1,0:T(8,128)(2,1)} %wm.7, ...), custom_call_target="tpu_custom_call" | custom-call | flops 1207959552 | bytes 1572864 | tf_op jit(solution)/shard_map/front/pallas_call | solution.py:275
  18.8 1.6 collective-permute-start.4
  21.2 3.6 %collective-permute-done.4 = bf16[2,48,1088]{2,1,0:T(8,128)(2,1)S(1)} collective-permute-done((bf16[2,48,1088]{2,1,0:T(8,128)(2,1)S(1)}, bf16[2,48,1088]{2,1,0:T(8,128)(2,1)S(1)}, u32[]{:S(2)}, u32[]{:S(2)}) %collective-permute-start.4) | collective-permute-done | bytes 208928 | tf_op jit(solution)/shard_map/ppermute | solution.py:437
  25.0 3.6 %collective-permute-done.1.refs_1_ = bf16[384,512]{1,0:T(8,128)(2,1)S(1)} collective-permute-done((bf16[384,512]{1,0:T(8,128)(2,1)S(1)}, bf16[384,512]{1,0:T(8,128)(2,1)S(1)}, u32[]{:S(2)}, u32[]{:S(2)}) %collective-permute-start.1) | collective-permute-done | bytes 393248 | tf_op jit(solution)/shard_map/ppermute | solution.py:417
  29.4 11.2 %front.5 = (bf16[4,384,512]{2,1,0:T(8,128)(2,1)}, bf16[8,4,192,128]{3,2,1,0:T(8,128)(2,1)}) custom-call(s32[3]{0:T(128)} %slice.52.where_ref, bf16[4,384,512]{2,1,0:T(8,128)(2,1)} %bitcast.59, s32[4,1,384]{2,1,0:T(1,128)} %broadcast_in_dim.197.back_ref, s32[4,1,384]{2,1,0:T(1,128)} %broadcast_in_dim.199.rank_ref, ...), custom_call_target="tpu_custom_call", output_to_operand_aliasing={{0}: (12, {}), {1}: (13, {})} | custom-call | flops 3623878656 | bytes 4718592 | tf_op jit(solution)/shard_map/front/pallas_call | solution.py:275
  40.5 3.6 %all-to-all-start = ((bf16[8,4,192,128]{3,2,1,0:T(8,128)(2,1)}), bf16[8,4,192,128]{3,2,1,0:T(8,128)(2,1)S(1)}, u32[]{:S(2)}, u32[]{:S(2)}) async-start(bf16[8,4,192,128]{3,2,1,0:T(8,128)(2,1)} %get-tuple-element.37), calls=%async_computation | async-start | bytes 3145728 | tf_op jit(solution)/shard_map/all_to_all | solution.py:421
  44.9 1.3 collective-permute-done.5
  46.7 7.0 %tables.1 = (s32[8,4,1,384]{3,2,1,0:T(1,128)S(1)}, bf16[8,6,256,256]{3,2,1,0:T(8,128)(2,1)S(1)}) custom-call(s32[8]{0:T(128)S(1)} %select_reduce_fusion.9.places_ref, s32[4]{0:T(128)S(1)} %copy-done.15, s32[4]{0:T(128)S(1)} %select_reduce_fusion.10.position_ref, s32[8,4,1,384]{3,2,1,0:T(1,128)S(1)} %broadcast_in_dim_reshape.2.entry_ref, ...), custom_call_target="tpu_custom_call" | custom-call | bytes 25165824 | tf_op jit(solution)/shard_map/tables/pallas_call | solution.py:338
  53.7 2.6 copy-done
  56.8 25.0 %all-to-all-done.recv_ref = bf16[8,4,192,128]{3,2,1,0:T(8,128)(2,1)S(1)} async-done(((bf16[8,4,192,128]{3,2,1,0:T(8,128)(2,1)}), bf16[8,4,192,128]{3,2,1,0:T(8,128)(2,1)S(1)}, u32[]{:S(2)}, u32[]{:S(2)}) %all-to-all-start) | async-done | bytes 1572896 | tf_op jit(solution)/shard_map/all_to_all | solution.py:421
  81.9 2.8 %copy-done.1 = bf16[8,6,256,256]{3,2,1,0:T(8,128)(2,1)S(1)} copy-done((bf16[8,6,256,256]{3,2,1,0:T(8,128)(2,1)S(1)}, bf16[8,6,256,256]{3,2,1,0:T(8,128)(2,1)}, u32[]{:S(2)}) %copy-start.1) | copy-done | bytes 6291480
  84.7 14.2 %mix.2 = bf16[4,8,192,128]{3,2,1,0:T(8,128)(2,1)} custom-call(s32[8,8]{1,0:T(8,128)S(1)} %get-tuple-element.50.owner_ref, s32[8,8]{1,0:T(8,128)S(1)} %get-tuple-element.49.place_ref, s32[4]{0:T(128)S(1)} %copy-done.15, bf16[8,4,192,128]{3,2,1,0:T(8,128)(2,1)S(1)} %all-to-all-done.recv_ref, s32[8,4,1,384]{3,2,1,0:T(1,128)S(1)} %get-tuple-element.38.rank_ref, ...), custom_call_target="tpu_custom_call" | custom-call | flops 1509949440 | bytes 18874368 | tf_op jit(solution)/shard_map/mix/pallas_call | solution.py:368
  98.8 2.9 %all-to-all-start.1 = ((bf16[32,192,128]{2,1,0:T(8,128)(2,1)}), bf16[32,192,128]{2,1,0:T(8,128)(2,1)S(1)}, u32[]{:S(2)}, u32[]{:S(2)}) async-start(bf16[32,192,128]{2,1,0:T(8,128)(2,1)} %bitcast.7), calls=%async_computation.1 | async-start | bytes 3145728 | tf_op jit(solution)/shard_map/all_to_all | solution.py:509
  101.8 2.6 collective-permute-start.6
  105.4 6.6 %collective-permute-done.6 = s32[384]{0:T(512)S(1)} collective-permute-done((s32[384]{0:T(512)S(1)}, s32[384]{0:T(512)S(1)}, u32[]{:S(2)}, u32[]{:S(2)}) %collective-permute-start.6) | collective-permute-done | bytes 1568 | tf_op jit(solution)/shard_map/ppermute | solution.py:417
  112.8 1.0 slice-done.2
  114.3 26.1 %all-to-all-done.1 = bf16[32,192,128]{2,1,0:T(8,128)(2,1)S(1)} async-done(((bf16[32,192,128]{2,1,0:T(8,128)(2,1)}), bf16[32,192,128]{2,1,0:T(8,128)(2,1)S(1)}, u32[]{:S(2)}, u32[]{:S(2)}) %all-to-all-start.1) | async-done | bytes 1572896 | tf_op jit(solution)/shard_map/all_to_all | solution.py:509
  140.5 1.4 copy-done.2
  141.9 4.7 %back.4.cur_ref = bf16[2,384,512]{2,1,0:T(8,128)(2,1)S(1)} custom-call(s32[2]{0:T(128)S(1)} %get-tuple-element.69.from_ref, s32[2]{0:T(128)S(1)} %iota.79.to_ref, bf16[4,384,512]{2,1,0:T(8,128)(2,1)S(1)} %copy-done.2, bf16[4,8,192,128]{3,2,1,0:T(8,128)(2,1)S(1)} %bitcast.52, s32[4,1,384]{2,1,0:T(1,128)S(1)} %broadcast_in_dim.218.rank_ref, ...), custom_call_target="tpu_custom_call" | custom-call | flops 1610612736 | bytes 2359296 | tf_op jit(solution)/shard_map/back/pallas_call | solution.py:309
  147.3 4.7 %back.3.cur_ref = bf16[2,384,512]{2,1,0:T(8,128)(2,1)S(1)} custom-call(s32[2]{0:T(128)S(1)} %get-tuple-element.70.from_ref, s32[2]{0:T(128)S(1)} %iota.75.to_ref, bf16[4,384,512]{2,1,0:T(8,128)(2,1)S(1)} %copy-done.3, bf16[4,8,192,128]{3,2,1,0:T(8,128)(2,1)S(1)} %bitcast.53, s32[4,1,384]{2,1,0:T(1,128)S(1)} %broadcast_in_dim.218.rank_ref, ...), custom_call_target="tpu_custom_call" | custom-call | flops 1610612736 | bytes 2359296 | tf_op jit(solution)/shard_map/back/pallas_call | solution.py:309
  152.7 2.4 collective-permute-start.9
  155.1 4.6 %collective-permute-done.11.refs_0_ = bf16[384,512]{1,0:T(8,128)(2,1)S(1)} collective-permute-done((bf16[384,512]{1,0:T(8,128)(2,1)S(1)}, bf16[384,512]{1,0:T(8,128)(2,1)S(1)}, u32[]{:S(2)}, u32[]{:S(2)}) %collective-permute-start.11) | collective-permute-done | bytes 393248 | tf_op jit(solution)/shard_map/ppermute | solution.py:417
  159.7 5.6 %front.6 = (bf16[4,384,512]{2,1,0:T(8,128)(2,1)S(1)}, bf16[8,4,192,128]{3,2,1,0:T(8,128)(2,1)S(1)}) custom-call(s32[2]{0:T(128)S(1)} %iota.78.where_ref, bf16[2,384,512]{2,1,0:T(8,128)(2,1)S(1)} %back.4.cur_ref, s32[4,1,384]{2,1,0:T(1,128)S(1)} %copy-done.13, s32[4,1,384]{2,1,0:T(1,128)S(1)} %copy-done.12, bf16[2,512,512]{2,1,0:T(8,128)(2,1)S(1)} %copy-done.4, ...), custom_call_target="tpu_custom_call" | custom-call | flops 2415919104 | bytes 3145728 | tf_op jit(solution)/shard_map/front/pallas_call | solution.py:275
  165.3 1.4 collective-permute-done.10.refs_1_
  166.7 5.6 %front.7 = (bf16[4,384,512]{2,1,0:T(8,128)(2,1)S(1)}, bf16[8,4,192,128]{3,2,1,0:T(8,128)(2,1)S(1)}) custom-call(s32[2]{0:T(128)S(1)} %iota.74.where_ref, bf16[2,384,512]{2,1,0:T(8,128)(2,1)S(1)} %back.3.cur_ref, s32[4,1,384]{2,1,0:T(1,128)S(1)} %copy-done.13, s32[4,1,384]{2,1,0:T(1,128)S(1)} %copy-done.12, ...), custom_call_target="tpu_custom_call", output_to_operand_aliasing={{0}: (11, {}), {1}: (12, {})} | custom-call | flops 2415919104 | bytes 3145728 | tf_op jit(solution)/shard_map/front/pallas_call | solution.py:275
  172.3 40.3 %all_to_all.20.recv_ref = bf16[8,4,192,128]{3,2,1,0:T(8,128)(2,1)S(1)} all-to-all(bf16[8,4,192,128]{3,2,1,0:T(8,128)(2,1)S(1)} %get-tuple-element.48), channel_id=1, replica_groups=mesh['wide'=4,'narrow'=8] {'narrow'}, dimensions={0} | all-to-all | bytes 3145728 | tf_op jit(solution)/shard_map/all_to_all | solution.py:421
  212.5 13.0 %mix.3 = bf16[4,8,192,128]{3,2,1,0:T(8,128)(2,1)S(1)} custom-call(s32[8,8]{1,0:T(8,128)S(1)} %get-tuple-element.50.owner_ref, s32[8,8]{1,0:T(8,128)S(1)} %get-tuple-element.49.place_ref, s32[4]{0:T(128)S(1)} %copy-done.15, bf16[8,4,192,128]{3,2,1,0:T(8,128)(2,1)S(1)} %all_to_all.20.recv_ref, s32[8,4,1,384]{3,2,1,0:T(1,128)S(1)} %get-tuple-element.38.rank_ref, ...), custom_call_target="tpu_custom_call" | custom-call | flops 1509949440 | bytes 18874368 | tf_op jit(solution)/shard_map/mix/pallas_call | solution.py:368
  225.6 40.9 %all_to_all.21 = bf16[32,192,128]{2,1,0:T(8,128)(2,1)S(1)} all-to-all(bf16[32,192,128]{2,1,0:T(8,128)(2,1)S(1)} %bitcast.54), channel_id=1, replica_groups=mesh['wide'=4,'narrow'=8] {'wide','narrow'}, dimensions={0} | all-to-all | bytes 3145728 | tf_op jit(solution)/shard_map/all_to_all | solution.py:509
  266.5 9.7 %back.5 = bf16[4,384,512]{2,1,0:T(8,128)(2,1)} custom-call(s32[4]{0:T(128)S(1)} %copy-done.15, s32[4]{0:T(128)S(1)} %copy-done.15, bf16[4,384,512]{2,1,0:T(8,128)(2,1)S(1)} %get-tuple-element.47.second_ref, bf16[4,8,192,128]{3,2,1,0:T(8,128)(2,1)S(1)} %bitcast.55, s32[4,1,384]{2,1,0:T(1,128)S(1)} %broadcast_in_dim.218.rank_ref, ...), custom_call_target="tpu_custom_call" | custom-call | flops 3221225472 | bytes 4718592 | tf_op jit(solution)/shard_map/back/pallas_call | solution.py:309
  (117 shorter events, 12.5 us)
Async XLA Ops:
  0.0 3.8 %copy-start.17 = (s32[1536]{0:T(1024)S(1)}, s32[1536]{0:T(1024)}, u32[]{:S(2)}) copy-start(s32[1536]{0:T(1024)} %param.19) | copy-start | bytes 18436
  0.0 4.5 %copy-start.16 = (bf16[48,1024]{1,0:T(8,128)(2,1)S(1)}, bf16[48,1024]{1,0:T(8,128)(2,1)}, u32[]{:S(2)}) copy-start(bf16[48,1024]{1,0:T(8,128)(2,1)} %param.20) | copy-start | bytes 294916
  0.7 11.4 %copy-start.14 = (s32[4]{0:T(128)}, s32[4]{0:T(128)S(1)}, u32[]{:S(2)}) copy-start(s32[4]{0:T(128)S(1)} %broadcast_xor_fusion.order_ref.from_ref.to_ref) | copy-start | bytes 52
  4.5 14.2 %collective-permute-start.3 = (bf16[1,48,1088]{2,1,0:T(8,128)(2,1)S(1)}, bf16[1,48,1088]{2,1,0:T(8,128)(2,1)S(1)}, u32[]{:S(2)}, u32[]{:S(2)}) collective-permute-start(bf16[1,48,1088]{2,1,0:T(8,128)(2,1)S(1)} %maximum_bitcast_fusion), channel_id=1, source_target_pairs={{0,4},{1,5},{2,6},{3,7},{4,0},{5,1},{6,2},{7,3},{8,12},{9,13},{10,... | collective-permute-start | bytes 313352 | tf_op jit(solution)/shard_map/ppermute | solution.py:437
  8.6 16.3 %collective-permute-start = (bf16[384,512]{1,0:T(8,128)(2,1)S(1)}, bf16[384,512]{1,0:T(8,128)(2,1)S(1)}, u32[]{:S(2)}, u32[]{:S(2)}) collective-permute-start(bf16[384,512]{1,0:T(8,128)(2,1)S(1)} %get-tuple-element.27), channel_id=1, source_target_pairs={{0,24},{8,16},{16,8},{24,0},{1,25},{9,17},{17,9},{25,1},{2,26},{10... | collective-permute-start | bytes 1179656 | tf_op jit(solution)/shard_map/ppermute | solution.py:417
  11.0 17.6 %collective-permute-start.1 = (bf16[384,512]{1,0:T(8,128)(2,1)S(1)}, bf16[384,512]{1,0:T(8,128)(2,1)S(1)}, u32[]{:S(2)}, u32[]{:S(2)}) collective-permute-start(bf16[384,512]{1,0:T(8,128)(2,1)S(1)} %get-tuple-element.28), channel_id=1, source_target_pairs={{0,8},{8,0},{16,24},{24,16},{1,9},{9,1},{17,25},{25,17},{2,10},{10... | collective-permute-start | bytes 1179656 | tf_op jit(solution)/shard_map/ppermute | solution.py:417
  11.6 17.0 %collective-permute-start.2 = (bf16[384,512]{1,0:T(8,128)(2,1)S(1)}, bf16[384,512]{1,0:T(8,128)(2,1)}, u32[]{:S(2)}, u32[]{:S(2)}) collective-permute-start(bf16[384,512]{1,0:T(8,128)(2,1)S(1)} %get-tuple-element.29), channel_id=1, source_target_pairs={{0,16},{8,24},{16,0},{24,8},{1,17},{9,25},{17,1},{25,9},{2,18},{10... | collective-permute-start | bytes 1179656 | tf_op jit(solution)/shard_map/ppermute | solution.py:417
  13.3 7.1 %copy-start.15 = (s32[4]{0:T(128)S(1)}, s32[4]{0:T(128)}, u32[]{:S(2)}) copy-start(s32[4]{0:T(128)} %copy-done.14) | copy-start | bytes 52
  13.3 7.8 %copy-start.21 = (s32[8]{0:T(128)S(1)}, s32[8]{0:T(128)}, u32[]{:S(2)}) copy-start(s32[8]{0:T(128)} %constant.76.clone) | copy-start | bytes 100
  18.8 6.1 %collective-permute-start.4 = (bf16[2,48,1088]{2,1,0:T(8,128)(2,1)S(1)}, bf16[2,48,1088]{2,1,0:T(8,128)(2,1)S(1)}, u32[]{:S(2)}, u32[]{:S(2)}) collective-permute-start(bf16[2,48,1088]{2,1,0:T(8,128)(2,1)S(1)} %pad_maximum_fusion.2), channel_id=1, source_target_pairs={{0,2},{1,3},{2,0},{3,1},{4,6},{5,7},{6,4},{7,5},{8,10},{9,11},{10,... | collective-permute-start | bytes 626696 | tf_op jit(solution)/shard_map/ppermute | solution.py:437
  40.5 41.3 %all-to-all-start = ((bf16[8,4,192,128]{3,2,1,0:T(8,128)(2,1)}), bf16[8,4,192,128]{3,2,1,0:T(8,128)(2,1)S(1)}, u32[]{:S(2)}, u32[]{:S(2)}) async-start(bf16[8,4,192,128]{3,2,1,0:T(8,128)(2,1)} %get-tuple-element.37), calls=%async_computation | async-start | bytes 3145728 | tf_op jit(solution)/shard_map/all_to_all | solution.py:421
  44.3 1.9 collective-permute-start.5
  98.8 41.6 %all-to-all-start.1 = ((bf16[32,192,128]{2,1,0:T(8,128)(2,1)}), bf16[32,192,128]{2,1,0:T(8,128)(2,1)S(1)}, u32[]{:S(2)}, u32[]{:S(2)}) async-start(bf16[32,192,128]{2,1,0:T(8,128)(2,1)} %bitcast.7), calls=%async_computation.1 | async-start | bytes 3145728 | tf_op jit(solution)/shard_map/all_to_all | solution.py:509
  101.8 10.2 %collective-permute-start.6 = (s32[384]{0:T(512)S(1)}, s32[384]{0:T(512)S(1)}, u32[]{:S(2)}, u32[]{:S(2)}) collective-permute-start(s32[384]{0:T(512)S(1)} %get-tuple-element.51), channel_id=1, source_target_pairs={{0,24},{8,16},{16,8},{24,0},{1,25},{9,17},{17,9},{25,1},{2,26},{10... | collective-permute-start | bytes 4616 | tf_op jit(solution)/shard_map/ppermute | solution.py:417
  104.4 7.6 %collective-permute-start.8 = (s32[384]{0:T(512)S(1)}, s32[384]{0:T(512)S(1)}, u32[]{:S(2)}, u32[]{:S(2)}) collective-permute-start(s32[384]{0:T(512)S(1)} %get-tuple-element.52), channel_id=1, source_target_pairs={{0,16},{8,24},{16,0},{24,8},{1,17},{9,25},{17,1},{25,9},{2,18},{10... | collective-permute-start | bytes 4616 | tf_op jit(solution)/shard_map/ppermute | solution.py:417
  104.9 7.3 %collective-permute-start.7 = (s32[384]{0:T(512)S(1)}, s32[384]{0:T(512)S(1)}, u32[]{:S(2)}, u32[]{:S(2)}) collective-permute-start(s32[384]{0:T(512)S(1)} %get-tuple-element.53), channel_id=1, source_target_pairs={{0,8},{8,0},{16,24},{24,16},{1,9},{9,1},{17,25},{25,17},{2,10},{10... | collective-permute-start | bytes 4616 | tf_op jit(solution)/shard_map/ppermute | solution.py:417
  141.9 5.4 %copy-start.3 = (bf16[4,384,512]{2,1,0:T(8,128)(2,1)S(1)}, bf16[4,384,512]{2,1,0:T(8,128)(2,1)}, u32[]{:S(2)}) copy-start(bf16[4,384,512]{2,1,0:T(8,128)(2,1)} %get-tuple-element.32.second_ref) | copy-start | bytes 4718596
  146.6 13.0 %collective-permute-start.11 = (bf16[384,512]{1,0:T(8,128)(2,1)S(1)}, bf16[384,512]{1,0:T(8,128)(2,1)S(1)}, u32[]{:S(2)}, u32[]{:S(2)}) collective-permute-start(bf16[384,512]{1,0:T(8,128)(2,1)S(1)} %slice_bitcast_fusion), channel_id=1, source_target_pairs={{0,24},{8,16},{16,8},{24,0},{1,25},{9,17},{17,9},{25,1},{2,26},{10... | collective-permute-start | bytes 1179656 | tf_op jit(solution)/shard_map/ppermute | solution.py:417
  147.2 12.4 %copy-start.5 = (bf16[2,512,512]{2,1,0:T(8,128)(2,1)S(1)}, bf16[2,512,512]{2,1,0:T(8,128)(2,1)}, u32[]{:S(2)}) copy-start(bf16[2,512,512]{2,1,0:T(8,128)(2,1)} %wr.7) | copy-start | bytes 3145732
  147.2 12.4 %copy-start.6 = (bf16[2,512,512]{2,1,0:T(8,128)(2,1)S(1)}, bf16[2,512,512]{2,1,0:T(8,128)(2,1)}, u32[]{:S(2)}) copy-start(bf16[2,512,512]{2,1,0:T(8,128)(2,1)} %wc.7) | copy-start | bytes 3145732
  147.3 12.4 %copy-start.7 = (bf16[2,512,512]{2,1,0:T(8,128)(2,1)S(1)}, bf16[2,512,512]{2,1,0:T(8,128)(2,1)}, u32[]{:S(2)}) copy-start(bf16[2,512,512]{2,1,0:T(8,128)(2,1)} %wi.7) | copy-start | bytes 3145732
  147.3 12.4 %copy-start.8 = (bf16[2,512,512]{2,1,0:T(8,128)(2,1)S(1)}, bf16[2,512,512]{2,1,0:T(8,128)(2,1)}, u32[]{:S(2)}) copy-start(bf16[2,512,512]{2,1,0:T(8,128)(2,1)} %wo.7) | copy-start | bytes 3145732
  152.0 7.7 %copy-start.4 = (bf16[2,512,512]{2,1,0:T(8,128)(2,1)S(1)}, bf16[2,512,512]{2,1,0:T(8,128)(2,1)}, u32[]{:S(2)}) copy-start(bf16[2,512,512]{2,1,0:T(8,128)(2,1)} %wm.7) | copy-start | bytes 3145732
  152.0 7.7 %copy-start.12 = (s32[4,1,384]{2,1,0:T(1,128)S(1)}, s32[4,1,384]{2,1,0:T(1,128)}, u32[]{:S(2)}) copy-start(s32[4,1,384]{2,1,0:T(1,128)} %broadcast_in_dim.199.rank_ref) | copy-start | bytes 18436
  152.0 7.7 %copy-start.13 = (s32[4,1,384]{2,1,0:T(1,128)S(1)}, s32[4,1,384]{2,1,0:T(1,128)}, u32[]{:S(2)}) copy-start(s32[4,1,384]{2,1,0:T(1,128)} %broadcast_in_dim.197.back_ref) | copy-start | bytes 18436
  152.1 14.6 %collective-permute-start.10 = (bf16[384,512]{1,0:T(8,128)(2,1)S(1)}, bf16[384,512]{1,0:T(8,128)(2,1)S(1)}, u32[]{:S(2)}, u32[]{:S(2)}) collective-permute-start(bf16[384,512]{1,0:T(8,128)(2,1)S(1)} %get-tuple-element.62), channel_id=1, source_target_pairs={{0,16},{8,24},{16,0},{24,8},{1,17},{9,25},{17,1},{25,9},{2,18},{10... | collective-permute-start | bytes 1179656 | tf_op jit(solution)/shard_map/ppermute | solution.py:417
  152.7 14.0 %collective-permute-start.9 = (bf16[384,512]{1,0:T(8,128)(2,1)S(1)}, bf16[384,512]{1,0:T(8,128)(2,1)S(1)}, u32[]{:S(2)}, u32[]{:S(2)}) collective-permute-start(bf16[384,512]{1,0:T(8,128)(2,1)S(1)} %get-tuple-element.63), channel_id=1, source_target_pairs={{0,8},{8,0},{16,24},{24,16},{1,9},{9,1},{17,25},{25,17},{2,10},{10... | collective-permute-start | bytes 1179656 | tf_op jit(solution)/shard_map/ppermute | solution.py:417
  159.7 52.8 %slice-start = ((s8[6291456]{0:T(1024)(128)(4,1)}), s8[4194304]{0:T(1024)(128)(4,1)S(1)}, s32[]{:S(2)}) async-start(s8[6291456]{0:T(1024)(128)(4,1)} %bitcast.50), calls=%async_computation.4 | async-start | bytes 8388608
  166.7 45.8 %slice-start.1 = ((s8[6291456]{0:T(1024)(128)(4,1)}), s8[2097152]{0:T(1024)(128)(4,1)S(1)}, s32[]{:S(2)}) async-start(s8[6291456]{0:T(1024)(128)(4,1)} %bitcast.50), calls=%async_computation.5 | async-start | bytes 4194304
  225.6 40.9 %copy-start.9 = (bf16[2,512,512]{2,1,0:T(8,128)(2,1)S(1)}, bf16[2,512,512]{2,1,0:T(8,128)(2,1)}, u32[]{:S(2)}) copy-start(bf16[2,512,512]{2,1,0:T(8,128)(2,1)} %wd.1) | copy-start | bytes 3145732
  225.6 40.9 %copy-start.10 = (bf16[2,512,512]{2,1,0:T(8,128)(2,1)S(1)}, bf16[2,512,512]{2,1,0:T(8,128)(2,1)}, u32[]{:S(2)}) copy-start(bf16[2,512,512]{2,1,0:T(8,128)(2,1)} %we.1) | copy-start | bytes 3145732
  225.6 40.9 %copy-start.11 = (bf16[2,512,512]{2,1,0:T(8,128)(2,1)S(1)}, bf16[2,512,512]{2,1,0:T(8,128)(2,1)}, u32[]{:S(2)}) copy-start(bf16[2,512,512]{2,1,0:T(8,128)(2,1)} %wl.1) | copy-start | bytes 3145732
  (9 other events, 18.4 us)

commit v6 on v5

--- a/solution.py
+++ b/solution.py
@@ -106,6 +106,11 @@
     return jnp.where(mask, 1.0, 0.0).astype(jnp.bfloat16)
 
 
+def row_parts(rows):
+    half = rows // 2
+    return [slice(0, half), slice(half, rows)]
+
+
 def front_kernel(own, count, where_ref, cur_ref, back_ref, rank_ref, wm, wr, wc, wi, wo, *refs):
     recv_refs, (second_ref, packed_ref, reverse_ref) = refs[: count - own], refs[-3:]
     rows_iota, lanes_iota = iotas(cur_ref.shape[1])
@@ -118,12 +123,15 @@
         def _():
             reverse_ref[...] = dot(hot, sources[index][...]).astype(jnp.bfloat16)
 
-    current = cur_ref[0]
-    hidden = silu(dot(current, wm[0]) + dot(reverse_ref[...], wr[0])).astype(jnp.bfloat16)
-    first_res = halve(current, dot(hidden, wc[0]))
-    inner = silu(dot(first_res, wi[0])).astype(jnp.bfloat16)
-    second = halve(first_res, silu(dot(inner, wo[0])))
-    second_ref[0] = second
+    parts = row_parts(cur_ref.shape[1])
+    current = [cur_ref[0, part, :] for part in parts]
+    sums = [dot(rows, wm[0]) + dot(reverse_ref[part, :], wr[0]) for rows, part in zip(current, parts)]
+    hidden = [silu(rows).astype(jnp.bfloat16) for rows in sums]
+    first_res = [halve(rows, dot(left, wc[0])) for rows, left in zip(current, hidden)]
+    inner = [silu(dot(rows, wi[0])).astype(jnp.bfloat16) for rows in first_res]
+    for rows, left, part in zip(first_res, inner, parts):
+        second_ref[0, part, :] = halve(rows, silu(dot(left, wo[0])))
+    second = second_ref[0]
     ordered = dot(one_hot(rows_iota == rank_ref[0]), second)
     half = ordered.shape[0] // 2
     low = lax.broadcasted_iota(jnp.int32, (half, LANES), 1) < HALF
@@ -148,10 +156,15 @@
         [jnp.concatenate(tops, axis=1), jnp.concatenate(bottoms, axis=1)], axis=0
     )
     source = as_column(rank_ref[0], rows_iota, lanes_iota)
-    turned = dot(one_hot(source == lanes_iota), ordered).astype(jnp.bfloat16)
-    third_res = halve(second_ref[0], silu(dot(turned, wl[0])))
-    expand = silu(dot(third_res, we[0])).astype(jnp.bfloat16)
-    out_ref[0] = halve(third_res, silu(dot(expand, wd[0])))
+    hot = one_hot(source == lanes_iota)
+    parts = row_parts(hot.shape[0])
+    turned = [dot(hot[part, :], ordered).astype(jnp.bfloat16) for part in parts]
+    third_res = [
+        halve(second_ref[0, part, :], silu(dot(rows, wl[0]))) for rows, part in zip(turned, parts)
+    ]
+    expand = [silu(dot(rows, we[0])).astype(jnp.bfloat16) for rows in third_res]
+    for rows, left, part in zip(third_res, expand, parts):
+        out_ref[0, part, :] = halve(rows, silu(dot(left, wd[0])))
 
 
 def table_kernel(places_ref, order_ref, position_ref, entry_ref, angles_ref, rank_ref, blocks_ref):
@@ -470,7 +483,9 @@
     sent = [
         lax.dynamic_index_in_dim(blocks_of, group_id ^ offset, 0, False) for offset in offsets[1:]
     ]
-    *sent, atom_slots = lax.optimization_barrier((*sent, atom_slots))
+    *sent, atom_slots, route_slot, reverse_position = lax.optimization_barrier(
+        (*sent, atom_slots, route_slot, reverse_position)
+    )
     received = {offset: shift(part, offset, wide) for offset, part in zip(offsets[1:], sent)}
     listed = atom_slots.reshape(atoms // GROUP, GROUP, wide, SLOTS // wide)
     listed = reorder(jnp.transpose(listed, (2, 0, 3, 1)).reshape(wide, rows), order)

time: 277 us -> 272 us (0.982)
  Pallas kernels: 81 us -> 75.9 us
    pallas_call x3, Pallas kernels: 19.1 us -> 15.1 us  [run_back(): pl.pallas_call(back_kernel, grid_spec=pltpu.PrefetchScalarGridSpec(num_sc...]
    unnamed x50 -> x54, local copies, waits for them, and re-layouts: 7.7 us -> 7.74 us
where the time goes in v6:
time: 272 us; the launch traced here: 271 us
  blocking collectives  81.1 us (30%)
  Pallas kernels  75.9 us (28%)
  waiting for transfers between devices  73.8 us (27%)
  starting transfers between devices  23.4 us (9%)
  local copies, waits for them, and re-layouts  13.1 us (5%)
  other arithmetic  3.24 us (1%)
    all_to_all x1, blocking collectives, tiled_local(): returned = lax.all_to_all(mixed, ('wide', 'narrow'), 0, 0, tiled=True)  40.9 us
    all_to_all x1, blocking collectives, swap(): return lax.all_to_all(values, 'narrow', 0, 0, tiled=True)  40.3 us
    pallas_call x2, Pallas kernels, run_mix(): pl.pallas_call(mix_kernel, grid=(devices,), in_specs=[smem, smem, smem, w...  27.2 us
    pallas_call x4, Pallas kernels, run_front(): pl.pallas_call(functools.partial(front_kernel, own, count), grid_spec=plt...  26.6 us
    all_to_all x1, waiting for transfers between devices, tiled_local(): returned = lax.all_to_all(mixed, ('wide', 'narrow'), 0, 0, tiled=True)  26.1 us
    all_to_all x1, waiting for transfers between devices, swap(): return lax.all_to_all(values, 'narrow', 0, 0, tiled=True)  25 us
    ppermute x9, waiting for transfers between devices, shift(): return lax.ppermute(values, 'wide', [(i, i ^ offset) for i in range(wide)])  17.8 us
    pallas_call x3, Pallas kernels, run_back(): pl.pallas_call(back_kernel, grid_spec=pltpu.PrefetchScalarGridSpec(num_sc...  15.1 us
  transfers between devices with their start and end apart: 14, of which 9 were waited for; matrix products, arithmetic and copies ran while one was open for 2% of the time, Pallas kernels for 8%

profile of v6, /device:TPU:0, one launch (start us, length us, event | category | flops | bytes accessed | tf_op | source)
XLA Modules:
  0.0 271.1 jit_solution(16942263958628930464)
XLA Ops:
  0.8 1.3 dynamic-slice_bitcast_fusion
  3.1 4.1 %collective-permute-start.3 = (bf16[1,48,1088]{2,1,0:T(8,128)(2,1)S(1)}, bf16[1,48,1088]{2,1,0:T(8,128)(2,1)S(1)}, u32[]{:S(2)}, u32[]{:S(2)}) collective-permute-start(bf16[1,48,1088]{2,1,0:T(8,128)(2,1)S(1)} %maximum_bitcast_fusion), channel_id=1, source_target_pairs={{0,4},{1,5},{2,6},{3,7},{4,0},{5,1},{6,2},{7,3},{8,12},{9,13},{10,... | collective-permute-start | bytes 313352 | tf_op jit(solution)/shard_map/ppermute | solution.py:450
  7.2 2.4 collective-permute-start
  11.9 5.3 %front.4 = (bf16[4,384,512]{2,1,0:T(8,128)(2,1)}, bf16[8,4,192,128]{3,2,1,0:T(8,128)(2,1)}) custom-call(s32[1]{0:T(128)} %bitcast.56, bf16[4,384,512]{2,1,0:T(8,128)(2,1)} %bitcast.58, s32[4,1,384]{2,1,0:T(1,128)} %broadcast_in_dim.197.back_ref, s32[4,1,384]{2,1,0:T(1,128)} %broadcast_in_dim.199.rank_ref, bf16[2,512,512]{2,1,0:T(8,128)(2,1)} %wm.7, ...), custom_call_target="tpu_custom_call" | custom-call | flops 1207959552 | bytes 1572864 | tf_op jit(solution)/shard_map/front/pallas_call | solution.py:288
  17.3 1.6 collective-permute-start.4
  19.8 3.6 %collective-permute-done.4 = bf16[2,48,1088]{2,1,0:T(8,128)(2,1)S(1)} collective-permute-done((bf16[2,48,1088]{2,1,0:T(8,128)(2,1)S(1)}, bf16[2,48,1088]{2,1,0:T(8,128)(2,1)S(1)}, u32[]{:S(2)}, u32[]{:S(2)}) %collective-permute-start.4) | collective-permute-done | bytes 208928 | tf_op jit(solution)/shard_map/ppermute | solution.py:450
  23.5 3.7 %collective-permute-done.1.refs_1_ = bf16[384,512]{1,0:T(8,128)(2,1)S(1)} collective-permute-done((bf16[384,512]{1,0:T(8,128)(2,1)S(1)}, bf16[384,512]{1,0:T(8,128)(2,1)S(1)}, u32[]{:S(2)}, u32[]{:S(2)}) %collective-permute-start.1) | collective-permute-done | bytes 393248 | tf_op jit(solution)/shard_map/ppermute | solution.py:430
  28.0 10.7 %front.5 = (bf16[4,384,512]{2,1,0:T(8,128)(2,1)}, bf16[8,4,192,128]{3,2,1,0:T(8,128)(2,1)}) custom-call(s32[3]{0:T(128)} %slice.52.where_ref, bf16[4,384,512]{2,1,0:T(8,128)(2,1)} %bitcast.59, s32[4,1,384]{2,1,0:T(1,128)} %broadcast_in_dim.197.back_ref, s32[4,1,384]{2,1,0:T(1,128)} %broadcast_in_dim.199.rank_ref, ...), custom_call_target="tpu_custom_call", output_to_operand_aliasing={{0}: (12, {}), {1}: (13, {})} | custom-call | flops 3623878656 | bytes 4718592 | tf_op jit(solution)/shard_map/front/pallas_call | solution.py:288
  38.7 3.6 %all-to-all-start = ((bf16[8,4,192,128]{3,2,1,0:T(8,128)(2,1)}), bf16[8,4,192,128]{3,2,1,0:T(8,128)(2,1)S(1)}, u32[]{:S(2)}, u32[]{:S(2)}) async-start(bf16[8,4,192,128]{3,2,1,0:T(8,128)(2,1)} %get-tuple-element.41), calls=%async_computation | async-start | bytes 3145728 | tf_op jit(solution)/shard_map/all_to_all | solution.py:434
  43.1 1.3 collective-permute-done.5
  44.9 7.0 %tables.1 = (s32[8,4,1,384]{3,2,1,0:T(1,128)S(1)}, bf16[8,6,256,256]{3,2,1,0:T(8,128)(2,1)S(1)}) custom-call(s32[8]{0:T(128)S(1)} %select_reduce_fusion.9.places_ref, s32[4]{0:T(128)S(1)} %copy-done.15, s32[4]{0:T(128)S(1)} %select_reduce_fusion.10.position_ref, s32[8,4,1,384]{3,2,1,0:T(1,128)S(1)} %broadcast_in_dim_reshape.2.entry_ref, ...), custom_call_target="tpu_custom_call" | custom-call | bytes 25165824 | tf_op jit(solution)/shard_map/tables/pallas_call | solution.py:351
  51.9 2.7 copy-done
  55.1 25.0 %all-to-all-done.recv_ref = bf16[8,4,192,128]{3,2,1,0:T(8,128)(2,1)S(1)} async-done(((bf16[8,4,192,128]{3,2,1,0:T(8,128)(2,1)}), bf16[8,4,192,128]{3,2,1,0:T(8,128)(2,1)S(1)}, u32[]{:S(2)}, u32[]{:S(2)}) %all-to-all-start) | async-done | bytes 1572896 | tf_op jit(solution)/shard_map/all_to_all | solution.py:434
  80.1 2.8 %copy-done.1 = bf16[8,6,256,256]{3,2,1,0:T(8,128)(2,1)S(1)} copy-done((bf16[8,6,256,256]{3,2,1,0:T(8,128)(2,1)S(1)}, bf16[8,6,256,256]{3,2,1,0:T(8,128)(2,1)}, u32[]{:S(2)}) %copy-start.1) | copy-done | bytes 6291480
  82.8 14.2 %mix.2 = bf16[4,8,192,128]{3,2,1,0:T(8,128)(2,1)} custom-call(s32[8,8]{1,0:T(8,128)S(1)} %get-tuple-element.54.owner_ref, s32[8,8]{1,0:T(8,128)S(1)} %get-tuple-element.53.place_ref, s32[4]{0:T(128)S(1)} %copy-done.15, bf16[8,4,192,128]{3,2,1,0:T(8,128)(2,1)S(1)} %all-to-all-done.recv_ref, s32[8,4,1,384]{3,2,1,0:T(1,128)S(1)} %get-tuple-element.42.rank_ref, ...), custom_call_target="tpu_custom_call" | custom-call | flops 1509949440 | bytes 18874368 | tf_op jit(solution)/shard_map/mix/pallas_call | solution.py:381
  97.0 2.9 %all-to-all-start.1 = ((bf16[32,192,128]{2,1,0:T(8,128)(2,1)}), bf16[32,192,128]{2,1,0:T(8,128)(2,1)S(1)}, u32[]{:S(2)}, u32[]{:S(2)}) async-start(bf16[32,192,128]{2,1,0:T(8,128)(2,1)} %bitcast.7), calls=%async_computation.1 | async-start | bytes 3145728 | tf_op jit(solution)/shard_map/all_to_all | solution.py:524
  100.0 2.6 collective-permute-start.6
  103.6 6.6 %collective-permute-done.6 = s32[384]{0:T(512)S(1)} collective-permute-done((s32[384]{0:T(512)S(1)}, s32[384]{0:T(512)S(1)}, u32[]{:S(2)}, u32[]{:S(2)}) %collective-permute-start.6) | collective-permute-done | bytes 1568 | tf_op jit(solution)/shard_map/ppermute | solution.py:430
  111.0 1.0 slice-done.2
  112.5 26.1 %all-to-all-done.1 = bf16[32,192,128]{2,1,0:T(8,128)(2,1)S(1)} async-done(((bf16[32,192,128]{2,1,0:T(8,128)(2,1)}), bf16[32,192,128]{2,1,0:T(8,128)(2,1)S(1)}, u32[]{:S(2)}, u32[]{:S(2)}) %all-to-all-start.1) | async-done | bytes 1572896 | tf_op jit(solution)/shard_map/all_to_all | solution.py:524
  138.6 1.4 copy-done.2
  140.0 3.7 %back.4.cur_ref = bf16[2,384,512]{2,1,0:T(8,128)(2,1)S(1)} custom-call(s32[2]{0:T(128)S(1)} %get-tuple-element.73.from_ref, s32[2]{0:T(128)S(1)} %iota.79.to_ref, bf16[4,384,512]{2,1,0:T(8,128)(2,1)S(1)} %copy-done.2, bf16[4,8,192,128]{3,2,1,0:T(8,128)(2,1)S(1)} %bitcast.52, s32[4,1,384]{2,1,0:T(1,128)S(1)} %broadcast_in_dim.218.rank_ref, ...), custom_call_target="tpu_custom_call" | custom-call | flops 1610612736 | bytes 2359296 | tf_op jit(solution)/shard_map/back/pallas_call | solution.py:322
  144.5 3.7 %back.3.cur_ref = bf16[2,384,512]{2,1,0:T(8,128)(2,1)S(1)} custom-call(s32[2]{0:T(128)S(1)} %get-tuple-element.74.from_ref, s32[2]{0:T(128)S(1)} %iota.75.to_ref, bf16[4,384,512]{2,1,0:T(8,128)(2,1)S(1)} %copy-done.3, bf16[4,8,192,128]{3,2,1,0:T(8,128)(2,1)S(1)} %bitcast.53, s32[4,1,384]{2,1,0:T(1,128)S(1)} %broadcast_in_dim.218.rank_ref, ...), custom_call_target="tpu_custom_call" | custom-call | flops 1610612736 | bytes 2359296 | tf_op jit(solution)/shard_map/back/pallas_call | solution.py:322
  148.9 2.4 collective-permute-start.9
  151.3 5.6 %collective-permute-done.11.refs_0_ = bf16[384,512]{1,0:T(8,128)(2,1)S(1)} collective-permute-done((bf16[384,512]{1,0:T(8,128)(2,1)S(1)}, bf16[384,512]{1,0:T(8,128)(2,1)S(1)}, u32[]{:S(2)}, u32[]{:S(2)}) %collective-permute-start.11) | collective-permute-done | bytes 393248 | tf_op jit(solution)/shard_map/ppermute | solution.py:430
  156.9 5.3 %front.6 = (bf16[4,384,512]{2,1,0:T(8,128)(2,1)S(1)}, bf16[8,4,192,128]{3,2,1,0:T(8,128)(2,1)S(1)}) custom-call(s32[2]{0:T(128)S(1)} %iota.78.where_ref, bf16[2,384,512]{2,1,0:T(8,128)(2,1)S(1)} %back.4.cur_ref, s32[4,1,384]{2,1,0:T(1,128)S(1)} %copy-done.13, s32[4,1,384]{2,1,0:T(1,128)S(1)} %copy-done.12, bf16[2,512,512]{2,1,0:T(8,128)(2,1)S(1)} %copy-done.4, ...), custom_call_target="tpu_custom_call" | custom-call | flops 2415919104 | bytes 3145728 | tf_op jit(solution)/shard_map/front/pallas_call | solution.py:288
  162.2 1.7 collective-permute-done.10.refs_1_
  163.9 5.3 %front.7 = (bf16[4,384,512]{2,1,0:T(8,128)(2,1)S(1)}, bf16[8,4,192,128]{3,2,1,0:T(8,128)(2,1)S(1)}) custom-call(s32[2]{0:T(128)S(1)} %iota.74.where_ref, bf16[2,384,512]{2,1,0:T(8,128)(2,1)S(1)} %back.3.cur_ref, s32[4,1,384]{2,1,0:T(1,128)S(1)} %copy-done.13, s32[4,1,384]{2,1,0:T(1,128)S(1)} %copy-done.12, ...), custom_call_target="tpu_custom_call", output_to_operand_aliasing={{0}: (11, {}), {1}: (12, {})} | custom-call | flops 2415919104 | bytes 3145728 | tf_op jit(solution)/shard_map/front/pallas_call | solution.py:288
  169.2 40.3 %all_to_all.20.recv_ref = bf16[8,4,192,128]{3,2,1,0:T(8,128)(2,1)S(1)} all-to-all(bf16[8,4,192,128]{3,2,1,0:T(8,128)(2,1)S(1)} %get-tuple-element.52), channel_id=1, replica_groups=mesh['wide'=4,'narrow'=8] {'narrow'}, dimensions={0} | all-to-all | bytes 3145728 | tf_op jit(solution)/shard_map/all_to_all | solution.py:434
  209.5 13.0 %mix.3 = bf16[4,8,192,128]{3,2,1,0:T(8,128)(2,1)S(1)} custom-call(s32[8,8]{1,0:T(8,128)S(1)} %get-tuple-element.54.owner_ref, s32[8,8]{1,0:T(8,128)S(1)} %get-tuple-element.53.place_ref, s32[4]{0:T(128)S(1)} %copy-done.15, bf16[8,4,192,128]{3,2,1,0:T(8,128)(2,1)S(1)} %all_to_all.20.recv_ref, s32[8,4,1,384]{3,2,1,0:T(1,128)S(1)} %get-tuple-element.42.rank_ref, ...), custom_call_target="tpu_custom_call" | custom-call | flops 1509949440 | bytes 18874368 | tf_op jit(solution)/shard_map/mix/pallas_call | solution.py:381
  222.5 40.9 %all_to_all.21 = bf16[32,192,128]{2,1,0:T(8,128)(2,1)S(1)} all-to-all(bf16[32,192,128]{2,1,0:T(8,128)(2,1)S(1)} %bitcast.54), channel_id=1, replica_groups=mesh['wide'=4,'narrow'=8] {'wide','narrow'}, dimensions={0} | all-to-all | bytes 3145728 | tf_op jit(solution)/shard_map/all_to_all | solution.py:524
  263.4 7.7 %back.5 = bf16[4,384,512]{2,1,0:T(8,128)(2,1)} custom-call(s32[4]{0:T(128)S(1)} %copy-done.15, s32[4]{0:T(128)S(1)} %copy-done.15, bf16[4,384,512]{2,1,0:T(8,128)(2,1)S(1)} %get-tuple-element.51.second_ref, bf16[4,8,192,128]{3,2,1,0:T(8,128)(2,1)S(1)} %bitcast.55, s32[4,1,384]{2,1,0:T(1,128)S(1)} %broadcast_in_dim.218.rank_ref, ...), custom_call_target="tpu_custom_call" | custom-call | flops 3221225472 | bytes 4718592 | tf_op jit(solution)/shard_map/back/pallas_call | solution.py:322
  (121 shorter events, 11.1 us)
Async XLA Ops:
  0.7 10.0 %copy-start.14 = (s32[4]{0:T(128)}, s32[4]{0:T(128)S(1)}, u32[]{:S(2)}) copy-start(s32[4]{0:T(128)S(1)} %broadcast_xor_fusion.order_ref.from_ref.to_ref) | copy-start | bytes 52
  3.1 14.2 %collective-permute-start.3 = (bf16[1,48,1088]{2,1,0:T(8,128)(2,1)S(1)}, bf16[1,48,1088]{2,1,0:T(8,128)(2,1)S(1)}, u32[]{:S(2)}, u32[]{:S(2)}) collective-permute-start(bf16[1,48,1088]{2,1,0:T(8,128)(2,1)S(1)} %maximum_bitcast_fusion), channel_id=1, source_target_pairs={{0,4},{1,5},{2,6},{3,7},{4,0},{5,1},{6,2},{7,3},{8,12},{9,13},{10,... | collective-permute-start | bytes 313352 | tf_op jit(solution)/shard_map/ppermute | solution.py:450
  7.2 16.2 %collective-permute-start = (bf16[384,512]{1,0:T(8,128)(2,1)S(1)}, bf16[384,512]{1,0:T(8,128)(2,1)S(1)}, u32[]{:S(2)}, u32[]{:S(2)}) collective-permute-start(bf16[384,512]{1,0:T(8,128)(2,1)S(1)} %get-tuple-element.31), channel_id=1, source_target_pairs={{0,24},{8,16},{16,8},{24,0},{1,25},{9,17},{17,9},{25,1},{2,26},{10... | collective-permute-start | bytes 1179656 | tf_op jit(solution)/shard_map/ppermute | solution.py:430
  9.7 17.6 %collective-permute-start.1 = (bf16[384,512]{1,0:T(8,128)(2,1)S(1)}, bf16[384,512]{1,0:T(8,128)(2,1)S(1)}, u32[]{:S(2)}, u32[]{:S(2)}) collective-permute-start(bf16[384,512]{1,0:T(8,128)(2,1)S(1)} %get-tuple-element.32), channel_id=1, source_target_pairs={{0,8},{8,0},{16,24},{24,16},{1,9},{9,1},{17,25},{25,17},{2,10},{10... | collective-permute-start | bytes 1179656 | tf_op jit(solution)/shard_map/ppermute | solution.py:430
  10.2 17.0 %collective-permute-start.2 = (bf16[384,512]{1,0:T(8,128)(2,1)S(1)}, bf16[384,512]{1,0:T(8,128)(2,1)}, u32[]{:S(2)}, u32[]{:S(2)}) collective-permute-start(bf16[384,512]{1,0:T(8,128)(2,1)S(1)} %get-tuple-element.33), channel_id=1, source_target_pairs={{0,16},{8,24},{16,0},{24,8},{1,17},{9,25},{17,1},{25,9},{2,18},{10... | collective-permute-start | bytes 1179656 | tf_op jit(solution)/shard_map/ppermute | solution.py:430
  11.9 7.0 %copy-start.15 = (s32[4]{0:T(128)S(1)}, s32[4]{0:T(128)}, u32[]{:S(2)}) copy-start(s32[4]{0:T(128)} %copy-done.14) | copy-start | bytes 52
  11.9 7.7 %copy-start.23 = (s32[8]{0:T(128)S(1)}, s32[8]{0:T(128)}, u32[]{:S(2)}) copy-start(s32[8]{0:T(128)} %constant.76.clone) | copy-start | bytes 100
  17.3 6.1 %collective-permute-start.4 = (bf16[2,48,1088]{2,1,0:T(8,128)(2,1)S(1)}, bf16[2,48,1088]{2,1,0:T(8,128)(2,1)S(1)}, u32[]{:S(2)}, u32[]{:S(2)}) collective-permute-start(bf16[2,48,1088]{2,1,0:T(8,128)(2,1)S(1)} %pad_maximum_fusion.2), channel_id=1, source_target_pairs={{0,2},{1,3},{2,0},{3,1},{4,6},{5,7},{6,4},{7,5},{8,10},{9,11},{10,... | collective-permute-start | bytes 626696 | tf_op jit(solution)/shard_map/ppermute | solution.py:450
  23.5 3.8 %copy-start.20 = (bf16[384,512]{1,0:T(8,128)(2,1)}, bf16[384,512]{1,0:T(8,128)(2,1)S(1)}, u32[]{:S(2)}) copy-start(bf16[384,512]{1,0:T(8,128)(2,1)S(1)} %collective-permute-done.refs_0_) | copy-start | bytes 1179652
  38.7 3.6 %copy-start.22 = (s32[4]{0:T(128)S(1)}, s32[4]{0:T(128)}, u32[]{:S(2)}) copy-start(s32[4]{0:T(128)} %constant.75.clone) | copy-start | bytes 52
  38.7 41.3 %all-to-all-start = ((bf16[8,4,192,128]{3,2,1,0:T(8,128)(2,1)}), bf16[8,4,192,128]{3,2,1,0:T(8,128)(2,1)S(1)}, u32[]{:S(2)}, u32[]{:S(2)}) async-start(bf16[8,4,192,128]{3,2,1,0:T(8,128)(2,1)} %get-tuple-element.41), calls=%async_computation | async-start | bytes 3145728 | tf_op jit(solution)/shard_map/all_to_all | solution.py:434
  42.5 1.9 collective-permute-start.5
  97.0 41.6 %all-to-all-start.1 = ((bf16[32,192,128]{2,1,0:T(8,128)(2,1)}), bf16[32,192,128]{2,1,0:T(8,128)(2,1)S(1)}, u32[]{:S(2)}, u32[]{:S(2)}) async-start(bf16[32,192,128]{2,1,0:T(8,128)(2,1)} %bitcast.7), calls=%async_computation.1 | async-start | bytes 3145728 | tf_op jit(solution)/shard_map/all_to_all | solution.py:524
  100.0 10.2 %collective-permute-start.6 = (s32[384]{0:T(512)S(1)}, s32[384]{0:T(512)S(1)}, u32[]{:S(2)}, u32[]{:S(2)}) collective-permute-start(s32[384]{0:T(512)S(1)} %get-tuple-element.55), channel_id=1, source_target_pairs={{0,24},{8,16},{16,8},{24,0},{1,25},{9,17},{17,9},{25,1},{2,26},{10... | collective-permute-start | bytes 4616 | tf_op jit(solution)/shard_map/ppermute | solution.py:430
  102.5 7.6 %collective-permute-start.8 = (s32[384]{0:T(512)S(1)}, s32[384]{0:T(512)S(1)}, u32[]{:S(2)}, u32[]{:S(2)}) collective-permute-start(s32[384]{0:T(512)S(1)} %get-tuple-element.56), channel_id=1, source_target_pairs={{0,16},{8,24},{16,0},{24,8},{1,17},{9,25},{17,1},{25,9},{2,18},{10... | collective-permute-start | bytes 4616 | tf_op jit(solution)/shard_map/ppermute | solution.py:430
  103.1 7.3 %collective-permute-start.7 = (s32[384]{0:T(512)S(1)}, s32[384]{0:T(512)S(1)}, u32[]{:S(2)}, u32[]{:S(2)}) collective-permute-start(s32[384]{0:T(512)S(1)} %get-tuple-element.57), channel_id=1, source_target_pairs={{0,8},{8,0},{16,24},{24,16},{1,9},{9,1},{17,25},{25,17},{2,10},{10... | collective-permute-start | bytes 4616 | tf_op jit(solution)/shard_map/ppermute | solution.py:430
  140.0 4.4 %copy-start.3 = (bf16[4,384,512]{2,1,0:T(8,128)(2,1)S(1)}, bf16[4,384,512]{2,1,0:T(8,128)(2,1)}, u32[]{:S(2)}) copy-start(bf16[4,384,512]{2,1,0:T(8,128)(2,1)} %get-tuple-element.36.second_ref) | copy-start | bytes 4718596
  143.8 13.0 %collective-permute-start.11 = (bf16[384,512]{1,0:T(8,128)(2,1)S(1)}, bf16[384,512]{1,0:T(8,128)(2,1)S(1)}, u32[]{:S(2)}, u32[]{:S(2)}) collective-permute-start(bf16[384,512]{1,0:T(8,128)(2,1)S(1)} %slice_bitcast_fusion), channel_id=1, source_target_pairs={{0,24},{8,16},{16,8},{24,0},{1,25},{9,17},{17,9},{25,1},{2,26},{10... | collective-permute-start | bytes 1179656 | tf_op jit(solution)/shard_map/ppermute | solution.py:430
  144.4 12.4 %copy-start.5 = (bf16[2,512,512]{2,1,0:T(8,128)(2,1)S(1)}, bf16[2,512,512]{2,1,0:T(8,128)(2,1)}, u32[]{:S(2)}) copy-start(bf16[2,512,512]{2,1,0:T(8,128)(2,1)} %wr.7) | copy-start | bytes 3145732
  144.4 12.4 %copy-start.6 = (bf16[2,512,512]{2,1,0:T(8,128)(2,1)S(1)}, bf16[2,512,512]{2,1,0:T(8,128)(2,1)}, u32[]{:S(2)}) copy-start(bf16[2,512,512]{2,1,0:T(8,128)(2,1)} %wc.7) | copy-start | bytes 3145732
  144.4 12.4 %copy-start.7 = (bf16[2,512,512]{2,1,0:T(8,128)(2,1)S(1)}, bf16[2,512,512]{2,1,0:T(8,128)(2,1)}, u32[]{:S(2)}) copy-start(bf16[2,512,512]{2,1,0:T(8,128)(2,1)} %wi.7) | copy-start | bytes 3145732
  144.4 12.4 %copy-start.8 = (bf16[2,512,512]{2,1,0:T(8,128)(2,1)S(1)}, bf16[2,512,512]{2,1,0:T(8,128)(2,1)}, u32[]{:S(2)}) copy-start(bf16[2,512,512]{2,1,0:T(8,128)(2,1)} %wo.7) | copy-start | bytes 3145732
  148.2 8.7 %copy-start.4 = (bf16[2,512,512]{2,1,0:T(8,128)(2,1)S(1)}, bf16[2,512,512]{2,1,0:T(8,128)(2,1)}, u32[]{:S(2)}) copy-start(bf16[2,512,512]{2,1,0:T(8,128)(2,1)} %wm.7) | copy-start | bytes 3145732
  148.2 8.7 %copy-start.12 = (s32[4,1,384]{2,1,0:T(1,128)S(1)}, s32[4,1,384]{2,1,0:T(1,128)}, u32[]{:S(2)}) copy-start(s32[4,1,384]{2,1,0:T(1,128)} %broadcast_in_dim.199.rank_ref) | copy-start | bytes 18436
  148.2 8.7 %copy-start.13 = (s32[4,1,384]{2,1,0:T(1,128)S(1)}, s32[4,1,384]{2,1,0:T(1,128)}, u32[]{:S(2)}) copy-start(s32[4,1,384]{2,1,0:T(1,128)} %broadcast_in_dim.197.back_ref) | copy-start | bytes 18436
  148.3 15.6 %collective-permute-start.10 = (bf16[384,512]{1,0:T(8,128)(2,1)S(1)}, bf16[384,512]{1,0:T(8,128)(2,1)S(1)}, u32[]{:S(2)}, u32[]{:S(2)}) collective-permute-start(bf16[384,512]{1,0:T(8,128)(2,1)S(1)} %get-tuple-element.66), channel_id=1, source_target_pairs={{0,16},{8,24},{16,0},{24,8},{1,17},{9,25},{17,1},{25,9},{2,18},{10... | collective-permute-start | bytes 1179656 | tf_op jit(solution)/shard_map/ppermute | solution.py:430
  148.9 15.0 %collective-permute-start.9 = (bf16[384,512]{1,0:T(8,128)(2,1)S(1)}, bf16[384,512]{1,0:T(8,128)(2,1)S(1)}, u32[]{:S(2)}, u32[]{:S(2)}) collective-permute-start(bf16[384,512]{1,0:T(8,128)(2,1)S(1)} %get-tuple-element.67), channel_id=1, source_target_pairs={{0,8},{8,0},{16,24},{24,16},{1,9},{9,1},{17,25},{25,17},{2,10},{10... | collective-permute-start | bytes 1179656 | tf_op jit(solution)/shard_map/ppermute | solution.py:430
  156.9 52.6 %slice-start = ((s8[6291456]{0:T(1024)(128)(4,1)}), s8[4194304]{0:T(1024)(128)(4,1)S(1)}, s32[]{:S(2)}) async-start(s8[6291456]{0:T(1024)(128)(4,1)} %bitcast.50), calls=%async_computation.4 | async-start | bytes 8388608
  163.9 45.6 %slice-start.1 = ((s8[6291456]{0:T(1024)(128)(4,1)}), s8[2097152]{0:T(1024)(128)(4,1)S(1)}, s32[]{:S(2)}) async-start(s8[6291456]{0:T(1024)(128)(4,1)} %bitcast.50), calls=%async_computation.5 | async-start | bytes 4194304
  222.5 40.9 %copy-start.9 = (bf16[2,512,512]{2,1,0:T(8,128)(2,1)S(1)}, bf16[2,512,512]{2,1,0:T(8,128)(2,1)}, u32[]{:S(2)}) copy-start(bf16[2,512,512]{2,1,0:T(8,128)(2,1)} %wd.1) | copy-start | bytes 3145732
  222.5 40.9 %copy-start.10 = (bf16[2,512,512]{2,1,0:T(8,128)(2,1)S(1)}, bf16[2,512,512]{2,1,0:T(8,128)(2,1)}, u32[]{:S(2)}) copy-start(bf16[2,512,512]{2,1,0:T(8,128)(2,1)} %we.1) | copy-start | bytes 3145732
  222.5 40.9 %copy-start.11 = (bf16[2,512,512]{2,1,0:T(8,128)(2,1)S(1)}, bf16[2,512,512]{2,1,0:T(8,128)(2,1)}, u32[]{:S(2)}) copy-start(bf16[2,512,512]{2,1,0:T(8,128)(2,1)} %wl.1) | copy-start | bytes 3145732
  (11 other events, 21.0 us)

commit v7 on v6

--- a/solution.py
+++ b/solution.py
@@ -12,6 +12,7 @@
 LANES = 128
 HALF = LANES // 2
 GROUP = 8
+PAIR = 2
 
 
 ROOT_HALF = 0.7071067811865476
@@ -219,26 +220,30 @@
                     ins[side, owner, place] = block
 
     rows_iota, lanes_iota = iotas(rows)
-    gathered = []
+    pair = range(PAIR)
+    gathered = [[] for _ in pair]
     for side in range(sides):
-        source = as_column(rank_ref[0, side], rows_iota, lanes_iota)
-        operand = ins[side, step].reshape(rows, LANES)
-        gathered.append(dot(one_hot(source == lanes_iota), operand).astype(jnp.bfloat16))
-    mixed = []
+        for index in pair:
+            source = as_column(rank_ref[index, side], rows_iota, lanes_iota)
+            operand = ins[side, PAIR * step + index].reshape(rows, LANES)
+            gathered[index].append(dot(one_hot(source == lanes_iota), operand).astype(jnp.bfloat16))
+    mixed = [[] for _ in pair]
     for group in range(groups):
-        operand = jnp.concatenate(
-            [part[group * strip : (group + 1) * strip] for part in gathered], axis=0
-        )
-        mixed.append(dot(blocks_ref[0, group], operand).astype(jnp.bfloat16))
+        for index in pair:
+            operand = jnp.concatenate(
+                [part[group * strip : (group + 1) * strip] for part in gathered[index]], axis=0
+            )
+            mixed[index].append(dot(blocks_ref[index, group], operand).astype(jnp.bfloat16))
     for side in range(sides):
-        operand = jnp.concatenate(
-            [part[side * strip : (side + 1) * strip] for part in mixed], axis=0
-        )
-        outs[side, step] = (
-            dot(one_hot(rows_iota == rank_ref[0, side]), operand)
-            .astype(jnp.bfloat16)
-            .reshape(devices, unit, LANES)
-        )
+        for index in pair:
+            operand = jnp.concatenate(
+                [part[side * strip : (side + 1) * strip] for part in mixed[index]], axis=0
+            )
+            outs[side, PAIR * step + index] = (
+                dot(one_hot(rows_iota == rank_ref[index, side]), operand)
+                .astype(jnp.bfloat16)
+                .reshape(devices, unit, LANES)
+            )
 
     @pl.when(step == pl.num_programs(0) - 1)
     def _():
@@ -380,14 +385,14 @@
     scratch = pltpu.VMEM((sides, devices, devices, unit, LANES), jnp.bfloat16)
     return pl.pallas_call(
         mix_kernel,
-        grid=(devices,),
+        grid=(devices // PAIR,),
         in_specs=[
             smem,
             smem,
             smem,
             whole_spec(received),
-            rank_spec(rank),
-            pl.BlockSpec((1,) + blocks.shape[1:], lambda i: (i, 0, 0, 0)),
+            pl.BlockSpec((PAIR,) + rank.shape[1:], lambda i: (i, 0, 0, 0)),
+            pl.BlockSpec((PAIR,) + blocks.shape[1:], lambda i: (i, 0, 0, 0)),
         ],
         out_specs=pl.BlockSpec(shape, lambda i: (0, 0, 0, 0)),
         out_shape=jax.ShapeDtypeStruct(shape, jnp.bfloat16),

time: 272 us -> 268 us (0.985)
  Pallas kernels: 75.9 us -> 72.4 us
    pallas_call x2, Pallas kernels: 27.2 us -> 23.7 us  [run_mix(): pl.pallas_call(mix_kernel, grid=(devices // PAIR,), in_specs=[smem, smem,...]
where the time goes in v7:
time: 268 us
  blocking collectives  81.1 us (30%)
  waiting for transfers between devices  73.8 us (28%)
  Pallas kernels  72.4 us (27%)
  starting transfers between devices  23.4 us (9%)
  local copies, waits for them, and re-layouts  13.1 us (5%)
  other arithmetic  3.24 us (1%)
    all_to_all x1, blocking collectives, tiled_local(): returned = lax.all_to_all(mixed, ('wide', 'narrow'), 0, 0, tiled=True)  40.9 us
    all_to_all x1, blocking collectives, swap(): return lax.all_to_all(values, 'narrow', 0, 0, tiled=True)  40.3 us
    pallas_call x4, Pallas kernels, run_front(): pl.pallas_call(functools.partial(front_kernel, own, count), grid_spec=plt...  26.6 us
    all_to_all x1, waiting for transfers between devices, tiled_local(): returned = lax.all_to_all(mixed, ('wide', 'narrow'), 0, 0, tiled=True)  26.1 us
    all_to_all x1, waiting for transfers between devices, swap(): return lax.all_to_all(values, 'narrow', 0, 0, tiled=True)  25 us
    pallas_call x2, Pallas kernels, run_mix(): pl.pallas_call(mix_kernel, grid=(devices // PAIR,), in_specs=[smem, smem,...  23.7 us
    ppermute x9, waiting for transfers between devices, shift(): return lax.ppermute(values, 'wide', [(i, i ^ offset) for i in range(wide)])  17.7 us
    pallas_call x3, Pallas kernels, run_back(): pl.pallas_call(back_kernel, grid_spec=pltpu.PrefetchScalarGridSpec(num_sc...  15.1 us
  transfers between devices with their start and end apart: 14, of which 9 were waited for; matrix products, arithmetic and copies ran while one was open for 2% of the time, Pallas kernels for 8%

profile of v7, /device:TPU:0, one launch (start us, length us, event | category | flops | bytes accessed | tf_op | source)
XLA Modules:
  0.0 267.6 jit_solution(5586288353257127870)
XLA Ops:
  0.8 1.3 dynamic-slice_bitcast_fusion
  3.1 4.1 %collective-permute-start.3 = (bf16[1,48,1088]{2,1,0:T(8,128)(2,1)S(1)}, bf16[1,48,1088]{2,1,0:T(8,128)(2,1)S(1)}, u32[]{:S(2)}, u32[]{:S(2)}) collective-permute-start(bf16[1,48,1088]{2,1,0:T(8,128)(2,1)S(1)} %maximum_bitcast_fusion), channel_id=1, source_target_pairs={{0,4},{1,5},{2,6},{3,7},{4,0},{5,1},{6,2},{7,3},{8,12},{9,13},{10,... | collective-permute-start | bytes 313352 | tf_op jit(solution)/shard_map/ppermute | solution.py:455
  7.2 2.4 collective-permute-start
  11.9 5.3 %front.4 = (bf16[4,384,512]{2,1,0:T(8,128)(2,1)}, bf16[8,4,192,128]{3,2,1,0:T(8,128)(2,1)}) custom-call(s32[1]{0:T(128)} %bitcast.56, bf16[4,384,512]{2,1,0:T(8,128)(2,1)} %bitcast.58, s32[4,1,384]{2,1,0:T(1,128)} %broadcast_in_dim.197.back_ref, s32[4,1,384]{2,1,0:T(1,128)} %broadcast_in_dim.199.rank_ref, bf16[2,512,512]{2,1,0:T(8,128)(2,1)} %wm.7, ...), custom_call_target="tpu_custom_call" | custom-call | flops 1207959552 | bytes 1572864 | tf_op jit(solution)/shard_map/front/pallas_call | solution.py:293
  17.3 1.6 collective-permute-start.4
  19.8 3.6 %collective-permute-done.4 = bf16[2,48,1088]{2,1,0:T(8,128)(2,1)S(1)} collective-permute-done((bf16[2,48,1088]{2,1,0:T(8,128)(2,1)S(1)}, bf16[2,48,1088]{2,1,0:T(8,128)(2,1)S(1)}, u32[]{:S(2)}, u32[]{:S(2)}) %collective-permute-start.4) | collective-permute-done | bytes 208928 | tf_op jit(solution)/shard_map/ppermute | solution.py:455
  23.5 3.7 %collective-permute-done.1.refs_1_ = bf16[384,512]{1,0:T(8,128)(2,1)S(1)} collective-permute-done((bf16[384,512]{1,0:T(8,128)(2,1)S(1)}, bf16[384,512]{1,0:T(8,128)(2,1)S(1)}, u32[]{:S(2)}, u32[]{:S(2)}) %collective-permute-start.1) | collective-permute-done | bytes 393248 | tf_op jit(solution)/shard_map/ppermute | solution.py:435
  28.0 10.7 %front.5 = (bf16[4,384,512]{2,1,0:T(8,128)(2,1)}, bf16[8,4,192,128]{3,2,1,0:T(8,128)(2,1)}) custom-call(s32[3]{0:T(128)} %slice.52.where_ref, bf16[4,384,512]{2,1,0:T(8,128)(2,1)} %bitcast.59, s32[4,1,384]{2,1,0:T(1,128)} %broadcast_in_dim.197.back_ref, s32[4,1,384]{2,1,0:T(1,128)} %broadcast_in_dim.199.rank_ref, ...), custom_call_target="tpu_custom_call", output_to_operand_aliasing={{0}: (12, {}), {1}: (13, {})} | custom-call | flops 3623878656 | bytes 4718592 | tf_op jit(solution)/shard_map/front/pallas_call | solution.py:293
  38.7 3.6 %all-to-all-start = ((bf16[8,4,192,128]{3,2,1,0:T(8,128)(2,1)}), bf16[8,4,192,128]{3,2,1,0:T(8,128)(2,1)S(1)}, u32[]{:S(2)}, u32[]{:S(2)}) async-start(bf16[8,4,192,128]{3,2,1,0:T(8,128)(2,1)} %get-tuple-element.41), calls=%async_computation | async-start | bytes 3145728 | tf_op jit(solution)/shard_map/all_to_all | solution.py:439
  43.1 1.3 collective-permute-done.5
  44.9 7.0 %tables.1 = (s32[8,4,1,384]{3,2,1,0:T(1,128)S(1)}, bf16[8,6,256,256]{3,2,1,0:T(8,128)(2,1)S(1)}) custom-call(s32[8]{0:T(128)S(1)} %select_reduce_fusion.9.places_ref, s32[4]{0:T(128)S(1)} %copy-done.15, s32[4]{0:T(128)S(1)} %select_reduce_fusion.10.position_ref, s32[8,4,1,384]{3,2,1,0:T(1,128)S(1)} %broadcast_in_dim_reshape.2.entry_ref, ...), custom_call_target="tpu_custom_call" | custom-call | bytes 25165824 | tf_op jit(solution)/shard_map/tables/pallas_call | solution.py:356
  51.9 2.7 copy-done
  55.1 25.0 %all-to-all-done.recv_ref = bf16[8,4,192,128]{3,2,1,0:T(8,128)(2,1)S(1)} async-done(((bf16[8,4,192,128]{3,2,1,0:T(8,128)(2,1)}), bf16[8,4,192,128]{3,2,1,0:T(8,128)(2,1)S(1)}, u32[]{:S(2)}, u32[]{:S(2)}) %all-to-all-start) | async-done | bytes 1572896 | tf_op jit(solution)/shard_map/all_to_all | solution.py:439
  80.1 2.8 %copy-done.1 = bf16[8,6,256,256]{3,2,1,0:T(8,128)(2,1)S(1)} copy-done((bf16[8,6,256,256]{3,2,1,0:T(8,128)(2,1)S(1)}, bf16[8,6,256,256]{3,2,1,0:T(8,128)(2,1)}, u32[]{:S(2)}) %copy-start.1) | copy-done | bytes 6291480
  82.8 12.4 %mix.2 = bf16[4,8,192,128]{3,2,1,0:T(8,128)(2,1)} custom-call(s32[8,8]{1,0:T(8,128)S(1)} %get-tuple-element.54.owner_ref, s32[8,8]{1,0:T(8,128)S(1)} %get-tuple-element.53.place_ref, s32[4]{0:T(128)S(1)} %copy-done.15, bf16[8,4,192,128]{3,2,1,0:T(8,128)(2,1)S(1)} %all-to-all-done.recv_ref, s32[8,4,1,384]{3,2,1,0:T(1,128)S(1)} %get-tuple-element.42.rank_ref, ...), custom_call_target="tpu_custom_call" | custom-call | flops 1509949440 | bytes 18874368 | tf_op jit(solution)/shard_map/mix/pallas_call | solution.py:386
  95.3 2.9 %all-to-all-start.1 = ((bf16[32,192,128]{2,1,0:T(8,128)(2,1)}), bf16[32,192,128]{2,1,0:T(8,128)(2,1)S(1)}, u32[]{:S(2)}, u32[]{:S(2)}) async-start(bf16[32,192,128]{2,1,0:T(8,128)(2,1)} %bitcast.7), calls=%async_computation.1 | async-start | bytes 3145728 | tf_op jit(solution)/shard_map/all_to_all | solution.py:529
  98.2 2.6 collective-permute-start.6
  101.8 6.6 %collective-permute-done.6 = s32[384]{0:T(512)S(1)} collective-permute-done((s32[384]{0:T(512)S(1)}, s32[384]{0:T(512)S(1)}, u32[]{:S(2)}, u32[]{:S(2)}) %collective-permute-start.6) | collective-permute-done | bytes 1568 | tf_op jit(solution)/shard_map/ppermute | solution.py:435
  109.2 1.0 slice-done.2
  110.7 26.1 %all-to-all-done.1 = bf16[32,192,128]{2,1,0:T(8,128)(2,1)S(1)} async-done(((bf16[32,192,128]{2,1,0:T(8,128)(2,1)}), bf16[32,192,128]{2,1,0:T(8,128)(2,1)S(1)}, u32[]{:S(2)}, u32[]{:S(2)}) %all-to-all-start.1) | async-done | bytes 1572896 | tf_op jit(solution)/shard_map/all_to_all | solution.py:529
  136.9 1.4 copy-done.2
  138.3 3.7 %back.4.cur_ref = bf16[2,384,512]{2,1,0:T(8,128)(2,1)S(1)} custom-call(s32[2]{0:T(128)S(1)} %get-tuple-element.73.from_ref, s32[2]{0:T(128)S(1)} %iota.79.to_ref, bf16[4,384,512]{2,1,0:T(8,128)(2,1)S(1)} %copy-done.2, bf16[4,8,192,128]{3,2,1,0:T(8,128)(2,1)S(1)} %bitcast.52, s32[4,1,384]{2,1,0:T(1,128)S(1)} %broadcast_in_dim.218.rank_ref, ...), custom_call_target="tpu_custom_call" | custom-call | flops 1610612736 | bytes 2359296 | tf_op jit(solution)/shard_map/back/pallas_call | solution.py:327
  142.7 3.7 %back.3.cur_ref = bf16[2,384,512]{2,1,0:T(8,128)(2,1)S(1)} custom-call(s32[2]{0:T(128)S(1)} %get-tuple-element.74.from_ref, s32[2]{0:T(128)S(1)} %iota.75.to_ref, bf16[4,384,512]{2,1,0:T(8,128)(2,1)S(1)} %copy-done.3, bf16[4,8,192,128]{3,2,1,0:T(8,128)(2,1)S(1)} %bitcast.53, s32[4,1,384]{2,1,0:T(1,128)S(1)} %broadcast_in_dim.218.rank_ref, ...), custom_call_target="tpu_custom_call" | custom-call | flops 1610612736 | bytes 2359296 | tf_op jit(solution)/shard_map/back/pallas_call | solution.py:327
  147.1 2.4 collective-permute-start.9
  149.5 5.6 %collective-permute-done.11.refs_0_ = bf16[384,512]{1,0:T(8,128)(2,1)S(1)} collective-permute-done((bf16[384,512]{1,0:T(8,128)(2,1)S(1)}, bf16[384,512]{1,0:T(8,128)(2,1)S(1)}, u32[]{:S(2)}, u32[]{:S(2)}) %collective-permute-start.11) | collective-permute-done | bytes 393248 | tf_op jit(solution)/shard_map/ppermute | solution.py:435
  155.2 5.3 %front.6 = (bf16[4,384,512]{2,1,0:T(8,128)(2,1)S(1)}, bf16[8,4,192,128]{3,2,1,0:T(8,128)(2,1)S(1)}) custom-call(s32[2]{0:T(128)S(1)} %iota.78.where_ref, bf16[2,384,512]{2,1,0:T(8,128)(2,1)S(1)} %back.4.cur_ref, s32[4,1,384]{2,1,0:T(1,128)S(1)} %copy-done.13, s32[4,1,384]{2,1,0:T(1,128)S(1)} %copy-done.12, bf16[2,512,512]{2,1,0:T(8,128)(2,1)S(1)} %copy-done.4, ...), custom_call_target="tpu_custom_call" | custom-call | flops 2415919104 | bytes 3145728 | tf_op jit(solution)/shard_map/front/pallas_call | solution.py:293
  160.5 1.6 collective-permute-done.10.refs_1_
  162.1 5.3 %front.7 = (bf16[4,384,512]{2,1,0:T(8,128)(2,1)S(1)}, bf16[8,4,192,128]{3,2,1,0:T(8,128)(2,1)S(1)}) custom-call(s32[2]{0:T(128)S(1)} %iota.74.where_ref, bf16[2,384,512]{2,1,0:T(8,128)(2,1)S(1)} %back.3.cur_ref, s32[4,1,384]{2,1,0:T(1,128)S(1)} %copy-done.13, s32[4,1,384]{2,1,0:T(1,128)S(1)} %copy-done.12, ...), custom_call_target="tpu_custom_call", output_to_operand_aliasing={{0}: (11, {}), {1}: (12, {})} | custom-call | flops 2415919104 | bytes 3145728 | tf_op jit(solution)/shard_map/front/pallas_call | solution.py:293
  167.4 40.3 %all_to_all.20.recv_ref = bf16[8,4,192,128]{3,2,1,0:T(8,128)(2,1)S(1)} all-to-all(bf16[8,4,192,128]{3,2,1,0:T(8,128)(2,1)S(1)} %get-tuple-element.52), channel_id=1, replica_groups=mesh['wide'=4,'narrow'=8] {'narrow'}, dimensions={0} | all-to-all | bytes 3145728 | tf_op jit(solution)/shard_map/all_to_all | solution.py:439
  207.7 11.3 %mix.3 = bf16[4,8,192,128]{3,2,1,0:T(8,128)(2,1)S(1)} custom-call(s32[8,8]{1,0:T(8,128)S(1)} %get-tuple-element.54.owner_ref, s32[8,8]{1,0:T(8,128)S(1)} %get-tuple-element.53.place_ref, s32[4]{0:T(128)S(1)} %copy-done.15, bf16[8,4,192,128]{3,2,1,0:T(8,128)(2,1)S(1)} %all_to_all.20.recv_ref, s32[8,4,1,384]{3,2,1,0:T(1,128)S(1)} %get-tuple-element.42.rank_ref, ...), custom_call_target="tpu_custom_call" | custom-call | flops 1509949440 | bytes 18874368 | tf_op jit(solution)/shard_map/mix/pallas_call | solution.py:386
  219.0 40.9 %all_to_all.21 = bf16[32,192,128]{2,1,0:T(8,128)(2,1)S(1)} all-to-all(bf16[32,192,128]{2,1,0:T(8,128)(2,1)S(1)} %bitcast.54), channel_id=1, replica_groups=mesh['wide'=4,'narrow'=8] {'wide','narrow'}, dimensions={0} | all-to-all | bytes 3145728 | tf_op jit(solution)/shard_map/all_to_all | solution.py:529
  259.9 7.7 %back.5 = bf16[4,384,512]{2,1,0:T(8,128)(2,1)} custom-call(s32[4]{0:T(128)S(1)} %copy-done.15, s32[4]{0:T(128)S(1)} %copy-done.15, bf16[4,384,512]{2,1,0:T(8,128)(2,1)S(1)} %get-tuple-element.51.second_ref, bf16[4,8,192,128]{3,2,1,0:T(8,128)(2,1)S(1)} %bitcast.55, s32[4,1,384]{2,1,0:T(1,128)S(1)} %broadcast_in_dim.218.rank_ref, ...), custom_call_target="tpu_custom_call" | custom-call | flops 3221225472 | bytes 4718592 | tf_op jit(solution)/shard_map/back/pallas_call | solution.py:327
  (121 shorter events, 11.1 us)
Async XLA Ops:
  0.7 10.0 %copy-start.14 = (s32[4]{0:T(128)}, s32[4]{0:T(128)S(1)}, u32[]{:S(2)}) copy-start(s32[4]{0:T(128)S(1)} %broadcast_xor_fusion.order_ref.from_ref.to_ref) | copy-start | bytes 52
  3.1 14.2 %collective-permute-start.3 = (bf16[1,48,1088]{2,1,0:T(8,128)(2,1)S(1)}, bf16[1,48,1088]{2,1,0:T(8,128)(2,1)S(1)}, u32[]{:S(2)}, u32[]{:S(2)}) collective-permute-start(bf16[1,48,1088]{2,1,0:T(8,128)(2,1)S(1)} %maximum_bitcast_fusion), channel_id=1, source_target_pairs={{0,4},{1,5},{2,6},{3,7},{4,0},{5,1},{6,2},{7,3},{8,12},{9,13},{10,... | collective-permute-start | bytes 313352 | tf_op jit(solution)/shard_map/ppermute | solution.py:455
  7.2 16.2 %collective-permute-start = (bf16[384,512]{1,0:T(8,128)(2,1)S(1)}, bf16[384,512]{1,0:T(8,128)(2,1)S(1)}, u32[]{:S(2)}, u32[]{:S(2)}) collective-permute-start(bf16[384,512]{1,0:T(8,128)(2,1)S(1)} %get-tuple-element.31), channel_id=1, source_target_pairs={{0,24},{8,16},{16,8},{24,0},{1,25},{9,17},{17,9},{25,1},{2,26},{10... | collective-permute-start | bytes 1179656 | tf_op jit(solution)/shard_map/ppermute | solution.py:435
  9.7 17.6 %collective-permute-start.1 = (bf16[384,512]{1,0:T(8,128)(2,1)S(1)}, bf16[384,512]{1,0:T(8,128)(2,1)S(1)}, u32[]{:S(2)}, u32[]{:S(2)}) collective-permute-start(bf16[384,512]{1,0:T(8,128)(2,1)S(1)} %get-tuple-element.32), channel_id=1, source_target_pairs={{0,8},{8,0},{16,24},{24,16},{1,9},{9,1},{17,25},{25,17},{2,10},{10... | collective-permute-start | bytes 1179656 | tf_op jit(solution)/shard_map/ppermute | solution.py:435
  10.2 17.0 %collective-permute-start.2 = (bf16[384,512]{1,0:T(8,128)(2,1)S(1)}, bf16[384,512]{1,0:T(8,128)(2,1)}, u32[]{:S(2)}, u32[]{:S(2)}) collective-permute-start(bf16[384,512]{1,0:T(8,128)(2,1)S(1)} %get-tuple-element.33), channel_id=1, source_target_pairs={{0,16},{8,24},{16,0},{24,8},{1,17},{9,25},{17,1},{25,9},{2,18},{10... | collective-permute-start | bytes 1179656 | tf_op jit(solution)/shard_map/ppermute | solution.py:435
  11.9 7.0 %copy-start.15 = (s32[4]{0:T(128)S(1)}, s32[4]{0:T(128)}, u32[]{:S(2)}) copy-start(s32[4]{0:T(128)} %copy-done.14) | copy-start | bytes 52
  11.9 7.7 %copy-start.23 = (s32[8]{0:T(128)S(1)}, s32[8]{0:T(128)}, u32[]{:S(2)}) copy-start(s32[8]{0:T(128)} %constant.76.clone) | copy-start | bytes 100
  17.3 6.1 %collective-permute-start.4 = (bf16[2,48,1088]{2,1,0:T(8,128)(2,1)S(1)}, bf16[2,48,1088]{2,1,0:T(8,128)(2,1)S(1)}, u32[]{:S(2)}, u32[]{:S(2)}) collective-permute-start(bf16[2,48,1088]{2,1,0:T(8,128)(2,1)S(1)} %pad_maximum_fusion.2), channel_id=1, source_target_pairs={{0,2},{1,3},{2,0},{3,1},{4,6},{5,7},{6,4},{7,5},{8,10},{9,11},{10,... | collective-permute-start | bytes 626696 | tf_op jit(solution)/shard_map/ppermute | solution.py:455
  23.5 3.8 %copy-start.20 = (bf16[384,512]{1,0:T(8,128)(2,1)}, bf16[384,512]{1,0:T(8,128)(2,1)S(1)}, u32[]{:S(2)}) copy-start(bf16[384,512]{1,0:T(8,128)(2,1)S(1)} %collective-permute-done.refs_0_) | copy-start | bytes 1179652
  38.7 3.6 %copy-start.22 = (s32[4]{0:T(128)S(1)}, s32[4]{0:T(128)}, u32[]{:S(2)}) copy-start(s32[4]{0:T(128)} %constant.75.clone) | copy-start | bytes 52
  38.7 41.3 %all-to-all-start = ((bf16[8,4,192,128]{3,2,1,0:T(8,128)(2,1)}), bf16[8,4,192,128]{3,2,1,0:T(8,128)(2,1)S(1)}, u32[]{:S(2)}, u32[]{:S(2)}) async-start(bf16[8,4,192,128]{3,2,1,0:T(8,128)(2,1)} %get-tuple-element.41), calls=%async_computation | async-start | bytes 3145728 | tf_op jit(solution)/shard_map/all_to_all | solution.py:439
  42.5 1.9 collective-permute-start.5
  95.3 41.6 %all-to-all-start.1 = ((bf16[32,192,128]{2,1,0:T(8,128)(2,1)}), bf16[32,192,128]{2,1,0:T(8,128)(2,1)S(1)}, u32[]{:S(2)}, u32[]{:S(2)}) async-start(bf16[32,192,128]{2,1,0:T(8,128)(2,1)} %bitcast.7), calls=%async_computation.1 | async-start | bytes 3145728 | tf_op jit(solution)/shard_map/all_to_all | solution.py:529
  98.2 10.2 %collective-permute-start.6 = (s32[384]{0:T(512)S(1)}, s32[384]{0:T(512)S(1)}, u32[]{:S(2)}, u32[]{:S(2)}) collective-permute-start(s32[384]{0:T(512)S(1)} %get-tuple-element.55), channel_id=1, source_target_pairs={{0,24},{8,16},{16,8},{24,0},{1,25},{9,17},{17,9},{25,1},{2,26},{10... | collective-permute-start | bytes 4616 | tf_op jit(solution)/shard_map/ppermute | solution.py:435
  100.8 7.6 %collective-permute-start.8 = (s32[384]{0:T(512)S(1)}, s32[384]{0:T(512)S(1)}, u32[]{:S(2)}, u32[]{:S(2)}) collective-permute-start(s32[384]{0:T(512)S(1)} %get-tuple-element.56), channel_id=1, source_target_pairs={{0,16},{8,24},{16,0},{24,8},{1,17},{9,25},{17,1},{25,9},{2,18},{10... | collective-permute-start | bytes 4616 | tf_op jit(solution)/shard_map/ppermute | solution.py:435
  101.3 7.3 %collective-permute-start.7 = (s32[384]{0:T(512)S(1)}, s32[384]{0:T(512)S(1)}, u32[]{:S(2)}, u32[]{:S(2)}) collective-permute-start(s32[384]{0:T(512)S(1)} %get-tuple-element.57), channel_id=1, source_target_pairs={{0,8},{8,0},{16,24},{24,16},{1,9},{9,1},{17,25},{25,17},{2,10},{10... | collective-permute-start | bytes 4616 | tf_op jit(solution)/shard_map/ppermute | solution.py:435
  138.3 4.4 %copy-start.3 = (bf16[4,384,512]{2,1,0:T(8,128)(2,1)S(1)}, bf16[4,384,512]{2,1,0:T(8,128)(2,1)}, u32[]{:S(2)}) copy-start(bf16[4,384,512]{2,1,0:T(8,128)(2,1)} %get-tuple-element.36.second_ref) | copy-start | bytes 4718596
  142.1 13.0 %collective-permute-start.11 = (bf16[384,512]{1,0:T(8,128)(2,1)S(1)}, bf16[384,512]{1,0:T(8,128)(2,1)S(1)}, u32[]{:S(2)}, u32[]{:S(2)}) collective-permute-start(bf16[384,512]{1,0:T(8,128)(2,1)S(1)} %slice_bitcast_fusion), channel_id=1, source_target_pairs={{0,24},{8,16},{16,8},{24,0},{1,25},{9,17},{17,9},{25,1},{2,26},{10... | collective-permute-start | bytes 1179656 | tf_op jit(solution)/shard_map/ppermute | solution.py:435
  142.6 12.5 %copy-start.5 = (bf16[2,512,512]{2,1,0:T(8,128)(2,1)S(1)}, bf16[2,512,512]{2,1,0:T(8,128)(2,1)}, u32[]{:S(2)}) copy-start(bf16[2,512,512]{2,1,0:T(8,128)(2,1)} %wr.7) | copy-start | bytes 3145732
  142.6 12.5 %copy-start.6 = (bf16[2,512,512]{2,1,0:T(8,128)(2,1)S(1)}, bf16[2,512,512]{2,1,0:T(8,128)(2,1)}, u32[]{:S(2)}) copy-start(bf16[2,512,512]{2,1,0:T(8,128)(2,1)} %wc.7) | copy-start | bytes 3145732
  142.7 12.5 %copy-start.7 = (bf16[2,512,512]{2,1,0:T(8,128)(2,1)S(1)}, bf16[2,512,512]{2,1,0:T(8,128)(2,1)}, u32[]{:S(2)}) copy-start(bf16[2,512,512]{2,1,0:T(8,128)(2,1)} %wi.7) | copy-start | bytes 3145732
  142.7 12.5 %copy-start.8 = (bf16[2,512,512]{2,1,0:T(8,128)(2,1)S(1)}, bf16[2,512,512]{2,1,0:T(8,128)(2,1)}, u32[]{:S(2)}) copy-start(bf16[2,512,512]{2,1,0:T(8,128)(2,1)} %wo.7) | copy-start | bytes 3145732
  146.4 8.7 %copy-start.4 = (bf16[2,512,512]{2,1,0:T(8,128)(2,1)S(1)}, bf16[2,512,512]{2,1,0:T(8,128)(2,1)}, u32[]{:S(2)}) copy-start(bf16[2,512,512]{2,1,0:T(8,128)(2,1)} %wm.7) | copy-start | bytes 3145732
  146.4 8.7 %copy-start.12 = (s32[4,1,384]{2,1,0:T(1,128)S(1)}, s32[4,1,384]{2,1,0:T(1,128)}, u32[]{:S(2)}) copy-start(s32[4,1,384]{2,1,0:T(1,128)} %broadcast_in_dim.199.rank_ref) | copy-start | bytes 18436
  146.4 8.7 %copy-start.13 = (s32[4,1,384]{2,1,0:T(1,128)S(1)}, s32[4,1,384]{2,1,0:T(1,128)}, u32[]{:S(2)}) copy-start(s32[4,1,384]{2,1,0:T(1,128)} %broadcast_in_dim.197.back_ref) | copy-start | bytes 18436
  146.5 15.6 %collective-permute-start.10 = (bf16[384,512]{1,0:T(8,128)(2,1)S(1)}, bf16[384,512]{1,0:T(8,128)(2,1)S(1)}, u32[]{:S(2)}, u32[]{:S(2)}) collective-permute-start(bf16[384,512]{1,0:T(8,128)(2,1)S(1)} %get-tuple-element.66), channel_id=1, source_target_pairs={{0,16},{8,24},{16,0},{24,8},{1,17},{9,25},{17,1},{25,9},{2,18},{10... | collective-permute-start | bytes 1179656 | tf_op jit(solution)/shard_map/ppermute | solution.py:435
  147.1 15.0 %collective-permute-start.9 = (bf16[384,512]{1,0:T(8,128)(2,1)S(1)}, bf16[384,512]{1,0:T(8,128)(2,1)S(1)}, u32[]{:S(2)}, u32[]{:S(2)}) collective-permute-start(bf16[384,512]{1,0:T(8,128)(2,1)S(1)} %get-tuple-element.67), channel_id=1, source_target_pairs={{0,8},{8,0},{16,24},{24,16},{1,9},{9,1},{17,25},{25,17},{2,10},{10... | collective-permute-start | bytes 1179656 | tf_op jit(solution)/shard_map/ppermute | solution.py:435
  155.2 52.5 %slice-start = ((s8[6291456]{0:T(1024)(128)(4,1)}), s8[4194304]{0:T(1024)(128)(4,1)S(1)}, s32[]{:S(2)}) async-start(s8[6291456]{0:T(1024)(128)(4,1)} %bitcast.50), calls=%async_computation.4 | async-start | bytes 8388608
  162.1 45.6 %slice-start.1 = ((s8[6291456]{0:T(1024)(128)(4,1)}), s8[2097152]{0:T(1024)(128)(4,1)S(1)}, s32[]{:S(2)}) async-start(s8[6291456]{0:T(1024)(128)(4,1)} %bitcast.50), calls=%async_computation.5 | async-start | bytes 4194304
  219.0 40.9 %copy-start.9 = (bf16[2,512,512]{2,1,0:T(8,128)(2,1)S(1)}, bf16[2,512,512]{2,1,0:T(8,128)(2,1)}, u32[]{:S(2)}) copy-start(bf16[2,512,512]{2,1,0:T(8,128)(2,1)} %wd.1) | copy-start | bytes 3145732
  219.0 40.9 %copy-start.10 = (bf16[2,512,512]{2,1,0:T(8,128)(2,1)S(1)}, bf16[2,512,512]{2,1,0:T(8,128)(2,1)}, u32[]{:S(2)}) copy-start(bf16[2,512,512]{2,1,0:T(8,128)(2,1)} %we.1) | copy-start | bytes 3145732
  219.0 40.9 %copy-start.11 = (bf16[2,512,512]{2,1,0:T(8,128)(2,1)S(1)}, bf16[2,512,512]{2,1,0:T(8,128)(2,1)}, u32[]{:S(2)}) copy-start(bf16[2,512,512]{2,1,0:T(8,128)(2,1)} %wl.1) | copy-start | bytes 3145732
  (11 other events, 21.0 us)

commit v8 on v7

--- a/solution.py
+++ b/solution.py
@@ -12,7 +12,7 @@
 LANES = 128
 HALF = LANES // 2
 GROUP = 8
-PAIR = 2
+PAIR = 4
 
 
 ROOT_HALF = 0.7071067811865476
@@ -482,7 +482,8 @@
     position = jnp.sum(jnp.where(owners_wide == jnp.arange(wide), inverse, 0), axis=1)
     half = wide // 2
     pieces = [(0, 1), (1, wide - 1)]
-    halves = [(0, half), (half, wide - half)]
+    halves = [(half, wide - half), (0, half)]
+    later = [(half, wide - half), (0, 1), (1, half - 1)]
 
     blocks_of = messages.reshape(wide, rows, features)
     sent = [
@@ -502,7 +503,7 @@
     for section in range(BLOCKS):
         last = section == BLOCKS - 1
         targets = []
-        for start, count in halves if section else pieces:
+        for start, count in later if section else pieces:
             array, where = current[start]
             needed = [received[offset] for offset in offsets[start : start + count] if offset]
             targets = list(run_front(
@@ -535,7 +536,9 @@
             plain = jnp.arange(count, dtype=jnp.int32)
             where = order[start : start + count]
             result = run_back(second, returned, where, plain, start, turned_rank, late, at, count)
-            current[start] = (result, plain)
+            for first, number in later:
+                if start <= first < start + count:
+                    current[first] = (result, first - start + jnp.arange(number, dtype=jnp.int32))
             for index, offset in enumerate(offsets[start : start + count]):
                 if offset:
                     received[offset] = shift(result[index], offset, wide)
@@ -575,6 +578,7 @@
         and unit % 16 == 0
         and narrow % 2 == 0
         and wide >= 4
+        and narrow % PAIR == 0
         and wide & (wide - 1) == 0
         and narrow & (narrow - 1) == 0
         and angles.shape[0] % GROUP == 0

time: 268 us -> 264 us (0.985)
    pallas_call x4 -> x5, Pallas kernels: 26.6 us -> 25.6 us  [run_front(): pl.pallas_call(functools.partial(front_kernel, own, count), grid_spec=plt...]
  transfers between devices with their start and end apart: 14 -> 14, of which waited for: 9 -> 10; matrix products, arithmetic and copies ran while one was open for 2% -> 2% of each run, Pallas kernels for 8% -> 9%
where the time goes in v8:
time: 264 us; the launch traced here: 263 us
  blocking collectives  81.3 us (31%)
  waiting for transfers between devices  72 us (27%)
  Pallas kernels  70 us (27%)
  starting transfers between devices  23.2 us (9%)
  local copies, waits for them, and re-layouts  13.2 us (5%)
  other arithmetic  3.24 us (1%)
    all_to_all x1, blocking collectives, tiled_local(): returned = lax.all_to_all(mixed, ('wide', 'narrow'), 0, 0, tiled=True)  41 us
    all_to_all x1, blocking collectives, swap(): return lax.all_to_all(values, 'narrow', 0, 0, tiled=True)  40.3 us
    all_to_all x1, waiting for transfers between devices, tiled_local(): returned = lax.all_to_all(mixed, ('wide', 'narrow'), 0, 0, tiled=True)  26.1 us
    pallas_call x5, Pallas kernels, run_front(): pl.pallas_call(functools.partial(front_kernel, own, count), grid_spec=plt...  25.6 us
    all_to_all x1, waiting for transfers between devices, swap(): return lax.all_to_all(values, 'narrow', 0, 0, tiled=True)  25 us
    pallas_call x2, Pallas kernels, run_mix(): pl.pallas_call(mix_kernel, grid=(devices // PAIR,), in_specs=[smem, smem,...  22.2 us
    ppermute x9, waiting for transfers between devices, shift(): return lax.ppermute(values, 'wide', [(i, i ^ offset) for i in range(wide)])  15.9 us
    pallas_call x3, Pallas kernels, run_back(): pl.pallas_call(back_kernel, grid_spec=pltpu.PrefetchScalarGridSpec(num_sc...  15.2 us
  transfers between devices with their start and end apart: 14, of which 10 were waited for; matrix products, arithmetic and copies ran while one was open for 2% of the time, Pallas kernels for 9%

profile of v8, /device:TPU:0, one launch (start us, length us, event | category | flops | bytes accessed | tf_op | source)
XLA Modules:
  0.0 263.4 jit_solution(1624568609929059510)
XLA Ops:
  0.8 1.3 dynamic-slice_bitcast_fusion
  3.1 4.1 %collective-permute-start.3 = (bf16[1,48,1088]{2,1,0:T(8,128)(2,1)S(1)}, bf16[1,48,1088]{2,1,0:T(8,128)(2,1)S(1)}, u32[]{:S(2)}, u32[]{:S(2)}) collective-permute-start(bf16[1,48,1088]{2,1,0:T(8,128)(2,1)S(1)} %maximum_bitcast_fusion), channel_id=1, source_target_pairs={{0,4},{1,5},{2,6},{3,7},{4,0},{5,1},{6,2},{7,3},{8,12},{9,13},{10,... | collective-permute-start | bytes 313352 | tf_op jit(solution)/shard_map/ppermute | solution.py:455
  7.2 2.4 collective-permute-start
  11.9 5.3 %front.5 = (bf16[4,384,512]{2,1,0:T(8,128)(2,1)}, bf16[8,4,192,128]{3,2,1,0:T(8,128)(2,1)}) custom-call(s32[1]{0:T(128)} %bitcast.56, bf16[4,384,512]{2,1,0:T(8,128)(2,1)} %bitcast.58, s32[4,1,384]{2,1,0:T(1,128)} %broadcast_in_dim.199.back_ref, s32[4,1,384]{2,1,0:T(1,128)} %broadcast_in_dim.201.rank_ref, bf16[2,512,512]{2,1,0:T(8,128)(2,1)} %wm.9, ...), custom_call_target="tpu_custom_call" | custom-call | flops 1207959552 | bytes 1572864 | tf_op jit(solution)/shard_map/front/pallas_call | solution.py:293
  17.3 1.6 collective-permute-start.4
  19.8 3.7 %collective-permute-done.4 = bf16[2,48,1088]{2,1,0:T(8,128)(2,1)S(1)} collective-permute-done((bf16[2,48,1088]{2,1,0:T(8,128)(2,1)S(1)}, bf16[2,48,1088]{2,1,0:T(8,128)(2,1)S(1)}, u32[]{:S(2)}, u32[]{:S(2)}) %collective-permute-start.4) | collective-permute-done | bytes 208928 | tf_op jit(solution)/shard_map/ppermute | solution.py:455
  23.5 3.7 %collective-permute-done.1.refs_1_ = bf16[384,512]{1,0:T(8,128)(2,1)S(1)} collective-permute-done((bf16[384,512]{1,0:T(8,128)(2,1)S(1)}, bf16[384,512]{1,0:T(8,128)(2,1)S(1)}, u32[]{:S(2)}, u32[]{:S(2)}) %collective-permute-start.1) | collective-permute-done | bytes 393248 | tf_op jit(solution)/shard_map/ppermute | solution.py:435
  28.0 10.7 %front.6 = (bf16[4,384,512]{2,1,0:T(8,128)(2,1)}, bf16[8,4,192,128]{3,2,1,0:T(8,128)(2,1)}) custom-call(s32[3]{0:T(128)} %slice.52.where_ref, bf16[4,384,512]{2,1,0:T(8,128)(2,1)} %bitcast.59, s32[4,1,384]{2,1,0:T(1,128)} %broadcast_in_dim.199.back_ref, s32[4,1,384]{2,1,0:T(1,128)} %broadcast_in_dim.201.rank_ref, ...), custom_call_target="tpu_custom_call", output_to_operand_aliasing={{0}: (12, {}), {1}: (13, {})} | custom-call | flops 3623878656 | bytes 4718592 | tf_op jit(solution)/shard_map/front/pallas_call | solution.py:293
  38.7 3.6 %all-to-all-start = ((bf16[8,4,192,128]{3,2,1,0:T(8,128)(2,1)}), bf16[8,4,192,128]{3,2,1,0:T(8,128)(2,1)S(1)}, u32[]{:S(2)}, u32[]{:S(2)}) async-start(bf16[8,4,192,128]{3,2,1,0:T(8,128)(2,1)} %get-tuple-element.43), calls=%async_computation | async-start | bytes 3145728 | tf_op jit(solution)/shard_map/all_to_all | solution.py:439
  43.1 1.3 collective-permute-done.5
  44.9 7.0 %tables.1 = (s32[8,4,1,384]{3,2,1,0:T(1,128)S(1)}, bf16[8,6,256,256]{3,2,1,0:T(8,128)(2,1)S(1)}) custom-call(s32[8]{0:T(128)S(1)} %select_reduce_fusion.9.places_ref, s32[4]{0:T(128)S(1)} %copy-done.15, s32[4]{0:T(128)S(1)} %select_reduce_fusion.10.position_ref, s32[8,4,1,384]{3,2,1,0:T(1,128)S(1)} %broadcast_in_dim_reshape.2.entry_ref, ...), custom_call_target="tpu_custom_call" | custom-call | bytes 25165824 | tf_op jit(solution)/shard_map/tables/pallas_call | solution.py:356
  51.9 2.7 %copy-done = bf16[8,6,256,256]{3,2,1,0:T(8,128)(2,1)} copy-done((bf16[8,6,256,256]{3,2,1,0:T(8,128)(2,1)}, bf16[8,6,256,256]{3,2,1,0:T(8,128)(2,1)S(1)}, u32[]{:S(2)}) %copy-start) | copy-done | bytes 6291480
  55.1 25.0 %all-to-all-done.recv_ref = bf16[8,4,192,128]{3,2,1,0:T(8,128)(2,1)S(1)} async-done(((bf16[8,4,192,128]{3,2,1,0:T(8,128)(2,1)}), bf16[8,4,192,128]{3,2,1,0:T(8,128)(2,1)S(1)}, u32[]{:S(2)}, u32[]{:S(2)}) %all-to-all-start) | async-done | bytes 1572896 | tf_op jit(solution)/shard_map/all_to_all | solution.py:439
  80.1 2.8 %copy-done.1 = bf16[8,6,256,256]{3,2,1,0:T(8,128)(2,1)S(1)} copy-done((bf16[8,6,256,256]{3,2,1,0:T(8,128)(2,1)S(1)}, bf16[8,6,256,256]{3,2,1,0:T(8,128)(2,1)}, u32[]{:S(2)}) %copy-start.1) | copy-done | bytes 6291480
  82.8 11.7 %mix.2 = bf16[4,8,192,128]{3,2,1,0:T(8,128)(2,1)} custom-call(s32[8,8]{1,0:T(8,128)S(1)} %get-tuple-element.58.owner_ref, s32[8,8]{1,0:T(8,128)S(1)} %get-tuple-element.57.place_ref, s32[4]{0:T(128)S(1)} %copy-done.15, bf16[8,4,192,128]{3,2,1,0:T(8,128)(2,1)S(1)} %all-to-all-done.recv_ref, s32[8,4,1,384]{3,2,1,0:T(1,128)S(1)} %get-tuple-element.44.rank_ref, ...), custom_call_target="tpu_custom_call" | custom-call | flops 1509949440 | bytes 18874368 | tf_op jit(solution)/shard_map/mix/pallas_call | solution.py:386
  94.5 2.9 %all-to-all-start.1 = ((bf16[32,192,128]{2,1,0:T(8,128)(2,1)}), bf16[32,192,128]{2,1,0:T(8,128)(2,1)S(1)}, u32[]{:S(2)}, u32[]{:S(2)}) async-start(bf16[32,192,128]{2,1,0:T(8,128)(2,1)} %bitcast.7), calls=%async_computation.1 | async-start | bytes 3145728 | tf_op jit(solution)/shard_map/all_to_all | solution.py:530
  97.5 2.6 collective-permute-start.6
  101.1 6.6 %collective-permute-done.6 = s32[384]{0:T(512)S(1)} collective-permute-done((s32[384]{0:T(512)S(1)}, s32[384]{0:T(512)S(1)}, u32[]{:S(2)}, u32[]{:S(2)}) %collective-permute-start.6) | collective-permute-done | bytes 1568 | tf_op jit(solution)/shard_map/ppermute | solution.py:435
  110.0 26.1 %all-to-all-done.1 = bf16[32,192,128]{2,1,0:T(8,128)(2,1)S(1)} async-done(((bf16[32,192,128]{2,1,0:T(8,128)(2,1)}), bf16[32,192,128]{2,1,0:T(8,128)(2,1)S(1)}, u32[]{:S(2)}, u32[]{:S(2)}) %all-to-all-start.1) | async-done | bytes 1572896 | tf_op jit(solution)/shard_map/all_to_all | solution.py:530
  136.1 1.4 copy-done.7
  137.5 3.7 %back.4.cur_ref = bf16[2,384,512]{2,1,0:T(8,128)(2,1)S(1)} custom-call(s32[2]{0:T(128)S(1)} %get-tuple-element.77.from_ref, s32[2]{0:T(128)S(1)} %iota.77.to_ref, bf16[4,384,512]{2,1,0:T(8,128)(2,1)S(1)} %copy-done.7, bf16[4,8,192,128]{3,2,1,0:T(8,128)(2,1)S(1)} %bitcast.52, s32[4,1,384]{2,1,0:T(1,128)S(1)} %broadcast_in_dim.220.rank_ref, ...), custom_call_target="tpu_custom_call" | custom-call | flops 1610612736 | bytes 2359296 | tf_op jit(solution)/shard_map/back/pallas_call | solution.py:327
  142.7 3.7 %back.3.cur_ref = bf16[2,384,512]{2,1,0:T(8,128)(2,1)S(1)} custom-call(s32[2]{0:T(128)S(1)} %get-tuple-element.78.from_ref, s32[2]{0:T(128)S(1)} %iota.73.to_ref, bf16[4,384,512]{2,1,0:T(8,128)(2,1)S(1)} %copy-done.8, bf16[4,8,192,128]{3,2,1,0:T(8,128)(2,1)S(1)} %bitcast.53, s32[4,1,384]{2,1,0:T(1,128)S(1)} %broadcast_in_dim.220.rank_ref, ...), custom_call_target="tpu_custom_call" | custom-call | flops 1610612736 | bytes 2359296 | tf_op jit(solution)/shard_map/back/pallas_call | solution.py:327
  146.5 2.3 collective-permute-start.9
  148.8 3.8 %collective-permute-done.11.refs_1_ = bf16[384,512]{1,0:T(8,128)(2,1)S(1)} collective-permute-done((bf16[384,512]{1,0:T(8,128)(2,1)S(1)}, bf16[384,512]{1,0:T(8,128)(2,1)S(1)}, u32[]{:S(2)}, u32[]{:S(2)}) %collective-permute-start.11) | collective-permute-done | bytes 393248 | tf_op jit(solution)/shard_map/ppermute | solution.py:435
  152.6 1.4 collective-permute-done.10.refs_0_
  154.0 5.3 %front.7 = (bf16[4,384,512]{2,1,0:T(8,128)(2,1)S(1)}, bf16[8,4,192,128]{3,2,1,0:T(8,128)(2,1)S(1)}) custom-call(s32[2]{0:T(128)S(1)} %iota.76.where_ref, bf16[2,384,512]{2,1,0:T(8,128)(2,1)S(1)} %back.4.cur_ref, s32[4,1,384]{2,1,0:T(1,128)S(1)} %copy-done.13, s32[4,1,384]{2,1,0:T(1,128)S(1)} %copy-done.12, bf16[2,512,512]{2,1,0:T(8,128)(2,1)S(1)} %copy-done.2, ...), custom_call_target="tpu_custom_call" | custom-call | flops 2415919104 | bytes 3145728 | tf_op jit(solution)/shard_map/front/pallas_call | solution.py:293
  159.3 2.1 front.8
  161.7 2.1 front.9
  163.8 40.3 %all_to_all.20.recv_ref = bf16[8,4,192,128]{3,2,1,0:T(8,128)(2,1)S(1)} all-to-all(bf16[8,4,192,128]{3,2,1,0:T(8,128)(2,1)S(1)} %get-tuple-element.56), channel_id=1, replica_groups=mesh['wide'=4,'narrow'=8] {'narrow'}, dimensions={0} | all-to-all | bytes 3145728 | tf_op jit(solution)/shard_map/all_to_all | solution.py:439
  204.1 10.6 %mix.3 = bf16[4,8,192,128]{3,2,1,0:T(8,128)(2,1)S(1)} custom-call(s32[8,8]{1,0:T(8,128)S(1)} %get-tuple-element.58.owner_ref, s32[8,8]{1,0:T(8,128)S(1)} %get-tuple-element.57.place_ref, s32[4]{0:T(128)S(1)} %copy-done.15, bf16[8,4,192,128]{3,2,1,0:T(8,128)(2,1)S(1)} %all_to_all.20.recv_ref, s32[8,4,1,384]{3,2,1,0:T(1,128)S(1)} %get-tuple-element.44.rank_ref, ...), custom_call_target="tpu_custom_call" | custom-call | flops 1509949440 | bytes 18874368 | tf_op jit(solution)/shard_map/mix/pallas_call | solution.py:386
  214.7 41.0 %all_to_all.21 = bf16[32,192,128]{2,1,0:T(8,128)(2,1)S(1)} all-to-all(bf16[32,192,128]{2,1,0:T(8,128)(2,1)S(1)} %bitcast.54), channel_id=1, replica_groups=mesh['wide'=4,'narrow'=8] {'wide','narrow'}, dimensions={0} | all-to-all | bytes 3145728 | tf_op jit(solution)/shard_map/all_to_all | solution.py:530
  255.7 7.7 %back.5 = bf16[4,384,512]{2,1,0:T(8,128)(2,1)} custom-call(s32[4]{0:T(128)S(1)} %copy-done.15, s32[4]{0:T(128)S(1)} %copy-done.15, bf16[4,384,512]{2,1,0:T(8,128)(2,1)S(1)} %get-tuple-element.55.second_ref, bf16[4,8,192,128]{3,2,1,0:T(8,128)(2,1)S(1)} %bitcast.55, s32[4,1,384]{2,1,0:T(1,128)S(1)} %broadcast_in_dim.220.rank_ref, ...), custom_call_target="tpu_custom_call" | custom-call | flops 3221225472 | bytes 4718592 | tf_op jit(solution)/shard_map/back/pallas_call | solution.py:327
  (121 shorter events, 12.4 us)
Async XLA Ops:
  0.0 3.1 %copy-start.16 = (bf16[48,1024]{1,0:T(8,128)(2,1)S(1)}, bf16[48,1024]{1,0:T(8,128)(2,1)}, u32[]{:S(2)}) copy-start(bf16[48,1024]{1,0:T(8,128)(2,1)} %param.20) | copy-start | bytes 294916
  0.7 10.0 %copy-start.14 = (s32[4]{0:T(128)}, s32[4]{0:T(128)S(1)}, u32[]{:S(2)}) copy-start(s32[4]{0:T(128)S(1)} %broadcast_xor_fusion.order_ref.from_ref.to_ref) | copy-start | bytes 52
  3.1 14.2 %collective-permute-start.3 = (bf16[1,48,1088]{2,1,0:T(8,128)(2,1)S(1)}, bf16[1,48,1088]{2,1,0:T(8,128)(2,1)S(1)}, u32[]{:S(2)}, u32[]{:S(2)}) collective-permute-start(bf16[1,48,1088]{2,1,0:T(8,128)(2,1)S(1)} %maximum_bitcast_fusion), channel_id=1, source_target_pairs={{0,4},{1,5},{2,6},{3,7},{4,0},{5,1},{6,2},{7,3},{8,12},{9,13},{10,... | collective-permute-start | bytes 313352 | tf_op jit(solution)/shard_map/ppermute | solution.py:455
  7.2 16.3 %collective-permute-start = (bf16[384,512]{1,0:T(8,128)(2,1)S(1)}, bf16[384,512]{1,0:T(8,128)(2,1)S(1)}, u32[]{:S(2)}, u32[]{:S(2)}) collective-permute-start(bf16[384,512]{1,0:T(8,128)(2,1)S(1)} %get-tuple-element.33), channel_id=1, source_target_pairs={{0,24},{8,16},{16,8},{24,0},{1,25},{9,17},{17,9},{25,1},{2,26},{10... | collective-permute-start | bytes 1179656 | tf_op jit(solution)/shard_map/ppermute | solution.py:435
  9.7 17.6 %collective-permute-start.1 = (bf16[384,512]{1,0:T(8,128)(2,1)S(1)}, bf16[384,512]{1,0:T(8,128)(2,1)S(1)}, u32[]{:S(2)}, u32[]{:S(2)}) collective-permute-start(bf16[384,512]{1,0:T(8,128)(2,1)S(1)} %get-tuple-element.34), channel_id=1, source_target_pairs={{0,8},{8,0},{16,24},{24,16},{1,9},{9,1},{17,25},{25,17},{2,10},{10... | collective-permute-start | bytes 1179656 | tf_op jit(solution)/shard_map/ppermute | solution.py:435
  10.2 17.0 %collective-permute-start.2 = (bf16[384,512]{1,0:T(8,128)(2,1)S(1)}, bf16[384,512]{1,0:T(8,128)(2,1)}, u32[]{:S(2)}, u32[]{:S(2)}) collective-permute-start(bf16[384,512]{1,0:T(8,128)(2,1)S(1)} %get-tuple-element.35), channel_id=1, source_target_pairs={{0,16},{8,24},{16,0},{24,8},{1,17},{9,25},{17,1},{25,9},{2,18},{10... | collective-permute-start | bytes 1179656 | tf_op jit(solution)/shard_map/ppermute | solution.py:435
  11.9 7.1 %copy-start.15 = (s32[4]{0:T(128)S(1)}, s32[4]{0:T(128)}, u32[]{:S(2)}) copy-start(s32[4]{0:T(128)} %copy-done.14) | copy-start | bytes 52
  11.9 7.6 %copy-start.23 = (s32[8]{0:T(128)S(1)}, s32[8]{0:T(128)}, u32[]{:S(2)}) copy-start(s32[8]{0:T(128)} %constant.80.clone) | copy-start | bytes 100
  17.3 6.1 %collective-permute-start.4 = (bf16[2,48,1088]{2,1,0:T(8,128)(2,1)S(1)}, bf16[2,48,1088]{2,1,0:T(8,128)(2,1)S(1)}, u32[]{:S(2)}, u32[]{:S(2)}) collective-permute-start(bf16[2,48,1088]{2,1,0:T(8,128)(2,1)S(1)} %pad_maximum_fusion.2), channel_id=1, source_target_pairs={{0,2},{1,3},{2,0},{3,1},{4,6},{5,7},{6,4},{7,5},{8,10},{9,11},{10,... | collective-permute-start | bytes 626696 | tf_op jit(solution)/shard_map/ppermute | solution.py:455
  23.5 3.7 %copy-start.20 = (bf16[384,512]{1,0:T(8,128)(2,1)}, bf16[384,512]{1,0:T(8,128)(2,1)S(1)}, u32[]{:S(2)}) copy-start(bf16[384,512]{1,0:T(8,128)(2,1)S(1)} %collective-permute-done.refs_0_) | copy-start | bytes 1179652
  38.7 3.6 %copy-start.22 = (s32[4]{0:T(128)S(1)}, s32[4]{0:T(128)}, u32[]{:S(2)}) copy-start(s32[4]{0:T(128)} %constant.79.clone) | copy-start | bytes 52
  38.7 41.3 %all-to-all-start = ((bf16[8,4,192,128]{3,2,1,0:T(8,128)(2,1)}), bf16[8,4,192,128]{3,2,1,0:T(8,128)(2,1)S(1)}, u32[]{:S(2)}, u32[]{:S(2)}) async-start(bf16[8,4,192,128]{3,2,1,0:T(8,128)(2,1)} %get-tuple-element.43), calls=%async_computation | async-start | bytes 3145728 | tf_op jit(solution)/shard_map/all_to_all | solution.py:439
  42.5 1.9 collective-permute-start.5
  94.5 41.6 %all-to-all-start.1 = ((bf16[32,192,128]{2,1,0:T(8,128)(2,1)}), bf16[32,192,128]{2,1,0:T(8,128)(2,1)S(1)}, u32[]{:S(2)}, u32[]{:S(2)}) async-start(bf16[32,192,128]{2,1,0:T(8,128)(2,1)} %bitcast.7), calls=%async_computation.1 | async-start | bytes 3145728 | tf_op jit(solution)/shard_map/all_to_all | solution.py:530
  97.5 10.2 %collective-permute-start.6 = (s32[384]{0:T(512)S(1)}, s32[384]{0:T(512)S(1)}, u32[]{:S(2)}, u32[]{:S(2)}) collective-permute-start(s32[384]{0:T(512)S(1)} %get-tuple-element.59), channel_id=1, source_target_pairs={{0,24},{8,16},{16,8},{24,0},{1,25},{9,17},{17,9},{25,1},{2,26},{10... | collective-permute-start | bytes 4616 | tf_op jit(solution)/shard_map/ppermute | solution.py:435
  100.0 7.6 %collective-permute-start.8 = (s32[384]{0:T(512)S(1)}, s32[384]{0:T(512)S(1)}, u32[]{:S(2)}, u32[]{:S(2)}) collective-permute-start(s32[384]{0:T(512)S(1)} %get-tuple-element.60), channel_id=1, source_target_pairs={{0,16},{8,24},{16,0},{24,8},{1,17},{9,25},{17,1},{25,9},{2,18},{10... | collective-permute-start | bytes 4616 | tf_op jit(solution)/shard_map/ppermute | solution.py:435
  100.6 7.3 %collective-permute-start.7 = (s32[384]{0:T(512)S(1)}, s32[384]{0:T(512)S(1)}, u32[]{:S(2)}, u32[]{:S(2)}) collective-permute-start(s32[384]{0:T(512)S(1)} %get-tuple-element.61), channel_id=1, source_target_pairs={{0,8},{8,0},{16,24},{24,16},{1,9},{9,1},{17,25},{25,17},{2,10},{10... | collective-permute-start | bytes 4616 | tf_op jit(solution)/shard_map/ppermute | solution.py:435
  141.3 11.2 %collective-permute-start.11 = (bf16[384,512]{1,0:T(8,128)(2,1)S(1)}, bf16[384,512]{1,0:T(8,128)(2,1)S(1)}, u32[]{:S(2)}, u32[]{:S(2)}) collective-permute-start(bf16[384,512]{1,0:T(8,128)(2,1)S(1)} %get-tuple-element.70), channel_id=1, source_target_pairs={{0,16},{8,24},{16,0},{24,8},{1,17},{9,25},{17,1},{25,9},{2,18},{10... | collective-permute-start | bytes 1179656 | tf_op jit(solution)/shard_map/ppermute | solution.py:435
  142.0 12.0 %collective-permute-start.10 = (bf16[384,512]{1,0:T(8,128)(2,1)S(1)}, bf16[384,512]{1,0:T(8,128)(2,1)S(1)}, u32[]{:S(2)}, u32[]{:S(2)}) collective-permute-start(bf16[384,512]{1,0:T(8,128)(2,1)S(1)} %get-tuple-element.71), channel_id=1, source_target_pairs={{0,8},{8,0},{16,24},{24,16},{1,9},{9,1},{17,25},{25,17},{2,10},{10... | collective-permute-start | bytes 1179656 | tf_op jit(solution)/shard_map/ppermute | solution.py:435
  142.7 11.3 %copy-start.2 = (bf16[2,512,512]{2,1,0:T(8,128)(2,1)S(1)}, bf16[2,512,512]{2,1,0:T(8,128)(2,1)}, u32[]{:S(2)}) copy-start(bf16[2,512,512]{2,1,0:T(8,128)(2,1)} %wm.9) | copy-start | bytes 3145732
  142.7 11.3 %copy-start.3 = (bf16[2,512,512]{2,1,0:T(8,128)(2,1)S(1)}, bf16[2,512,512]{2,1,0:T(8,128)(2,1)}, u32[]{:S(2)}) copy-start(bf16[2,512,512]{2,1,0:T(8,128)(2,1)} %wr.9) | copy-start | bytes 3145732
  142.7 11.3 %copy-start.4 = (bf16[2,512,512]{2,1,0:T(8,128)(2,1)S(1)}, bf16[2,512,512]{2,1,0:T(8,128)(2,1)}, u32[]{:S(2)}) copy-start(bf16[2,512,512]{2,1,0:T(8,128)(2,1)} %wc.9) | copy-start | bytes 3145732
  142.7 11.3 %copy-start.5 = (bf16[2,512,512]{2,1,0:T(8,128)(2,1)S(1)}, bf16[2,512,512]{2,1,0:T(8,128)(2,1)}, u32[]{:S(2)}) copy-start(bf16[2,512,512]{2,1,0:T(8,128)(2,1)} %wi.9) | copy-start | bytes 3145732
  142.7 11.3 %copy-start.6 = (bf16[2,512,512]{2,1,0:T(8,128)(2,1)S(1)}, bf16[2,512,512]{2,1,0:T(8,128)(2,1)}, u32[]{:S(2)}) copy-start(bf16[2,512,512]{2,1,0:T(8,128)(2,1)} %wo.9) | copy-start | bytes 3145732
  142.7 11.3 %copy-start.12 = (s32[4,1,384]{2,1,0:T(1,128)S(1)}, s32[4,1,384]{2,1,0:T(1,128)}, u32[]{:S(2)}) copy-start(s32[4,1,384]{2,1,0:T(1,128)} %broadcast_in_dim.201.rank_ref) | copy-start | bytes 18436
  142.7 11.3 %copy-start.13 = (s32[4,1,384]{2,1,0:T(1,128)S(1)}, s32[4,1,384]{2,1,0:T(1,128)}, u32[]{:S(2)}) copy-start(s32[4,1,384]{2,1,0:T(1,128)} %broadcast_in_dim.199.back_ref) | copy-start | bytes 18436
  146.5 15.2 %collective-permute-start.9 = (bf16[384,512]{1,0:T(8,128)(2,1)S(1)}, bf16[384,512]{1,0:T(8,128)(2,1)S(1)}, u32[]{:S(2)}, u32[]{:S(2)}) collective-permute-start(bf16[384,512]{1,0:T(8,128)(2,1)S(1)} %slice_bitcast_fusion.2), channel_id=1, source_target_pairs={{0,24},{8,16},{16,8},{24,0},{1,25},{9,17},{17,9},{25,1},{2,26},{10... | collective-permute-start | bytes 1179656 | tf_op jit(solution)/shard_map/ppermute | solution.py:435
  159.3 44.8 %slice-start = ((s8[6291456]{0:T(1024)(128)(4,1)}), s8[4194304]{0:T(1024)(128)(4,1)S(1)}, s32[]{:S(2)}) async-start(s8[6291456]{0:T(1024)(128)(4,1)} %bitcast.50), calls=%async_computation.4 | async-start | bytes 8388608
  161.7 42.4 %slice-start.1 = ((s8[6291456]{0:T(1024)(128)(4,1)}), s8[2097152]{0:T(1024)(128)(4,1)S(1)}, s32[]{:S(2)}) async-start(s8[6291456]{0:T(1024)(128)(4,1)} %bitcast.50), calls=%async_computation.5 | async-start | bytes 4194304
  214.6 41.0 %copy-start.9 = (bf16[2,512,512]{2,1,0:T(8,128)(2,1)S(1)}, bf16[2,512,512]{2,1,0:T(8,128)(2,1)}, u32[]{:S(2)}) copy-start(bf16[2,512,512]{2,1,0:T(8,128)(2,1)} %wd.1) | copy-start | bytes 3145732
  214.7 41.0 %copy-start.10 = (bf16[2,512,512]{2,1,0:T(8,128)(2,1)S(1)}, bf16[2,512,512]{2,1,0:T(8,128)(2,1)}, u32[]{:S(2)}) copy-start(bf16[2,512,512]{2,1,0:T(8,128)(2,1)} %we.1) | copy-start | bytes 3145732
  214.7 41.0 %copy-start.11 = (bf16[2,512,512]{2,1,0:T(8,128)(2,1)S(1)}, bf16[2,512,512]{2,1,0:T(8,128)(2,1)}, u32[]{:S(2)}) copy-start(bf16[2,512,512]{2,1,0:T(8,128)(2,1)} %wl.1) | copy-start | bytes 3145732
  (11 other events, 19.3 us)

commit v9 on v8

--- a/solution.py
+++ b/solution.py
@@ -108,8 +108,8 @@
 
 
 def row_parts(rows):
-    half = rows // 2
-    return [slice(0, half), slice(half, rows)]
+    size = rows // 3 if rows % 48 == 0 else rows // 2
+    return [slice(start, start + size) for start in range(0, rows, size)]
 
 
 def front_kernel(own, count, where_ref, cur_ref, back_ref, rank_ref, wm, wr, wc, wi, wo, *refs):

time: 264 us -> 263 us (level)
  no operation moved by 1% of the time
where the time goes in v9:
time: 263 us; the launch traced here: 262 us
  blocking collectives  81.1 us (31%)
  waiting for transfers between devices  72.5 us (28%)
  Pallas kernels  68.6 us (26%)
  starting transfers between devices  23.2 us (9%)
  local copies, waits for them, and re-layouts  13.2 us (5%)
  other arithmetic  3.24 us (1%)
    all_to_all x1, blocking collectives, tiled_local(): returned = lax.all_to_all(mixed, ('wide', 'narrow'), 0, 0, tiled=True)  40.9 us
    all_to_all x1, blocking collectives, swap(): return lax.all_to_all(values, 'narrow', 0, 0, tiled=True)  40.3 us
    all_to_all x1, waiting for transfers between devices, tiled_local(): returned = lax.all_to_all(mixed, ('wide', 'narrow'), 0, 0, tiled=True)  26.1 us
    pallas_call x5, Pallas kernels, run_front(): pl.pallas_call(functools.partial(front_kernel, own, count), grid_spec=plt...  25.1 us
    all_to_all x1, waiting for transfers between devices, swap(): return lax.all_to_all(values, 'narrow', 0, 0, tiled=True)  25 us
    pallas_call x2, Pallas kernels, run_mix(): pl.pallas_call(mix_kernel, grid=(devices // PAIR,), in_specs=[smem, smem,...  22.2 us
    ppermute x9, waiting for transfers between devices, shift(): return lax.ppermute(values, 'wide', [(i, i ^ offset) for i in range(wide)])  16.4 us
    pallas_call x3, Pallas kernels, run_back(): pl.pallas_call(back_kernel, grid_spec=pltpu.PrefetchScalarGridSpec(num_sc...  14.3 us
  transfers between devices with their start and end apart: 14, of which 10 were waited for; matrix products, arithmetic and copies ran while one was open for 2% of the time, Pallas kernels for 9%

profile of v9, /device:TPU:0, one launch (start us, length us, event | category | flops | bytes accessed | tf_op | source)
XLA Modules:
  0.0 262.4 jit_solution(7958759986921565374)
XLA Ops:
  0.8 1.3 dynamic-slice_bitcast_fusion
  3.1 4.1 %collective-permute-start.3 = (bf16[1,48,1088]{2,1,0:T(8,128)(2,1)S(1)}, bf16[1,48,1088]{2,1,0:T(8,128)(2,1)S(1)}, u32[]{:S(2)}, u32[]{:S(2)}) collective-permute-start(bf16[1,48,1088]{2,1,0:T(8,128)(2,1)S(1)} %maximum_bitcast_fusion), channel_id=1, source_target_pairs={{0,4},{1,5},{2,6},{3,7},{4,0},{5,1},{6,2},{7,3},{8,12},{9,13},{10,... | collective-permute-start | bytes 313352 | tf_op jit(solution)/shard_map/ppermute | solution.py:455
  7.2 2.4 collective-permute-start
  11.9 5.3 %front.5 = (bf16[4,384,512]{2,1,0:T(8,128)(2,1)}, bf16[8,4,192,128]{3,2,1,0:T(8,128)(2,1)}) custom-call(s32[1]{0:T(128)} %bitcast.56, bf16[4,384,512]{2,1,0:T(8,128)(2,1)} %bitcast.58, s32[4,1,384]{2,1,0:T(1,128)} %broadcast_in_dim.199.back_ref, s32[4,1,384]{2,1,0:T(1,128)} %broadcast_in_dim.201.rank_ref, bf16[2,512,512]{2,1,0:T(8,128)(2,1)} %wm.9, ...), custom_call_target="tpu_custom_call" | custom-call | flops 1207959552 | bytes 1572864 | tf_op jit(solution)/shard_map/front/pallas_call | solution.py:293
  17.3 1.6 collective-permute-start.4
  19.7 3.7 %collective-permute-done.4 = bf16[2,48,1088]{2,1,0:T(8,128)(2,1)S(1)} collective-permute-done((bf16[2,48,1088]{2,1,0:T(8,128)(2,1)S(1)}, bf16[2,48,1088]{2,1,0:T(8,128)(2,1)S(1)}, u32[]{:S(2)}, u32[]{:S(2)}) %collective-permute-start.4) | collective-permute-done | bytes 208928 | tf_op jit(solution)/shard_map/ppermute | solution.py:455
  23.5 3.8 %collective-permute-done.1.refs_1_ = bf16[384,512]{1,0:T(8,128)(2,1)S(1)} collective-permute-done((bf16[384,512]{1,0:T(8,128)(2,1)S(1)}, bf16[384,512]{1,0:T(8,128)(2,1)S(1)}, u32[]{:S(2)}, u32[]{:S(2)}) %collective-permute-start.1) | collective-permute-done | bytes 393248 | tf_op jit(solution)/shard_map/ppermute | solution.py:435
  28.0 10.5 %front.6 = (bf16[4,384,512]{2,1,0:T(8,128)(2,1)}, bf16[8,4,192,128]{3,2,1,0:T(8,128)(2,1)}) custom-call(s32[3]{0:T(128)} %slice.52.where_ref, bf16[4,384,512]{2,1,0:T(8,128)(2,1)} %bitcast.59, s32[4,1,384]{2,1,0:T(1,128)} %broadcast_in_dim.199.back_ref, s32[4,1,384]{2,1,0:T(1,128)} %broadcast_in_dim.201.rank_ref, ...), custom_call_target="tpu_custom_call", output_to_operand_aliasing={{0}: (12, {}), {1}: (13, {})} | custom-call | flops 3623878656 | bytes 4718592 | tf_op jit(solution)/shard_map/front/pallas_call | solution.py:293
  38.5 3.6 %all-to-all-start = ((bf16[8,4,192,128]{3,2,1,0:T(8,128)(2,1)}), bf16[8,4,192,128]{3,2,1,0:T(8,128)(2,1)S(1)}, u32[]{:S(2)}, u32[]{:S(2)}) async-start(bf16[8,4,192,128]{3,2,1,0:T(8,128)(2,1)} %get-tuple-element.43), calls=%async_computation | async-start | bytes 3145728 | tf_op jit(solution)/shard_map/all_to_all | solution.py:439
  42.9 1.3 collective-permute-done.5
  44.7 7.0 %tables.1 = (s32[8,4,1,384]{3,2,1,0:T(1,128)S(1)}, bf16[8,6,256,256]{3,2,1,0:T(8,128)(2,1)S(1)}) custom-call(s32[8]{0:T(128)S(1)} %select_reduce_fusion.9.places_ref, s32[4]{0:T(128)S(1)} %copy-done.15, s32[4]{0:T(128)S(1)} %select_reduce_fusion.10.position_ref, s32[8,4,1,384]{3,2,1,0:T(1,128)S(1)} %broadcast_in_dim_reshape.2.entry_ref, ...), custom_call_target="tpu_custom_call" | custom-call | bytes 25165824 | tf_op jit(solution)/shard_map/tables/pallas_call | solution.py:356
  51.7 2.7 %copy-done = bf16[8,6,256,256]{3,2,1,0:T(8,128)(2,1)} copy-done((bf16[8,6,256,256]{3,2,1,0:T(8,128)(2,1)}, bf16[8,6,256,256]{3,2,1,0:T(8,128)(2,1)S(1)}, u32[]{:S(2)}) %copy-start) | copy-done | bytes 6291480
  54.9 25.0 %all-to-all-done.recv_ref = bf16[8,4,192,128]{3,2,1,0:T(8,128)(2,1)S(1)} async-done(((bf16[8,4,192,128]{3,2,1,0:T(8,128)(2,1)}), bf16[8,4,192,128]{3,2,1,0:T(8,128)(2,1)S(1)}, u32[]{:S(2)}, u32[]{:S(2)}) %all-to-all-start) | async-done | bytes 1572896 | tf_op jit(solution)/shard_map/all_to_all | solution.py:439
  79.9 2.8 %copy-done.1 = bf16[8,6,256,256]{3,2,1,0:T(8,128)(2,1)S(1)} copy-done((bf16[8,6,256,256]{3,2,1,0:T(8,128)(2,1)S(1)}, bf16[8,6,256,256]{3,2,1,0:T(8,128)(2,1)}, u32[]{:S(2)}) %copy-start.1) | copy-done | bytes 6291480
  82.6 11.7 %mix.2 = bf16[4,8,192,128]{3,2,1,0:T(8,128)(2,1)} custom-call(s32[8,8]{1,0:T(8,128)S(1)} %get-tuple-element.58.owner_ref, s32[8,8]{1,0:T(8,128)S(1)} %get-tuple-element.57.place_ref, s32[4]{0:T(128)S(1)} %copy-done.15, bf16[8,4,192,128]{3,2,1,0:T(8,128)(2,1)S(1)} %all-to-all-done.recv_ref, s32[8,4,1,384]{3,2,1,0:T(1,128)S(1)} %get-tuple-element.44.rank_ref, ...), custom_call_target="tpu_custom_call" | custom-call | flops 1509949440 | bytes 18874368 | tf_op jit(solution)/shard_map/mix/pallas_call | solution.py:386
  94.3 2.9 %all-to-all-start.1 = ((bf16[32,192,128]{2,1,0:T(8,128)(2,1)}), bf16[32,192,128]{2,1,0:T(8,128)(2,1)S(1)}, u32[]{:S(2)}, u32[]{:S(2)}) async-start(bf16[32,192,128]{2,1,0:T(8,128)(2,1)} %bitcast.7), calls=%async_computation.1 | async-start | bytes 3145728 | tf_op jit(solution)/shard_map/all_to_all | solution.py:530
  97.3 2.6 collective-permute-start.6
  100.9 6.6 %collective-permute-done.6 = s32[384]{0:T(512)S(1)} collective-permute-done((s32[384]{0:T(512)S(1)}, s32[384]{0:T(512)S(1)}, u32[]{:S(2)}, u32[]{:S(2)}) %collective-permute-start.6) | collective-permute-done | bytes 1568 | tf_op jit(solution)/shard_map/ppermute | solution.py:435
  109.8 26.1 %all-to-all-done.1 = bf16[32,192,128]{2,1,0:T(8,128)(2,1)S(1)} async-done(((bf16[32,192,128]{2,1,0:T(8,128)(2,1)}), bf16[32,192,128]{2,1,0:T(8,128)(2,1)S(1)}, u32[]{:S(2)}, u32[]{:S(2)}) %all-to-all-start.1) | async-done | bytes 1572896 | tf_op jit(solution)/shard_map/all_to_all | solution.py:530
  135.9 1.4 copy-done.7
  137.3 3.5 %back.4.cur_ref = bf16[2,384,512]{2,1,0:T(8,128)(2,1)S(1)} custom-call(s32[2]{0:T(128)S(1)} %get-tuple-element.77.from_ref, s32[2]{0:T(128)S(1)} %iota.77.to_ref, bf16[4,384,512]{2,1,0:T(8,128)(2,1)S(1)} %copy-done.7, bf16[4,8,192,128]{3,2,1,0:T(8,128)(2,1)S(1)} %bitcast.52, s32[4,1,384]{2,1,0:T(1,128)S(1)} %broadcast_in_dim.220.rank_ref, ...), custom_call_target="tpu_custom_call" | custom-call | flops 1610612736 | bytes 2359296 | tf_op jit(solution)/shard_map/back/pallas_call | solution.py:327
  142.3 3.5 %back.3.cur_ref = bf16[2,384,512]{2,1,0:T(8,128)(2,1)S(1)} custom-call(s32[2]{0:T(128)S(1)} %get-tuple-element.78.from_ref, s32[2]{0:T(128)S(1)} %iota.73.to_ref, bf16[4,384,512]{2,1,0:T(8,128)(2,1)S(1)} %copy-done.8, bf16[4,8,192,128]{3,2,1,0:T(8,128)(2,1)S(1)} %bitcast.53, s32[4,1,384]{2,1,0:T(1,128)S(1)} %broadcast_in_dim.220.rank_ref, ...), custom_call_target="tpu_custom_call" | custom-call | flops 1610612736 | bytes 2359296 | tf_op jit(solution)/shard_map/back/pallas_call | solution.py:327
  145.8 2.3 collective-permute-start.9
  148.1 4.0 %collective-permute-done.11.refs_1_ = bf16[384,512]{1,0:T(8,128)(2,1)S(1)} collective-permute-done((bf16[384,512]{1,0:T(8,128)(2,1)S(1)}, bf16[384,512]{1,0:T(8,128)(2,1)S(1)}, u32[]{:S(2)}, u32[]{:S(2)}) %collective-permute-start.11) | collective-permute-done | bytes 393248 | tf_op jit(solution)/shard_map/ppermute | solution.py:435
  152.1 1.4 collective-permute-done.10.refs_0_
  153.5 5.2 %front.7 = (bf16[4,384,512]{2,1,0:T(8,128)(2,1)S(1)}, bf16[8,4,192,128]{3,2,1,0:T(8,128)(2,1)S(1)}) custom-call(s32[2]{0:T(128)S(1)} %iota.76.where_ref, bf16[2,384,512]{2,1,0:T(8,128)(2,1)S(1)} %back.4.cur_ref, s32[4,1,384]{2,1,0:T(1,128)S(1)} %copy-done.13, s32[4,1,384]{2,1,0:T(1,128)S(1)} %copy-done.12, bf16[2,512,512]{2,1,0:T(8,128)(2,1)S(1)} %copy-done.2, ...), custom_call_target="tpu_custom_call" | custom-call | flops 2415919104 | bytes 3145728 | tf_op jit(solution)/shard_map/front/pallas_call | solution.py:293
  158.8 2.0 front.8
  161.3 2.1 front.9
  163.3 40.3 %all_to_all.20.recv_ref = bf16[8,4,192,128]{3,2,1,0:T(8,128)(2,1)S(1)} all-to-all(bf16[8,4,192,128]{3,2,1,0:T(8,128)(2,1)S(1)} %get-tuple-element.56), channel_id=1, replica_groups=mesh['wide'=4,'narrow'=8] {'narrow'}, dimensions={0} | all-to-all | bytes 3145728 | tf_op jit(solution)/shard_map/all_to_all | solution.py:439
  203.6 10.6 %mix.3 = bf16[4,8,192,128]{3,2,1,0:T(8,128)(2,1)S(1)} custom-call(s32[8,8]{1,0:T(8,128)S(1)} %get-tuple-element.58.owner_ref, s32[8,8]{1,0:T(8,128)S(1)} %get-tuple-element.57.place_ref, s32[4]{0:T(128)S(1)} %copy-done.15, bf16[8,4,192,128]{3,2,1,0:T(8,128)(2,1)S(1)} %all_to_all.20.recv_ref, s32[8,4,1,384]{3,2,1,0:T(1,128)S(1)} %get-tuple-element.44.rank_ref, ...), custom_call_target="tpu_custom_call" | custom-call | flops 1509949440 | bytes 18874368 | tf_op jit(solution)/shard_map/mix/pallas_call | solution.py:386
  214.2 40.9 %all_to_all.21 = bf16[32,192,128]{2,1,0:T(8,128)(2,1)S(1)} all-to-all(bf16[32,192,128]{2,1,0:T(8,128)(2,1)S(1)} %bitcast.54), channel_id=1, replica_groups=mesh['wide'=4,'narrow'=8] {'wide','narrow'}, dimensions={0} | all-to-all | bytes 3145728 | tf_op jit(solution)/shard_map/all_to_all | solution.py:530
  255.1 7.3 %back.5 = bf16[4,384,512]{2,1,0:T(8,128)(2,1)} custom-call(s32[4]{0:T(128)S(1)} %copy-done.15, s32[4]{0:T(128)S(1)} %copy-done.15, bf16[4,384,512]{2,1,0:T(8,128)(2,1)S(1)} %get-tuple-element.55.second_ref, bf16[4,8,192,128]{3,2,1,0:T(8,128)(2,1)S(1)} %bitcast.55, s32[4,1,384]{2,1,0:T(1,128)S(1)} %broadcast_in_dim.220.rank_ref, ...), custom_call_target="tpu_custom_call" | custom-call | flops 3221225472 | bytes 4718592 | tf_op jit(solution)/shard_map/back/pallas_call | solution.py:327
  (121 shorter events, 12.6 us)
Async XLA Ops:
  0.0 3.1 %copy-start.16 = (bf16[48,1024]{1,0:T(8,128)(2,1)S(1)}, bf16[48,1024]{1,0:T(8,128)(2,1)}, u32[]{:S(2)}) copy-start(bf16[48,1024]{1,0:T(8,128)(2,1)} %param.20) | copy-start | bytes 294916
  0.7 10.0 %copy-start.14 = (s32[4]{0:T(128)}, s32[4]{0:T(128)S(1)}, u32[]{:S(2)}) copy-start(s32[4]{0:T(128)S(1)} %broadcast_xor_fusion.order_ref.from_ref.to_ref) | copy-start | bytes 52
  3.1 14.1 %collective-permute-start.3 = (bf16[1,48,1088]{2,1,0:T(8,128)(2,1)S(1)}, bf16[1,48,1088]{2,1,0:T(8,128)(2,1)S(1)}, u32[]{:S(2)}, u32[]{:S(2)}) collective-permute-start(bf16[1,48,1088]{2,1,0:T(8,128)(2,1)S(1)} %maximum_bitcast_fusion), channel_id=1, source_target_pairs={{0,4},{1,5},{2,6},{3,7},{4,0},{5,1},{6,2},{7,3},{8,12},{9,13},{10,... | collective-permute-start | bytes 313352 | tf_op jit(solution)/shard_map/ppermute | solution.py:455
  7.2 16.2 %collective-permute-start = (bf16[384,512]{1,0:T(8,128)(2,1)S(1)}, bf16[384,512]{1,0:T(8,128)(2,1)S(1)}, u32[]{:S(2)}, u32[]{:S(2)}) collective-permute-start(bf16[384,512]{1,0:T(8,128)(2,1)S(1)} %get-tuple-element.33), channel_id=1, source_target_pairs={{0,24},{8,16},{16,8},{24,0},{1,25},{9,17},{17,9},{25,1},{2,26},{10... | collective-permute-start | bytes 1179656 | tf_op jit(solution)/shard_map/ppermute | solution.py:435
  9.7 17.6 %collective-permute-start.1 = (bf16[384,512]{1,0:T(8,128)(2,1)S(1)}, bf16[384,512]{1,0:T(8,128)(2,1)S(1)}, u32[]{:S(2)}, u32[]{:S(2)}) collective-permute-start(bf16[384,512]{1,0:T(8,128)(2,1)S(1)} %get-tuple-element.34), channel_id=1, source_target_pairs={{0,8},{8,0},{16,24},{24,16},{1,9},{9,1},{17,25},{25,17},{2,10},{10... | collective-permute-start | bytes 1179656 | tf_op jit(solution)/shard_map/ppermute | solution.py:435
  10.2 17.0 %collective-permute-start.2 = (bf16[384,512]{1,0:T(8,128)(2,1)S(1)}, bf16[384,512]{1,0:T(8,128)(2,1)}, u32[]{:S(2)}, u32[]{:S(2)}) collective-permute-start(bf16[384,512]{1,0:T(8,128)(2,1)S(1)} %get-tuple-element.35), channel_id=1, source_target_pairs={{0,16},{8,24},{16,0},{24,8},{1,17},{9,25},{17,1},{25,9},{2,18},{10... | collective-permute-start | bytes 1179656 | tf_op jit(solution)/shard_map/ppermute | solution.py:435
  11.9 7.0 %copy-start.15 = (s32[4]{0:T(128)S(1)}, s32[4]{0:T(128)}, u32[]{:S(2)}) copy-start(s32[4]{0:T(128)} %copy-done.14) | copy-start | bytes 52
  11.9 7.6 %copy-start.23 = (s32[8]{0:T(128)S(1)}, s32[8]{0:T(128)}, u32[]{:S(2)}) copy-start(s32[8]{0:T(128)} %constant.80.clone) | copy-start | bytes 100
  17.3 6.1 %collective-permute-start.4 = (bf16[2,48,1088]{2,1,0:T(8,128)(2,1)S(1)}, bf16[2,48,1088]{2,1,0:T(8,128)(2,1)S(1)}, u32[]{:S(2)}, u32[]{:S(2)}) collective-permute-start(bf16[2,48,1088]{2,1,0:T(8,128)(2,1)S(1)} %pad_maximum_fusion.2), channel_id=1, source_target_pairs={{0,2},{1,3},{2,0},{3,1},{4,6},{5,7},{6,4},{7,5},{8,10},{9,11},{10,... | collective-permute-start | bytes 626696 | tf_op jit(solution)/shard_map/ppermute | solution.py:455
  23.5 3.8 %copy-start.20 = (bf16[384,512]{1,0:T(8,128)(2,1)}, bf16[384,512]{1,0:T(8,128)(2,1)S(1)}, u32[]{:S(2)}) copy-start(bf16[384,512]{1,0:T(8,128)(2,1)S(1)} %collective-permute-done.refs_0_) | copy-start | bytes 1179652
  38.5 3.6 %copy-start.22 = (s32[4]{0:T(128)S(1)}, s32[4]{0:T(128)}, u32[]{:S(2)}) copy-start(s32[4]{0:T(128)} %constant.79.clone) | copy-start | bytes 52
  38.5 41.3 %all-to-all-start = ((bf16[8,4,192,128]{3,2,1,0:T(8,128)(2,1)}), bf16[8,4,192,128]{3,2,1,0:T(8,128)(2,1)S(1)}, u32[]{:S(2)}, u32[]{:S(2)}) async-start(bf16[8,4,192,128]{3,2,1,0:T(8,128)(2,1)} %get-tuple-element.43), calls=%async_computation | async-start | bytes 3145728 | tf_op jit(solution)/shard_map/all_to_all | solution.py:439
  42.3 1.9 collective-permute-start.5
  94.3 41.6 %all-to-all-start.1 = ((bf16[32,192,128]{2,1,0:T(8,128)(2,1)}), bf16[32,192,128]{2,1,0:T(8,128)(2,1)S(1)}, u32[]{:S(2)}, u32[]{:S(2)}) async-start(bf16[32,192,128]{2,1,0:T(8,128)(2,1)} %bitcast.7), calls=%async_computation.1 | async-start | bytes 3145728 | tf_op jit(solution)/shard_map/all_to_all | solution.py:530
  97.3 10.2 %collective-permute-start.6 = (s32[384]{0:T(512)S(1)}, s32[384]{0:T(512)S(1)}, u32[]{:S(2)}, u32[]{:S(2)}) collective-permute-start(s32[384]{0:T(512)S(1)} %get-tuple-element.59), channel_id=1, source_target_pairs={{0,24},{8,16},{16,8},{24,0},{1,25},{9,17},{17,9},{25,1},{2,26},{10... | collective-permute-start | bytes 4616 | tf_op jit(solution)/shard_map/ppermute | solution.py:435
  99.8 7.6 %collective-permute-start.8 = (s32[384]{0:T(512)S(1)}, s32[384]{0:T(512)S(1)}, u32[]{:S(2)}, u32[]{:S(2)}) collective-permute-start(s32[384]{0:T(512)S(1)} %get-tuple-element.60), channel_id=1, source_target_pairs={{0,16},{8,24},{16,0},{24,8},{1,17},{9,25},{17,1},{25,9},{2,18},{10... | collective-permute-start | bytes 4616 | tf_op jit(solution)/shard_map/ppermute | solution.py:435
  100.4 7.3 %collective-permute-start.7 = (s32[384]{0:T(512)S(1)}, s32[384]{0:T(512)S(1)}, u32[]{:S(2)}, u32[]{:S(2)}) collective-permute-start(s32[384]{0:T(512)S(1)} %get-tuple-element.61), channel_id=1, source_target_pairs={{0,8},{8,0},{16,24},{24,16},{1,9},{9,1},{17,25},{25,17},{2,10},{10... | collective-permute-start | bytes 4616 | tf_op jit(solution)/shard_map/ppermute | solution.py:435
  140.9 11.2 %collective-permute-start.11 = (bf16[384,512]{1,0:T(8,128)(2,1)S(1)}, bf16[384,512]{1,0:T(8,128)(2,1)S(1)}, u32[]{:S(2)}, u32[]{:S(2)}) collective-permute-start(bf16[384,512]{1,0:T(8,128)(2,1)S(1)} %get-tuple-element.70), channel_id=1, source_target_pairs={{0,16},{8,24},{16,0},{24,8},{1,17},{9,25},{17,1},{25,9},{2,18},{10... | collective-permute-start | bytes 1179656 | tf_op jit(solution)/shard_map/ppermute | solution.py:435
  141.5 12.0 %collective-permute-start.10 = (bf16[384,512]{1,0:T(8,128)(2,1)S(1)}, bf16[384,512]{1,0:T(8,128)(2,1)S(1)}, u32[]{:S(2)}, u32[]{:S(2)}) collective-permute-start(bf16[384,512]{1,0:T(8,128)(2,1)S(1)} %get-tuple-element.71), channel_id=1, source_target_pairs={{0,8},{8,0},{16,24},{24,16},{1,9},{9,1},{17,25},{25,17},{2,10},{10... | collective-permute-start | bytes 1179656 | tf_op jit(solution)/shard_map/ppermute | solution.py:435
  142.3 11.2 %copy-start.2 = (bf16[2,512,512]{2,1,0:T(8,128)(2,1)S(1)}, bf16[2,512,512]{2,1,0:T(8,128)(2,1)}, u32[]{:S(2)}) copy-start(bf16[2,512,512]{2,1,0:T(8,128)(2,1)} %wm.9) | copy-start | bytes 3145732
  142.3 11.2 %copy-start.3 = (bf16[2,512,512]{2,1,0:T(8,128)(2,1)S(1)}, bf16[2,512,512]{2,1,0:T(8,128)(2,1)}, u32[]{:S(2)}) copy-start(bf16[2,512,512]{2,1,0:T(8,128)(2,1)} %wr.9) | copy-start | bytes 3145732
  142.3 11.2 %copy-start.4 = (bf16[2,512,512]{2,1,0:T(8,128)(2,1)S(1)}, bf16[2,512,512]{2,1,0:T(8,128)(2,1)}, u32[]{:S(2)}) copy-start(bf16[2,512,512]{2,1,0:T(8,128)(2,1)} %wc.9) | copy-start | bytes 3145732
  142.3 11.2 %copy-start.5 = (bf16[2,512,512]{2,1,0:T(8,128)(2,1)S(1)}, bf16[2,512,512]{2,1,0:T(8,128)(2,1)}, u32[]{:S(2)}) copy-start(bf16[2,512,512]{2,1,0:T(8,128)(2,1)} %wi.9) | copy-start | bytes 3145732
  142.3 11.3 %copy-start.6 = (bf16[2,512,512]{2,1,0:T(8,128)(2,1)S(1)}, bf16[2,512,512]{2,1,0:T(8,128)(2,1)}, u32[]{:S(2)}) copy-start(bf16[2,512,512]{2,1,0:T(8,128)(2,1)} %wo.9) | copy-start | bytes 3145732
  142.3 11.3 %copy-start.12 = (s32[4,1,384]{2,1,0:T(1,128)S(1)}, s32[4,1,384]{2,1,0:T(1,128)}, u32[]{:S(2)}) copy-start(s32[4,1,384]{2,1,0:T(1,128)} %broadcast_in_dim.201.rank_ref) | copy-start | bytes 18436
  142.3 11.3 %copy-start.13 = (s32[4,1,384]{2,1,0:T(1,128)S(1)}, s32[4,1,384]{2,1,0:T(1,128)}, u32[]{:S(2)}) copy-start(s32[4,1,384]{2,1,0:T(1,128)} %broadcast_in_dim.199.back_ref) | copy-start | bytes 18436
  145.8 15.4 %collective-permute-start.9 = (bf16[384,512]{1,0:T(8,128)(2,1)S(1)}, bf16[384,512]{1,0:T(8,128)(2,1)S(1)}, u32[]{:S(2)}, u32[]{:S(2)}) collective-permute-start(bf16[384,512]{1,0:T(8,128)(2,1)S(1)} %slice_bitcast_fusion.2), channel_id=1, source_target_pairs={{0,24},{8,16},{16,8},{24,0},{1,25},{9,17},{17,9},{25,1},{2,26},{10... | collective-permute-start | bytes 1179656 | tf_op jit(solution)/shard_map/ppermute | solution.py:435
  158.7 44.9 %slice-start = ((s8[6291456]{0:T(1024)(128)(4,1)}), s8[4194304]{0:T(1024)(128)(4,1)S(1)}, s32[]{:S(2)}) async-start(s8[6291456]{0:T(1024)(128)(4,1)} %bitcast.50), calls=%async_computation.4 | async-start | bytes 8388608
  161.3 42.3 %slice-start.1 = ((s8[6291456]{0:T(1024)(128)(4,1)}), s8[2097152]{0:T(1024)(128)(4,1)S(1)}, s32[]{:S(2)}) async-start(s8[6291456]{0:T(1024)(128)(4,1)} %bitcast.50), calls=%async_computation.5 | async-start | bytes 4194304
  214.2 40.9 %copy-start.9 = (bf16[2,512,512]{2,1,0:T(8,128)(2,1)S(1)}, bf16[2,512,512]{2,1,0:T(8,128)(2,1)}, u32[]{:S(2)}) copy-start(bf16[2,512,512]{2,1,0:T(8,128)(2,1)} %wd.1) | copy-start | bytes 3145732
  214.2 40.9 %copy-start.10 = (bf16[2,512,512]{2,1,0:T(8,128)(2,1)S(1)}, bf16[2,512,512]{2,1,0:T(8,128)(2,1)}, u32[]{:S(2)}) copy-start(bf16[2,512,512]{2,1,0:T(8,128)(2,1)} %we.1) | copy-start | bytes 3145732
  214.2 40.9 %copy-start.11 = (bf16[2,512,512]{2,1,0:T(8,128)(2,1)S(1)}, bf16[2,512,512]{2,1,0:T(8,128)(2,1)}, u32[]{:S(2)}) copy-start(bf16[2,512,512]{2,1,0:T(8,128)(2,1)} %wl.1) | copy-start | bytes 3145732
  (11 other events, 19.3 us)

commit v10 on v9

--- a/solution.py
+++ b/solution.py
@@ -108,7 +108,7 @@
 
 
 def row_parts(rows):
-    size = rows // 3 if rows % 48 == 0 else rows // 2
+    size = rows // 4 if rows % 64 == 0 else rows // 2
     return [slice(start, start + size) for start in range(0, rows, size)]
 
 
@@ -120,9 +120,13 @@
     sources = ([cur_ref.at[0]] if own else []) + list(recv_refs)
     for index in range(count):
 
-        @pl.when(pl.program_id(0) == index)
-        def _():
+        def permute():
             reverse_ref[...] = dot(hot, sources[index][...]).astype(jnp.bfloat16)
+
+        if count == 1:
+            permute()
+        else:
+            pl.when(pl.program_id(0) == index)(permute)
 
     parts = row_parts(cur_ref.shape[1])
     current = [cur_ref[0, part, :] for part in parts]

time: 263 us -> 269 us (1.023)
  Pallas kernels: 68.6 us -> 76.3 us
    pallas_call x5, Pallas kernels: 25.1 us -> 29.5 us  [run_front(): pl.pallas_call(functools.partial(front_kernel, own, count), grid_spec=plt...]
    pallas_call x3, Pallas kernels: 14.3 us -> 17.5 us  [run_back(): pl.pallas_call(back_kernel, grid_spec=pltpu.PrefetchScalarGridSpec(num_sc...]
  transfers between devices with their start and end apart: 14 -> 14, of which waited for: 10 -> 8; matrix products, arithmetic and copies ran while one was open for 2% -> 2% of each run, Pallas kernels for 9% -> 10%
where the time goes in v10:
time: 269 us
  blocking collectives  81.5 us (30%)
  Pallas kernels  76.3 us (28%)
  waiting for transfers between devices  70.6 us (26%)
  starting transfers between devices  23.3 us (9%)
  local copies, waits for them, and re-layouts  13.2 us (5%)
  other arithmetic  3.24 us (1%)
    all_to_all x1, blocking collectives, tiled_local(): returned = lax.all_to_all(mixed, ('wide', 'narrow'), 0, 0, tiled=True)  41.3 us
    all_to_all x1, blocking collectives, swap(): return lax.all_to_all(values, 'narrow', 0, 0, tiled=True)  40.3 us
    pallas_call x5, Pallas kernels, run_front(): pl.pallas_call(functools.partial(front_kernel, own, count), grid_spec=plt...  29.5 us
    all_to_all x1, waiting for transfers between devices, tiled_local(): returned = lax.all_to_all(mixed, ('wide', 'narrow'), 0, 0, tiled=True)  26.3 us
    all_to_all x1, waiting for transfers between devices, swap(): return lax.all_to_all(values, 'narrow', 0, 0, tiled=True)  24.8 us
    pallas_call x2, Pallas kernels, run_mix(): pl.pallas_call(mix_kernel, grid=(devices // PAIR,), in_specs=[smem, smem,...  22.2 us
    pallas_call x3, Pallas kernels, run_back(): pl.pallas_call(back_kernel, grid_spec=pltpu.PrefetchScalarGridSpec(num_sc...  17.5 us
    ppermute x9, waiting for transfers between devices, shift(): return lax.ppermute(values, 'wide', [(i, i ^ offset) for i in range(wide)])  14.3 us
  transfers between devices with their start and end apart: 14, of which 8 were waited for; matrix products, arithmetic and copies ran while one was open for 2% of the time, Pallas kernels for 10%

profile of v10, /device:TPU:0, one launch (start us, length us, event | category | flops | bytes accessed | tf_op | source)
XLA Modules:
  0.0 268.7 jit_solution(6721487110843425890)
XLA Ops:
  0.8 1.3 dynamic-slice_bitcast_fusion
  3.1 4.1 %collective-permute-start.3 = (bf16[1,48,1088]{2,1,0:T(8,128)(2,1)S(1)}, bf16[1,48,1088]{2,1,0:T(8,128)(2,1)S(1)}, u32[]{:S(2)}, u32[]{:S(2)}) collective-permute-start(bf16[1,48,1088]{2,1,0:T(8,128)(2,1)S(1)} %maximum_bitcast_fusion), channel_id=1, source_target_pairs={{0,4},{1,5},{2,6},{3,7},{4,0},{5,1},{6,2},{7,3},{8,12},{9,13},{10,... | collective-permute-start | bytes 313352 | tf_op jit(solution)/shard_map/ppermute | solution.py:459
  7.2 2.4 collective-permute-start
  11.9 5.8 %front.5 = (bf16[4,384,512]{2,1,0:T(8,128)(2,1)}, bf16[8,4,192,128]{3,2,1,0:T(8,128)(2,1)}) custom-call(s32[1]{0:T(128)} %bitcast.56, bf16[4,384,512]{2,1,0:T(8,128)(2,1)} %bitcast.58, s32[4,1,384]{2,1,0:T(1,128)} %broadcast_in_dim.199.back_ref, s32[4,1,384]{2,1,0:T(1,128)} %broadcast_in_dim.201.rank_ref, bf16[2,512,512]{2,1,0:T(8,128)(2,1)} %wm.9, ...), custom_call_target="tpu_custom_call" | custom-call | flops 1207959552 | bytes 1572864 | tf_op jit(solution)/shard_map/front/pallas_call | solution.py:297
  17.8 1.6 collective-permute-start.4
  20.3 3.7 %collective-permute-done.4 = bf16[2,48,1088]{2,1,0:T(8,128)(2,1)S(1)} collective-permute-done((bf16[2,48,1088]{2,1,0:T(8,128)(2,1)S(1)}, bf16[2,48,1088]{2,1,0:T(8,128)(2,1)S(1)}, u32[]{:S(2)}, u32[]{:S(2)}) %collective-permute-start.4) | collective-permute-done | bytes 208928 | tf_op jit(solution)/shard_map/ppermute | solution.py:459
  24.0 3.2 %collective-permute-done.1.refs_1_ = bf16[384,512]{1,0:T(8,128)(2,1)S(1)} collective-permute-done((bf16[384,512]{1,0:T(8,128)(2,1)S(1)}, bf16[384,512]{1,0:T(8,128)(2,1)S(1)}, u32[]{:S(2)}, u32[]{:S(2)}) %collective-permute-start.1) | collective-permute-done | bytes 393248 | tf_op jit(solution)/shard_map/ppermute | solution.py:439
  28.0 12.2 %front.6 = (bf16[4,384,512]{2,1,0:T(8,128)(2,1)}, bf16[8,4,192,128]{3,2,1,0:T(8,128)(2,1)}) custom-call(s32[3]{0:T(128)} %slice.52.where_ref, bf16[4,384,512]{2,1,0:T(8,128)(2,1)} %bitcast.59, s32[4,1,384]{2,1,0:T(1,128)} %broadcast_in_dim.199.back_ref, s32[4,1,384]{2,1,0:T(1,128)} %broadcast_in_dim.201.rank_ref, ...), custom_call_target="tpu_custom_call", output_to_operand_aliasing={{0}: (12, {}), {1}: (13, {})} | custom-call | flops 3623878656 | bytes 4718592 | tf_op jit(solution)/shard_map/front/pallas_call | solution.py:297
  40.2 3.8 %all-to-all-start = ((bf16[8,4,192,128]{3,2,1,0:T(8,128)(2,1)}), bf16[8,4,192,128]{3,2,1,0:T(8,128)(2,1)S(1)}, u32[]{:S(2)}, u32[]{:S(2)}) async-start(bf16[8,4,192,128]{3,2,1,0:T(8,128)(2,1)} %get-tuple-element.43), calls=%async_computation | async-start | bytes 3145728 | tf_op jit(solution)/shard_map/all_to_all | solution.py:443
  44.5 1.5 collective-permute-done.5
  46.5 7.0 %tables.1 = (s32[8,4,1,384]{3,2,1,0:T(1,128)S(1)}, bf16[8,6,256,256]{3,2,1,0:T(8,128)(2,1)S(1)}) custom-call(s32[8]{0:T(128)S(1)} %select_reduce_fusion.9.places_ref, s32[4]{0:T(128)S(1)} %copy-done.15, s32[4]{0:T(128)S(1)} %select_reduce_fusion.10.position_ref, s32[8,4,1,384]{3,2,1,0:T(1,128)S(1)} %broadcast_in_dim_reshape.2.entry_ref, ...), custom_call_target="tpu_custom_call" | custom-call | bytes 25165824 | tf_op jit(solution)/shard_map/tables/pallas_call | solution.py:360
  53.5 2.7 copy-done
  56.7 24.8 %all-to-all-done.recv_ref = bf16[8,4,192,128]{3,2,1,0:T(8,128)(2,1)S(1)} async-done(((bf16[8,4,192,128]{3,2,1,0:T(8,128)(2,1)}), bf16[8,4,192,128]{3,2,1,0:T(8,128)(2,1)S(1)}, u32[]{:S(2)}, u32[]{:S(2)}) %all-to-all-start) | async-done | bytes 1572896 | tf_op jit(solution)/shard_map/all_to_all | solution.py:443
  81.5 2.8 %copy-done.1 = bf16[8,6,256,256]{3,2,1,0:T(8,128)(2,1)S(1)} copy-done((bf16[8,6,256,256]{3,2,1,0:T(8,128)(2,1)S(1)}, bf16[8,6,256,256]{3,2,1,0:T(8,128)(2,1)}, u32[]{:S(2)}) %copy-start.1) | copy-done | bytes 6291480
  84.3 11.7 %mix.2 = bf16[4,8,192,128]{3,2,1,0:T(8,128)(2,1)} custom-call(s32[8,8]{1,0:T(8,128)S(1)} %get-tuple-element.58.owner_ref, s32[8,8]{1,0:T(8,128)S(1)} %get-tuple-element.57.place_ref, s32[4]{0:T(128)S(1)} %copy-done.15, bf16[8,4,192,128]{3,2,1,0:T(8,128)(2,1)S(1)} %all-to-all-done.recv_ref, s32[8,4,1,384]{3,2,1,0:T(1,128)S(1)} %get-tuple-element.44.rank_ref, ...), custom_call_target="tpu_custom_call" | custom-call | flops 1509949440 | bytes 18874368 | tf_op jit(solution)/shard_map/mix/pallas_call | solution.py:390
  96.0 3.0 %all-to-all-start.1 = ((bf16[32,192,128]{2,1,0:T(8,128)(2,1)}), bf16[32,192,128]{2,1,0:T(8,128)(2,1)S(1)}, u32[]{:S(2)}, u32[]{:S(2)}) async-start(bf16[32,192,128]{2,1,0:T(8,128)(2,1)} %bitcast.7), calls=%async_computation.1 | async-start | bytes 3145728 | tf_op jit(solution)/shard_map/all_to_all | solution.py:534
  99.0 2.5 collective-permute-start.6
  102.6 6.5 %collective-permute-done.6 = s32[384]{0:T(512)S(1)} collective-permute-done((s32[384]{0:T(512)S(1)}, s32[384]{0:T(512)S(1)}, u32[]{:S(2)}, u32[]{:S(2)}) %collective-permute-start.6) | collective-permute-done | bytes 1568 | tf_op jit(solution)/shard_map/ppermute | solution.py:439
  111.3 26.3 %all-to-all-done.1 = bf16[32,192,128]{2,1,0:T(8,128)(2,1)S(1)} async-done(((bf16[32,192,128]{2,1,0:T(8,128)(2,1)}), bf16[32,192,128]{2,1,0:T(8,128)(2,1)S(1)}, u32[]{:S(2)}, u32[]{:S(2)}) %all-to-all-start.1) | async-done | bytes 1572896 | tf_op jit(solution)/shard_map/all_to_all | solution.py:534
  137.6 1.4 copy-done.7
  139.0 4.3 %back.4.cur_ref = bf16[2,384,512]{2,1,0:T(8,128)(2,1)S(1)} custom-call(s32[2]{0:T(128)S(1)} %get-tuple-element.77.from_ref, s32[2]{0:T(128)S(1)} %iota.77.to_ref, bf16[4,384,512]{2,1,0:T(8,128)(2,1)S(1)} %copy-done.7, bf16[4,8,192,128]{3,2,1,0:T(8,128)(2,1)S(1)} %bitcast.52, s32[4,1,384]{2,1,0:T(1,128)S(1)} %broadcast_in_dim.220.rank_ref, ...), custom_call_target="tpu_custom_call" | custom-call | flops 1610612736 | bytes 2359296 | tf_op jit(solution)/shard_map/back/pallas_call | solution.py:331
  144.8 4.3 %back.3.cur_ref = bf16[2,384,512]{2,1,0:T(8,128)(2,1)S(1)} custom-call(s32[2]{0:T(128)S(1)} %get-tuple-element.78.from_ref, s32[2]{0:T(128)S(1)} %iota.73.to_ref, bf16[4,384,512]{2,1,0:T(8,128)(2,1)S(1)} %copy-done.8, bf16[4,8,192,128]{3,2,1,0:T(8,128)(2,1)S(1)} %bitcast.53, s32[4,1,384]{2,1,0:T(1,128)S(1)} %broadcast_in_dim.220.rank_ref, ...), custom_call_target="tpu_custom_call" | custom-call | flops 1610612736 | bytes 2359296 | tf_op jit(solution)/shard_map/back/pallas_call | solution.py:331
  149.1 2.3 collective-permute-start.9
  151.4 3.2 %collective-permute-done.11.refs_1_ = bf16[384,512]{1,0:T(8,128)(2,1)S(1)} collective-permute-done((bf16[384,512]{1,0:T(8,128)(2,1)S(1)}, bf16[384,512]{1,0:T(8,128)(2,1)S(1)}, u32[]{:S(2)}, u32[]{:S(2)}) %collective-permute-start.11) | collective-permute-done | bytes 393248 | tf_op jit(solution)/shard_map/ppermute | solution.py:439
  154.6 1.4 collective-permute-done.10.refs_0_
  156.0 6.3 %front.7 = (bf16[4,384,512]{2,1,0:T(8,128)(2,1)S(1)}, bf16[8,4,192,128]{3,2,1,0:T(8,128)(2,1)S(1)}) custom-call(s32[2]{0:T(128)S(1)} %iota.76.where_ref, bf16[2,384,512]{2,1,0:T(8,128)(2,1)S(1)} %back.4.cur_ref, s32[4,1,384]{2,1,0:T(1,128)S(1)} %copy-done.13, s32[4,1,384]{2,1,0:T(1,128)S(1)} %copy-done.12, bf16[2,512,512]{2,1,0:T(8,128)(2,1)S(1)} %copy-done.2, ...), custom_call_target="tpu_custom_call" | custom-call | flops 2415919104 | bytes 3145728 | tf_op jit(solution)/shard_map/front/pallas_call | solution.py:297
  162.3 2.6 front.8
  164.9 2.6 front.9
  167.6 40.3 %all_to_all.20.recv_ref = bf16[8,4,192,128]{3,2,1,0:T(8,128)(2,1)S(1)} all-to-all(bf16[8,4,192,128]{3,2,1,0:T(8,128)(2,1)S(1)} %get-tuple-element.56), channel_id=1, replica_groups=mesh['wide'=4,'narrow'=8] {'narrow'}, dimensions={0} | all-to-all | bytes 3145728 | tf_op jit(solution)/shard_map/all_to_all | solution.py:443
  207.8 10.6 %mix.3 = bf16[4,8,192,128]{3,2,1,0:T(8,128)(2,1)S(1)} custom-call(s32[8,8]{1,0:T(8,128)S(1)} %get-tuple-element.58.owner_ref, s32[8,8]{1,0:T(8,128)S(1)} %get-tuple-element.57.place_ref, s32[4]{0:T(128)S(1)} %copy-done.15, bf16[8,4,192,128]{3,2,1,0:T(8,128)(2,1)S(1)} %all_to_all.20.recv_ref, s32[8,4,1,384]{3,2,1,0:T(1,128)S(1)} %get-tuple-element.44.rank_ref, ...), custom_call_target="tpu_custom_call" | custom-call | flops 1509949440 | bytes 18874368 | tf_op jit(solution)/shard_map/mix/pallas_call | solution.py:390
  218.4 41.3 %all_to_all.21 = bf16[32,192,128]{2,1,0:T(8,128)(2,1)S(1)} all-to-all(bf16[32,192,128]{2,1,0:T(8,128)(2,1)S(1)} %bitcast.54), channel_id=1, replica_groups=mesh['wide'=4,'narrow'=8] {'wide','narrow'}, dimensions={0} | all-to-all | bytes 3145728 | tf_op jit(solution)/shard_map/all_to_all | solution.py:534
  259.7 9.0 %back.5 = bf16[4,384,512]{2,1,0:T(8,128)(2,1)} custom-call(s32[4]{0:T(128)S(1)} %copy-done.15, s32[4]{0:T(128)S(1)} %copy-done.15, bf16[4,384,512]{2,1,0:T(8,128)(2,1)S(1)} %get-tuple-element.55.second_ref, bf16[4,8,192,128]{3,2,1,0:T(8,128)(2,1)S(1)} %bitcast.55, s32[4,1,384]{2,1,0:T(1,128)S(1)} %broadcast_in_dim.220.rank_ref, ...), custom_call_target="tpu_custom_call" | custom-call | flops 3221225472 | bytes 4718592 | tf_op jit(solution)/shard_map/back/pallas_call | solution.py:331
  (121 shorter events, 11.8 us)
Async XLA Ops:
  0.0 3.1 %copy-start.16 = (bf16[48,1024]{1,0:T(8,128)(2,1)S(1)}, bf16[48,1024]{1,0:T(8,128)(2,1)}, u32[]{:S(2)}) copy-start(bf16[48,1024]{1,0:T(8,128)(2,1)} %param.20) | copy-start | bytes 294916
  0.7 10.0 %copy-start.14 = (s32[4]{0:T(128)}, s32[4]{0:T(128)S(1)}, u32[]{:S(2)}) copy-start(s32[4]{0:T(128)S(1)} %broadcast_xor_fusion.order_ref.from_ref.to_ref) | copy-start | bytes 52
  3.1 14.7 %collective-permute-start.3 = (bf16[1,48,1088]{2,1,0:T(8,128)(2,1)S(1)}, bf16[1,48,1088]{2,1,0:T(8,128)(2,1)S(1)}, u32[]{:S(2)}, u32[]{:S(2)}) collective-permute-start(bf16[1,48,1088]{2,1,0:T(8,128)(2,1)S(1)} %maximum_bitcast_fusion), channel_id=1, source_target_pairs={{0,4},{1,5},{2,6},{3,7},{4,0},{5,1},{6,2},{7,3},{8,12},{9,13},{10,... | collective-permute-start | bytes 313352 | tf_op jit(solution)/shard_map/ppermute | solution.py:459
  7.2 16.8 %collective-permute-start = (bf16[384,512]{1,0:T(8,128)(2,1)S(1)}, bf16[384,512]{1,0:T(8,128)(2,1)S(1)}, u32[]{:S(2)}, u32[]{:S(2)}) collective-permute-start(bf16[384,512]{1,0:T(8,128)(2,1)S(1)} %get-tuple-element.33), channel_id=1, source_target_pairs={{0,24},{8,16},{16,8},{24,0},{1,25},{9,17},{17,9},{25,1},{2,26},{10... | collective-permute-start | bytes 1179656 | tf_op jit(solution)/shard_map/ppermute | solution.py:439
  9.7 17.6 %collective-permute-start.1 = (bf16[384,512]{1,0:T(8,128)(2,1)S(1)}, bf16[384,512]{1,0:T(8,128)(2,1)S(1)}, u32[]{:S(2)}, u32[]{:S(2)}) collective-permute-start(bf16[384,512]{1,0:T(8,128)(2,1)S(1)} %get-tuple-element.34), channel_id=1, source_target_pairs={{0,8},{8,0},{16,24},{24,16},{1,9},{9,1},{17,25},{25,17},{2,10},{10... | collective-permute-start | bytes 1179656 | tf_op jit(solution)/shard_map/ppermute | solution.py:439
  10.2 17.0 %collective-permute-start.2 = (bf16[384,512]{1,0:T(8,128)(2,1)S(1)}, bf16[384,512]{1,0:T(8,128)(2,1)}, u32[]{:S(2)}, u32[]{:S(2)}) collective-permute-start(bf16[384,512]{1,0:T(8,128)(2,1)S(1)} %get-tuple-element.35), channel_id=1, source_target_pairs={{0,16},{8,24},{16,0},{24,8},{1,17},{9,25},{17,1},{25,9},{2,18},{10... | collective-permute-start | bytes 1179656 | tf_op jit(solution)/shard_map/ppermute | solution.py:439
  11.9 7.5 %copy-start.15 = (s32[4]{0:T(128)S(1)}, s32[4]{0:T(128)}, u32[]{:S(2)}) copy-start(s32[4]{0:T(128)} %copy-done.14) | copy-start | bytes 52
  11.9 8.1 %copy-start.23 = (s32[8]{0:T(128)S(1)}, s32[8]{0:T(128)}, u32[]{:S(2)}) copy-start(s32[8]{0:T(128)} %constant.80.clone) | copy-start | bytes 100
  17.8 6.1 %collective-permute-start.4 = (bf16[2,48,1088]{2,1,0:T(8,128)(2,1)S(1)}, bf16[2,48,1088]{2,1,0:T(8,128)(2,1)S(1)}, u32[]{:S(2)}, u32[]{:S(2)}) collective-permute-start(bf16[2,48,1088]{2,1,0:T(8,128)(2,1)S(1)} %pad_maximum_fusion.2), channel_id=1, source_target_pairs={{0,2},{1,3},{2,0},{3,1},{4,6},{5,7},{6,4},{7,5},{8,10},{9,11},{10,... | collective-permute-start | bytes 626696 | tf_op jit(solution)/shard_map/ppermute | solution.py:459
  24.0 3.2 %copy-start.20 = (bf16[384,512]{1,0:T(8,128)(2,1)}, bf16[384,512]{1,0:T(8,128)(2,1)S(1)}, u32[]{:S(2)}) copy-start(bf16[384,512]{1,0:T(8,128)(2,1)S(1)} %collective-permute-done.refs_0_) | copy-start | bytes 1179652
  40.2 3.8 %copy-start.22 = (s32[4]{0:T(128)S(1)}, s32[4]{0:T(128)}, u32[]{:S(2)}) copy-start(s32[4]{0:T(128)} %constant.79.clone) | copy-start | bytes 52
  40.2 41.4 %all-to-all-start = ((bf16[8,4,192,128]{3,2,1,0:T(8,128)(2,1)}), bf16[8,4,192,128]{3,2,1,0:T(8,128)(2,1)S(1)}, u32[]{:S(2)}, u32[]{:S(2)}) async-start(bf16[8,4,192,128]{3,2,1,0:T(8,128)(2,1)} %get-tuple-element.43), calls=%async_computation | async-start | bytes 3145728 | tf_op jit(solution)/shard_map/all_to_all | solution.py:443
  44.1 1.9 collective-permute-start.5
  96.0 41.6 %all-to-all-start.1 = ((bf16[32,192,128]{2,1,0:T(8,128)(2,1)}), bf16[32,192,128]{2,1,0:T(8,128)(2,1)S(1)}, u32[]{:S(2)}, u32[]{:S(2)}) async-start(bf16[32,192,128]{2,1,0:T(8,128)(2,1)} %bitcast.7), calls=%async_computation.1 | async-start | bytes 3145728 | tf_op jit(solution)/shard_map/all_to_all | solution.py:534
  99.0 10.2 %collective-permute-start.6 = (s32[384]{0:T(512)S(1)}, s32[384]{0:T(512)S(1)}, u32[]{:S(2)}, u32[]{:S(2)}) collective-permute-start(s32[384]{0:T(512)S(1)} %get-tuple-element.59), channel_id=1, source_target_pairs={{0,24},{8,16},{16,8},{24,0},{1,25},{9,17},{17,9},{25,1},{2,26},{10... | collective-permute-start | bytes 4616 | tf_op jit(solution)/shard_map/ppermute | solution.py:439
  101.5 7.6 %collective-permute-start.8 = (s32[384]{0:T(512)S(1)}, s32[384]{0:T(512)S(1)}, u32[]{:S(2)}, u32[]{:S(2)}) collective-permute-start(s32[384]{0:T(512)S(1)} %get-tuple-element.60), channel_id=1, source_target_pairs={{0,16},{8,24},{16,0},{24,8},{1,17},{9,25},{17,1},{25,9},{2,18},{10... | collective-permute-start | bytes 4616 | tf_op jit(solution)/shard_map/ppermute | solution.py:439
  102.1 7.1 %collective-permute-start.7 = (s32[384]{0:T(512)S(1)}, s32[384]{0:T(512)S(1)}, u32[]{:S(2)}, u32[]{:S(2)}) collective-permute-start(s32[384]{0:T(512)S(1)} %get-tuple-element.61), channel_id=1, source_target_pairs={{0,8},{8,0},{16,24},{24,16},{1,9},{9,1},{17,25},{25,17},{2,10},{10... | collective-permute-start | bytes 4616 | tf_op jit(solution)/shard_map/ppermute | solution.py:439
  143.4 11.2 %collective-permute-start.11 = (bf16[384,512]{1,0:T(8,128)(2,1)S(1)}, bf16[384,512]{1,0:T(8,128)(2,1)S(1)}, u32[]{:S(2)}, u32[]{:S(2)}) collective-permute-start(bf16[384,512]{1,0:T(8,128)(2,1)S(1)} %get-tuple-element.70), channel_id=1, source_target_pairs={{0,16},{8,24},{16,0},{24,8},{1,17},{9,25},{17,1},{25,9},{2,18},{10... | collective-permute-start | bytes 1179656 | tf_op jit(solution)/shard_map/ppermute | solution.py:439
  144.0 12.0 %collective-permute-start.10 = (bf16[384,512]{1,0:T(8,128)(2,1)S(1)}, bf16[384,512]{1,0:T(8,128)(2,1)S(1)}, u32[]{:S(2)}, u32[]{:S(2)}) collective-permute-start(bf16[384,512]{1,0:T(8,128)(2,1)S(1)} %get-tuple-element.71), channel_id=1, source_target_pairs={{0,8},{8,0},{16,24},{24,16},{1,9},{9,1},{17,25},{25,17},{2,10},{10... | collective-permute-start | bytes 1179656 | tf_op jit(solution)/shard_map/ppermute | solution.py:439
  144.7 11.2 %copy-start.2 = (bf16[2,512,512]{2,1,0:T(8,128)(2,1)S(1)}, bf16[2,512,512]{2,1,0:T(8,128)(2,1)}, u32[]{:S(2)}) copy-start(bf16[2,512,512]{2,1,0:T(8,128)(2,1)} %wm.9) | copy-start | bytes 3145732
  144.7 11.2 %copy-start.3 = (bf16[2,512,512]{2,1,0:T(8,128)(2,1)S(1)}, bf16[2,512,512]{2,1,0:T(8,128)(2,1)}, u32[]{:S(2)}) copy-start(bf16[2,512,512]{2,1,0:T(8,128)(2,1)} %wr.9) | copy-start | bytes 3145732
  144.7 11.2 %copy-start.4 = (bf16[2,512,512]{2,1,0:T(8,128)(2,1)S(1)}, bf16[2,512,512]{2,1,0:T(8,128)(2,1)}, u32[]{:S(2)}) copy-start(bf16[2,512,512]{2,1,0:T(8,128)(2,1)} %wc.9) | copy-start | bytes 3145732
  144.7 11.2 %copy-start.5 = (bf16[2,512,512]{2,1,0:T(8,128)(2,1)S(1)}, bf16[2,512,512]{2,1,0:T(8,128)(2,1)}, u32[]{:S(2)}) copy-start(bf16[2,512,512]{2,1,0:T(8,128)(2,1)} %wi.9) | copy-start | bytes 3145732
  144.7 11.3 %copy-start.6 = (bf16[2,512,512]{2,1,0:T(8,128)(2,1)S(1)}, bf16[2,512,512]{2,1,0:T(8,128)(2,1)}, u32[]{:S(2)}) copy-start(bf16[2,512,512]{2,1,0:T(8,128)(2,1)} %wo.9) | copy-start | bytes 3145732
  144.7 11.3 %copy-start.12 = (s32[4,1,384]{2,1,0:T(1,128)S(1)}, s32[4,1,384]{2,1,0:T(1,128)}, u32[]{:S(2)}) copy-start(s32[4,1,384]{2,1,0:T(1,128)} %broadcast_in_dim.201.rank_ref) | copy-start | bytes 18436
  144.7 11.3 %copy-start.13 = (s32[4,1,384]{2,1,0:T(1,128)S(1)}, s32[4,1,384]{2,1,0:T(1,128)}, u32[]{:S(2)}) copy-start(s32[4,1,384]{2,1,0:T(1,128)} %broadcast_in_dim.199.back_ref) | copy-start | bytes 18436
  149.1 15.9 %collective-permute-start.9 = (bf16[384,512]{1,0:T(8,128)(2,1)S(1)}, bf16[384,512]{1,0:T(8,128)(2,1)S(1)}, u32[]{:S(2)}, u32[]{:S(2)}) collective-permute-start(bf16[384,512]{1,0:T(8,128)(2,1)S(1)} %slice_bitcast_fusion.2), channel_id=1, source_target_pairs={{0,24},{8,16},{16,8},{24,0},{1,25},{9,17},{17,9},{25,1},{2,26},{10... | collective-permute-start | bytes 1179656 | tf_op jit(solution)/shard_map/ppermute | solution.py:439
  162.3 45.5 %slice-start = ((s8[6291456]{0:T(1024)(128)(4,1)}), s8[4194304]{0:T(1024)(128)(4,1)S(1)}, s32[]{:S(2)}) async-start(s8[6291456]{0:T(1024)(128)(4,1)} %bitcast.50), calls=%async_computation.4 | async-start | bytes 8388608
  164.9 42.9 %slice-start.1 = ((s8[6291456]{0:T(1024)(128)(4,1)}), s8[2097152]{0:T(1024)(128)(4,1)S(1)}, s32[]{:S(2)}) async-start(s8[6291456]{0:T(1024)(128)(4,1)} %bitcast.50), calls=%async_computation.5 | async-start | bytes 4194304
  218.4 41.3 %copy-start.9 = (bf16[2,512,512]{2,1,0:T(8,128)(2,1)S(1)}, bf16[2,512,512]{2,1,0:T(8,128)(2,1)}, u32[]{:S(2)}) copy-start(bf16[2,512,512]{2,1,0:T(8,128)(2,1)} %wd.1) | copy-start | bytes 3145732
  218.4 41.3 %copy-start.10 = (bf16[2,512,512]{2,1,0:T(8,128)(2,1)S(1)}, bf16[2,512,512]{2,1,0:T(8,128)(2,1)}, u32[]{:S(2)}) copy-start(bf16[2,512,512]{2,1,0:T(8,128)(2,1)} %we.1) | copy-start | bytes 3145732
  218.4 41.3 %copy-start.11 = (bf16[2,512,512]{2,1,0:T(8,128)(2,1)S(1)}, bf16[2,512,512]{2,1,0:T(8,128)(2,1)}, u32[]{:S(2)}) copy-start(bf16[2,512,512]{2,1,0:T(8,128)(2,1)} %wl.1) | copy-start | bytes 3145732
  (11 other events, 19.3 us)
